TPU v7x, 512 devices: a whole 4x8x8 slice. The times are simulated.
512 devices in a mesh: dp: 8 (over y_lo, core), seq: 64 (over y_hi, x, z).
Axes of the slice: x: 4, y: 8 (y_hi: 2, y_lo: 4; y = y_hi * 4 + y_lo), z: 8, core: 2. Of those that a mesh axis runs over, the one named last changes fastest.
Arguments:
- query_key_value: bfloat16 [3, 8, 64, 128, 1152], P(None, 'dp', 'seq'), may hold values from -8 to 8
- out_weight: bfloat16 [768, 1152], P('seq'), may hold values from -0.1875 to 0.1875
- cotangent: bfloat16 [8, 64, 128, 768], P('dp', 'seq'), may hold values from -16 to 16
Outputs:
- projected: bfloat16 [8, 64, 128, 768], P('dp', 'seq')
- input_grads: bfloat16 [3, 8, 64, 128, 1152], P(None, 'dp', 'seq')
- weight_grad: float32 [768, 1152], P('seq')
All inputs are finite; a program needn't handle non-finite values.
Results may differ from a plain program's by a relative error of at most 0.007.
Values may be sent and summed in bfloat16 or wider, within the bound.
No kernel may reach another device: no remote copies, remote signals or barrier semaphores. Data moves between devices by JAX's collectives and lax.ppermute only.
A program may use at most 64 MiB of HBM per device.

v0:
```python
import math

import jax
import jax.numpy as jnp
from jax import lax
from jax.sharding import PartitionSpec as P

HEADS = 16
HEAD_DIM = 72


def by_heads(tensor):
    leading = tensor.shape
    return tensor.reshape(leading[0], leading[1], leading[3], HEADS, leading[4] // HEADS)


def temporal(query_in, key_in, value_in, grad_in):
    outline = query_in.shape
    inv_root = 1.0 / math.sqrt(HEAD_DIM)
    query_heads = by_heads(query_in)
    key_heads = by_heads(key_in)
    value_heads = by_heads(value_in)
    grad_heads = by_heads(grad_in)
    scores = (
        jnp.einsum("bqlhd,bklhd->blhqk", query_heads, key_heads, preferred_element_type=jnp.float32)
        * inv_root
    )
    weights = jax.nn.softmax(scores, axis=-1)
    rounded_weights = weights.astype(jnp.bfloat16)
    attended = jnp.einsum(
        "blhqk,bklhd->bqlhd", rounded_weights, value_heads, preferred_element_type=jnp.float32
    ).astype(jnp.bfloat16)
    grad_value = jnp.einsum(
        "blhqk,bqlhd->bklhd", rounded_weights, grad_heads, preferred_element_type=jnp.float32
    ).astype(jnp.bfloat16)
    grad_weights = jnp.einsum(
        "bqlhd,bklhd->blhqk", grad_heads, value_heads, preferred_element_type=jnp.float32
    )
    centred = grad_weights - jnp.sum(weights * grad_weights, axis=-1, keepdims=True)
    grad_scores = (weights * centred * inv_root).astype(jnp.bfloat16)
    grad_query = jnp.einsum(
        "blhqk,bklhd->bqlhd", grad_scores, key_heads, preferred_element_type=jnp.float32
    ).astype(jnp.bfloat16)
    grad_key = jnp.einsum(
        "blhqk,bqlhd->bklhd", grad_scores, query_heads, preferred_element_type=jnp.float32
    ).astype(jnp.bfloat16)
    return tuple(
        (member.reshape(outline) for member in (attended, grad_query, grad_key, grad_value))
    )


def project_rows(attended_rows, weight_full):
    return lax.dot_general(
        attended_rows, weight_full, (((1,), (1,)), ((), ())), preferred_element_type=jnp.float32
    ).astype(jnp.bfloat16)


def on_device(query_key_value, out_weight, cotangent):
    devices_seq = lax.axis_size("seq")
    groups = lax.axis_size("dp")
    samples_dev, frames_dev, spatial, model_width = query_key_value.shape[1:]
    out_cols = cotangent.shape[3]
    places = spatial // devices_seq
    weight_full = lax.all_gather(out_weight, "seq", axis=0, tiled=True)
    arranged = query_key_value.reshape(3, samples_dev, frames_dev, devices_seq, places, model_width)
    upstream_rows = cotangent.reshape(-1, out_cols)
    grad_attended = jnp.dot(upstream_rows, weight_full, preferred_element_type=jnp.float32).astype(
        jnp.bfloat16
    )
    grad_arranged = grad_attended.reshape(
        1, samples_dev, frames_dev, devices_seq, places, model_width
    )
    gathered = lax.all_to_all(arranged, "seq", split_axis=3, concat_axis=2, tiled=True)
    grad_part = lax.all_to_all(grad_arranged, "seq", split_axis=3, concat_axis=2, tiled=True)
    attended, grad_query, grad_key, grad_value = temporal(
        gathered[0], gathered[1], gathered[2], grad_part[0]
    )
    attended_places = attended[None]
    grads_places = jnp.stack([grad_query, grad_key, grad_value])
    attended_frames, grads_frames = (
        lax.all_to_all(attended_places, "seq", split_axis=2, concat_axis=3, tiled=True),
        lax.all_to_all(grads_places, "seq", split_axis=2, concat_axis=3, tiled=True),
    )
    attended_rows = attended_frames.reshape(-1, model_width)
    projected = project_rows(attended_rows, weight_full).reshape(
        samples_dev, frames_dev, spatial, out_cols
    )
    input_grads = grads_frames.reshape(3, samples_dev, frames_dev, spatial, model_width)
    token_count = samples_dev * frames_dev * spatial * devices_seq * groups
    factor = 1.0 / math.sqrt(token_count)
    local_share = lax.psum_scatter(
        lax.dot_general(
            upstream_rows,
            attended_rows,
            (((0,), (0,)), ((), ())),
            preferred_element_type=jnp.float32,
        ),
        "seq",
        scatter_dimension=0,
        tiled=True,
    )
    owned_rows = lax.psum(local_share, "dp")
    return (projected, input_grads, owned_rows * factor)


def solution(mesh):
    in_specs = (P(None, "dp", "seq", None, None), P("seq", None), P("dp", "seq", None, None))
    out_specs = (P("dp", "seq", None, None), P(None, "dp", "seq", None, None), P("seq", None))
    return jax.shard_map(
        on_device, mesh=mesh, in_specs=in_specs, out_specs=out_specs, check_vma=False
    )
```

profile of v0, /device:TPU:1, one launch (start us, length us, event | category | flops | bytes accessed | tf_op | source)
XLA Modules:
  0.0 1072.4 jit_solution(3273239022529231578)
XLA Ops:
  7.2 0.0 copy-start
  7.2 2.3 reshape.114
  9.5 1.5 copy.70
  11.0 19.6 %all-to-all-start = ((bf16[3,1,1,64,2,1152]{5,4,2,1,0,3:T(2,128)(2,1)}), bf16[3,1,1,64,2,1152]{5,4,2,1,0,3:T(2,128)(2,1)S(1)}, u32[]{:S(2)}, u32[]{:S(2)}) async-start(bf16[3,1,1,64,2,1152]{5,4,2,1,0,3:T(2,128)(2,1)} %copy.70), calls=%async_computation | async-start | bytes 1769472 | tf_op jit(solution)/shard_map/all_to_all | solution.py:73
  30.6 0.0 all-gather.3.cloned.1.call-start
  30.7 0.7 all-gather.3.cloned.1.call-update
  31.4 0.0 all-reduce.3.cloned.1.call-start
  31.4 21.9 %all-to-all-done = bf16[3,1,1,64,2,1152]{5,4,2,1,0,3:T(2,128)(2,1)S(1)} async-done(((bf16[3,1,1,64,2,1152]{5,4,2,1,0,3:T(2,128)(2,1)}), bf16[3,1,1,64,2,1152]{5,4,2,1,0,3:T(2,128)(2,1)S(1)}, u32[]{:S(2)}, u32[]{:S(2)}) %all-to-all-start) | async-done | bytes 884768 | tf_op jit(solution)/shard_map/all_to_all | solution.py:73
  53.4 0.6 fusion.47
  54.0 1.1 reshape.130
  55.0 0.0 copy-start.3
  55.1 1.1 reshape.131
  56.1 0.0 copy-start.4
  56.2 1.1 reshape.132
  57.2 1.6 fusion.48
  58.9 0.0 copy-done.3
  58.9 0.0 copy-done.4
  58.9 1.6 fusion.8
  60.5 0.3 copy.97
  60.8 0.9 reshape.126
  61.8 27.1 %all_to_all.16 = bf16[1,1,64,1,2,1152]{5,4,3,1,0,2:T(2,128)(2,1)S(1)} all-to-all(bf16[1,1,64,1,2,1152]{5,4,3,1,0,2:T(2,128)(2,1)S(1)} %reshape.126), channel_id=1, replica_groups=mesh['dp'=8,'seq'=64] {'seq'}, dimensions={2} | all-to-all | bytes 589824 | tf_op jit(solution)/shard_map/all_to_all | solution.py:81
  88.9 0.1 reshape.118
  89.0 0.0 copy-done
  89.0 2.5 convolution_bitcast_fusion
  91.5 0.0 all-reduce.3.cloned.1.call-update
  91.5 78.7 %all-gather.3.cloned.1.call-done = bf16[64,12,1152]{2,1,0:T(8,128)(2,1)} async-done(((bf16[1,12,1152]{2,1,0:T(8,128)(2,1)}), bf16[64,12,1152]{2,1,0:T(8,128)(2,1)}) %all-gather.3.cloned.1.call-update) | async-done | bytes 1769488 | tf_op jit(solution)/shard_map/all_gather | solution.py:64
  170.2 2.5 reshape.125
  172.8 0.4 convolution_convert_fusion
  173.2 0.1 reshape.121
  173.3 21.4 %all_to_all.17 = bf16[1,1,1,64,2,1152]{5,4,2,1,0,3:T(2,128)(2,1)} all-to-all(bf16[1,1,1,64,2,1152]{5,4,2,1,0,3:T(2,128)(2,1)S(1)} %bitcast.69), channel_id=1, replica_groups=mesh['dp'=8,'seq'=64] {'seq'}, dimensions={3} | all-to-all | bytes 589824 | tf_op jit(solution)/shard_map/all_to_all | solution.py:74
  194.7 1.9 reshape.133
  196.6 1.4 fusion.21
  198.0 3.8 fusion.9
  201.8 1.4 copy.86
  203.2 1.2 stack_reshape.9
  204.5 4.0 fusion.10
  208.4 1.4 copy.88
  209.8 1.3 stack_reshape.10
  211.1 1.6 fusion.11
  212.7 0.0 copy-start.1
  212.7 0.0 copy-start.2
  212.7 0.3 copy.90
  213.0 1.2 stack_reshape.11
  214.3 0.0 copy-done.1
  214.3 0.0 copy-done.2
  214.3 1.1 pad_maximum_fusion
  215.4 1.8 copy.91
  217.2 5.4 all-to-all-start.3
  222.6 1.3 dynamic-slice
  224.6 1.3 fusion.12
  225.9 13.9 %all-to-all-done.3 = bf16[3,1,64,1,2,1152]{5,4,3,1,0,2:T(2,128)(2,1)S(1)} async-done(((bf16[3,1,64,1,2,1152]{5,4,3,1,0,2:T(2,128)(2,1)}), bf16[3,1,64,1,2,1152]{5,4,3,1,0,2:T(2,128)(2,1)S(1)}, u32[]{:S(2)}, u32[]{:S(2)}) %all-to-all-start.3) | async-done | bytes 884768 | tf_op jit(solution)/shard_map/all_to_all | solution.py:82
  239.7 0.6 copy.92
  240.3 1.2 reshape.123
  241.6 747.7 %all-reduce.3.cloned.1.call-done = f32[768,1152]{0,1:T(8,128)} async-done(((f32[768,1152]{0,1:T(8,128)}), f32[768,1152]{0,1:T(8,128)}) %all-reduce.3.cloned.1.call-update) | async-done | bytes 3538960
  989.3 1.5 constant_dynamic-slice_fusion
  990.8 73.8 %psum.7 = f32[12,1152]{0,1:T(8,128)S(1)} all-reduce(f32[12,1152]{0,1:T(8,128)S(1)} %constant_dynamic-slice_fusion), channel_id=1, replica_groups=mesh['dp'=8,'seq'=64] {'dp'}, use_global_device_ids=true, to_apply=%region_4.0 | all-reduce | flops 13824 | bytes 110592 | tf_op jit(solution)/shard_map/psum | solution.py:102
  1064.7 0.9 copy.94
  (1 shorter events, 0.0 us)
Async XLA Ops:
  7.2 81.8 %copy-start = (bf16[1,1,128,768]{3,2,1,0:T(8,128)(2,1)S(1)}, bf16[1,1,128,768]{3,2,1,0:T(8,128)(2,1)}, u32[]{:S(2)}) copy-start(bf16[1,1,128,768]{3,2,1,0:T(8,128)(2,1)} %param.5) | copy-start | bytes 589828
  11.0 42.3 %all-to-all-start = ((bf16[3,1,1,64,2,1152]{5,4,2,1,0,3:T(2,128)(2,1)}), bf16[3,1,1,64,2,1152]{5,4,2,1,0,3:T(2,128)(2,1)S(1)}, u32[]{:S(2)}, u32[]{:S(2)}) async-start(bf16[3,1,1,64,2,1152]{5,4,2,1,0,3:T(2,128)(2,1)} %copy.70), calls=%async_computation | async-start | bytes 1769472 | tf_op jit(solution)/shard_map/all_to_all | solution.py:73
  30.6 139.6 %all-gather.3.cloned.1.call-start = ((), (), s32[]{:S(2)}) async-start(), calls=%async_computation.4 | async-start | bytes 2396160 | tf_op jit(solution)/shard_map/all_gather | solution.py:64
  31.4 957.9 %all-reduce.3.cloned.1.call-start = ((), (), s32[]{:S(2)}) async-start(), calls=%async_computation.5 | async-start | bytes 7077888
  55.0 3.8 copy-start.3
  56.1 2.7 copy-start.4
  212.7 1.6 copy-start.1
  212.7 1.6 copy-start.2
  217.2 22.6 %all-to-all-start.3 = ((bf16[3,1,64,1,2,1152]{5,4,3,1,0,2:T(2,128)(2,1)}), bf16[3,1,64,1,2,1152]{5,4,3,1,0,2:T(2,128)(2,1)S(1)}, u32[]{:S(2)}, u32[]{:S(2)}) async-start(bf16[3,1,64,1,2,1152]{5,4,3,1,0,2:T(2,128)(2,1)} %copy.91), calls=%async_computation.3 | async-start | bytes 1769472 | tf_op jit(solution)/shard_map/all_to_all | solution.py:82
Sparse Core Ops, SparseCore 0:
  36.0 134.1 all-gather.2
  173.1 816.1 all-reduce.2
where the time goes:
time: 1070 us
  waiting for transfers between devices  863 us (81%)
  blocking collectives  122 us (11%)
  local copies, waits for them, and re-layouts  27.8 us (3%)
  starting transfers between devices  25.1 us (2%)
  matrix products  18.2 us (2%)
  between operations  14.9 us (1%)
    unnamed x3, waiting for transfers between devices  748 us
    all_gather x1, waiting for transfers between devices, on_device(): weight_full = lax.all_gather(out_weight, 'seq', axis=0, tiled=True)  78.7 us
    psum x1, blocking collectives, on_device(): owned_rows = lax.psum(local_share, 'dp')  73.8 us
    all_to_all x1, blocking collectives, on_device(): lax.all_to_all(attended_places, 'seq', split_axis=2, concat_axis=3, tiled...  27.1 us
    all_to_all x1, waiting for transfers between devices, on_device(): lax.all_to_all(arranged, 'seq', split_axis=3, concat_axis=2, tiled=True)  21.9 us
  transfers between devices with their start and end apart: 4, of which 4 were waited for; matrix products, arithmetic and copies ran while one was open for 4% of the time, Pallas kernels for 0%

commit v1 on v0

v1 whole, which is shorter than its diff:
```python
import math

import jax
import jax.numpy as jnp
from jax import lax
from jax.experimental import pallas as pl
from jax.experimental.pallas import tpu as pltpu
from jax.sharding import Mesh
from jax.sharding import PartitionSpec as P

HEADS = 16
HEAD_DIM = 72
ROWS = 128
WIDTH = 1152
OUT = 768
HALF = OUT // 2
COLS = 3 * WIDTH + OUT
INV_ROOT = 1.0 / math.sqrt(HEAD_DIM)
BF16 = jnp.bfloat16
F32 = jnp.float32

SEQ = ("yh", "x", "z")
RING = ("x", "z")
YAXIS = ("yl", "yh")


def dot(lhs, rhs, lhs_dim, rhs_dim):
    return lax.dot_general(
        lhs, rhs, (((lhs_dim,), (rhs_dim,)), ((), ())), preferred_element_type=F32
    )


def head(ref, part, index):
    start = part * WIDTH + index * HEAD_DIM
    return ref[:, start : start + HEAD_DIM]


def forward_kernel(rows_ref, attended_ref, weights_ref):
    row = lax.broadcasted_iota(jnp.int32, (ROWS, ROWS), 0)
    col = lax.broadcasted_iota(jnp.int32, (ROWS, ROWS), 1)
    same_place = ((row ^ col) & 1) == 0
    attended = []
    for index in range(HEADS):
        query, key, value = (head(rows_ref, part, index) for part in range(3))
        scores = jnp.where(same_place, dot(query, key, 1, 1) * INV_ROOT, -1e30)
        powers = jnp.exp(scores - jnp.max(scores, axis=1, keepdims=True))
        weights = powers / jnp.sum(powers, axis=1, keepdims=True)
        weights_ref[index] = weights
        attended.append(dot(weights.astype(BF16), value, 1, 0).astype(BF16))
    attended_ref[...] = jnp.concatenate(attended, axis=1)


def backward_kernel(rows_ref, weights_ref, attended_ref, matrix_ref, out_ref, upstream_ref):
    upstream_ref[...] = dot(rows_ref[:, 3 * WIDTH :], matrix_ref[...], 1, 0).astype(BF16)
    out_ref[:, 3 * WIDTH :] = dot(attended_ref[...], matrix_ref[...], 1, 1).astype(BF16)
    grads = ([], [], [])
    for index in range(HEADS):
        query, key, value = (head(rows_ref, part, index) for part in range(3))
        upstream = head(upstream_ref, 0, index)
        weights = weights_ref[index]
        grads[2].append(dot(weights.astype(BF16), upstream, 0, 0).astype(BF16))
        grad_weights = dot(upstream, value, 1, 1)
        centred = grad_weights - jnp.sum(weights * grad_weights, axis=1, keepdims=True)
        grad_scores = (weights * centred * INV_ROOT).astype(BF16)
        grads[0].append(dot(grad_scores, key, 1, 0).astype(BF16))
        grads[1].append(dot(grad_scores, query, 0, 0).astype(BF16))
    for part in range(3):
        out_ref[:, part * WIDTH : (part + 1) * WIDTH] = jnp.concatenate(grads[part], axis=1)


WHOLE = pl.BlockSpec(memory_space=pltpu.VMEM)
PARAMS = pltpu.CompilerParams(vmem_limit_bytes=24 << 20)


def forward(rows):
    return pl.pallas_call(
        forward_kernel,
        out_shape=(
            jax.ShapeDtypeStruct((ROWS, WIDTH), BF16),
            jax.ShapeDtypeStruct((HEADS, ROWS, ROWS), F32),
        ),
        in_specs=[WHOLE],
        out_specs=(WHOLE, WHOLE),
        compiler_params=PARAMS,
        name="forward",
    )(rows)


def backward(rows, weights, attended, matrix):
    return pl.pallas_call(
        backward_kernel,
        out_shape=jax.ShapeDtypeStruct((ROWS, COLS), BF16),
        in_specs=[WHOLE] * 4,
        out_specs=WHOLE,
        scratch_shapes=[pltpu.VMEM((ROWS, WIDTH), BF16)],
        compiler_params=PARAMS,
        name="backward",
    )(rows, weights, attended, matrix)


def exchange(value, axes):
    return lax.all_to_all(value, axes, 0, 0, tiled=True)


def swap(value, axis):
    return lax.ppermute(value, axis, [(0, 1), (1, 0)])


def fold(blocks):
    return blocks.reshape(-1, 3, 4, WIDTH).transpose(0, 2, 1, 3).reshape(-1, 4, 3 * WIDTH)


def unfold(blocks):
    return blocks.reshape(-1, 4, 3, WIDTH).transpose(0, 2, 1, 3).reshape(-1, WIDTH)


def gather_weight(own_rows, core, y_high):
    rows = jnp.where(core == y_high, own_rows, swap(own_rows, "yh"))
    half = unfold(exchange(jnp.broadcast_to(fold(rows[None]), (32, 4, 3 * WIDTH)), RING))
    other = swap(half, "c")
    return jnp.where(
        core == 0, jnp.concatenate([half, other]), jnp.concatenate([other, half])
    )


def weight_gradient(cotangent, attended, core, y_high):
    low, high = cotangent[:, :HALF], cotangent[:, HALF:]
    mine = jnp.where(core == 0, low, high)
    theirs = jnp.where(core == 0, high, low)
    columns = jnp.concatenate([mine, swap(theirs, "c")])
    features = jnp.concatenate([attended, swap(attended, "c")])
    partial = dot(columns, features, 0, 0).astype(BF16)
    terms = exchange(fold(partial.reshape(32, 12, WIDTH)), RING)
    rows = jnp.sum(terms.astype(F32), axis=0).reshape(108, 128)
    everyone = exchange(jnp.broadcast_to(rows[None], (8, 108, 128)), YAXIS)
    total = unfold(jnp.sum(everyone, axis=0).reshape(1, 4, 3 * WIDTH))
    return jnp.where(core == y_high, total, swap(total, "c"))


def on_device(query_key_value, out_weight, cotangent):
    core, y_high = lax.axis_index("c"), lax.axis_index("yh")
    parts = query_key_value.reshape(3, ROWS, WIDTH)
    sent = jnp.concatenate([parts[0], parts[1], parts[2], cotangent.reshape(ROWS, OUT)], axis=1)
    rows = exchange(sent.reshape(64, 2, COLS), SEQ).reshape(ROWS, COLS)
    matrix = gather_weight(out_weight, core, y_high)
    attended, weights = forward(rows)
    owned = weight_gradient(rows[:, 3 * WIDTH :], attended, core, y_high)
    results = backward(rows, weights, attended, matrix)
    back = exchange(results.reshape(64, 2, COLS), SEQ).reshape(ROWS, COLS)
    grads = jnp.stack([back[:, part * WIDTH : (part + 1) * WIDTH] for part in range(3)])
    return (
        back[:, 3 * WIDTH :].reshape(1, 1, ROWS, OUT),
        grads.reshape(3, 1, 1, ROWS, WIDTH),
        owned * (1.0 / math.sqrt(512 * ROWS)),
    )


def solution(mesh):
    split = Mesh(mesh.devices.reshape(4, 2, 2, 4, 8), ("yl", "c", "yh", "x", "z"))
    groups, frames = ("yl", "c"), SEQ
    in_specs = (P(None, groups, frames, None, None), P(frames, None), P(groups, frames, None, None))
    out_specs = (P(groups, frames, None, None), P(None, groups, frames, None, None), P(frames, None))
    return jax.shard_map(
        on_device, mesh=split, in_specs=in_specs, out_specs=out_specs, check_vma=False
    )
```

time: 1070 us -> 188 us (0.18)
  the two profiles are of different devices: /device:TPU:1 before, /device:TPU:14 now
where the time goes in v1:
time: 188 us; the launch traced here: 187 us
  waiting for transfers between devices  85.6 us (46%)
  starting transfers between devices  60.6 us (32%)
  local copies, waits for them, and re-layouts  19.7 us (10%)
  Pallas kernels  11.5 us (6%)
  other arithmetic  6.91 us (4%)
    all_to_all x5, waiting for transfers between devices, exchange(): return lax.all_to_all(value, axes, 0, 0, tiled=True)  58.8 us
    all_to_all x5, starting transfers between devices, exchange(): return lax.all_to_all(value, axes, 0, 0, tiled=True)  44.8 us
    ppermute x5, waiting for transfers between devices, swap(): return lax.ppermute(value, axis, [(0, 1), (1, 0)])  26.8 us
    ppermute x5, starting transfers between devices, swap(): return lax.ppermute(value, axis, [(0, 1), (1, 0)])  15.8 us
    pallas_call x1, Pallas kernels, backward(): pl.pallas_call(backward_kernel, out_shape=jax.ShapeDtypeStruct((ROWS, COL...  5.92 us
    reshape x2, local copies, waits for them, and re-layouts, fold(): blocks.reshape(-1, 3, 4, WIDTH).transpose(0, 2, 1, 3)  5.91 us
    pallas_call x1, Pallas kernels, forward(): pl.pallas_call(forward_kernel, out_shape=(jax.ShapeDtypeStruct((ROWS, WID...  5.59 us
    another operation x3, local copies, waits for them, and re-layouts, fold(): blocks.reshape(-1, 3, 4, WIDTH).transpose(0, 2, 1, 3)  5.19 us
  transfers between devices with their start and end apart: 10, of which 8 were waited for; matrix products, arithmetic and copies ran while one was open for 11% of the time, Pallas kernels for 6%

profile of v1, /device:TPU:14, one launch (start us, length us, event | category | flops | bytes accessed | tf_op | source)
XLA Modules:
  0.0 186.6 jit_solution(8841098556662303475)
XLA Ops:
  0.6 1.0 concatenate.27
  1.6 1.2 fusion.7
  2.9 0.1 concatenate.24
  3.0 0.1 concatenate.26
  3.1 0.1 concatenate.25
  3.2 0.0 copy-start
  3.2 1.8 pad_maximum_fusion
  5.0 18.2 %all-to-all-start = ((bf16[64,2,4224]{2,1,0:T(2,128)(2,1)}), bf16[64,2,4224]{2,1,0:T(2,128)(2,1)S(1)}, u32[]{:S(2)}, u32[]{:S(2)}) async-start(bf16[64,2,4224]{2,1,0:T(2,128)(2,1)} %pad_maximum_fusion), calls=%async_computation | async-start | bytes 2162688 | tf_op jit(solution)/shard_map/all_to_all | solution.py:102
  23.3 0.0 copy-done
  23.3 7.5 %collective-permute-start = (bf16[12,1152]{1,0:T(8,128)(2,1)S(1)}, bf16[12,1152]{1,0:T(8,128)(2,1)S(1)}, u32[]{:S(2)}, u32[]{:S(2)}) collective-permute-start(bf16[12,1152]{1,0:T(8,128)(2,1)S(1)} %copy-done), channel_id=1, source_target_pairs={{0,32},{32,0},{1,33},{33,1},{2,34},{34,2},{3,35},{35,3},{4,36},{36... | collective-permute-start | bytes 82952 | tf_op jit(solution)/shard_map/ppermute | solution.py:106
  30.8 22.9 %collective-permute-done = bf16[12,1152]{1,0:T(8,128)(2,1)S(1)} collective-permute-done((bf16[12,1152]{1,0:T(8,128)(2,1)S(1)}, bf16[12,1152]{1,0:T(8,128)(2,1)S(1)}, u32[]{:S(2)}, u32[]{:S(2)}) %collective-permute-start) | collective-permute-done | bytes 27680 | tf_op jit(solution)/shard_map/ppermute | solution.py:106
  53.7 6.0 %all-to-all-done = bf16[64,2,4224]{2,1,0:T(2,128)(2,1)S(1)} async-done(((bf16[64,2,4224]{2,1,0:T(2,128)(2,1)}), bf16[64,2,4224]{2,1,0:T(2,128)(2,1)S(1)}, u32[]{:S(2)}, u32[]{:S(2)}) %all-to-all-start) | async-done | bytes 1081376 | tf_op jit(solution)/shard_map/all_to_all | solution.py:102
  59.8 1.1 broadcast_in_dim.15
  60.9 4.7 %all-to-all-start.1 = ((bf16[32,4,3456]{2,1,0:T(4,128)(2,1)}), bf16[32,4,3456]{2,1,0:T(4,128)(2,1)S(1)}, u32[]{:S(2)}, u32[]{:S(2)}) async-start(bf16[32,4,3456]{2,1,0:T(4,128)(2,1)} %broadcast_in_dim.15), calls=%async_computation.1 | async-start | bytes 1769472 | tf_op jit(solution)/shard_map/all_to_all | solution.py:102
  65.6 0.5 reshape.53.rows_ref
  66.1 5.6 %forward.1 = (bf16[128,1152]{1,0:T(8,128)(2,1)S(1)}, f32[16,128,128]{2,1,0:T(8,128)S(1)}) custom-call(bf16[128,4224]{1,0:T(8,128)(2,1)S(1)} %reshape.53.rows_ref), custom_call_target="tpu_custom_call" | custom-call | tf_op jit(solution)/shard_map/forward/pallas_call | solution.py:76
  71.7 1.9 %collective-permute-start.3 = (bf16[128,1152]{1,0:T(8,128)(2,1)S(1)}, bf16[128,1152]{1,0:T(8,128)(2,1)S(1)}, u32[]{:S(2)}, u32[]{:S(2)}) collective-permute-start(bf16[128,1152]{1,0:T(8,128)(2,1)S(1)} %get-tuple-element.6.attended_ref), channel_id=1, source_target_pairs={{0,64},{64,0},{1,65},{65,1},{2,66},{66,2},{3,67},{67,3},{4,68},{68... | collective-permute-start | bytes 884744 | tf_op jit(solution)/shard_map/ppermute | solution.py:106
  73.6 2.4 %collective-permute-start.2 = (bf16[128,384]{1,0:T(8,128)(2,1)S(1)}, bf16[128,384]{1,0:T(8,128)(2,1)S(1)}, u32[]{:S(2)}, u32[]{:S(2)}) collective-permute-start(bf16[128,384]{1,0:T(8,128)(2,1)S(1)} %get-tuple-element.8), channel_id=1, source_target_pairs={{0,64},{64,0},{1,65},{65,1},{2,66},{66,2},{3,67},{67,3},{4,68},{68... | collective-permute-start | bytes 294920 | tf_op jit(solution)/shard_map/ppermute | solution.py:106
  76.1 0.9 collective-permute-done.2
  77.0 0.0 collective-permute-done.3
  77.0 1.4 convolution_convert_fusion
  78.4 2.5 %reshape_reshape.6 = bf16[32,3,4,1152]{3,2,1,0:T(4,128)(2,1)} reshape(bf16[384,1152]{1,0:T(8,128)(2,1)} %convolution_convert_fusion) | data formatting | bytes 1769472 | tf_op jit(solution)/shard_map/reshape;reshape | solution.py:110
  80.9 2.7 %copy.24 = bf16[32,3,4,1152]{3,1,0,2:T(4,128)(2,1)} copy(bf16[32,3,4,1152]{3,2,1,0:T(4,128)(2,1)} %reshape_reshape.6) | data formatting | bytes 1769472 | tf_op jit(solution)/shard_map/reshape;reshape | solution.py:110
  83.5 3.3 %reshape.60 = bf16[32,4,3456]{2,0,1:T(8,128)(2,1)} reshape(bf16[32,4,3,1152]{3,2,0,1:T(4,128)(2,1)} %bitcast.30) | data formatting | bytes 1769472 | tf_op jit(solution)/shard_map/reshape | solution.py:110
  86.9 2.6 %copy.17 = bf16[32,4,3456]{2,1,0:T(4,128)(2,1)} copy(bf16[32,4,3456]{2,0,1:T(8,128)(2,1)} %reshape.60) | data formatting | bytes 1769472 | tf_op jit(solution)/shard_map/reshape | solution.py:110
  89.4 0.0 all-to-all-done.1
  89.5 9.8 %all-to-all-start.3 = ((bf16[32,4,3456]{2,1,0:T(4,128)(2,1)}), bf16[32,4,3456]{2,1,0:T(4,128)(2,1)}, u32[]{:S(2)}, u32[]{:S(2)}) async-start(bf16[32,4,3456]{2,1,0:T(4,128)(2,1)} %copy.17), calls=%async_computation.3 | async-start | bytes 1769472 | tf_op jit(solution)/shard_map/all_to_all | solution.py:102
  99.3 1.1 reshape.55
  100.4 2.1 %collective-permute-start.1 = (bf16[384,1152]{1,0:T(8,128)(2,1)}, bf16[384,1152]{1,0:T(8,128)(2,1)S(1)}, u32[]{:S(2)}, u32[]{:S(2)}) collective-permute-start(bf16[384,1152]{1,0:T(8,128)(2,1)} %reshape.55), channel_id=1, source_target_pairs={{0,64},{64,0},{1,65},{65,1},{2,66},{66,2},{3,67},{67,3},{4,68},{68... | collective-permute-start | bytes 2654216 | tf_op jit(solution)/shard_map/ppermute | solution.py:106
  102.5 2.4 %collective-permute-done.1 = bf16[384,1152]{1,0:T(8,128)(2,1)S(1)} collective-permute-done((bf16[384,1152]{1,0:T(8,128)(2,1)}, bf16[384,1152]{1,0:T(8,128)(2,1)S(1)}, u32[]{:S(2)}, u32[]{:S(2)}) %collective-permute-start.1) | collective-permute-done | bytes 884768 | tf_op jit(solution)/shard_map/ppermute | solution.py:106
  104.9 2.0 %maximum_select_fusion.matrix_ref = bf16[768,1152]{1,0:T(8,128)(2,1)S(1)} fusion(bf16[384,1152]{1,0:T(8,128)(2,1)S(1)} %collective-permute-done.1, bf16[384,1152]{1,0:T(8,128)(2,1)} %reshape.55, pred[]{:T(512)S(6)} %eq.4), kind=kLoop, calls=%fused_computation.1 | loop fusion | flops 7962624 | bytes 3538945 | tf_op jit(solution)/shard_map/jit(_where)/select_n | solution.py:121
  106.9 5.9 %backward.1 = bf16[128,4224]{1,0:T(8,128)(2,1)S(1)} custom-call(bf16[128,4224]{1,0:T(8,128)(2,1)S(1)} %reshape.53.rows_ref, f32[16,128,128]{2,1,0:T(8,128)S(1)} %get-tuple-element.5.weights_ref, bf16[128,1152]{1,0:T(8,128)(2,1)S(1)} %get-tuple-element.6.attended_ref, bf16[768,1152]{1,0:T(8,128)(2,1)S(1)} %maximum_select_fusion.matrix_ref), custom_call_target="tpu_custom_call" | custom-call | tf_op jit(solution)/shard_map/backward/pallas_call | solution.py:90
  112.8 1.2 reshape.56
  114.1 8.2 %all-to-all-done.3 = bf16[32,4,3456]{2,1,0:T(4,128)(2,1)} async-done(((bf16[32,4,3456]{2,1,0:T(4,128)(2,1)}), bf16[32,4,3456]{2,1,0:T(4,128)(2,1)}, u32[]{:S(2)}, u32[]{:S(2)}) %all-to-all-start.3) | async-done | bytes 884768 | tf_op jit(solution)/shard_map/all_to_all | solution.py:102
  122.2 8.2 %all-to-all-start.2 = ((bf16[64,2,4224]{2,1,0:T(2,128)(2,1)}), bf16[64,2,4224]{2,1,0:T(2,128)(2,1)S(1)}, u32[]{:S(2)}, u32[]{:S(2)}) async-start(bf16[64,2,4224]{2,1,0:T(2,128)(2,1)} %reshape.56), calls=%async_computation.2 | async-start | bytes 2162688 | tf_op jit(solution)/shard_map/all_to_all | solution.py:102
  130.5 1.4 convert_reduce_fusion
  131.9 32.7 %all-to-all-done.2 = bf16[64,2,4224]{2,1,0:T(2,128)(2,1)S(1)} async-done(((bf16[64,2,4224]{2,1,0:T(2,128)(2,1)}), bf16[64,2,4224]{2,1,0:T(2,128)(2,1)S(1)}, u32[]{:S(2)}, u32[]{:S(2)}) %all-to-all-start.2) | async-done | bytes 1081376 | tf_op jit(solution)/shard_map/all_to_all | solution.py:102
  164.6 0.8 broadcast_in_dim.17
  165.4 3.8 %all-to-all-start.4 = ((f32[8,108,128]{2,1,0:T(8,128)}), f32[8,108,128]{2,1,0:T(8,128)S(1)}, u32[]{:S(2)}, u32[]{:S(2)}) async-start(f32[8,108,128]{2,1,0:T(8,128)} %broadcast_in_dim.17), calls=%async_computation.4 | async-start | bytes 917504 | tf_op jit(solution)/shard_map/all_to_all | solution.py:102
  169.2 0.4 reshape.57
  169.6 0.1 slice_bitcast_fusion.2
  169.7 1.0 maximum_bitcast_fusion
  170.8 11.9 %all-to-all-done.4 = f32[8,108,128]{2,1,0:T(8,128)S(1)} async-done(((f32[8,108,128]{2,1,0:T(8,128)}), f32[8,108,128]{2,1,0:T(8,128)S(1)}, u32[]{:S(2)}, u32[]{:S(2)}) %all-to-all-start.4) | async-done | bytes 442400 | tf_op jit(solution)/shard_map/all_to_all | solution.py:102
  182.8 1.9 %collective-permute-start.4 = (f32[12,1152]{1,0:T(8,128)S(1)}, f32[12,1152]{1,0:T(8,128)S(1)}, u32[]{:S(2)}, u32[]{:S(2)}) collective-permute-start(f32[12,1152]{1,0:T(8,128)S(1)} %reshape.61), channel_id=1, source_target_pairs={{0,64},{64,0},{1,65},{65,1},{2,66},{66,2},{3,67},{67,3},{4,68},{68... | collective-permute-start | bytes 165896 | tf_op jit(solution)/shard_map/ppermute | solution.py:106
  184.7 0.7 slice_bitcast_fusion.3
  185.4 0.5 collective-permute-done.4
  185.9 0.6 select_multiply_fusion
  (8 shorter events, 0.2 us)
Async XLA Ops:
  3.2 20.1 %copy-start = (bf16[12,1152]{1,0:T(8,128)(2,1)S(1)}, bf16[12,1152]{1,0:T(8,128)(2,1)}, u32[]{:S(2)}) copy-start(bf16[12,1152]{1,0:T(8,128)(2,1)} %param.4) | copy-start | bytes 82948
  5.0 54.7 %all-to-all-start = ((bf16[64,2,4224]{2,1,0:T(2,128)(2,1)}), bf16[64,2,4224]{2,1,0:T(2,128)(2,1)S(1)}, u32[]{:S(2)}, u32[]{:S(2)}) async-start(bf16[64,2,4224]{2,1,0:T(2,128)(2,1)} %pad_maximum_fusion), calls=%async_computation | async-start | bytes 2162688 | tf_op jit(solution)/shard_map/all_to_all | solution.py:102
  23.3 30.4 %collective-permute-start = (bf16[12,1152]{1,0:T(8,128)(2,1)S(1)}, bf16[12,1152]{1,0:T(8,128)(2,1)S(1)}, u32[]{:S(2)}, u32[]{:S(2)}) collective-permute-start(bf16[12,1152]{1,0:T(8,128)(2,1)S(1)} %copy-done), channel_id=1, source_target_pairs={{0,32},{32,0},{1,33},{33,1},{2,34},{34,2},{3,35},{35,3},{4,36},{36... | collective-permute-start | bytes 82952 | tf_op jit(solution)/shard_map/ppermute | solution.py:106
  60.9 28.6 %all-to-all-start.1 = ((bf16[32,4,3456]{2,1,0:T(4,128)(2,1)}), bf16[32,4,3456]{2,1,0:T(4,128)(2,1)S(1)}, u32[]{:S(2)}, u32[]{:S(2)}) async-start(bf16[32,4,3456]{2,1,0:T(4,128)(2,1)} %broadcast_in_dim.15), calls=%async_computation.1 | async-start | bytes 1769472 | tf_op jit(solution)/shard_map/all_to_all | solution.py:102
  71.7 5.3 %collective-permute-start.3 = (bf16[128,1152]{1,0:T(8,128)(2,1)S(1)}, bf16[128,1152]{1,0:T(8,128)(2,1)S(1)}, u32[]{:S(2)}, u32[]{:S(2)}) collective-permute-start(bf16[128,1152]{1,0:T(8,128)(2,1)S(1)} %get-tuple-element.6.attended_ref), channel_id=1, source_target_pairs={{0,64},{64,0},{1,65},{65,1},{2,66},{66,2},{3,67},{67,3},{4,68},{68... | collective-permute-start | bytes 884744 | tf_op jit(solution)/shard_map/ppermute | solution.py:106
  73.6 3.3 %collective-permute-start.2 = (bf16[128,384]{1,0:T(8,128)(2,1)S(1)}, bf16[128,384]{1,0:T(8,128)(2,1)S(1)}, u32[]{:S(2)}, u32[]{:S(2)}) collective-permute-start(bf16[128,384]{1,0:T(8,128)(2,1)S(1)} %get-tuple-element.8), channel_id=1, source_target_pairs={{0,64},{64,0},{1,65},{65,1},{2,66},{66,2},{3,67},{67,3},{4,68},{68... | collective-permute-start | bytes 294920 | tf_op jit(solution)/shard_map/ppermute | solution.py:106
  89.5 32.8 %all-to-all-start.3 = ((bf16[32,4,3456]{2,1,0:T(4,128)(2,1)}), bf16[32,4,3456]{2,1,0:T(4,128)(2,1)}, u32[]{:S(2)}, u32[]{:S(2)}) async-start(bf16[32,4,3456]{2,1,0:T(4,128)(2,1)} %copy.17), calls=%async_computation.3 | async-start | bytes 1769472 | tf_op jit(solution)/shard_map/all_to_all | solution.py:102
  100.4 4.5 %collective-permute-start.1 = (bf16[384,1152]{1,0:T(8,128)(2,1)}, bf16[384,1152]{1,0:T(8,128)(2,1)S(1)}, u32[]{:S(2)}, u32[]{:S(2)}) collective-permute-start(bf16[384,1152]{1,0:T(8,128)(2,1)} %reshape.55), channel_id=1, source_target_pairs={{0,64},{64,0},{1,65},{65,1},{2,66},{66,2},{3,67},{67,3},{4,68},{68... | collective-permute-start | bytes 2654216 | tf_op jit(solution)/shard_map/ppermute | solution.py:106
  122.2 42.3 %all-to-all-start.2 = ((bf16[64,2,4224]{2,1,0:T(2,128)(2,1)}), bf16[64,2,4224]{2,1,0:T(2,128)(2,1)S(1)}, u32[]{:S(2)}, u32[]{:S(2)}) async-start(bf16[64,2,4224]{2,1,0:T(2,128)(2,1)} %reshape.56), calls=%async_computation.2 | async-start | bytes 2162688 | tf_op jit(solution)/shard_map/all_to_all | solution.py:102
  165.4 17.3 %all-to-all-start.4 = ((f32[8,108,128]{2,1,0:T(8,128)}), f32[8,108,128]{2,1,0:T(8,128)S(1)}, u32[]{:S(2)}, u32[]{:S(2)}) async-start(f32[8,108,128]{2,1,0:T(8,128)} %broadcast_in_dim.17), calls=%async_computation.4 | async-start | bytes 917504 | tf_op jit(solution)/shard_map/all_to_all | solution.py:102
  182.8 3.2 %collective-permute-start.4 = (f32[12,1152]{1,0:T(8,128)S(1)}, f32[12,1152]{1,0:T(8,128)S(1)}, u32[]{:S(2)}, u32[]{:S(2)}) collective-permute-start(f32[12,1152]{1,0:T(8,128)S(1)} %reshape.61), channel_id=1, source_target_pairs={{0,64},{64,0},{1,65},{65,1},{2,66},{66,2},{3,67},{67,3},{4,68},{68... | collective-permute-start | bytes 165896 | tf_op jit(solution)/shard_map/ppermute | solution.py:106

commit v2 on v1

v2 whole, which is shorter than its diff:
```python
import math

import jax
import jax.numpy as jnp
from jax import lax
from jax.experimental import pallas as pl
from jax.experimental.pallas import tpu as pltpu
from jax.sharding import Mesh
from jax.sharding import PartitionSpec as P

HEADS = 16
HEAD_DIM = 72
ROWS = 128
LANES = 128
WIDTH = 1152
TILES = WIDTH // LANES
OUT = 768
HALF = OUT // 2
BASE = 3 * WIDTH + OUT
PIECE = 896
PIECE_TILES = PIECE // LANES
COLS = BASE + PIECE
INV_ROOT = 1.0 / math.sqrt(HEAD_DIM)
BF16 = jnp.bfloat16
F32 = jnp.float32

SEQ = ("yh", "x", "z")
GROUPS = ("yl", "c")


def dot(lhs, rhs, lhs_dim, rhs_dim):
    return lax.dot_general(
        lhs, rhs, (((lhs_dim,), (rhs_dim,)), ((), ())), preferred_element_type=F32
    )


def head(ref, part, index):
    start = part * WIDTH + index * HEAD_DIM
    return ref[:, start : start + HEAD_DIM]


def channel_order():
    natural = lax.broadcasted_iota(jnp.int32, (OUT, OUT), 0)
    place = lax.broadcasted_iota(jnp.int32, (OUT, OUT), 1)
    source = 12 * ((place & 127) >> 1) + 2 * (place >> 7) + (place & 1)
    return jnp.where(natural == source, 1.0, 0.0).astype(BF16)


def half_tiles():
    return [
        (tile // PIECE_TILES, tile % PIECE_TILES, tile // TILES, tile % TILES)
        for tile in range(3 * TILES)
    ]


def lanes(tile):
    return slice(tile * LANES, (tile + 1) * LANES)


def pack_kernel(core_ref, parts_ref, cotangent_ref, weight_ref, out_ref):
    for part in range(3):
        out_ref[:, part * WIDTH : (part + 1) * WIDTH] = parts_ref[part]
    out_ref[:, 3 * WIDTH : BASE] = cotangent_ref[...]
    row = lax.broadcasted_iota(jnp.int32, (16, 12), 0)
    col = lax.broadcasted_iota(jnp.int32, (16, 12), 1)
    repeated = []
    for pair in range(3):
        chosen = col == 6 * core_ref[0] + 2 * pair + (row & 1)
        repeated.append(
            dot(jnp.where(chosen, 1.0, 0.0).astype(BF16), weight_ref[...], 1, 0).astype(BF16)
        )
    for high in range(2):
        for piece, place, pair, tile in half_tiles():
            start = 64 * high + 16 * piece
            out_ref[start : start + 16, BASE + place * LANES : BASE + (place + 1) * LANES] = (
                repeated[pair][:, lanes(tile)]
            )
        start = 64 * high + 48
        out_ref[start : start + 16, COLS - LANES :] = jnp.zeros((16, LANES), BF16)


def forward_kernel(core_ref, rows_ref, share_ref, channels_ref, weights_ref):
    row = lax.broadcasted_iota(jnp.int32, (ROWS, ROWS), 0)
    col = lax.broadcasted_iota(jnp.int32, (ROWS, ROWS), 1)
    same_place = ((row ^ col) & 1) == 0
    attended = []
    for index in range(HEADS):
        query, key, value = (head(rows_ref, part, index) for part in range(3))
        scores = jnp.where(same_place, dot(query, key, 1, 1) * INV_ROOT, -1e30)
        powers = jnp.exp(scores - jnp.max(scores, axis=1, keepdims=True))
        weights = powers / jnp.sum(powers, axis=1, keepdims=True)
        weights_ref[index] = weights
        attended.append(dot(weights.astype(BF16), value, 1, 0).astype(BF16))
    share_ref[:, :WIDTH] = jnp.concatenate(attended, axis=1)
    channels_ref[...] = dot(rows_ref[:, 3 * WIDTH : BASE], channel_order(), 1, 0).astype(BF16)
    other = pl.multiple_of((1 - core_ref[0]) * HALF, HALF)
    share_ref[:, WIDTH:] = channels_ref[:, pl.ds(other, HALF)]


def weight_grad_kernel(core_ref, share_ref, received_ref, channels_ref, out_ref):
    own = pl.multiple_of(core_ref[0] * HALF, HALF)
    columns = jnp.concatenate([channels_ref[:, pl.ds(own, HALF)], received_ref[:, WIDTH:]], axis=0)
    features = jnp.concatenate([share_ref[:, :WIDTH], received_ref[:, :WIDTH]], axis=0)
    partial = dot(columns, features, 0, 0).astype(BF16)
    for piece, place, pair, tile in half_tiles():
        out_ref[piece, :, lanes(place)] = partial[pair * ROWS : (pair + 1) * ROWS, lanes(tile)]
    out_ref[3, :, lanes(PIECE_TILES - 1)] = jnp.zeros((ROWS, LANES), BF16)


def backward_kernel(
    core_ref, rows_ref, weights_ref, share_ref, channels_ref, mine_ref, theirs_ref,
    out_ref, matrix_ref, upstream_ref,
):
    own = pl.multiple_of(core_ref[0] * HALF, HALF)
    other = pl.multiple_of((1 - core_ref[0]) * HALF, HALF)
    for piece, place, pair, tile in half_tiles():
        for start, half_ref in ((own, mine_ref), (other, theirs_ref)):
            matrix_ref[pl.ds(start + pair * ROWS, ROWS), lanes(tile)] = half_ref[
                piece, :, lanes(place)
            ]
    matrix = matrix_ref[...]
    upstream_ref[...] = dot(channels_ref[...], matrix, 1, 0).astype(BF16)
    projected = dot(share_ref[:, :WIDTH], matrix, 1, 1).astype(BF16)
    out_ref[:, 3 * WIDTH :] = dot(projected, channel_order(), 1, 1).astype(BF16)
    grads = ([], [], [])
    for index in range(HEADS):
        query, key, value = (head(rows_ref, part, index) for part in range(3))
        upstream = head(upstream_ref, 0, index)
        weights = weights_ref[index]
        grads[2].append(dot(weights.astype(BF16), upstream, 0, 0).astype(BF16))
        grad_weights = dot(upstream, value, 1, 1)
        centred = grad_weights - jnp.sum(weights * grad_weights, axis=1, keepdims=True)
        grad_scores = (weights * centred * INV_ROOT).astype(BF16)
        grads[0].append(dot(grad_scores, key, 1, 0).astype(BF16))
        grads[1].append(dot(grad_scores, query, 0, 0).astype(BF16))
    for part in range(3):
        out_ref[:, part * WIDTH : (part + 1) * WIDTH] = jnp.concatenate(grads[part], axis=1)


def call(kernel, name, out_shapes, scratch, core, *operands):
    whole = pl.BlockSpec(memory_space=pltpu.VMEM)
    return pl.pallas_call(
        kernel,
        out_shape=[jax.ShapeDtypeStruct(shape, dtype) for shape, dtype in out_shapes],
        in_specs=[pl.BlockSpec(memory_space=pltpu.SMEM)] + [whole] * len(operands),
        out_specs=[whole] * len(out_shapes),
        scratch_shapes=scratch,
        compiler_params=pltpu.CompilerParams(vmem_limit_bytes=24 << 20),
        name=name,
    )(core, *operands)


def exchange(value, axes):
    return lax.all_to_all(value, axes, 0, 0, tiled=True)


def swap(value):
    return lax.ppermute(value, "c", [(0, 1), (1, 0)])


def on_device(query_key_value, out_weight, cotangent):
    core = lax.axis_index("c").astype(jnp.int32).reshape(1)
    parts = query_key_value.reshape(3, ROWS, WIDTH)
    (packed,) = call(
        pack_kernel, "pack", [((ROWS, COLS), BF16)], [],
        core, parts, cotangent.reshape(ROWS, OUT), out_weight,
    )
    rows = exchange(packed.reshape(64, 2, COLS), SEQ).reshape(ROWS, COLS)
    piece = jnp.broadcast_to(rows[None, :, BASE:], (4, ROWS, PIECE))
    mine = exchange(piece, "x")
    share, channels, weights = call(
        forward_kernel, "forward",
        [((ROWS, WIDTH + HALF), BF16), ((ROWS, OUT), BF16), ((HEADS, ROWS, ROWS), F32)], [],
        core, rows,
    )
    (partial,) = call(
        weight_grad_kernel, "weight_grad", [((4, ROWS, PIECE), BF16)], [],
        core, share, swap(share), channels,
    )
    terms = exchange(partial, "x")
    theirs = swap(mine)
    (results,) = call(
        backward_kernel, "backward", [((ROWS, BASE), BF16)],
        [pltpu.VMEM((OUT, WIDTH), BF16), pltpu.VMEM((ROWS, WIDTH), BF16)],
        core, rows, weights, share, channels, mine, theirs,
    )
    summed = jnp.sum(terms.astype(F32), axis=0).astype(BF16)
    sent = jnp.concatenate([results.reshape(64, 2, BASE), summed.reshape(64, 2, PIECE)], axis=2)
    back = exchange(sent, SEQ)
    owned = jnp.sum(back[:, :, BASE:].astype(F32).reshape(2, 4, 8, 2, PIECE), axis=(0, 2))
    everyone = exchange(jnp.broadcast_to(owned[None], (8, 4, 2, PIECE)), GROUPS)
    total = jnp.sum(everyone.reshape(4, 2, 4, 2, PIECE), axis=0)
    pairs = total.transpose(0, 2, 1, 3).reshape(2, 2, 4 * PIECE)[:, :, : 3 * WIDTH]
    own_rows = pairs.reshape(2, 2, 3, WIDTH).transpose(0, 2, 1, 3).reshape(12, WIDTH)
    frames = back.reshape(ROWS, COLS)
    grads = jnp.stack([frames[:, part * WIDTH : (part + 1) * WIDTH] for part in range(3)])
    return (
        frames[:, 3 * WIDTH : BASE].reshape(1, 1, ROWS, OUT),
        grads.reshape(3, 1, 1, ROWS, WIDTH),
        own_rows * (1.0 / math.sqrt(512 * ROWS)),
    )


def solution(mesh):
    split = Mesh(mesh.devices.reshape(4, 2, 2, 4, 8), ("yl", "c", "yh", "x", "z"))
    in_specs = (P(None, GROUPS, SEQ, None, None), P(SEQ, None), P(GROUPS, SEQ, None, None))
    out_specs = (P(GROUPS, SEQ, None, None), P(None, GROUPS, SEQ, None, None), P(SEQ, None))
    return jax.shard_map(
        on_device, mesh=split, in_specs=in_specs, out_specs=out_specs, check_vma=False
    )
```

time: 188 us -> 180 us (0.957)
  the two profiles are of different devices: /device:TPU:14 before, /device:TPU:1 now
where the time goes in v2:
time: 180 us; the launch traced here: 179 us
  blocking collectives  106 us (59%)
  starting transfers between devices  31.7 us (18%)
  local copies, waits for them, and re-layouts  15.5 us (9%)
  Pallas kernels  14.4 us (8%)
  waiting for transfers between devices  6.33 us (4%)
  other arithmetic  3.74 us (2%)
    all_to_all x3, blocking collectives, exchange(): return lax.all_to_all(value, axes, 0, 0, tiled=True)  106 us
    all_to_all x2, starting transfers between devices, exchange(): return lax.all_to_all(value, axes, 0, 0, tiled=True)  19.2 us
    pallas_call x4, Pallas kernels, call(): pl.pallas_call(kernel, out_shape=[jax.ShapeDtypeStruct(shape, dtype) for...  14.4 us
    ppermute x2, starting transfers between devices, swap(): return lax.ppermute(value, 'c', [(0, 1), (1, 0)])  12.5 us
    unnamed x16, local copies, waits for them, and re-layouts  6.51 us
    all_to_all x2, waiting for transfers between devices, exchange(): return lax.all_to_all(value, axes, 0, 0, tiled=True)  6.33 us
    reshape x2, local copies, waits for them, and re-layouts, on_device(): rows = exchange(packed.reshape(64, 2, COLS), SEQ).reshape(ROWS, COLS)  3.65 us
  transfers between devices with their start and end apart: 4, of which 1 were waited for; matrix products, arithmetic and copies ran while one was open for 2% of the time, Pallas kernels for 3%

profile of v2, /device:TPU:1, one launch (start us, length us, event | category | flops | bytes accessed | tf_op | source)
XLA Modules:
  0.0 178.8 jit_solution(12902104066556936474)
XLA Ops:
  0.6 0.0 copy-start.4
  0.6 1.2 copy-done.4
  1.8 0.0 copy-start.5
  1.8 0.9 copy-done.5
  2.7 0.0 copy-start.6
  2.7 0.8 copy-done.6
  3.5 0.2 pack.1
  3.7 0.5 reshape.59
  4.3 49.3 %all_to_all.25 = bf16[64,2,5120]{2,1,0:T(2,128)(2,1)} all-to-all(bf16[64,2,5120]{2,1,0:T(2,128)(2,1)S(1)} %reshape.59), channel_id=1, replica_groups=mesh['yl'=4,'c'=2,'yh'=2,'x'=4,'z'=8] {'yh','x','z'}, dimensions={0} | all-to-all | bytes 2621440 | tf_op jit(solution)/shard_map/all_to_all | solution.py:154
  53.6 3.1 %reshape.60.rows_ref = bf16[128,5120]{1,0:T(8,128)(2,1)S(1)} reshape(bf16[64,2,5120]{2,1,0:T(2,128)(2,1)} %all_to_all.25) | data formatting | bytes 2621440 | tf_op jit(solution)/shard_map/reshape | solution.py:168
  56.7 1.1 broadcast_in_dim.4
  57.8 5.1 %all-to-all-start.1 = ((bf16[4,128,896]{2,1,0:T(8,128)(2,1)}), bf16[4,128,896]{2,1,0:T(8,128)(2,1)S(1)}, u32[]{:S(2)}, u32[]{:S(2)}) async-start(bf16[4,128,896]{2,1,0:T(8,128)(2,1)} %broadcast_in_dim.4), calls=%async_computation.1 | async-start | bytes 1835008 | tf_op jit(solution)/shard_map/all_to_all | solution.py:154
  62.9 5.5 %forward.1 = (bf16[128,1536]{1,0:T(8,128)(2,1)S(1)}, bf16[128,768]{1,0:T(8,128)(2,1)S(1)}, f32[16,128,128]{2,1,0:T(8,128)S(1)}) custom-call(s32[1]{0:T(128)} %bitcast.core_ref, bf16[128,5120]{1,0:T(8,128)(2,1)S(1)} %reshape.60.rows_ref), custom_call_target="tpu_custom_call" | custom-call | tf_op jit(solution)/shard_map/forward/pallas_call | solution.py:142
  68.4 0.0 copy-start.2
  68.4 1.0 copy-done.2
  69.4 0.0 copy-start
  69.4 8.8 %collective-permute-start.1 = (bf16[128,1536]{1,0:T(8,128)(2,1)S(1)}, bf16[128,1536]{1,0:T(8,128)(2,1)S(1)}, u32[]{:S(2)}, u32[]{:S(2)}) collective-permute-start(bf16[128,1536]{1,0:T(8,128)(2,1)S(1)} %get-tuple-element.7.share_ref), channel_id=1, source_target_pairs={{0,64},{64,0},{1,65},{65,1},{2,66},{66,2},{3,67},{67,3},{4,68},{68... | collective-permute-start | bytes 1179656 | tf_op jit(solution)/shard_map/ppermute | solution.py:158
  78.2 0.0 all-to-all-done.1.mine_ref
  78.2 3.7 %collective-permute-start = (bf16[4,128,896]{2,1,0:T(8,128)(2,1)S(1)}, bf16[4,128,896]{2,1,0:T(8,128)(2,1)}, u32[]{:S(2)}, u32[]{:S(2)}) collective-permute-start(bf16[4,128,896]{2,1,0:T(8,128)(2,1)S(1)} %all-to-all-done.1.mine_ref), channel_id=1, source_target_pairs={{0,64},{64,0},{1,65},{65,1},{2,66},{66,2},{3,67},{67,3},{4,68},{68... | collective-permute-start | bytes 2752520 | tf_op jit(solution)/shard_map/ppermute | solution.py:158
  81.9 0.0 collective-permute-done.1.received_ref
  81.9 0.5 weight_grad.1
  82.4 16.7 %all_to_all.26 = bf16[4,128,896]{2,1,0:T(8,128)(2,1)} all-to-all(bf16[4,128,896]{2,1,0:T(8,128)(2,1)S(1)} %weight_grad.1), channel_id=1, replica_groups=mesh['yl'=4,'c'=2,'yh'=2,'x'=4,'z'=8] {'x'}, dimensions={0} | all-to-all | bytes 1835008 | tf_op jit(solution)/shard_map/all_to_all | solution.py:154
  99.1 0.0 copy-done
  99.1 1.3 reduce_sum.30
  100.4 0.8 reshape.62
  101.2 0.0 collective-permute-done.theirs_ref
  101.2 0.0 copy-start.1
  101.2 1.0 copy-done.1
  102.2 0.0 copy-start.3
  102.2 1.2 copy-done.3
  103.4 8.2 %backward.1 = bf16[128,4224]{1,0:T(8,128)(2,1)S(1)} custom-call(s32[1]{0:T(128)} %bitcast.core_ref, bf16[128,5120]{1,0:T(8,128)(2,1)S(1)} %reshape.60.rows_ref, f32[16,128,128]{2,1,0:T(8,128)S(1)} %copy-done.3, bf16[128,1536]{1,0:T(8,128)(2,1)S(1)} %copy-done.1, bf16[128,768]{1,0:T(8,128)(2,1)S(1)} %get-tuple-element.8.channels_ref, ...), custom_call_target="tpu_custom_call" | custom-call | tf_op jit(solution)/shard_map/backward/pallas_call | solution.py:142
  111.7 0.0 copy-start.7
  111.7 0.5 reshape.61
  112.1 0.5 copy-done.7
  112.6 1.1 pad_maximum_fusion
  113.7 40.3 %all_to_all.27 = bf16[64,2,5120]{2,1,0:T(2,128)(2,1)S(1)} all-to-all(bf16[64,2,5120]{2,1,0:T(2,128)(2,1)S(1)} %pad_maximum_fusion), channel_id=1, replica_groups=mesh['yl'=4,'c'=2,'yh'=2,'x'=4,'z'=8] {'yh','x','z'}, dimensions={0} | all-to-all | bytes 2621440 | tf_op jit(solution)/shard_map/all_to_all | solution.py:154
  154.0 0.2 slice.33
  154.2 0.2 convert_reduce_fusion
  154.4 0.5 reshape.63
  154.9 0.1 slice_bitcast_fusion.2
  155.0 0.7 broadcast_in_dim.5
  155.7 14.1 %all-to-all-start.4 = ((f32[8,4,2,896]{3,1,2,0:T(4,128)}), f32[8,4,2,896]{3,1,2,0:T(4,128)S(1)}, u32[]{:S(2)}, u32[]{:S(2)}) async-start(f32[8,4,2,896]{3,1,2,0:T(4,128)} %broadcast_in_dim.5), calls=%async_computation.4 | async-start | bytes 458752 | tf_op jit(solution)/shard_map/all_to_all | solution.py:154
  169.9 0.7 slice_bitcast_fusion.3
  170.5 1.0 maximum_bitcast_fusion
  171.6 6.3 %all-to-all-done.4 = f32[8,4,2,896]{3,1,2,0:T(4,128)S(1)} async-done(((f32[8,4,2,896]{3,1,2,0:T(4,128)}), f32[8,4,2,896]{3,1,2,0:T(4,128)S(1)}, u32[]{:S(2)}, u32[]{:S(2)}) %all-to-all-start.4) | async-done | bytes 229408 | tf_op jit(solution)/shard_map/all_to_all | solution.py:154
  178.0 0.1 mul.17
  178.1 0.7 mul.19
  (6 shorter events, 0.2 us)
Async XLA Ops:
  0.6 1.2 copy-start.4
  1.8 0.9 copy-start.5
  2.7 0.8 copy-start.6
  57.8 20.4 %all-to-all-start.1 = ((bf16[4,128,896]{2,1,0:T(8,128)(2,1)}), bf16[4,128,896]{2,1,0:T(8,128)(2,1)S(1)}, u32[]{:S(2)}, u32[]{:S(2)}) async-start(bf16[4,128,896]{2,1,0:T(8,128)(2,1)} %broadcast_in_dim.4), calls=%async_computation.1 | async-start | bytes 1835008 | tf_op jit(solution)/shard_map/all_to_all | solution.py:154
  68.4 1.0 copy-start.2
  69.4 29.7 %copy-start = (bf16[128,1536]{1,0:T(8,128)(2,1)}, bf16[128,1536]{1,0:T(8,128)(2,1)S(1)}, u32[]{:S(2)}) copy-start(bf16[128,1536]{1,0:T(8,128)(2,1)S(1)} %get-tuple-element.7.share_ref) | copy-start | bytes 1179652
  69.4 12.5 %collective-permute-start.1 = (bf16[128,1536]{1,0:T(8,128)(2,1)S(1)}, bf16[128,1536]{1,0:T(8,128)(2,1)S(1)}, u32[]{:S(2)}, u32[]{:S(2)}) collective-permute-start(bf16[128,1536]{1,0:T(8,128)(2,1)S(1)} %get-tuple-element.7.share_ref), channel_id=1, source_target_pairs={{0,64},{64,0},{1,65},{65,1},{2,66},{66,2},{3,67},{67,3},{4,68},{68... | collective-permute-start | bytes 1179656 | tf_op jit(solution)/shard_map/ppermute | solution.py:158
  78.2 23.0 %collective-permute-start = (bf16[4,128,896]{2,1,0:T(8,128)(2,1)S(1)}, bf16[4,128,896]{2,1,0:T(8,128)(2,1)}, u32[]{:S(2)}, u32[]{:S(2)}) collective-permute-start(bf16[4,128,896]{2,1,0:T(8,128)(2,1)S(1)} %all-to-all-done.1.mine_ref), channel_id=1, source_target_pairs={{0,64},{64,0},{1,65},{65,1},{2,66},{66,2},{3,67},{67,3},{4,68},{68... | collective-permute-start | bytes 2752520 | tf_op jit(solution)/shard_map/ppermute | solution.py:158
  101.2 1.0 copy-start.1
  102.2 1.2 copy-start.3
  111.7 0.9 copy-start.7
  155.7 22.2 %all-to-all-start.4 = ((f32[8,4,2,896]{3,1,2,0:T(4,128)}), f32[8,4,2,896]{3,1,2,0:T(4,128)S(1)}, u32[]{:S(2)}, u32[]{:S(2)}) async-start(f32[8,4,2,896]{3,1,2,0:T(4,128)} %broadcast_in_dim.5), calls=%async_computation.4 | async-start | bytes 458752 | tf_op jit(solution)/shard_map/all_to_all | solution.py:154

commit v3 on v2

v3 whole, which is shorter than its diff:
```python
import math

import jax
import jax.numpy as jnp
from jax import lax
from jax.experimental import pallas as pl
from jax.experimental.pallas import tpu as pltpu
from jax.sharding import Mesh
from jax.sharding import PartitionSpec as P

HEADS = 16
HEAD_DIM = 72
ROWS = 128
LANES = 128
WIDTH = 1152
TILES = WIDTH // LANES
OUT = 768
HALF = OUT // 2
BASE = 3 * WIDTH + OUT
PIECE = 896
PIECE_TILES = PIECE // LANES
COLS = BASE + PIECE
INV_ROOT = 1.0 / math.sqrt(HEAD_DIM)
GRAD_SCALE = 1.0 / math.sqrt(512 * ROWS)
BF16 = jnp.bfloat16
F32 = jnp.float32

SEQ = ("yh", "x", "z")
GROUPS = ("yl", "c")


def dot(lhs, rhs, lhs_dim, rhs_dim):
    return lax.dot_general(
        lhs, rhs, (((lhs_dim,), (rhs_dim,)), ((), ())), preferred_element_type=F32
    )


def lanes(tile, base=0):
    return slice(base + tile * LANES, base + (tile + 1) * LANES)


def only_head(index, start, value):
    feature = lax.broadcasted_iota(jnp.int32, value.shape, 1) + start
    inside = (feature >= index * HEAD_DIM) & (feature < (index + 1) * HEAD_DIM)
    return jnp.where(inside, value, jnp.zeros_like(value))


def head_lanes(index):
    first = index * HEAD_DIM // LANES
    last = ((index + 1) * HEAD_DIM - 1) // LANES + 1
    return first * LANES, last * LANES


def head_products(lhs_ref, lhs_base, rhs_ref, rhs_base, index):
    start, stop = head_lanes(index)
    rhs = only_head(index, start, rhs_ref[:, rhs_base + start : rhs_base + stop])
    return dot(lhs_ref[:, lhs_base + start : lhs_base + stop], rhs, 1, 1)


def tile_heads(tile):
    return [
        index
        for index in range(HEADS)
        if index * HEAD_DIM < (tile + 1) * LANES and (index + 1) * HEAD_DIM > tile * LANES
    ]


def stacked_heads(ref, base, tile):
    value = ref[:, lanes(tile, base)]
    return jnp.concatenate(
        [only_head(index, tile * LANES, value) for index in tile_heads(tile)], axis=0
    )


def channel_order():
    natural = lax.broadcasted_iota(jnp.int32, (OUT, OUT), 0)
    place = lax.broadcasted_iota(jnp.int32, (OUT, OUT), 1)
    source = 12 * ((place & 127) >> 1) + 2 * (place >> 7) + (place & 1)
    return jnp.where(natural == source, 1.0, 0.0).astype(BF16)


def half_tiles():
    return [
        (tile // PIECE_TILES, tile % PIECE_TILES, tile // TILES, tile % TILES)
        for tile in range(3 * TILES)
    ]


def pack_kernel(
    core_ref, parts_hbm, cotangent_hbm, weight_hbm, out_ref, parts, cotangent, weight, sems
):
    pairs = [(parts_hbm.at[part], parts.at[part]) for part in range(3)]
    pairs += [(cotangent_hbm, cotangent), (weight_hbm, weight)]
    copies = [
        pltpu.make_async_copy(source, target, sems.at[place])
        for place, (source, target) in enumerate(pairs)
    ]
    for copy in copies:
        copy.start()
    row = lax.broadcasted_iota(jnp.int32, (ROWS, 12), 0)
    col = lax.broadcasted_iota(jnp.int32, (ROWS, 12), 1)
    copies[4].wait()
    repeated = []
    for pair in range(3):
        chosen = col == 6 * core_ref[0] + 2 * pair + (row & 1)
        repeated.append(
            dot(jnp.where(chosen, 1.0, 0.0).astype(BF16), weight[...], 1, 0).astype(BF16)
        )
    column = (lax.broadcasted_iota(jnp.int32, (ROWS, LANES), 0) >> 4) & 3
    for place in range(PIECE_TILES):
        value = jnp.zeros((ROWS, LANES), BF16)
        for piece, at, pair, tile in half_tiles():
            if at == place:
                value = jnp.where(column == piece, repeated[pair][:, lanes(tile)], value)
        out_ref[:, :, lanes(place, BASE)] = value.reshape(64, 2, LANES)
    for part in range(3):
        copies[part].wait()
        out_ref[:, :, part * WIDTH : (part + 1) * WIDTH] = parts[part].reshape(64, 2, WIDTH)
    copies[3].wait()
    out_ref[:, :, 3 * WIDTH : BASE] = cotangent[...].reshape(64, 2, OUT)


def forward_kernel(core_ref, sent_ref, share_ref, channels_ref, weights_ref, rows_ref):
    rows_ref[...] = sent_ref[...].reshape(ROWS, COLS)
    row = lax.broadcasted_iota(jnp.int32, (ROWS, ROWS), 0)
    col = lax.broadcasted_iota(jnp.int32, (ROWS, ROWS), 1)
    bias = jnp.where(((row ^ col) & 1) == 0, 0.0, -1e30)
    for index in range(HEADS):
        weights_ref[index] = head_products(rows_ref, 0, rows_ref, WIDTH, index)
    channels_ref[...] = dot(rows_ref[:, 3 * WIDTH : BASE], channel_order(), 1, 0).astype(BF16)
    for index in range(HEADS):
        scores = weights_ref[index] * INV_ROOT + bias
        powers = jnp.exp(scores - jnp.max(scores, axis=1, keepdims=True))
        weights_ref[index] = powers * (1.0 / jnp.sum(powers, axis=1, keepdims=True))
    for tile in range(TILES):
        rounded = [weights_ref[index].astype(BF16) for index in tile_heads(tile)]
        values = stacked_heads(rows_ref, 2 * WIDTH, tile)
        share_ref[:, lanes(tile)] = dot(jnp.concatenate(rounded, axis=1), values, 1, 0).astype(BF16)
    other = pl.multiple_of((1 - core_ref[0]) * HALF, HALF)
    share_ref[:, WIDTH:] = channels_ref[:, pl.ds(other, HALF)]


def weight_grad_kernel(core_ref, share_ref, received_ref, channels_ref, out_ref):
    own = pl.multiple_of(core_ref[0] * HALF, HALF)
    columns = jnp.concatenate([channels_ref[:, pl.ds(own, HALF)], received_ref[:, WIDTH:]], axis=0)
    features = jnp.concatenate([share_ref[:, :WIDTH], received_ref[:, :WIDTH]], axis=0)
    partial = dot(columns, features, 0, 0).astype(BF16)
    for piece, place, pair, tile in half_tiles():
        out_ref[piece, :, lanes(place)] = partial[pair * ROWS : (pair + 1) * ROWS, lanes(tile)]
    out_ref[3, :, lanes(PIECE_TILES - 1)] = jnp.zeros((ROWS, LANES), BF16)


def backward_kernel(
    core_ref, sent_ref, weights_ref, share_ref, channels_ref, mine_ref, theirs_ref,
    out_ref, rows_ref, matrix_ref, upstream_ref, grad_scores_ref,
):
    rows_ref[...] = sent_ref[...].reshape(ROWS, COLS)
    own = pl.multiple_of(core_ref[0] * HALF, HALF)
    other = pl.multiple_of((1 - core_ref[0]) * HALF, HALF)
    for piece, place, pair, tile in half_tiles():
        for start, half_ref in ((own, mine_ref), (other, theirs_ref)):
            matrix_ref[pl.ds(start + pair * ROWS, ROWS), lanes(tile)] = half_ref[
                piece, :, lanes(place)
            ]
    upstream_ref[...] = dot(channels_ref[...], matrix_ref[...], 1, 0).astype(BF16)
    products = [
        head_products(upstream_ref, 0, rows_ref, 2 * WIDTH, index) for index in range(HEADS)
    ]
    for index in range(HEADS):
        weights, grad_weights = weights_ref[index], products[index]
        centred = grad_weights - jnp.sum(weights * grad_weights, axis=1, keepdims=True)
        grad_scores_ref[index] = (weights * centred * INV_ROOT).astype(BF16)

    def put(start, value):
        out_ref[:, :, start : start + value.shape[1]] = value.astype(BF16).reshape(64, 2, -1)

    projected = dot(share_ref[:, :WIDTH], matrix_ref[...], 1, 1).astype(BF16)
    put(3 * WIDTH, dot(projected, channel_order(), 1, 1))
    for tile in range(TILES):
        heads = tile_heads(tile)
        grad_scores = [grad_scores_ref[index] for index in heads]
        rounded = [weights_ref[index].astype(BF16) for index in heads]
        across, down = jnp.concatenate(grad_scores, axis=1), jnp.concatenate(grad_scores, axis=0)
        put(tile * LANES, dot(across, stacked_heads(rows_ref, WIDTH, tile), 1, 0))
        put(WIDTH + tile * LANES, dot(down, stacked_heads(rows_ref, 0, tile), 0, 0))
        put(
            2 * WIDTH + tile * LANES,
            dot(jnp.concatenate(rounded, axis=0), stacked_heads(upstream_ref, 0, tile), 0, 0),
        )


def merge_kernel(terms_ref, results_ref, out_ref):
    total = terms_ref[0].astype(F32)
    for place in range(1, 4):
        total += terms_ref[place].astype(F32)
    out_ref[:, :, BASE:] = total.astype(BF16).reshape(64, 2, PIECE)


def owned_kernel(back_ref, out_ref):
    rows = back_ref[:, :, BASE:].reshape(ROWS, PIECE)
    target = lax.broadcasted_iota(jnp.int32, (8, ROWS), 0)
    source = lax.broadcasted_iota(jnp.int32, (8, ROWS), 1)
    chosen = target == 2 * ((source >> 4) & 3) + (source & 1)
    total = dot(jnp.where(chosen, 1.0, 0.0).astype(BF16), rows, 1, 0)
    for place in range(8):
        out_ref[place] = total


def total_kernel(terms_ref, out_ref):
    for core in range(2):
        total = terms_ref[core] + terms_ref[2 + core] + terms_ref[4 + core] + terms_ref[6 + core]
        total = total * GRAD_SCALE
        for piece, place, pair, tile in half_tiles():
            start = 6 * core + 2 * pair
            out_ref[start : start + 2, lanes(tile)] = total[
                2 * piece : 2 * piece + 2, lanes(place)
            ]


IN_VMEM = pl.BlockSpec(memory_space=pltpu.VMEM)
IN_SMEM = pl.BlockSpec(memory_space=pltpu.SMEM)
IN_HBM = pl.BlockSpec(memory_space=pltpu.HBM)


def call(kernel, name, operands, specs, outs, scratch=(), aliases=None, grant=12, micros=1):
    return pl.pallas_call(
        kernel,
        out_shape=[jax.ShapeDtypeStruct(shape, dtype) for shape, dtype in outs],
        in_specs=specs,
        out_specs=[IN_VMEM] * len(outs),
        scratch_shapes=list(scratch),
        input_output_aliases=aliases or {},
        compiler_params=pltpu.CompilerParams(vmem_limit_bytes=grant << 20),
        cost_estimate=pl.CostEstimate(
            flops=micros * 10**9, bytes_accessed=micros * 3 * 10**6, transcendentals=0
        ),
        name=name,
    )(*operands)


def exchange(value, axes):
    return lax.all_to_all(value, axes, 0, 0, tiled=True)


def swap(value):
    return lax.ppermute(value, "c", [(0, 1), (1, 0)])


def on_device(query_key_value, out_weight, cotangent):
    core = lax.axis_index("c").astype(jnp.int32).reshape(1)
    (packed,) = call(
        pack_kernel,
        "pack",
        (core, query_key_value.reshape(3, ROWS, WIDTH), cotangent.reshape(ROWS, OUT), out_weight),
        [IN_SMEM] + [IN_HBM] * 3,
        [((64, 2, COLS), BF16)],
        [
            pltpu.VMEM((3, ROWS, WIDTH), BF16),
            pltpu.VMEM((ROWS, OUT), BF16),
            pltpu.VMEM((12, WIDTH), BF16),
            pltpu.SemaphoreType.DMA((5,)),
        ],
        grant=56,
    )
    sent = exchange(packed, SEQ)
    piece = sent[:, :, BASE:].reshape(1, ROWS, PIECE)
    mine = exchange(jnp.broadcast_to(piece, (4, ROWS, PIECE)), "x")
    share, channels, weights = call(
        forward_kernel,
        "forward",
        (core, sent),
        [IN_SMEM, IN_VMEM],
        [((ROWS, WIDTH + HALF), BF16), ((ROWS, OUT), BF16), ((HEADS, ROWS, ROWS), F32)],
        [pltpu.VMEM((ROWS, COLS), BF16)],
        micros=3,
    )
    (partial,) = call(
        weight_grad_kernel,
        "weight_grad",
        (core, share, swap(share), channels),
        [IN_SMEM] + [IN_VMEM] * 3,
        [((4, ROWS, PIECE), BF16)],
    )
    mine, _ = lax.optimization_barrier((mine, share))
    partial, theirs = lax.optimization_barrier((partial, swap(mine)))
    terms = exchange(partial, "x")
    (results,) = call(
        backward_kernel,
        "backward",
        (core, sent, weights, share, channels, mine, theirs),
        [IN_SMEM] + [IN_VMEM] * 6,
        [((64, 2, COLS), BF16)],
        [
            pltpu.VMEM((ROWS, COLS), BF16),
            pltpu.VMEM((OUT, WIDTH), BF16),
            pltpu.VMEM((ROWS, WIDTH), BF16),
            pltpu.VMEM((HEADS, ROWS, ROWS), BF16),
        ],
        micros=4,
    )
    (results,) = call(
        merge_kernel, "merge", (terms, results), [IN_VMEM] * 2, [((64, 2, COLS), BF16)], (), {1: 0}
    )
    back = exchange(results, SEQ)
    (owned,) = call(owned_kernel, "owned", (back,), [IN_VMEM], [((8, 8, PIECE), F32)])
    (total,) = call(
        total_kernel, "total", (exchange(owned, GROUPS),), [IN_VMEM], [((12, WIDTH), F32)]
    )
    frames = back.reshape(ROWS, COLS)
    grads = jnp.stack([frames[:, part * WIDTH : (part + 1) * WIDTH] for part in range(3)])
    return (
        frames[:, 3 * WIDTH : BASE].reshape(1, 1, ROWS, OUT),
        grads.reshape(3, 1, 1, ROWS, WIDTH),
        total,
    )


def solution(mesh):
    split = Mesh(mesh.devices.reshape(4, 2, 2, 4, 8), ("yl", "c", "yh", "x", "z"))
    in_specs = (P(None, GROUPS, SEQ, None, None), P(SEQ, None), P(GROUPS, SEQ, None, None))
    out_specs = (P(GROUPS, SEQ, None, None), P(None, GROUPS, SEQ, None, None), P(SEQ, None))
    return jax.shard_map(
        on_device, mesh=split, in_specs=in_specs, out_specs=out_specs, check_vma=False
    )
```

time: 180 us -> 169 us (0.939)
  blocking collectives: 106 us -> 90 us
  waiting for transfers between devices: 6.33 us -> 20.3 us
  local copies, waits for them, and re-layouts: 15.5 us -> 9.47 us
  starting transfers between devices: 31.7 us -> 34.7 us
  other arithmetic: 3.74 us -> 1.03 us
  Pallas kernels: 14.4 us -> 11.7 us
    all_to_all x3 -> x2, blocking collectives: 106 us -> 90 us  [exchange(): return lax.all_to_all(value, axes, 0, 0, tiled=True)]
    all_to_all x2 -> x3, waiting for transfers between devices: 6.33 us -> 18.7 us  [exchange(): return lax.all_to_all(value, axes, 0, 0, tiled=True)]
    reshape x5 -> x0, local copies, waits for them, and re-layouts: 4.94 us -> none  [the longest x2 3.65 us: on_device(): rows = exchange(packed.reshape(64, 2, COLS), SEQ).reshape(ROWS, COLS)]
    all_to_all x2 -> x3, starting transfers between devices: 19.2 us -> 22.9 us  [exchange(): return lax.all_to_all(value, axes, 0, 0, tiled=True)]
    pallas_call x4 -> x7, Pallas kernels: 14.4 us -> 11.7 us  [call(): pl.pallas_call(kernel, out_shape=[jax.ShapeDtypeStruct(shape, dtype) for...]
    unnamed x16 -> x18, local copies, waits for them, and re-layouts: 6.51 us -> 6.9 us
  transfers between devices with their start and end apart: 4 -> 5, of which waited for: 1 -> 4; matrix products, arithmetic and copies ran while one was open for 2% -> 1% of each run, Pallas kernels for 3% -> 4%
where the time goes in v3:
time: 169 us; the launch traced here: 168 us
  blocking collectives  90 us (53%)
  starting transfers between devices  34.7 us (21%)
  waiting for transfers between devices  20.3 us (12%)
  Pallas kernels  11.7 us (7%)
  local copies, waits for them, and re-layouts  9.47 us (6%)
    all_to_all x2, blocking collectives, exchange(): return lax.all_to_all(value, axes, 0, 0, tiled=True)  90 us
    all_to_all x3, starting transfers between devices, exchange(): return lax.all_to_all(value, axes, 0, 0, tiled=True)  22.9 us
    all_to_all x3, waiting for transfers between devices, exchange(): return lax.all_to_all(value, axes, 0, 0, tiled=True)  18.7 us
    ppermute x2, starting transfers between devices, swap(): return lax.ppermute(value, 'c', [(0, 1), (1, 0)])  11.8 us
    pallas_call x7, Pallas kernels, call(): pl.pallas_call(kernel, out_shape=[jax.ShapeDtypeStruct(shape, dtype) for...  11.7 us
    unnamed x18, local copies, waits for them, and re-layouts  6.9 us
  transfers between devices with their start and end apart: 5, of which 4 were waited for; matrix products, arithmetic and copies ran while one was open for 1% of the time, Pallas kernels for 4%

profile of v3, /device:TPU:1, one launch (start us, length us, event | category | flops | bytes accessed | tf_op | source)
XLA Modules:
  0.0 168.0 jit_solution(8378977071775571931)
XLA Ops:
  0.6 3.0 %pack.1 = bf16[64,2,5120]{2,1,0:T(2,128)(2,1)} custom-call(s32[1]{0:T(128)} %bitcast.core_ref, bf16[3,128,1152]{2,1,0:T(8,128)(2,1)} %bitcast.13, bf16[128,768]{1,0:T(8,128)(2,1)} %bitcast.14, bf16[12,1152]{1,0:T(8,128)(2,1)} %weight_hbm.1), custom_call_target="tpu_custom_call" | custom-call | flops 1000000000 | bytes 3000000 | tf_op jit(solution)/shard_map/pack/pallas_call | solution.py:226
  3.6 49.5 %all_to_all.25.sent_ref = bf16[64,2,5120]{2,1,0:T(2,128)(2,1)S(1)} all-to-all(bf16[64,2,5120]{2,1,0:T(2,128)(2,1)} %pack.1), channel_id=1, replica_groups=mesh['yl'=4,'c'=2,'yh'=2,'x'=4,'z'=8] {'yh','x','z'}, dimensions={0} | all-to-all | bytes 2621440 | tf_op jit(solution)/shard_map/all_to_all | solution.py:242
  53.2 0.2 slice.20
  53.3 0.1 broadcast_in_dim.7
  53.4 1.0 broadcast_in_dim.8
  54.5 5.1 %all-to-all-start.1 = ((bf16[4,128,896]{2,1,0:T(8,128)(2,1)}), bf16[4,128,896]{2,1,0:T(8,128)(2,1)S(1)}, u32[]{:S(2)}, u32[]{:S(2)}) async-start(bf16[4,128,896]{2,1,0:T(8,128)(2,1)} %broadcast_in_dim.8), calls=%async_computation.1 | async-start | bytes 1835008 | tf_op jit(solution)/shard_map/all_to_all | solution.py:242
  59.5 1.4 forward.1
  60.9 0.0 copy-start.4
  60.9 0.7 copy-done.4
  61.6 0.0 copy-start.7
  61.6 1.0 copy-done.7
  62.6 0.0 copy-start.2
  62.6 6.0 %all-to-all-done.1.mine_ref = bf16[4,128,896]{2,1,0:T(8,128)(2,1)S(1)} async-done(((bf16[4,128,896]{2,1,0:T(8,128)(2,1)}), bf16[4,128,896]{2,1,0:T(8,128)(2,1)S(1)}, u32[]{:S(2)}, u32[]{:S(2)}) %all-to-all-start.1) | async-done | bytes 917536 | tf_op jit(solution)/shard_map/all_to_all | solution.py:242
  68.6 9.9 %collective-permute-start.1 = (bf16[4,128,896]{2,1,0:T(8,128)(2,1)S(1)}, bf16[4,128,896]{2,1,0:T(8,128)(2,1)S(1)}, u32[]{:S(2)}, u32[]{:S(2)}) collective-permute-start(bf16[4,128,896]{2,1,0:T(8,128)(2,1)S(1)} %all-to-all-done.1.mine_ref), channel_id=1, source_target_pairs={{0,64},{64,0},{1,65},{65,1},{2,66},{66,2},{3,67},{67,3},{4,68},{68... | collective-permute-start | bytes 2752520 | tf_op jit(solution)/shard_map/ppermute | solution.py:246
  78.5 1.9 %collective-permute-start = (bf16[128,1536]{1,0:T(8,128)(2,1)S(1)}, bf16[128,1536]{1,0:T(8,128)(2,1)S(1)}, u32[]{:S(2)}, u32[]{:S(2)}) collective-permute-start(bf16[128,1536]{1,0:T(8,128)(2,1)S(1)} %get-tuple-element.9.share_ref), channel_id=1, source_target_pairs={{0,64},{64,0},{1,65},{65,1},{2,66},{66,2},{3,67},{67,3},{4,68},{68... | collective-permute-start | bytes 1179656 | tf_op jit(solution)/shard_map/ppermute | solution.py:246
  80.4 1.7 %collective-permute-done.received_ref = bf16[128,1536]{1,0:T(8,128)(2,1)S(1)} collective-permute-done((bf16[128,1536]{1,0:T(8,128)(2,1)S(1)}, bf16[128,1536]{1,0:T(8,128)(2,1)S(1)}, u32[]{:S(2)}, u32[]{:S(2)}) %collective-permute-start) | collective-permute-done | bytes 393248 | tf_op jit(solution)/shard_map/ppermute | solution.py:246
  82.1 0.0 copy-start.5
  82.1 0.9 copy-done.5
  83.0 1.5 weight_grad.1
  84.4 0.0 copy-done.2
  84.5 0.0 collective-permute-done.1.theirs_ref
  84.5 0.0 copy-start
  84.5 4.2 %all-to-all-start.2 = ((bf16[4,128,896]{2,1,0:T(8,128)(2,1)}), bf16[4,128,896]{2,1,0:T(8,128)(2,1)}, u32[]{:S(2)}, u32[]{:S(2)}) async-start(bf16[4,128,896]{2,1,0:T(8,128)(2,1)} %weight_grad.1), calls=%async_computation.2 | async-start | bytes 1835008 | tf_op jit(solution)/shard_map/all_to_all | solution.py:242
  88.7 0.0 copy-done
  88.7 0.0 copy-start.1
  88.7 1.2 copy-done.1
  89.9 0.0 copy-start.3
  89.9 1.0 copy-done.3
  90.9 0.0 copy-start.6
  90.9 0.9 copy-done.6
  91.8 0.0 copy-start.8
  91.8 1.2 copy-done.8
  93.0 3.1 %backward.1.results_ref = bf16[64,2,5120]{2,1,0:T(2,128)(2,1)S(1)} custom-call(s32[1]{0:T(128)} %bitcast.core_ref, bf16[64,2,5120]{2,1,0:T(2,128)(2,1)S(1)} %all_to_all.25.sent_ref, f32[16,128,128]{2,1,0:T(8,128)S(1)} %copy-done.8, bf16[128,1536]{1,0:T(8,128)(2,1)S(1)} %copy-done.3, bf16[128,768]{1,0:T(8,128)(2,1)S(1)} %copy-done.6, ...), custom_call_target="tpu_custom_call" | custom-call | flops 4000000000 | bytes 12000000 | tf_op jit(solution)/shard_map/backward/pallas_call | solution.py:226
  96.1 6.3 %all-to-all-done.2.terms_ref = bf16[4,128,896]{2,1,0:T(8,128)(2,1)} async-done(((bf16[4,128,896]{2,1,0:T(8,128)(2,1)}), bf16[4,128,896]{2,1,0:T(8,128)(2,1)}, u32[]{:S(2)}, u32[]{:S(2)}) %all-to-all-start.2) | async-done | bytes 917536 | tf_op jit(solution)/shard_map/all_to_all | solution.py:242
  102.4 1.3 merge.1
  103.8 40.5 %all_to_all.26.back_ref = bf16[64,2,5120]{2,1,0:T(2,128)(2,1)S(1)} all-to-all(bf16[64,2,5120]{2,1,0:T(2,128)(2,1)S(1)} %merge.1), channel_id=1, replica_groups=mesh['yl'=4,'c'=2,'yh'=2,'x'=4,'z'=8] {'yh','x','z'}, dimensions={0} | all-to-all | bytes 2621440 | tf_op jit(solution)/shard_map/all_to_all | solution.py:242
  144.2 0.5 reshape.29
  144.8 0.1 slice_bitcast_fusion.2
  144.8 0.9 owned.1
  145.7 13.6 %all-to-all-start.4 = ((f32[8,8,896]{2,1,0:T(8,128)}), f32[8,8,896]{2,1,0:T(8,128)S(1)}, u32[]{:S(2)}, u32[]{:S(2)}) async-start(f32[8,8,896]{2,1,0:T(8,128)} %owned.1), calls=%async_computation.4 | async-start | bytes 458752 | tf_op jit(solution)/shard_map/all_to_all | solution.py:242
  159.3 0.7 slice_bitcast_fusion.3
  160.0 1.0 maximum_bitcast_fusion
  161.1 6.3 %all-to-all-done.4.terms_ref = f32[8,8,896]{2,1,0:T(8,128)S(1)} async-done(((f32[8,8,896]{2,1,0:T(8,128)}), f32[8,8,896]{2,1,0:T(8,128)S(1)}, u32[]{:S(2)}, u32[]{:S(2)}) %all-to-all-start.4) | async-done | bytes 229408 | tf_op jit(solution)/shard_map/all_to_all | solution.py:242
  167.4 0.7 total.1
Async XLA Ops:
  54.5 14.1 %all-to-all-start.1 = ((bf16[4,128,896]{2,1,0:T(8,128)(2,1)}), bf16[4,128,896]{2,1,0:T(8,128)(2,1)S(1)}, u32[]{:S(2)}, u32[]{:S(2)}) async-start(bf16[4,128,896]{2,1,0:T(8,128)(2,1)} %broadcast_in_dim.8), calls=%async_computation.1 | async-start | bytes 1835008 | tf_op jit(solution)/shard_map/all_to_all | solution.py:242
  60.9 0.7 copy-start.4
  61.6 1.0 copy-start.7
  62.6 21.9 %copy-start.2 = (bf16[128,1536]{1,0:T(8,128)(2,1)}, bf16[128,1536]{1,0:T(8,128)(2,1)S(1)}, u32[]{:S(2)}) copy-start(bf16[128,1536]{1,0:T(8,128)(2,1)S(1)} %get-tuple-element.9.share_ref) | copy-start | bytes 1179652
  68.6 15.9 %collective-permute-start.1 = (bf16[4,128,896]{2,1,0:T(8,128)(2,1)S(1)}, bf16[4,128,896]{2,1,0:T(8,128)(2,1)S(1)}, u32[]{:S(2)}, u32[]{:S(2)}) collective-permute-start(bf16[4,128,896]{2,1,0:T(8,128)(2,1)S(1)} %all-to-all-done.1.mine_ref), channel_id=1, source_target_pairs={{0,64},{64,0},{1,65},{65,1},{2,66},{66,2},{3,67},{67,3},{4,68},{68... | collective-permute-start | bytes 2752520 | tf_op jit(solution)/shard_map/ppermute | solution.py:246
  78.5 3.6 %collective-permute-start = (bf16[128,1536]{1,0:T(8,128)(2,1)S(1)}, bf16[128,1536]{1,0:T(8,128)(2,1)S(1)}, u32[]{:S(2)}, u32[]{:S(2)}) collective-permute-start(bf16[128,1536]{1,0:T(8,128)(2,1)S(1)} %get-tuple-element.9.share_ref), channel_id=1, source_target_pairs={{0,64},{64,0},{1,65},{65,1},{2,66},{66,2},{3,67},{67,3},{4,68},{68... | collective-permute-start | bytes 1179656 | tf_op jit(solution)/shard_map/ppermute | solution.py:246
  82.1 0.9 copy-start.5
  84.5 4.2 %copy-start = (bf16[4,128,896]{2,1,0:T(8,128)(2,1)}, bf16[4,128,896]{2,1,0:T(8,128)(2,1)S(1)}, u32[]{:S(2)}) copy-start(bf16[4,128,896]{2,1,0:T(8,128)(2,1)S(1)} %collective-permute-done.1.theirs_ref) | copy-start | bytes 2752516
  84.5 18.0 %all-to-all-start.2 = ((bf16[4,128,896]{2,1,0:T(8,128)(2,1)}), bf16[4,128,896]{2,1,0:T(8,128)(2,1)}, u32[]{:S(2)}, u32[]{:S(2)}) async-start(bf16[4,128,896]{2,1,0:T(8,128)(2,1)} %weight_grad.1), calls=%async_computation.2 | async-start | bytes 1835008 | tf_op jit(solution)/shard_map/all_to_all | solution.py:242
  88.7 1.2 copy-start.1
  89.9 1.0 copy-start.3
  90.9 0.9 copy-start.6
  91.8 1.2 copy-start.8
  145.7 21.7 %all-to-all-start.4 = ((f32[8,8,896]{2,1,0:T(8,128)}), f32[8,8,896]{2,1,0:T(8,128)S(1)}, u32[]{:S(2)}, u32[]{:S(2)}) async-start(f32[8,8,896]{2,1,0:T(8,128)} %owned.1), calls=%async_computation.4 | async-start | bytes 458752 | tf_op jit(solution)/shard_map/all_to_all | solution.py:242

commit v4 on v3

--- a/solution.py
+++ b/solution.py
@@ -87,7 +87,7 @@
 
 
 def pack_kernel(
-    core_ref, parts_hbm, cotangent_hbm, weight_hbm, out_ref, parts, cotangent, weight, sems
+    place_ref, parts_hbm, cotangent_hbm, weight_hbm, out_ref, parts, cotangent, weight, sems
 ):
     pairs = [(parts_hbm.at[part], parts.at[part]) for part in range(3)]
     pairs += [(cotangent_hbm, cotangent), (weight_hbm, weight)]
@@ -102,7 +102,7 @@
     copies[4].wait()
     repeated = []
     for pair in range(3):
-        chosen = col == 6 * core_ref[0] + 2 * pair + (row & 1)
+        chosen = col == 6 * place_ref[0] + 2 * pair + (row & 1)
         repeated.append(
             dot(jnp.where(chosen, 1.0, 0.0).astype(BF16), weight[...], 1, 0).astype(BF16)
         )
@@ -120,14 +120,12 @@
     out_ref[:, :, 3 * WIDTH : BASE] = cotangent[...].reshape(64, 2, OUT)
 
 
-def forward_kernel(core_ref, sent_ref, share_ref, channels_ref, weights_ref, rows_ref):
-    rows_ref[...] = sent_ref[...].reshape(ROWS, COLS)
+def attend(rows_ref, weights_ref, put):
     row = lax.broadcasted_iota(jnp.int32, (ROWS, ROWS), 0)
     col = lax.broadcasted_iota(jnp.int32, (ROWS, ROWS), 1)
     bias = jnp.where(((row ^ col) & 1) == 0, 0.0, -1e30)
     for index in range(HEADS):
         weights_ref[index] = head_products(rows_ref, 0, rows_ref, WIDTH, index)
-    channels_ref[...] = dot(rows_ref[:, 3 * WIDTH : BASE], channel_order(), 1, 0).astype(BF16)
     for index in range(HEADS):
         scores = weights_ref[index] * INV_ROOT + bias
         powers = jnp.exp(scores - jnp.max(scores, axis=1, keepdims=True))
@@ -135,28 +133,60 @@
     for tile in range(TILES):
         rounded = [weights_ref[index].astype(BF16) for index in tile_heads(tile)]
         values = stacked_heads(rows_ref, 2 * WIDTH, tile)
-        share_ref[:, lanes(tile)] = dot(jnp.concatenate(rounded, axis=1), values, 1, 0).astype(BF16)
-    other = pl.multiple_of((1 - core_ref[0]) * HALF, HALF)
+        put(tile, dot(jnp.concatenate(rounded, axis=1), values, 1, 0).astype(BF16))
+
+
+def ordered_channels(rows_ref):
+    return dot(rows_ref[:, 3 * WIDTH : BASE], channel_order(), 1, 0).astype(BF16)
+
+
+def forward_kernel(place_ref, sent_ref, share_ref, columns_ref, rows_ref, weights_ref, channels_ref):
+    rows_ref[...] = sent_ref[...].reshape(ROWS, COLS)
+    channels_ref[...] = ordered_channels(rows_ref)
+
+    def put(tile, value):
+        share_ref[:, lanes(tile)] = value
+
+    attend(rows_ref, weights_ref, put)
+    own = pl.multiple_of(place_ref[0] * HALF, HALF)
+    other = pl.multiple_of((1 - place_ref[0]) * HALF, HALF)
+    columns_ref[...] = channels_ref[:, pl.ds(own, HALF)]
     share_ref[:, WIDTH:] = channels_ref[:, pl.ds(other, HALF)]
 
 
-def weight_grad_kernel(core_ref, share_ref, received_ref, channels_ref, out_ref):
-    own = pl.multiple_of(core_ref[0] * HALF, HALF)
-    columns = jnp.concatenate([channels_ref[:, pl.ds(own, HALF)], received_ref[:, WIDTH:]], axis=0)
+def weight_grad_kernel(place_ref, share_ref, received_ref, columns_ref, *out_refs):
+    columns = jnp.concatenate([columns_ref[...], received_ref[:, WIDTH:]], axis=0)
     features = jnp.concatenate([share_ref[:, :WIDTH], received_ref[:, :WIDTH]], axis=0)
     partial = dot(columns, features, 0, 0).astype(BF16)
-    for piece, place, pair, tile in half_tiles():
-        out_ref[piece, :, lanes(place)] = partial[pair * ROWS : (pair + 1) * ROWS, lanes(tile)]
-    out_ref[3, :, lanes(PIECE_TILES - 1)] = jnp.zeros((ROWS, LANES), BF16)
+    for step, out_ref in enumerate(out_refs):
+        target = (place_ref[1] + step) & 3
+        for chosen in range(4):
+
+            @pl.when(target == chosen)
+            def _():
+                for piece, place, pair, tile in half_tiles():
+                    if piece == chosen:
+                        out_ref[:, lanes(place)] = partial[
+                            pair * ROWS : (pair + 1) * ROWS, lanes(tile)
+                        ]
+                if chosen == 3:
+                    out_ref[:, lanes(PIECE_TILES - 1)] = jnp.zeros((ROWS, LANES), BF16)
 
 
 def backward_kernel(
-    core_ref, sent_ref, weights_ref, share_ref, channels_ref, mine_ref, theirs_ref,
-    out_ref, rows_ref, matrix_ref, upstream_ref, grad_scores_ref,
+    place_ref, sent_ref, mine_ref, theirs_ref,
+    out_ref, rows_ref, weights_ref, channels_ref, attended_ref, matrix_ref, upstream_ref,
+    grad_scores_ref,
 ):
     rows_ref[...] = sent_ref[...].reshape(ROWS, COLS)
-    own = pl.multiple_of(core_ref[0] * HALF, HALF)
-    other = pl.multiple_of((1 - core_ref[0]) * HALF, HALF)
+    channels_ref[...] = ordered_channels(rows_ref)
+
+    def put_attended(tile, value):
+        attended_ref[:, lanes(tile)] = value
+
+    attend(rows_ref, weights_ref, put_attended)
+    own = pl.multiple_of(place_ref[0] * HALF, HALF)
+    other = pl.multiple_of((1 - place_ref[0]) * HALF, HALF)
     for piece, place, pair, tile in half_tiles():
         for start, half_ref in ((own, mine_ref), (other, theirs_ref)):
             matrix_ref[pl.ds(start + pair * ROWS, ROWS), lanes(tile)] = half_ref[
@@ -174,7 +204,7 @@
     def put(start, value):
         out_ref[:, :, start : start + value.shape[1]] = value.astype(BF16).reshape(64, 2, -1)
 
-    projected = dot(share_ref[:, :WIDTH], matrix_ref[...], 1, 1).astype(BF16)
+    projected = dot(attended_ref[...], matrix_ref[...], 1, 1).astype(BF16)
     put(3 * WIDTH, dot(projected, channel_order(), 1, 1))
     for tile in range(TILES):
         heads = tile_heads(tile)
@@ -189,10 +219,11 @@
         )
 
 
-def merge_kernel(terms_ref, results_ref, out_ref):
-    total = terms_ref[0].astype(F32)
-    for place in range(1, 4):
-        total += terms_ref[place].astype(F32)
+def merge_kernel(*refs):
+    *terms, _, out_ref = refs
+    total = terms[0][...].astype(F32)
+    for term in terms[1:]:
+        total += term[...].astype(F32)
     out_ref[:, :, BASE:] = total.astype(BF16).reshape(64, 2, PIECE)
 
 
@@ -201,15 +232,20 @@
     target = lax.broadcasted_iota(jnp.int32, (8, ROWS), 0)
     source = lax.broadcasted_iota(jnp.int32, (8, ROWS), 1)
     chosen = target == 2 * ((source >> 4) & 3) + (source & 1)
-    total = dot(jnp.where(chosen, 1.0, 0.0).astype(BF16), rows, 1, 0)
-    for place in range(8):
-        out_ref[place] = total
-
-
-def total_kernel(terms_ref, out_ref):
+    out_ref[...] = dot(jnp.where(chosen, 1.0, 0.0).astype(BF16), rows, 1, 0)
+
+
+def group_kernel(*refs):
+    *terms, out_ref = refs
+    total = terms[0][...]
+    for term in terms[1:]:
+        total += term[...]
+    out_ref[...] = total * GRAD_SCALE
+
+
+def total_kernel(place_ref, mine_ref, theirs_ref, out_ref):
     for core in range(2):
-        total = terms_ref[core] + terms_ref[2 + core] + terms_ref[4 + core] + terms_ref[6 + core]
-        total = total * GRAD_SCALE
+        total = jnp.where(place_ref[0] == core, mine_ref[...], theirs_ref[...])
         for piece, place, pair, tile in half_tiles():
             start = 6 * core + 2 * pair
             out_ref[start : start + 2, lanes(tile)] = total[
@@ -246,12 +282,16 @@
     return lax.ppermute(value, "c", [(0, 1), (1, 0)])
 
 
+def turn(value, axis, step):
+    return lax.ppermute(value, axis, [(place, (place + step) % 4) for place in range(4)])
+
+
 def on_device(query_key_value, out_weight, cotangent):
-    core = lax.axis_index("c").astype(jnp.int32).reshape(1)
+    place = jnp.stack([lax.axis_index("c"), lax.axis_index("x")]).astype(jnp.int32)
     (packed,) = call(
         pack_kernel,
         "pack",
-        (core, query_key_value.reshape(3, ROWS, WIDTH), cotangent.reshape(ROWS, OUT), out_weight),
+        (place, query_key_value.reshape(3, ROWS, WIDTH), cotangent.reshape(ROWS, OUT), out_weight),
         [IN_SMEM] + [IN_HBM] * 3,
         [((64, 2, COLS), BF16)],
         [
@@ -265,33 +305,39 @@
     sent = exchange(packed, SEQ)
     piece = sent[:, :, BASE:].reshape(1, ROWS, PIECE)
     mine = exchange(jnp.broadcast_to(piece, (4, ROWS, PIECE)), "x")
-    share, channels, weights = call(
+    share, columns = call(
         forward_kernel,
         "forward",
-        (core, sent),
+        (place, sent),
         [IN_SMEM, IN_VMEM],
-        [((ROWS, WIDTH + HALF), BF16), ((ROWS, OUT), BF16), ((HEADS, ROWS, ROWS), F32)],
-        [pltpu.VMEM((ROWS, COLS), BF16)],
+        [((ROWS, WIDTH + HALF), BF16), ((ROWS, HALF), BF16)],
+        [
+            pltpu.VMEM((ROWS, COLS), BF16),
+            pltpu.VMEM((HEADS, ROWS, ROWS), F32),
+            pltpu.VMEM((ROWS, OUT), BF16),
+        ],
         micros=3,
     )
-    (partial,) = call(
+    partial = call(
         weight_grad_kernel,
         "weight_grad",
-        (core, share, swap(share), channels),
+        (place, share, swap(share), columns),
         [IN_SMEM] + [IN_VMEM] * 3,
-        [((4, ROWS, PIECE), BF16)],
-    )
-    mine, _ = lax.optimization_barrier((mine, share))
-    partial, theirs = lax.optimization_barrier((partial, swap(mine)))
-    terms = exchange(partial, "x")
+        [((ROWS, PIECE), BF16)] * 4,
+    )
+    terms = [partial[0]] + [turn(partial[step], "x", step) for step in range(1, 4)]
+    mine, _ = lax.optimization_barrier((mine, partial[0]))
     (results,) = call(
         backward_kernel,
         "backward",
-        (core, sent, weights, share, channels, mine, theirs),
-        [IN_SMEM] + [IN_VMEM] * 6,
+        (place, sent, mine, swap(mine)),
+        [IN_SMEM] + [IN_VMEM] * 3,
         [((64, 2, COLS), BF16)],
         [
             pltpu.VMEM((ROWS, COLS), BF16),
+            pltpu.VMEM((HEADS, ROWS, ROWS), F32),
+            pltpu.VMEM((ROWS, OUT), BF16),
+            pltpu.VMEM((ROWS, WIDTH), BF16),
             pltpu.VMEM((OUT, WIDTH), BF16),
             pltpu.VMEM((ROWS, WIDTH), BF16),
             pltpu.VMEM((HEADS, ROWS, ROWS), BF16),
@@ -299,12 +345,28 @@
         micros=4,
     )
     (results,) = call(
-        merge_kernel, "merge", (terms, results), [IN_VMEM] * 2, [((64, 2, COLS), BF16)], (), {1: 0}
+        merge_kernel,
+        "merge",
+        (*terms, results),
+        [IN_VMEM] * 5,
+        [((64, 2, COLS), BF16)],
+        aliases={4: 0},
     )
     back = exchange(results, SEQ)
-    (owned,) = call(owned_kernel, "owned", (back,), [IN_VMEM], [((8, 8, PIECE), F32)])
+    (owned,) = call(owned_kernel, "owned", (back,), [IN_VMEM], [((8, PIECE), F32)])
+    (group,) = call(
+        group_kernel,
+        "group",
+        (owned, *(turn(owned, "yl", step) for step in range(1, 4))),
+        [IN_VMEM] * 4,
+        [((8, PIECE), F32)],
+    )
     (total,) = call(
-        total_kernel, "total", (exchange(owned, GROUPS),), [IN_VMEM], [((12, WIDTH), F32)]
+        total_kernel,
+        "total",
+        (place, group, swap(group)),
+        [IN_SMEM] + [IN_VMEM] * 2,
+        [((12, WIDTH), F32)],
     )
     frames = back.reshape(ROWS, COLS)
     grads = jnp.stack([frames[:, part * WIDTH : (part + 1) * WIDTH] for part in range(3)])

time: 169 us -> 170 us (level)
  starting transfers between devices: 34.7 us -> 47.3 us
  waiting for transfers between devices: 20.3 us -> 8.67 us
  local copies, waits for them, and re-layouts: 9.47 us -> 2.57 us
  blocking collectives: 90 us -> 95.4 us
    ppermute x0 -> x6, starting transfers between devices: none -> 23.4 us  [turn(): lax.ppermute(value, axis, [(place, (place + step) % 4) for place in range...]
    all_to_all x3 -> x1, waiting for transfers between devices: 18.7 us -> 0.01 us  [exchange(): return lax.all_to_all(value, axes, 0, 0, tiled=True)]
    all_to_all x3 -> x1, starting transfers between devices: 22.9 us -> 5.07 us  [exchange(): return lax.all_to_all(value, axes, 0, 0, tiled=True)]
    ppermute x0 -> x6, waiting for transfers between devices: none -> 7.2 us  [turn(): lax.ppermute(value, axis, [(place, (place + step) % 4) for place in range...]
    ppermute x2 -> x3, starting transfers between devices: 11.8 us -> 18.9 us  [swap(): return lax.ppermute(value, 'c', [(0, 1), (1, 0)])]
    unnamed x18 -> x2, local copies, waits for them, and re-layouts: 6.9 us -> 0.01 us
    all_to_all x2, blocking collectives: 90 us -> 95.4 us  [exchange(): return lax.all_to_all(value, axes, 0, 0, tiled=True)]
    pallas_call x7 -> x8, Pallas kernels: 11.7 us -> 12.7 us  [call(): pl.pallas_call(kernel, out_shape=[jax.ShapeDtypeStruct(shape, dtype) for...]
  transfers between devices with their start and end apart: 5 -> 10, of which waited for: 4 -> 5; matrix products, arithmetic and copies ran while one was open for 1% -> 1% of each run, Pallas kernels for 4% -> 5%
where the time goes in v4:
time: 170 us; the launch traced here: 169 us
  blocking collectives  95.4 us (56%)
  starting transfers between devices  47.3 us (28%)
  Pallas kernels  12.7 us (7%)
  waiting for transfers between devices  8.67 us (5%)
  local copies, waits for them, and re-layouts  2.57 us (2%)
    all_to_all x2, blocking collectives, exchange(): return lax.all_to_all(value, axes, 0, 0, tiled=True)  95.4 us
    ppermute x6, starting transfers between devices, turn(): lax.ppermute(value, axis, [(place, (place + step) % 4) for place in range...  23.4 us
    ppermute x3, starting transfers between devices, swap(): return lax.ppermute(value, 'c', [(0, 1), (1, 0)])  18.9 us
    pallas_call x8, Pallas kernels, call(): pl.pallas_call(kernel, out_shape=[jax.ShapeDtypeStruct(shape, dtype) for...  12.7 us
    ppermute x6, waiting for transfers between devices, turn(): lax.ppermute(value, axis, [(place, (place + step) % 4) for place in range...  7.2 us
    all_to_all x1, starting transfers between devices, exchange(): return lax.all_to_all(value, axes, 0, 0, tiled=True)  5.07 us
  transfers between devices with their start and end apart: 10, of which 5 were waited for; matrix products, arithmetic and copies ran while one was open for 1% of the time, Pallas kernels for 5%

profile of v4, /device:TPU:1, one launch (start us, length us, event | category | flops | bytes accessed | tf_op | source)
XLA Modules:
  0.0 169.0 jit_solution(13467570131093403044)
XLA Ops:
  0.6 0.6 pad_add_fusion.place_ref
  1.2 3.5 %pack.1 = bf16[64,2,5120]{2,1,0:T(2,128)(2,1)} custom-call(s32[2]{0:T(128)} %pad_add_fusion.place_ref, bf16[3,128,1152]{2,1,0:T(8,128)(2,1)} %bitcast.14, bf16[128,768]{1,0:T(8,128)(2,1)} %bitcast.15, bf16[12,1152]{1,0:T(8,128)(2,1)} %weight_hbm.1), custom_call_target="tpu_custom_call" | custom-call | flops 1000000000 | bytes 3000000 | tf_op jit(solution)/shard_map/pack/pallas_call | solution.py:262
  4.7 49.5 %all_to_all.15.sent_ref = bf16[64,2,5120]{2,1,0:T(2,128)(2,1)S(1)} all-to-all(bf16[64,2,5120]{2,1,0:T(2,128)(2,1)} %pack.1), channel_id=1, replica_groups=mesh['yl'=4,'c'=2,'yh'=2,'x'=4,'z'=8] {'yh','x','z'}, dimensions={0} | all-to-all | bytes 2621440 | tf_op jit(solution)/shard_map/all_to_all | solution.py:278
  54.3 0.2 slice.20
  54.4 0.1 broadcast_in_dim.7
  54.5 0.0 copy-start
  54.6 1.0 broadcast_in_dim.8
  55.6 5.1 %all-to-all-start.1 = ((bf16[4,128,896]{2,1,0:T(8,128)(2,1)}), bf16[4,128,896]{2,1,0:T(8,128)(2,1)S(1)}, u32[]{:S(2)}, u32[]{:S(2)}) async-start(bf16[4,128,896]{2,1,0:T(8,128)(2,1)} %broadcast_in_dim.8), calls=%async_computation.1 | async-start | bytes 1835008 | tf_op jit(solution)/shard_map/all_to_all | solution.py:278
  60.6 0.0 copy-done
  60.6 1.8 %forward.1 = (bf16[128,1536]{1,0:T(8,128)(2,1)S(1)}, bf16[128,384]{1,0:T(8,128)(2,1)S(1)}) custom-call(s32[2]{0:T(128)S(1)} %copy-done, bf16[64,2,5120]{2,1,0:T(2,128)(2,1)S(1)} %all_to_all.15.sent_ref), custom_call_target="tpu_custom_call" | custom-call | flops 3000000000 | bytes 9000000 | tf_op jit(solution)/shard_map/forward/pallas_call | solution.py:262
  62.5 8.7 %collective-permute-start = (bf16[128,1536]{1,0:T(8,128)(2,1)S(1)}, bf16[128,1536]{1,0:T(8,128)(2,1)S(1)}, u32[]{:S(2)}, u32[]{:S(2)}) collective-permute-start(bf16[128,1536]{1,0:T(8,128)(2,1)S(1)} %get-tuple-element.10.share_ref), channel_id=1, source_target_pairs={{0,64},{64,0},{1,65},{65,1},{2,66},{66,2},{3,67},{67,3},{4,68},{68... | collective-permute-start | bytes 1179656 | tf_op jit(solution)/shard_map/ppermute | solution.py:282
  71.2 1.3 collective-permute-done.received_ref
  72.5 1.2 weight_grad.1
  73.8 0.0 all-to-all-done.1.mine_ref
  73.8 5.8 %collective-permute-start.4 = (bf16[4,128,896]{2,1,0:T(8,128)(2,1)S(1)}, bf16[4,128,896]{2,1,0:T(8,128)(2,1)S(1)}, u32[]{:S(2)}, u32[]{:S(2)}) collective-permute-start(bf16[4,128,896]{2,1,0:T(8,128)(2,1)S(1)} %all-to-all-done.1.mine_ref), channel_id=1, source_target_pairs={{0,64},{64,0},{1,65},{65,1},{2,66},{66,2},{3,67},{67,3},{4,68},{68... | collective-permute-start | bytes 2752520 | tf_op jit(solution)/shard_map/ppermute | solution.py:282
  79.5 2.2 %collective-permute-start.1 = (bf16[128,896]{1,0:T(8,128)(2,1)S(1)}, bf16[128,896]{1,0:T(8,128)(2,1)S(1)}, u32[]{:S(2)}, u32[]{:S(2)}) collective-permute-start(bf16[128,896]{1,0:T(8,128)(2,1)S(1)} %get-tuple-element.13), channel_id=1, source_target_pairs={{0,8},{8,16},{16,24},{24,0},{1,9},{9,17},{17,25},{25,1},{2,10},{10... | collective-permute-start | bytes 688136 | tf_op jit(solution)/shard_map/ppermute | solution.py:286
  81.7 3.7 %collective-permute-start.2 = (bf16[128,896]{1,0:T(8,128)(2,1)S(1)}, bf16[128,896]{1,0:T(8,128)(2,1)S(1)}, u32[]{:S(2)}, u32[]{:S(2)}) collective-permute-start(bf16[128,896]{1,0:T(8,128)(2,1)S(1)} %get-tuple-element.14), channel_id=1, source_target_pairs={{0,16},{8,24},{16,0},{24,8},{1,17},{9,25},{17,1},{25,9},{2,18},{10... | collective-permute-start | bytes 688136 | tf_op jit(solution)/shard_map/ppermute | solution.py:286
  85.4 2.5 %collective-permute-start.3 = (bf16[128,896]{1,0:T(8,128)(2,1)S(1)}, bf16[128,896]{1,0:T(8,128)(2,1)S(1)}, u32[]{:S(2)}, u32[]{:S(2)}) collective-permute-start(bf16[128,896]{1,0:T(8,128)(2,1)S(1)} %get-tuple-element.15), channel_id=1, source_target_pairs={{0,24},{8,0},{16,8},{24,16},{1,25},{9,1},{17,9},{25,17},{2,26},{10... | collective-permute-start | bytes 688136 | tf_op jit(solution)/shard_map/ppermute | solution.py:286
  88.0 0.0 collective-permute-done.4.theirs_ref
  88.0 4.6 %backward.1.refs_4_ = bf16[64,2,5120]{2,1,0:T(2,128)(2,1)S(1)} custom-call(s32[2]{0:T(128)S(1)} %copy-done, bf16[64,2,5120]{2,1,0:T(2,128)(2,1)S(1)} %all_to_all.15.sent_ref, bf16[4,128,896]{2,1,0:T(8,128)(2,1)S(1)} %all-to-all-done.1.mine_ref, bf16[4,128,896]{2,1,0:T(8,128)(2,1)S(1)} %collective-permute-done.4.theirs_ref), custom_call_target="tpu_custom_call" | custom-call | flops 4000000000 | bytes 12000000 | tf_op jit(solution)/shard_map/backward/pallas_call | solution.py:262
  92.6 2.2 %collective-permute-done.1.refs_1_ = bf16[128,896]{1,0:T(8,128)(2,1)S(1)} collective-permute-done((bf16[128,896]{1,0:T(8,128)(2,1)S(1)}, bf16[128,896]{1,0:T(8,128)(2,1)S(1)}, u32[]{:S(2)}, u32[]{:S(2)}) %collective-permute-start.1) | collective-permute-done | bytes 229408 | tf_op jit(solution)/shard_map/ppermute | solution.py:286
  94.8 0.0 collective-permute-done.2.refs_2_
  94.8 2.2 %collective-permute-done.3.refs_3_ = bf16[128,896]{1,0:T(8,128)(2,1)S(1)} collective-permute-done((bf16[128,896]{1,0:T(8,128)(2,1)S(1)}, bf16[128,896]{1,0:T(8,128)(2,1)S(1)}, u32[]{:S(2)}, u32[]{:S(2)}) %collective-permute-start.3) | collective-permute-done | bytes 229408 | tf_op jit(solution)/shard_map/ppermute | solution.py:286
  97.0 0.2 merge.1
  97.2 45.8 %all_to_all.16.back_ref = bf16[64,2,5120]{2,1,0:T(2,128)(2,1)S(1)} all-to-all(bf16[64,2,5120]{2,1,0:T(2,128)(2,1)S(1)} %merge.1), channel_id=1, replica_groups=mesh['yl'=4,'c'=2,'yh'=2,'x'=4,'z'=8] {'yh','x','z'}, dimensions={0} | all-to-all | bytes 2621440 | tf_op jit(solution)/shard_map/all_to_all | solution.py:278
  143.0 0.2 owned.1.refs_0_
  143.1 2.4 %collective-permute-start.7 = (f32[8,896]{1,0:T(8,128)S(1)}, f32[8,896]{1,0:T(8,128)S(1)}, u32[]{:S(2)}, u32[]{:S(2)}) collective-permute-start(f32[8,896]{1,0:T(8,128)S(1)} %owned.1.refs_0_), channel_id=1, source_target_pairs={{0,384},{128,0},{256,128},{384,256},{1,385},{129,1},{257,129},{385... | collective-permute-start | bytes 86024 | tf_op jit(solution)/shard_map/ppermute | solution.py:286
  145.5 10.6 %collective-permute-start.6 = (f32[8,896]{1,0:T(8,128)S(1)}, f32[8,896]{1,0:T(8,128)S(1)}, u32[]{:S(2)}, u32[]{:S(2)}) collective-permute-start(f32[8,896]{1,0:T(8,128)S(1)} %owned.1.refs_0_), channel_id=1, source_target_pairs={{0,256},{128,384},{256,0},{384,128},{1,257},{129,385},{257,1},{385... | collective-permute-start | bytes 86024 | tf_op jit(solution)/shard_map/ppermute | solution.py:286
  156.2 1.9 %collective-permute-start.5 = (f32[8,896]{1,0:T(8,128)S(1)}, f32[8,896]{1,0:T(8,128)S(1)}, u32[]{:S(2)}, u32[]{:S(2)}) collective-permute-start(f32[8,896]{1,0:T(8,128)S(1)} %owned.1.refs_0_), channel_id=1, source_target_pairs={{0,128},{128,256},{256,384},{384,0},{1,129},{129,257},{257,385},{3... | collective-permute-start | bytes 86024 | tf_op jit(solution)/shard_map/ppermute | solution.py:286
  158.1 0.5 reshape.25
  158.6 0.1 slice_bitcast_fusion.2
  158.7 1.0 maximum_bitcast_fusion
  159.8 0.0 collective-permute-done.7.refs_3_
  159.8 0.0 collective-permute-done.6.refs_2_
  159.8 2.8 %collective-permute-done.5.refs_1_ = f32[8,896]{1,0:T(8,128)S(1)} collective-permute-done((f32[8,896]{1,0:T(8,128)S(1)}, f32[8,896]{1,0:T(8,128)S(1)}, u32[]{:S(2)}, u32[]{:S(2)}) %collective-permute-start.5) | collective-permute-done | bytes 28704 | tf_op jit(solution)/shard_map/ppermute | solution.py:286
  162.6 4.4 %collective-permute-start.8 = (f32[8,896]{1,0:T(8,128)S(1)}, f32[8,896]{1,0:T(8,128)S(1)}, u32[]{:S(2)}, u32[]{:S(2)}) collective-permute-start(f32[8,896]{1,0:T(8,128)S(1)} %group.1.mine_ref), channel_id=1, source_target_pairs={{0,64},{64,0},{1,65},{65,1},{2,66},{66,2},{3,67},{67,3},{4,68},{68... | collective-permute-start | bytes 86024 | tf_op jit(solution)/shard_map/ppermute | solution.py:282
  167.0 0.7 slice_bitcast_fusion.3
  167.7 0.1 collective-permute-done.8.theirs_ref
  167.9 1.2 total.1
  (1 shorter events, 0.0 us)
Async XLA Ops:
  54.5 6.1 %copy-start = (s32[2]{0:T(128)S(1)}, s32[2]{0:T(128)}, u32[]{:S(2)}) copy-start(s32[2]{0:T(128)} %pad_add_fusion.place_ref) | copy-start | bytes 28
  55.6 18.2 %all-to-all-start.1 = ((bf16[4,128,896]{2,1,0:T(8,128)(2,1)}), bf16[4,128,896]{2,1,0:T(8,128)(2,1)S(1)}, u32[]{:S(2)}, u32[]{:S(2)}) async-start(bf16[4,128,896]{2,1,0:T(8,128)(2,1)} %broadcast_in_dim.8), calls=%async_computation.1 | async-start | bytes 1835008 | tf_op jit(solution)/shard_map/all_to_all | solution.py:278
  62.5 10.1 %collective-permute-start = (bf16[128,1536]{1,0:T(8,128)(2,1)S(1)}, bf16[128,1536]{1,0:T(8,128)(2,1)S(1)}, u32[]{:S(2)}, u32[]{:S(2)}) collective-permute-start(bf16[128,1536]{1,0:T(8,128)(2,1)S(1)} %get-tuple-element.10.share_ref), channel_id=1, source_target_pairs={{0,64},{64,0},{1,65},{65,1},{2,66},{66,2},{3,67},{67,3},{4,68},{68... | collective-permute-start | bytes 1179656 | tf_op jit(solution)/shard_map/ppermute | solution.py:282
  73.8 14.2 %collective-permute-start.4 = (bf16[4,128,896]{2,1,0:T(8,128)(2,1)S(1)}, bf16[4,128,896]{2,1,0:T(8,128)(2,1)S(1)}, u32[]{:S(2)}, u32[]{:S(2)}) collective-permute-start(bf16[4,128,896]{2,1,0:T(8,128)(2,1)S(1)} %all-to-all-done.1.mine_ref), channel_id=1, source_target_pairs={{0,64},{64,0},{1,65},{65,1},{2,66},{66,2},{3,67},{67,3},{4,68},{68... | collective-permute-start | bytes 2752520 | tf_op jit(solution)/shard_map/ppermute | solution.py:282
  79.5 15.2 %collective-permute-start.1 = (bf16[128,896]{1,0:T(8,128)(2,1)S(1)}, bf16[128,896]{1,0:T(8,128)(2,1)S(1)}, u32[]{:S(2)}, u32[]{:S(2)}) collective-permute-start(bf16[128,896]{1,0:T(8,128)(2,1)S(1)} %get-tuple-element.13), channel_id=1, source_target_pairs={{0,8},{8,16},{16,24},{24,0},{1,9},{9,17},{17,25},{25,1},{2,10},{10... | collective-permute-start | bytes 688136 | tf_op jit(solution)/shard_map/ppermute | solution.py:286
  81.7 13.0 %collective-permute-start.2 = (bf16[128,896]{1,0:T(8,128)(2,1)S(1)}, bf16[128,896]{1,0:T(8,128)(2,1)S(1)}, u32[]{:S(2)}, u32[]{:S(2)}) collective-permute-start(bf16[128,896]{1,0:T(8,128)(2,1)S(1)} %get-tuple-element.14), channel_id=1, source_target_pairs={{0,16},{8,24},{16,0},{24,8},{1,17},{9,25},{17,1},{25,9},{2,18},{10... | collective-permute-start | bytes 688136 | tf_op jit(solution)/shard_map/ppermute | solution.py:286
  85.4 11.6 %collective-permute-start.3 = (bf16[128,896]{1,0:T(8,128)(2,1)S(1)}, bf16[128,896]{1,0:T(8,128)(2,1)S(1)}, u32[]{:S(2)}, u32[]{:S(2)}) collective-permute-start(bf16[128,896]{1,0:T(8,128)(2,1)S(1)} %get-tuple-element.15), channel_id=1, source_target_pairs={{0,24},{8,0},{16,8},{24,16},{1,25},{9,1},{17,9},{25,17},{2,26},{10... | collective-permute-start | bytes 688136 | tf_op jit(solution)/shard_map/ppermute | solution.py:286
  143.1 16.6 %collective-permute-start.7 = (f32[8,896]{1,0:T(8,128)S(1)}, f32[8,896]{1,0:T(8,128)S(1)}, u32[]{:S(2)}, u32[]{:S(2)}) collective-permute-start(f32[8,896]{1,0:T(8,128)S(1)} %owned.1.refs_0_), channel_id=1, source_target_pairs={{0,384},{128,0},{256,128},{384,256},{1,385},{129,1},{257,129},{385... | collective-permute-start | bytes 86024 | tf_op jit(solution)/shard_map/ppermute | solution.py:286
  145.5 14.2 %collective-permute-start.6 = (f32[8,896]{1,0:T(8,128)S(1)}, f32[8,896]{1,0:T(8,128)S(1)}, u32[]{:S(2)}, u32[]{:S(2)}) collective-permute-start(f32[8,896]{1,0:T(8,128)S(1)} %owned.1.refs_0_), channel_id=1, source_target_pairs={{0,256},{128,384},{256,0},{384,128},{1,257},{129,385},{257,1},{385... | collective-permute-start | bytes 86024 | tf_op jit(solution)/shard_map/ppermute | solution.py:286
  156.2 6.4 %collective-permute-start.5 = (f32[8,896]{1,0:T(8,128)S(1)}, f32[8,896]{1,0:T(8,128)S(1)}, u32[]{:S(2)}, u32[]{:S(2)}) collective-permute-start(f32[8,896]{1,0:T(8,128)S(1)} %owned.1.refs_0_), channel_id=1, source_target_pairs={{0,128},{128,256},{256,384},{384,0},{1,129},{129,257},{257,385},{3... | collective-permute-start | bytes 86024 | tf_op jit(solution)/shard_map/ppermute | solution.py:286
  162.6 5.3 %collective-permute-start.8 = (f32[8,896]{1,0:T(8,128)S(1)}, f32[8,896]{1,0:T(8,128)S(1)}, u32[]{:S(2)}, u32[]{:S(2)}) collective-permute-start(f32[8,896]{1,0:T(8,128)S(1)} %group.1.mine_ref), channel_id=1, source_target_pairs={{0,64},{64,0},{1,65},{65,1},{2,66},{66,2},{3,67},{67,3},{4,68},{68... | collective-permute-start | bytes 86024 | tf_op jit(solution)/shard_map/ppermute | solution.py:282

commit v5 on v4

--- a/solution.py
+++ b/solution.py
@@ -20,6 +20,7 @@
 PIECE = 896
 PIECE_TILES = PIECE // LANES
 COLS = BASE + PIECE
+HALF_WIDTH = 3 * WIDTH
 INV_ROOT = 1.0 / math.sqrt(HEAD_DIM)
 GRAD_SCALE = 1.0 / math.sqrt(512 * ROWS)
 BF16 = jnp.bfloat16
@@ -87,7 +88,7 @@
 
 
 def pack_kernel(
-    place_ref, parts_hbm, cotangent_hbm, weight_hbm, out_ref, parts, cotangent, weight, sems
+    core_ref, parts_hbm, cotangent_hbm, weight_hbm, out_ref, parts, cotangent, weight, sems
 ):
     pairs = [(parts_hbm.at[part], parts.at[part]) for part in range(3)]
     pairs += [(cotangent_hbm, cotangent), (weight_hbm, weight)]
@@ -102,7 +103,7 @@
     copies[4].wait()
     repeated = []
     for pair in range(3):
-        chosen = col == 6 * place_ref[0] + 2 * pair + (row & 1)
+        chosen = col == 6 * core_ref[0] + 2 * pair + (row & 1)
         repeated.append(
             dot(jnp.where(chosen, 1.0, 0.0).astype(BF16), weight[...], 1, 0).astype(BF16)
         )
@@ -140,7 +141,7 @@
     return dot(rows_ref[:, 3 * WIDTH : BASE], channel_order(), 1, 0).astype(BF16)
 
 
-def forward_kernel(place_ref, sent_ref, share_ref, columns_ref, rows_ref, weights_ref, channels_ref):
+def forward_kernel(core_ref, sent_ref, share_ref, columns_ref, rows_ref, weights_ref, channels_ref):
     rows_ref[...] = sent_ref[...].reshape(ROWS, COLS)
     channels_ref[...] = ordered_channels(rows_ref)
 
@@ -148,33 +149,29 @@
         share_ref[:, lanes(tile)] = value
 
     attend(rows_ref, weights_ref, put)
-    own = pl.multiple_of(place_ref[0] * HALF, HALF)
-    other = pl.multiple_of((1 - place_ref[0]) * HALF, HALF)
+    own = pl.multiple_of(core_ref[0] * HALF, HALF)
+    other = pl.multiple_of((1 - core_ref[0]) * HALF, HALF)
     columns_ref[...] = channels_ref[:, pl.ds(own, HALF)]
     share_ref[:, WIDTH:] = channels_ref[:, pl.ds(other, HALF)]
 
 
-def weight_grad_kernel(place_ref, share_ref, received_ref, columns_ref, *out_refs):
+def weight_grad_kernel(x_ref, share_ref, received_ref, columns_ref, *refs):
+    *out_refs, partial_ref = refs
     columns = jnp.concatenate([columns_ref[...], received_ref[:, WIDTH:]], axis=0)
     features = jnp.concatenate([share_ref[:, :WIDTH], received_ref[:, :WIDTH]], axis=0)
-    partial = dot(columns, features, 0, 0).astype(BF16)
+    partial_ref[...] = dot(columns, features, 0, 0).astype(BF16)
     for step, out_ref in enumerate(out_refs):
-        target = (place_ref[1] + step) & 3
-        for chosen in range(4):
-
-            @pl.when(target == chosen)
-            def _():
-                for piece, place, pair, tile in half_tiles():
-                    if piece == chosen:
-                        out_ref[:, lanes(place)] = partial[
-                            pair * ROWS : (pair + 1) * ROWS, lanes(tile)
-                        ]
-                if chosen == 3:
-                    out_ref[:, lanes(PIECE_TILES - 1)] = jnp.zeros((ROWS, LANES), BF16)
+        target = ((x_ref[0] + step) & 3) * 16
+        for high in range(2):
+            for pair in range(3):
+                start = pl.multiple_of(pair * ROWS + high * 64 + target, 16)
+                out_ref[high * 16 : high * 16 + 16, pair * WIDTH : (pair + 1) * WIDTH] = (
+                    partial_ref[pl.ds(start, 16), :]
+                )
 
 
 def backward_kernel(
-    place_ref, sent_ref, mine_ref, theirs_ref,
+    core_ref, sent_ref, mine_ref, theirs_ref,
     out_ref, rows_ref, weights_ref, channels_ref, attended_ref, matrix_ref, upstream_ref,
     grad_scores_ref,
 ):
@@ -185,8 +182,8 @@
         attended_ref[:, lanes(tile)] = value
 
     attend(rows_ref, weights_ref, put_attended)
-    own = pl.multiple_of(place_ref[0] * HALF, HALF)
-    other = pl.multiple_of((1 - place_ref[0]) * HALF, HALF)
+    own = pl.multiple_of(core_ref[0] * HALF, HALF)
+    other = pl.multiple_of((1 - core_ref[0]) * HALF, HALF)
     for piece, place, pair, tile in half_tiles():
         for start, half_ref in ((own, mine_ref), (other, theirs_ref)):
             matrix_ref[pl.ds(start + pair * ROWS, ROWS), lanes(tile)] = half_ref[
@@ -220,19 +217,19 @@
 
 
 def merge_kernel(*refs):
-    *terms, _, out_ref = refs
+    *terms, out_ref = refs
     total = terms[0][...].astype(F32)
     for term in terms[1:]:
         total += term[...].astype(F32)
-    out_ref[:, :, BASE:] = total.astype(BF16).reshape(64, 2, PIECE)
-
-
-def owned_kernel(back_ref, out_ref):
-    rows = back_ref[:, :, BASE:].reshape(ROWS, PIECE)
-    target = lax.broadcasted_iota(jnp.int32, (8, ROWS), 0)
-    source = lax.broadcasted_iota(jnp.int32, (8, ROWS), 1)
-    chosen = target == 2 * ((source >> 4) & 3) + (source & 1)
-    out_ref[...] = dot(jnp.where(chosen, 1.0, 0.0).astype(BF16), rows, 1, 0)
+    out_ref[...] = total.astype(BF16).reshape(16, 2, HALF_WIDTH)
+
+
+def owned_kernel(terms_ref, out_ref):
+    rows = terms_ref[...].reshape(32, HALF_WIDTH)
+    target = lax.broadcasted_iota(jnp.int32, (8, 32), 0)
+    source = lax.broadcasted_iota(jnp.int32, (8, 32), 1)
+    chosen = jnp.where(target == (source & 1), 1.0, 0.0).astype(BF16)
+    out_ref[...] = dot(chosen, rows, 1, 0)[:2]
 
 
 def group_kernel(*refs):
@@ -243,14 +240,12 @@
     out_ref[...] = total * GRAD_SCALE
 
 
-def total_kernel(place_ref, mine_ref, theirs_ref, out_ref):
+def total_kernel(core_ref, mine_ref, theirs_ref, out_ref):
     for core in range(2):
-        total = jnp.where(place_ref[0] == core, mine_ref[...], theirs_ref[...])
-        for piece, place, pair, tile in half_tiles():
+        total = jnp.where(core_ref[0] == core, mine_ref[...], theirs_ref[...])
+        for pair in range(3):
             start = 6 * core + 2 * pair
-            out_ref[start : start + 2, lanes(tile)] = total[
-                2 * piece : 2 * piece + 2, lanes(place)
-            ]
+            out_ref[start : start + 2, :] = total[:, pair * WIDTH : (pair + 1) * WIDTH]
 
 
 IN_VMEM = pl.BlockSpec(memory_space=pltpu.VMEM)
@@ -287,11 +282,12 @@
 
 
 def on_device(query_key_value, out_weight, cotangent):
-    place = jnp.stack([lax.axis_index("c"), lax.axis_index("x")]).astype(jnp.int32)
+    core = lax.axis_index("c").astype(jnp.int32).reshape(1)
+    x_place = lax.axis_index("x").astype(jnp.int32).reshape(1)
     (packed,) = call(
         pack_kernel,
         "pack",
-        (place, query_key_value.reshape(3, ROWS, WIDTH), cotangent.reshape(ROWS, OUT), out_weight),
+        (core, query_key_value.reshape(3, ROWS, WIDTH), cotangent.reshape(ROWS, OUT), out_weight),
         [IN_SMEM] + [IN_HBM] * 3,
         [((64, 2, COLS), BF16)],
         [
@@ -303,12 +299,10 @@
         grant=56,
     )
     sent = exchange(packed, SEQ)
-    piece = sent[:, :, BASE:].reshape(1, ROWS, PIECE)
-    mine = exchange(jnp.broadcast_to(piece, (4, ROWS, PIECE)), "x")
     share, columns = call(
         forward_kernel,
         "forward",
-        (place, sent),
+        (core, sent),
         [IN_SMEM, IN_VMEM],
         [((ROWS, WIDTH + HALF), BF16), ((ROWS, HALF), BF16)],
         [
@@ -318,21 +312,27 @@
         ],
         micros=3,
     )
+    piece, _ = lax.optimization_barrier((sent[:, :, BASE:], share))
+    mine = exchange(jnp.broadcast_to(piece.reshape(1, ROWS, PIECE), (4, ROWS, PIECE)), "x")
     partial = call(
         weight_grad_kernel,
         "weight_grad",
-        (place, share, swap(share), columns),
+        (x_place, share, swap(share), columns),
         [IN_SMEM] + [IN_VMEM] * 3,
-        [((ROWS, PIECE), BF16)] * 4,
+        [((32, HALF_WIDTH), BF16)] * 4,
+        [pltpu.VMEM((HALF, WIDTH), BF16)],
     )
     terms = [partial[0]] + [turn(partial[step], "x", step) for step in range(1, 4)]
-    mine, _ = lax.optimization_barrier((mine, partial[0]))
+    (summed,) = call(
+        merge_kernel, "merge", terms, [IN_VMEM] * 4, [((16, 2, HALF_WIDTH), BF16)]
+    )
+    mine, summed = lax.optimization_barrier((mine, summed))
     (results,) = call(
         backward_kernel,
         "backward",
-        (place, sent, mine, swap(mine)),
+        (core, sent, mine, swap(mine)),
         [IN_SMEM] + [IN_VMEM] * 3,
-        [((64, 2, COLS), BF16)],
+        [((64, 2, BASE), BF16)],
         [
             pltpu.VMEM((ROWS, COLS), BF16),
             pltpu.VMEM((HEADS, ROWS, ROWS), F32),
@@ -344,34 +344,25 @@
         ],
         micros=4,
     )
-    (results,) = call(
-        merge_kernel,
-        "merge",
-        (*terms, results),
-        [IN_VMEM] * 5,
-        [((64, 2, COLS), BF16)],
-        aliases={4: 0},
-    )
+    collected = exchange(summed, ("yh", "z"))
+    results, collected = lax.optimization_barrier((results, collected))
+    (owned,) = call(owned_kernel, "owned", (collected,), [IN_VMEM], [((2, HALF_WIDTH), F32)])
+    turned = [turn(owned, "yl", step) for step in range(1, 4)]
     back = exchange(results, SEQ)
-    (owned,) = call(owned_kernel, "owned", (back,), [IN_VMEM], [((8, PIECE), F32)])
     (group,) = call(
-        group_kernel,
-        "group",
-        (owned, *(turn(owned, "yl", step) for step in range(1, 4))),
-        [IN_VMEM] * 4,
-        [((8, PIECE), F32)],
+        group_kernel, "group", (owned, *turned), [IN_VMEM] * 4, [((2, HALF_WIDTH), F32)]
     )
     (total,) = call(
         total_kernel,
         "total",
-        (place, group, swap(group)),
+        (core, group, swap(group)),
         [IN_SMEM] + [IN_VMEM] * 2,
         [((12, WIDTH), F32)],
     )
-    frames = back.reshape(ROWS, COLS)
+    frames = back.reshape(ROWS, BASE)
     grads = jnp.stack([frames[:, part * WIDTH : (part + 1) * WIDTH] for part in range(3)])
     return (
-        frames[:, 3 * WIDTH : BASE].reshape(1, 1, ROWS, OUT),
+        frames[:, 3 * WIDTH :].reshape(1, 1, ROWS, OUT),
         grads.reshape(3, 1, 1, ROWS, WIDTH),
         total,
     )

time: 170 us -> 160 us (0.941)
  the two profiles are of different devices: /device:TPU:1 before, /device:TPU:14 now
where the time goes in v5:
time: 160 us; the launch traced here: 159 us
  blocking collectives  59 us (37%)
  waiting for transfers between devices  46.9 us (29%)
  starting transfers between devices  38 us (24%)
  Pallas kernels  11.3 us (7%)
  local copies, waits for them, and re-layouts  2.43 us (2%)
    all_to_all x1, blocking collectives, exchange(): return lax.all_to_all(value, axes, 0, 0, tiled=True)  59 us
    ppermute x6, waiting for transfers between devices, turn(): lax.ppermute(value, axis, [(place, (place + step) % 4) for place in range...  27.8 us
    all_to_all x3, waiting for transfers between devices, exchange(): return lax.all_to_all(value, axes, 0, 0, tiled=True)  17.9 us
    ppermute x6, starting transfers between devices, turn(): lax.ppermute(value, axis, [(place, (place + step) % 4) for place in range...  17.3 us
    all_to_all x3, starting transfers between devices, exchange(): return lax.all_to_all(value, axes, 0, 0, tiled=True)  15 us
    pallas_call x8, Pallas kernels, call(): pl.pallas_call(kernel, out_shape=[jax.ShapeDtypeStruct(shape, dtype) for...  11.3 us
    ppermute x3, starting transfers between devices, swap(): return lax.ppermute(value, 'c', [(0, 1), (1, 0)])  5.76 us
  transfers between devices with their start and end apart: 12, of which 7 were waited for; matrix products, arithmetic and copies ran while one was open for 1% of the time, Pallas kernels for 5%

profile of v5, /device:TPU:14, one launch (start us, length us, event | category | flops | bytes accessed | tf_op | source)
XLA Modules:
  0.0 159.5 jit_solution(11607208377544401135)
XLA Ops:
  0.6 2.8 %pack.1 = bf16[64,2,5120]{2,1,0:T(2,128)(2,1)} custom-call(s32[1]{0:T(128)} %bitcast.core_ref, bf16[3,128,1152]{2,1,0:T(8,128)(2,1)} %bitcast.14, bf16[128,768]{1,0:T(8,128)(2,1)} %bitcast.15, bf16[12,1152]{1,0:T(8,128)(2,1)} %weight_hbm.1), custom_call_target="tpu_custom_call" | custom-call | flops 1000000000 | bytes 3000000 | tf_op jit(solution)/shard_map/pack/pallas_call | solution.py:257
  3.5 59.0 %all_to_all.20.sent_ref = bf16[64,2,5120]{2,1,0:T(2,128)(2,1)S(1)} all-to-all(bf16[64,2,5120]{2,1,0:T(2,128)(2,1)} %pack.1), channel_id=1, replica_groups=mesh['yl'=4,'c'=2,'yh'=2,'x'=4,'z'=8] {'yh','x','z'}, dimensions={0} | all-to-all | bytes 2621440 | tf_op jit(solution)/shard_map/all_to_all | solution.py:273
  62.5 1.3 forward.1
  63.8 1.9 %collective-permute-start = (bf16[128,1536]{1,0:T(8,128)(2,1)S(1)}, bf16[128,1536]{1,0:T(8,128)(2,1)S(1)}, u32[]{:S(2)}, u32[]{:S(2)}) collective-permute-start(bf16[128,1536]{1,0:T(8,128)(2,1)S(1)} %get-tuple-element.14.share_ref), channel_id=1, source_target_pairs={{0,64},{64,0},{1,65},{65,1},{2,66},{66,2},{3,67},{67,3},{4,68},{68... | collective-permute-start | bytes 1179656 | tf_op jit(solution)/shard_map/ppermute | solution.py:277
  65.7 0.2 slice.20
  65.9 0.1 broadcast_in_dim.7
  66.0 1.0 broadcast_in_dim.8
  67.0 4.5 %all-to-all-start.1 = ((bf16[4,128,896]{2,1,0:T(8,128)(2,1)}), bf16[4,128,896]{2,1,0:T(8,128)(2,1)S(1)}, u32[]{:S(2)}, u32[]{:S(2)}) async-start(bf16[4,128,896]{2,1,0:T(8,128)(2,1)} %broadcast_in_dim.8), calls=%async_computation.1 | async-start | bytes 1835008 | tf_op jit(solution)/shard_map/all_to_all | solution.py:273
  71.5 0.0 collective-permute-done.received_ref
  71.5 0.5 weight_grad.1
  72.0 1.9 %collective-permute-start.1 = (bf16[32,3456]{1,0:T(8,128)(2,1)S(1)}, bf16[32,3456]{1,0:T(8,128)(2,1)S(1)}, u32[]{:S(2)}, u32[]{:S(2)}) collective-permute-start(bf16[32,3456]{1,0:T(8,128)(2,1)S(1)} %get-tuple-element.18), channel_id=1, source_target_pairs={{0,8},{8,16},{16,24},{24,0},{1,9},{9,17},{17,25},{25,1},{2,10},{10... | collective-permute-start | bytes 663560 | tf_op jit(solution)/shard_map/ppermute | solution.py:281
  73.9 4.8 %collective-permute-start.2 = (bf16[32,3456]{1,0:T(8,128)(2,1)S(1)}, bf16[32,3456]{1,0:T(8,128)(2,1)S(1)}, u32[]{:S(2)}, u32[]{:S(2)}) collective-permute-start(bf16[32,3456]{1,0:T(8,128)(2,1)S(1)} %get-tuple-element.19), channel_id=1, source_target_pairs={{0,16},{8,24},{16,0},{24,8},{1,17},{9,25},{17,1},{25,9},{2,18},{10... | collective-permute-start | bytes 663560 | tf_op jit(solution)/shard_map/ppermute | solution.py:281
  78.8 1.9 %collective-permute-start.3 = (bf16[32,3456]{1,0:T(8,128)(2,1)S(1)}, bf16[32,3456]{1,0:T(8,128)(2,1)S(1)}, u32[]{:S(2)}, u32[]{:S(2)}) collective-permute-start(bf16[32,3456]{1,0:T(8,128)(2,1)S(1)} %get-tuple-element.20), channel_id=1, source_target_pairs={{0,24},{8,0},{16,8},{24,16},{1,25},{9,1},{17,9},{25,17},{2,26},{10... | collective-permute-start | bytes 663560 | tf_op jit(solution)/shard_map/ppermute | solution.py:281
  80.7 8.0 %collective-permute-done.1.refs_1_ = bf16[32,3456]{1,0:T(8,128)(2,1)S(1)} collective-permute-done((bf16[32,3456]{1,0:T(8,128)(2,1)S(1)}, bf16[32,3456]{1,0:T(8,128)(2,1)S(1)}, u32[]{:S(2)}, u32[]{:S(2)}) %collective-permute-start.1) | collective-permute-done | bytes 221216 | tf_op jit(solution)/shard_map/ppermute | solution.py:281
  88.7 0.6 collective-permute-done.2.refs_2_
  89.3 4.0 %collective-permute-done.3.refs_3_ = bf16[32,3456]{1,0:T(8,128)(2,1)S(1)} collective-permute-done((bf16[32,3456]{1,0:T(8,128)(2,1)S(1)}, bf16[32,3456]{1,0:T(8,128)(2,1)S(1)}, u32[]{:S(2)}, u32[]{:S(2)}) %collective-permute-start.3) | collective-permute-done | bytes 221216 | tf_op jit(solution)/shard_map/ppermute | solution.py:281
  93.3 0.8 merge.1
  94.1 0.0 all-to-all-done.1.mine_ref
  94.1 1.9 %collective-permute-start.4 = (bf16[4,128,896]{2,1,0:T(8,128)(2,1)S(1)}, bf16[4,128,896]{2,1,0:T(8,128)(2,1)S(1)}, u32[]{:S(2)}, u32[]{:S(2)}) collective-permute-start(bf16[4,128,896]{2,1,0:T(8,128)(2,1)S(1)} %all-to-all-done.1.mine_ref), channel_id=1, source_target_pairs={{0,64},{64,0},{1,65},{65,1},{2,66},{66,2},{3,67},{67,3},{4,68},{68... | collective-permute-start | bytes 2752520 | tf_op jit(solution)/shard_map/ppermute | solution.py:277
  96.0 3.6 %all-to-all-start.2 = ((bf16[16,2,3456]{2,1,0:T(2,128)(2,1)}), bf16[16,2,3456]{2,1,0:T(2,128)(2,1)S(1)}, u32[]{:S(2)}, u32[]{:S(2)}) async-start(bf16[16,2,3456]{2,1,0:T(2,128)(2,1)} %merge.1), calls=%async_computation.2 | async-start | bytes 442368 | tf_op jit(solution)/shard_map/all_to_all | solution.py:273
  99.6 0.0 collective-permute-done.4.theirs_ref
  99.6 5.1 %backward.1 = bf16[64,2,4224]{2,1,0:T(2,128)(2,1)} custom-call(s32[1]{0:T(128)} %bitcast.core_ref, bf16[64,2,5120]{2,1,0:T(2,128)(2,1)S(1)} %all_to_all.20.sent_ref, bf16[4,128,896]{2,1,0:T(8,128)(2,1)S(1)} %all-to-all-done.1.mine_ref, bf16[4,128,896]{2,1,0:T(8,128)(2,1)S(1)} %collective-permute-done.4.theirs_ref), custom_call_target="tpu_custom_call" | custom-call | flops 4000000000 | bytes 12000000 | tf_op jit(solution)/shard_map/backward/pallas_call | solution.py:257
  104.7 10.3 %all-to-all-done.2.terms_ref = bf16[16,2,3456]{2,1,0:T(2,128)(2,1)S(1)} async-done(((bf16[16,2,3456]{2,1,0:T(2,128)(2,1)}), bf16[16,2,3456]{2,1,0:T(2,128)(2,1)S(1)}, u32[]{:S(2)}, u32[]{:S(2)}) %all-to-all-start.2) | async-done | bytes 221216 | tf_op jit(solution)/shard_map/all_to_all | solution.py:273
  115.0 6.9 %all-to-all-start.3 = ((bf16[64,2,4224]{2,1,0:T(2,128)(2,1)}), bf16[64,2,4224]{2,1,0:T(2,128)(2,1)S(1)}, u32[]{:S(2)}, u32[]{:S(2)}) async-start(bf16[64,2,4224]{2,1,0:T(2,128)(2,1)} %backward.1), calls=%async_computation.3 | async-start | bytes 2162688 | tf_op jit(solution)/shard_map/all_to_all | solution.py:273
  121.9 0.2 owned.1.refs_0_
  122.1 1.9 %collective-permute-start.7 = (f32[2,3456]{1,0:T(2,128)S(1)}, f32[2,3456]{1,0:T(2,128)S(1)}, u32[]{:S(2)}, u32[]{:S(2)}) collective-permute-start(f32[2,3456]{1,0:T(2,128)S(1)} %owned.1.refs_0_), channel_id=1, source_target_pairs={{0,384},{128,0},{256,128},{384,256},{1,385},{129,1},{257,129},{385... | collective-permute-start | bytes 82952 | tf_op jit(solution)/shard_map/ppermute | solution.py:281
  124.0 3.3 %collective-permute-start.6 = (f32[2,3456]{1,0:T(2,128)S(1)}, f32[2,3456]{1,0:T(2,128)S(1)}, u32[]{:S(2)}, u32[]{:S(2)}) collective-permute-start(f32[2,3456]{1,0:T(2,128)S(1)} %owned.1.refs_0_), channel_id=1, source_target_pairs={{0,256},{128,384},{256,0},{384,128},{1,257},{129,385},{257,1},{385... | collective-permute-start | bytes 82952 | tf_op jit(solution)/shard_map/ppermute | solution.py:281
  127.3 3.4 %collective-permute-start.5 = (f32[2,3456]{1,0:T(2,128)S(1)}, f32[2,3456]{1,0:T(2,128)S(1)}, u32[]{:S(2)}, u32[]{:S(2)}) collective-permute-start(f32[2,3456]{1,0:T(2,128)S(1)} %owned.1.refs_0_), channel_id=1, source_target_pairs={{0,128},{128,256},{256,384},{384,0},{1,129},{129,257},{257,385},{3... | collective-permute-start | bytes 82952 | tf_op jit(solution)/shard_map/ppermute | solution.py:281
  130.7 15.3 %collective-permute-done.7.refs_3_ = f32[2,3456]{1,0:T(2,128)S(1)} collective-permute-done((f32[2,3456]{1,0:T(2,128)S(1)}, f32[2,3456]{1,0:T(2,128)S(1)}, u32[]{:S(2)}, u32[]{:S(2)}) %collective-permute-start.7) | collective-permute-done | bytes 27680 | tf_op jit(solution)/shard_map/ppermute | solution.py:281
  145.9 0.0 collective-permute-done.6.refs_2_
  146.0 0.0 collective-permute-done.5.refs_1_
  146.0 1.9 %collective-permute-start.8 = (f32[2,3456]{1,0:T(2,128)S(1)}, f32[2,3456]{1,0:T(2,128)S(1)}, u32[]{:S(2)}, u32[]{:S(2)}) collective-permute-start(f32[2,3456]{1,0:T(2,128)S(1)} %group.1.mine_ref), channel_id=1, source_target_pairs={{0,64},{64,0},{1,65},{65,1},{2,66},{66,2},{3,67},{67,3},{4,68},{68... | collective-permute-start | bytes 82952 | tf_op jit(solution)/shard_map/ppermute | solution.py:277
  147.9 1.2 collective-permute-done.8.theirs_ref
  149.1 0.7 total.1
  149.7 7.5 %all-to-all-done.3 = bf16[64,2,4224]{2,1,0:T(2,128)(2,1)S(1)} async-done(((bf16[64,2,4224]{2,1,0:T(2,128)(2,1)}), bf16[64,2,4224]{2,1,0:T(2,128)(2,1)S(1)}, u32[]{:S(2)}, u32[]{:S(2)}) %all-to-all-start.3) | async-done | bytes 1081376 | tf_op jit(solution)/shard_map/all_to_all | solution.py:273
  157.3 0.4 reshape.33
  157.7 0.7 slice_bitcast_fusion.3
  158.4 0.1 slice_bitcast_fusion.2
  158.5 1.0 maximum_bitcast_fusion
  (1 shorter events, 0.0 us)
Async XLA Ops:
  63.8 7.7 %collective-permute-start = (bf16[128,1536]{1,0:T(8,128)(2,1)S(1)}, bf16[128,1536]{1,0:T(8,128)(2,1)S(1)}, u32[]{:S(2)}, u32[]{:S(2)}) collective-permute-start(bf16[128,1536]{1,0:T(8,128)(2,1)S(1)} %get-tuple-element.14.share_ref), channel_id=1, source_target_pairs={{0,64},{64,0},{1,65},{65,1},{2,66},{66,2},{3,67},{67,3},{4,68},{68... | collective-permute-start | bytes 1179656 | tf_op jit(solution)/shard_map/ppermute | solution.py:277
  67.0 27.1 %all-to-all-start.1 = ((bf16[4,128,896]{2,1,0:T(8,128)(2,1)}), bf16[4,128,896]{2,1,0:T(8,128)(2,1)S(1)}, u32[]{:S(2)}, u32[]{:S(2)}) async-start(bf16[4,128,896]{2,1,0:T(8,128)(2,1)} %broadcast_in_dim.8), calls=%async_computation.1 | async-start | bytes 1835008 | tf_op jit(solution)/shard_map/all_to_all | solution.py:273
  72.0 16.7 %collective-permute-start.1 = (bf16[32,3456]{1,0:T(8,128)(2,1)S(1)}, bf16[32,3456]{1,0:T(8,128)(2,1)S(1)}, u32[]{:S(2)}, u32[]{:S(2)}) collective-permute-start(bf16[32,3456]{1,0:T(8,128)(2,1)S(1)} %get-tuple-element.18), channel_id=1, source_target_pairs={{0,8},{8,16},{16,24},{24,0},{1,9},{9,17},{17,25},{25,1},{2,10},{10... | collective-permute-start | bytes 663560 | tf_op jit(solution)/shard_map/ppermute | solution.py:281
  73.9 15.3 %collective-permute-start.2 = (bf16[32,3456]{1,0:T(8,128)(2,1)S(1)}, bf16[32,3456]{1,0:T(8,128)(2,1)S(1)}, u32[]{:S(2)}, u32[]{:S(2)}) collective-permute-start(bf16[32,3456]{1,0:T(8,128)(2,1)S(1)} %get-tuple-element.19), channel_id=1, source_target_pairs={{0,16},{8,24},{16,0},{24,8},{1,17},{9,25},{17,1},{25,9},{2,18},{10... | collective-permute-start | bytes 663560 | tf_op jit(solution)/shard_map/ppermute | solution.py:281
  78.8 14.5 %collective-permute-start.3 = (bf16[32,3456]{1,0:T(8,128)(2,1)S(1)}, bf16[32,3456]{1,0:T(8,128)(2,1)S(1)}, u32[]{:S(2)}, u32[]{:S(2)}) collective-permute-start(bf16[32,3456]{1,0:T(8,128)(2,1)S(1)} %get-tuple-element.20), channel_id=1, source_target_pairs={{0,24},{8,0},{16,8},{24,16},{1,25},{9,1},{17,9},{25,17},{2,26},{10... | collective-permute-start | bytes 663560 | tf_op jit(solution)/shard_map/ppermute | solution.py:281
  94.1 5.5 %collective-permute-start.4 = (bf16[4,128,896]{2,1,0:T(8,128)(2,1)S(1)}, bf16[4,128,896]{2,1,0:T(8,128)(2,1)S(1)}, u32[]{:S(2)}, u32[]{:S(2)}) collective-permute-start(bf16[4,128,896]{2,1,0:T(8,128)(2,1)S(1)} %all-to-all-done.1.mine_ref), channel_id=1, source_target_pairs={{0,64},{64,0},{1,65},{65,1},{2,66},{66,2},{3,67},{67,3},{4,68},{68... | collective-permute-start | bytes 2752520 | tf_op jit(solution)/shard_map/ppermute | solution.py:277
  96.0 19.0 %all-to-all-start.2 = ((bf16[16,2,3456]{2,1,0:T(2,128)(2,1)}), bf16[16,2,3456]{2,1,0:T(2,128)(2,1)S(1)}, u32[]{:S(2)}, u32[]{:S(2)}) async-start(bf16[16,2,3456]{2,1,0:T(2,128)(2,1)} %merge.1), calls=%async_computation.2 | async-start | bytes 442368 | tf_op jit(solution)/shard_map/all_to_all | solution.py:273
  115.0 42.2 %all-to-all-start.3 = ((bf16[64,2,4224]{2,1,0:T(2,128)(2,1)}), bf16[64,2,4224]{2,1,0:T(2,128)(2,1)S(1)}, u32[]{:S(2)}, u32[]{:S(2)}) async-start(bf16[64,2,4224]{2,1,0:T(2,128)(2,1)} %backward.1), calls=%async_computation.3 | async-start | bytes 2162688 | tf_op jit(solution)/shard_map/all_to_all | solution.py:273
  122.1 23.9 %collective-permute-start.7 = (f32[2,3456]{1,0:T(2,128)S(1)}, f32[2,3456]{1,0:T(2,128)S(1)}, u32[]{:S(2)}, u32[]{:S(2)}) collective-permute-start(f32[2,3456]{1,0:T(2,128)S(1)} %owned.1.refs_0_), channel_id=1, source_target_pairs={{0,384},{128,0},{256,128},{384,256},{1,385},{129,1},{257,129},{385... | collective-permute-start | bytes 82952 | tf_op jit(solution)/shard_map/ppermute | solution.py:281
  124.0 22.0 %collective-permute-start.6 = (f32[2,3456]{1,0:T(2,128)S(1)}, f32[2,3456]{1,0:T(2,128)S(1)}, u32[]{:S(2)}, u32[]{:S(2)}) collective-permute-start(f32[2,3456]{1,0:T(2,128)S(1)} %owned.1.refs_0_), channel_id=1, source_target_pairs={{0,256},{128,384},{256,0},{384,128},{1,257},{129,385},{257,1},{385... | collective-permute-start | bytes 82952 | tf_op jit(solution)/shard_map/ppermute | solution.py:281
  127.3 18.7 %collective-permute-start.5 = (f32[2,3456]{1,0:T(2,128)S(1)}, f32[2,3456]{1,0:T(2,128)S(1)}, u32[]{:S(2)}, u32[]{:S(2)}) collective-permute-start(f32[2,3456]{1,0:T(2,128)S(1)} %owned.1.refs_0_), channel_id=1, source_target_pairs={{0,128},{128,256},{256,384},{384,0},{1,129},{129,257},{257,385},{3... | collective-permute-start | bytes 82952 | tf_op jit(solution)/shard_map/ppermute | solution.py:281
  146.0 3.1 %collective-permute-start.8 = (f32[2,3456]{1,0:T(2,128)S(1)}, f32[2,3456]{1,0:T(2,128)S(1)}, u32[]{:S(2)}, u32[]{:S(2)}) collective-permute-start(f32[2,3456]{1,0:T(2,128)S(1)} %group.1.mine_ref), channel_id=1, source_target_pairs={{0,64},{64,0},{1,65},{65,1},{2,66},{66,2},{3,67},{67,3},{4,68},{68... | collective-permute-start | bytes 82952 | tf_op jit(solution)/shard_map/ppermute | solution.py:277

commit v6 on v5

--- a/solution.py
+++ b/solution.py
@@ -155,23 +155,20 @@
     share_ref[:, WIDTH:] = channels_ref[:, pl.ds(other, HALF)]
 
 
-def weight_grad_kernel(x_ref, share_ref, received_ref, columns_ref, *refs):
-    *out_refs, partial_ref = refs
+def weight_grad_kernel(share_ref, received_ref, columns_ref, out_ref):
     columns = jnp.concatenate([columns_ref[...], received_ref[:, WIDTH:]], axis=0)
     features = jnp.concatenate([share_ref[:, :WIDTH], received_ref[:, :WIDTH]], axis=0)
-    partial_ref[...] = dot(columns, features, 0, 0).astype(BF16)
-    for step, out_ref in enumerate(out_refs):
-        target = ((x_ref[0] + step) & 3) * 16
-        for high in range(2):
-            for pair in range(3):
-                start = pl.multiple_of(pair * ROWS + high * 64 + target, 16)
-                out_ref[high * 16 : high * 16 + 16, pair * WIDTH : (pair + 1) * WIDTH] = (
-                    partial_ref[pl.ds(start, 16), :]
-                )
+    partial = dot(columns, features, 0, 0).astype(BF16)
+    for high in range(2):
+        for pair in range(3):
+            start, column = pair * ROWS + high * 64, high * HALF_WIDTH + pair * WIDTH
+            out_ref[:, :, column : column + WIDTH] = partial[start : start + 64].reshape(
+                32, 2, WIDTH
+            )
 
 
 def backward_kernel(
-    core_ref, sent_ref, mine_ref, theirs_ref,
+    core_ref, x_ref, sent_ref, mine_ref, theirs_ref,
     out_ref, rows_ref, weights_ref, channels_ref, attended_ref, matrix_ref, upstream_ref,
     grad_scores_ref,
 ):
@@ -184,11 +181,20 @@
     attend(rows_ref, weights_ref, put_attended)
     own = pl.multiple_of(core_ref[0] * HALF, HALF)
     other = pl.multiple_of((1 - core_ref[0]) * HALF, HALF)
-    for piece, place, pair, tile in half_tiles():
-        for start, half_ref in ((own, mine_ref), (other, theirs_ref)):
-            matrix_ref[pl.ds(start + pair * ROWS, ROWS), lanes(tile)] = half_ref[
-                piece, :, lanes(place)
-            ]
+    for step in range(4):
+        first = ((x_ref[0] - step) & 3) * PIECE_TILES
+        for place in range(PIECE_TILES):
+            tile = first + place
+            row = pl.multiple_of(lax.div(tile, TILES) * ROWS, ROWS)
+            column = pl.multiple_of(lax.rem(tile, TILES) * LANES, LANES)
+
+            @pl.when(tile < 3 * TILES)
+            def _():
+                for start, half_ref in ((own, mine_ref), (other, theirs_ref)):
+                    matrix_ref[pl.ds(start + row, ROWS), pl.ds(column, LANES)] = half_ref[
+                        step, :, lanes(place)
+                    ]
+
     upstream_ref[...] = dot(channels_ref[...], matrix_ref[...], 1, 0).astype(BF16)
     products = [
         head_products(upstream_ref, 0, rows_ref, 2 * WIDTH, index) for index in range(HEADS)
@@ -216,20 +222,16 @@
         )
 
 
-def merge_kernel(*refs):
-    *terms, out_ref = refs
-    total = terms[0][...].astype(F32)
-    for term in terms[1:]:
-        total += term[...].astype(F32)
-    out_ref[...] = total.astype(BF16).reshape(16, 2, HALF_WIDTH)
-
-
-def owned_kernel(terms_ref, out_ref):
-    rows = terms_ref[...].reshape(32, HALF_WIDTH)
-    target = lax.broadcasted_iota(jnp.int32, (8, 32), 0)
-    source = lax.broadcasted_iota(jnp.int32, (8, 32), 1)
+def owned_kernel(high_ref, terms_ref, keep_ref, send_ref, total_ref):
+    rows = terms_ref[...].reshape(64, 2 * HALF_WIDTH)
+    target = lax.broadcasted_iota(jnp.int32, (8, 64), 0)
+    source = lax.broadcasted_iota(jnp.int32, (8, 64), 1)
     chosen = jnp.where(target == (source & 1), 1.0, 0.0).astype(BF16)
-    out_ref[...] = dot(chosen, rows, 1, 0)[:2]
+    total_ref[...] = dot(chosen, rows, 1, 0)
+    own = pl.multiple_of(high_ref[0] * HALF_WIDTH, LANES)
+    other = pl.multiple_of((1 - high_ref[0]) * HALF_WIDTH, LANES)
+    keep_ref[...] = total_ref[0:2, pl.ds(own, HALF_WIDTH)]
+    send_ref[...] = total_ref[0:2, pl.ds(other, HALF_WIDTH)]
 
 
 def group_kernel(*refs):
@@ -281,9 +283,17 @@
     return lax.ppermute(value, axis, [(place, (place + step) % 4) for place in range(4)])
 
 
+def cross(value, step):
+    pairs = [
+        (2 * low + high, 2 * ((low + step) % 4) + 1 - high) for low in range(4) for high in range(2)
+    ]
+    return lax.ppermute(value, ("yl", "yh"), pairs)
+
+
 def on_device(query_key_value, out_weight, cotangent):
     core = lax.axis_index("c").astype(jnp.int32).reshape(1)
     x_place = lax.axis_index("x").astype(jnp.int32).reshape(1)
+    y_high = lax.axis_index("yh").astype(jnp.int32).reshape(1)
     (packed,) = call(
         pack_kernel,
         "pack",
@@ -312,26 +322,21 @@
         ],
         micros=3,
     )
-    piece, _ = lax.optimization_barrier((sent[:, :, BASE:], share))
-    mine = exchange(jnp.broadcast_to(piece.reshape(1, ROWS, PIECE), (4, ROWS, PIECE)), "x")
-    partial = call(
+    (partial,) = call(
         weight_grad_kernel,
         "weight_grad",
-        (x_place, share, swap(share), columns),
-        [IN_SMEM] + [IN_VMEM] * 3,
-        [((32, HALF_WIDTH), BF16)] * 4,
-        [pltpu.VMEM((HALF, WIDTH), BF16)],
-    )
-    terms = [partial[0]] + [turn(partial[step], "x", step) for step in range(1, 4)]
-    (summed,) = call(
-        merge_kernel, "merge", terms, [IN_VMEM] * 4, [((16, 2, HALF_WIDTH), BF16)]
-    )
-    mine, summed = lax.optimization_barrier((mine, summed))
+        (share, swap(share), columns),
+        [IN_VMEM] * 3,
+        [((32, 2, 2 * HALF_WIDTH), BF16)],
+    )
+    piece, partial = lax.optimization_barrier((sent[:, :, BASE:].reshape(ROWS, PIECE), partial))
+    collected = exchange(partial, ("x", "z"))
+    mine = jnp.stack([piece] + [turn(piece, "x", step) for step in range(1, 4)])
     (results,) = call(
         backward_kernel,
         "backward",
-        (core, sent, mine, swap(mine)),
-        [IN_SMEM] + [IN_VMEM] * 3,
+        (core, x_place, sent, mine, swap(mine)),
+        [IN_SMEM] * 2 + [IN_VMEM] * 3,
         [((64, 2, BASE), BF16)],
         [
             pltpu.VMEM((ROWS, COLS), BF16),
@@ -344,13 +349,20 @@
         ],
         micros=4,
     )
-    collected = exchange(summed, ("yh", "z"))
     results, collected = lax.optimization_barrier((results, collected))
-    (owned,) = call(owned_kernel, "owned", (collected,), [IN_VMEM], [((2, HALF_WIDTH), F32)])
-    turned = [turn(owned, "yl", step) for step in range(1, 4)]
     back = exchange(results, SEQ)
+    keep, send = call(
+        owned_kernel,
+        "owned",
+        (y_high, collected),
+        [IN_SMEM, IN_VMEM],
+        [((2, HALF_WIDTH), F32)] * 2,
+        [pltpu.VMEM((8, 2 * HALF_WIDTH), F32)],
+    )
+    turned = [turn(keep, "yl", step) for step in range(1, 4)]
+    turned += [cross(send, step) for step in range(4)]
     (group,) = call(
-        group_kernel, "group", (owned, *turned), [IN_VMEM] * 4, [((2, HALF_WIDTH), F32)]
+        group_kernel, "group", (keep, *turned), [IN_VMEM] * 8, [((2, HALF_WIDTH), F32)]
     )
     (total,) = call(
         total_kernel,

time: 160 us -> 168 us (1.050)
  the two profiles are of different devices: /device:TPU:14 before, /device:TPU:1 now
where the time goes in v6:
time: 168 us; the launch traced here: 167 us
  starting transfers between devices  65.3 us (39%)
  blocking collectives  49.5 us (29%)
  waiting for transfers between devices  35.9 us (21%)
  Pallas kernels  13 us (8%)
    all_to_all x1, blocking collectives, exchange(): return lax.all_to_all(value, axes, 0, 0, tiled=True)  49.5 us
    ppermute x6, waiting for transfers between devices, turn(): lax.ppermute(value, axis, [(place, (place + step) % 4) for place in range...  27.1 us
    ppermute x6, starting transfers between devices, turn(): lax.ppermute(value, axis, [(place, (place + step) % 4) for place in range...  17.8 us
    ppermute x4, starting transfers between devices, cross(): return lax.ppermute(value, ('yl', 'yh'), pairs)  17.7 us
    all_to_all x2, starting transfers between devices, exchange(): return lax.all_to_all(value, axes, 0, 0, tiled=True)  15.1 us
    ppermute x3, starting transfers between devices, swap(): return lax.ppermute(value, 'c', [(0, 1), (1, 0)])  14.6 us
    pallas_call x7, Pallas kernels, call(): pl.pallas_call(kernel, out_shape=[jax.ShapeDtypeStruct(shape, dtype) for...  13 us
    ppermute x4, waiting for transfers between devices, cross(): return lax.ppermute(value, ('yl', 'yh'), pairs)  4.63 us
  transfers between devices with their start and end apart: 15, of which 8 were waited for; matrix products, arithmetic and copies ran while one was open for 0% of the time, Pallas kernels for 4%

profile of v6, /device:TPU:1, one launch (start us, length us, event | category | flops | bytes accessed | tf_op | source)
XLA Modules:
  0.0 167.1 jit_solution(16693934972817555367)
XLA Ops:
  0.6 2.9 %pack.1 = bf16[64,2,5120]{2,1,0:T(2,128)(2,1)} custom-call(s32[1]{0:T(128)} %bitcast.core_ref, bf16[3,128,1152]{2,1,0:T(8,128)(2,1)} %bitcast.23, bf16[128,768]{1,0:T(8,128)(2,1)} %bitcast.24, bf16[12,1152]{1,0:T(8,128)(2,1)} %weight_hbm.1), custom_call_target="tpu_custom_call" | custom-call | flops 1000000000 | bytes 3000000 | tf_op jit(solution)/shard_map/pack/pallas_call | solution.py:259
  3.5 49.5 %all_to_all.15.sent_ref = bf16[64,2,5120]{2,1,0:T(2,128)(2,1)S(1)} all-to-all(bf16[64,2,5120]{2,1,0:T(2,128)(2,1)} %pack.1), channel_id=1, replica_groups=mesh['yl'=4,'c'=2,'yh'=2,'x'=4,'z'=8] {'yh','x','z'}, dimensions={0} | all-to-all | bytes 2621440 | tf_op jit(solution)/shard_map/all_to_all | solution.py:275
  53.0 1.3 forward.1
  54.3 8.0 %collective-permute-start = (bf16[128,1536]{1,0:T(8,128)(2,1)S(1)}, bf16[128,1536]{1,0:T(8,128)(2,1)S(1)}, u32[]{:S(2)}, u32[]{:S(2)}) collective-permute-start(bf16[128,1536]{1,0:T(8,128)(2,1)S(1)} %get-tuple-element.11.share_ref), channel_id=1, source_target_pairs={{0,64},{64,0},{1,65},{65,1},{2,66},{66,2},{3,67},{67,3},{4,68},{68... | collective-permute-start | bytes 1179656 | tf_op jit(solution)/shard_map/ppermute | solution.py:279
  62.3 0.2 slice.20
  62.5 0.1 reshape.37
  62.6 1.1 collective-permute-done.received_ref
  63.7 1.5 weight_grad.1
  65.1 6.3 %all-to-all-start.1 = ((bf16[32,2,6912]{2,1,0:T(2,128)(2,1)}), bf16[32,2,6912]{2,1,0:T(2,128)(2,1)S(1)}, u32[]{:S(2)}, u32[]{:S(2)}) async-start(bf16[32,2,6912]{2,1,0:T(2,128)(2,1)} %weight_grad.1), calls=%async_computation.1 | async-start | bytes 1769472 | tf_op jit(solution)/shard_map/all_to_all | solution.py:275
  71.5 4.4 %collective-permute-start.3 = (bf16[128,896]{1,0:T(8,128)(2,1)S(1)}, bf16[128,896]{1,0:T(8,128)(2,1)S(1)}, u32[]{:S(2)}, u32[]{:S(2)}) collective-permute-start(bf16[128,896]{1,0:T(8,128)(2,1)S(1)} %reshape.37), channel_id=1, source_target_pairs={{0,24},{8,0},{16,8},{24,16},{1,25},{9,1},{17,9},{25,17},{2,26},{10... | collective-permute-start | bytes 688136 | tf_op jit(solution)/shard_map/ppermute | solution.py:283
  75.9 2.4 %collective-permute-start.2 = (bf16[128,896]{1,0:T(8,128)(2,1)S(1)}, bf16[128,896]{1,0:T(8,128)(2,1)S(1)}, u32[]{:S(2)}, u32[]{:S(2)}) collective-permute-start(bf16[128,896]{1,0:T(8,128)(2,1)S(1)} %reshape.37), channel_id=1, source_target_pairs={{0,16},{8,24},{16,0},{24,8},{1,17},{9,25},{17,1},{25,9},{2,18},{10... | collective-permute-start | bytes 688136 | tf_op jit(solution)/shard_map/ppermute | solution.py:283
  78.3 2.5 %collective-permute-start.1 = (bf16[128,896]{1,0:T(8,128)(2,1)S(1)}, bf16[128,896]{1,0:T(8,128)(2,1)S(1)}, u32[]{:S(2)}, u32[]{:S(2)}) collective-permute-start(bf16[128,896]{1,0:T(8,128)(2,1)S(1)} %reshape.37), channel_id=1, source_target_pairs={{0,8},{8,16},{16,24},{24,0},{1,9},{9,17},{17,25},{25,1},{2,10},{10... | collective-permute-start | bytes 688136 | tf_op jit(solution)/shard_map/ppermute | solution.py:283
  80.8 3.6 %collective-permute-done.3 = bf16[128,896]{1,0:T(8,128)(2,1)S(1)} collective-permute-done((bf16[128,896]{1,0:T(8,128)(2,1)S(1)}, bf16[128,896]{1,0:T(8,128)(2,1)S(1)}, u32[]{:S(2)}, u32[]{:S(2)}) %collective-permute-start.3) | collective-permute-done | bytes 229408 | tf_op jit(solution)/shard_map/ppermute | solution.py:283
  84.4 6.7 %collective-permute-done.2 = bf16[128,896]{1,0:T(8,128)(2,1)S(1)} collective-permute-done((bf16[128,896]{1,0:T(8,128)(2,1)S(1)}, bf16[128,896]{1,0:T(8,128)(2,1)S(1)}, u32[]{:S(2)}, u32[]{:S(2)}) %collective-permute-start.2) | collective-permute-done | bytes 229408 | tf_op jit(solution)/shard_map/ppermute | solution.py:283
  91.2 7.3 %collective-permute-done.1 = bf16[128,896]{1,0:T(8,128)(2,1)S(1)} collective-permute-done((bf16[128,896]{1,0:T(8,128)(2,1)S(1)}, bf16[128,896]{1,0:T(8,128)(2,1)S(1)}, u32[]{:S(2)}, u32[]{:S(2)}) %collective-permute-start.1) | collective-permute-done | bytes 229408 | tf_op jit(solution)/shard_map/ppermute | solution.py:283
  98.5 0.1 pad_maximum_fusion.mine_ref
  98.6 2.4 %collective-permute-start.4 = (bf16[4,128,896]{2,1,0:T(8,128)(2,1)S(1)}, bf16[4,128,896]{2,1,0:T(8,128)(2,1)}, u32[]{:S(2)}, u32[]{:S(2)}) collective-permute-start(bf16[4,128,896]{2,1,0:T(8,128)(2,1)S(1)} %pad_maximum_fusion.mine_ref), channel_id=1, source_target_pairs={{0,64},{64,0},{1,65},{65,1},{2,66},{66,2},{3,67},{67,3},{4,68},{68... | collective-permute-start | bytes 2752520 | tf_op jit(solution)/shard_map/ppermute | solution.py:279
  101.1 2.2 %collective-permute-done.4.theirs_ref = bf16[4,128,896]{2,1,0:T(8,128)(2,1)} collective-permute-done((bf16[4,128,896]{2,1,0:T(8,128)(2,1)S(1)}, bf16[4,128,896]{2,1,0:T(8,128)(2,1)}, u32[]{:S(2)}, u32[]{:S(2)}) %collective-permute-start.4) | collective-permute-done | bytes 917536 | tf_op jit(solution)/shard_map/ppermute | solution.py:279
  103.3 6.4 %backward.1 = bf16[64,2,4224]{2,1,0:T(2,128)(2,1)} custom-call(s32[1]{0:T(128)} %bitcast.core_ref, s32[1]{0:T(128)} %bitcast.1.x_ref, bf16[64,2,5120]{2,1,0:T(2,128)(2,1)S(1)} %all_to_all.15.sent_ref, bf16[4,128,896]{2,1,0:T(8,128)(2,1)S(1)} %pad_maximum_fusion.mine_ref, bf16[4,128,896]{2,1,0:T(8,128)(2,1)} %collective-permute-done.4.theirs_ref), custom_call_target="tpu_custom_call" | custom-call | flops 4000000000 | bytes 12000000 | tf_op jit(solution)/shard_map/backward/pallas_call | solution.py:259
  109.7 0.0 all-to-all-done.1.terms_ref
  109.7 8.8 %all-to-all-start.2 = ((bf16[64,2,4224]{2,1,0:T(2,128)(2,1)}), bf16[64,2,4224]{2,1,0:T(2,128)(2,1)S(1)}, u32[]{:S(2)}, u32[]{:S(2)}) async-start(bf16[64,2,4224]{2,1,0:T(2,128)(2,1)} %backward.1), calls=%async_computation.2 | async-start | bytes 2162688 | tf_op jit(solution)/shard_map/all_to_all | solution.py:275
  118.5 0.3 owned.1
  118.8 3.1 %collective-permute-start.7 = (f32[2,3456]{1,0:T(2,128)S(1)}, f32[2,3456]{1,0:T(2,128)S(1)}, u32[]{:S(2)}, u32[]{:S(2)}) collective-permute-start(f32[2,3456]{1,0:T(2,128)S(1)} %get-tuple-element.17.refs_0_), channel_id=1, source_target_pairs={{0,384},{128,0},{256,128},{384,256},{1,385},{129,1},{257,129},{385... | collective-permute-start | bytes 82952 | tf_op jit(solution)/shard_map/ppermute | solution.py:283
  121.9 3.5 %collective-permute-start.6 = (f32[2,3456]{1,0:T(2,128)S(1)}, f32[2,3456]{1,0:T(2,128)S(1)}, u32[]{:S(2)}, u32[]{:S(2)}) collective-permute-start(f32[2,3456]{1,0:T(2,128)S(1)} %get-tuple-element.17.refs_0_), channel_id=1, source_target_pairs={{0,256},{128,384},{256,0},{384,128},{1,257},{129,385},{257,1},{385... | collective-permute-start | bytes 82952 | tf_op jit(solution)/shard_map/ppermute | solution.py:283
  125.4 1.9 %collective-permute-start.5 = (f32[2,3456]{1,0:T(2,128)S(1)}, f32[2,3456]{1,0:T(2,128)S(1)}, u32[]{:S(2)}, u32[]{:S(2)}) collective-permute-start(f32[2,3456]{1,0:T(2,128)S(1)} %get-tuple-element.17.refs_0_), channel_id=1, source_target_pairs={{0,128},{128,256},{256,384},{384,0},{1,129},{129,257},{257,385},{3... | collective-permute-start | bytes 82952 | tf_op jit(solution)/shard_map/ppermute | solution.py:283
  127.3 7.2 %collective-permute-start.11 = (f32[2,3456]{1,0:T(2,128)S(1)}, f32[2,3456]{1,0:T(2,128)S(1)}, u32[]{:S(2)}, u32[]{:S(2)}) collective-permute-start(f32[2,3456]{1,0:T(2,128)S(1)} %get-tuple-element.18), channel_id=1, source_target_pairs={{0,416},{32,384},{128,32},{160,0},{256,160},{288,128},{384,288},{4... | collective-permute-start | bytes 82952 | tf_op jit(solution)/shard_map/ppermute | solution.py:290
  134.5 1.9 %collective-permute-start.10 = (f32[2,3456]{1,0:T(2,128)S(1)}, f32[2,3456]{1,0:T(2,128)S(1)}, u32[]{:S(2)}, u32[]{:S(2)}) collective-permute-start(f32[2,3456]{1,0:T(2,128)S(1)} %get-tuple-element.18), channel_id=1, source_target_pairs={{0,288},{32,256},{128,416},{160,384},{256,32},{288,0},{384,160},{4... | collective-permute-start | bytes 82952 | tf_op jit(solution)/shard_map/ppermute | solution.py:290
  136.4 9.4 %collective-permute-done.7.refs_3_ = f32[2,3456]{1,0:T(2,128)S(1)} collective-permute-done((f32[2,3456]{1,0:T(2,128)S(1)}, f32[2,3456]{1,0:T(2,128)S(1)}, u32[]{:S(2)}, u32[]{:S(2)}) %collective-permute-start.7) | collective-permute-done | bytes 27680 | tf_op jit(solution)/shard_map/ppermute | solution.py:283
  145.9 4.8 %collective-permute-start.9 = (f32[2,3456]{1,0:T(2,128)S(1)}, f32[2,3456]{1,0:T(2,128)S(1)}, u32[]{:S(2)}, u32[]{:S(2)}) collective-permute-start(f32[2,3456]{1,0:T(2,128)S(1)} %get-tuple-element.18), channel_id=1, source_target_pairs={{0,160},{32,128},{128,288},{160,256},{256,416},{288,384},{384,32},... | collective-permute-start | bytes 82952 | tf_op jit(solution)/shard_map/ppermute | solution.py:290
  150.6 0.0 collective-permute-done.6.refs_2_
  150.6 3.8 %collective-permute-start.8 = (f32[2,3456]{1,0:T(2,128)S(1)}, f32[2,3456]{1,0:T(2,128)S(1)}, u32[]{:S(2)}, u32[]{:S(2)}) collective-permute-start(f32[2,3456]{1,0:T(2,128)S(1)} %get-tuple-element.18), channel_id=1, source_target_pairs={{0,32},{32,0},{128,160},{160,128},{256,288},{288,256},{384,416},{4... | collective-permute-start | bytes 82952 | tf_op jit(solution)/shard_map/ppermute | solution.py:290
  154.5 0.0 collective-permute-done.5.refs_1_
  154.5 0.0 collective-permute-done.11.refs_7_
  154.5 0.0 collective-permute-done.10.refs_6_
  154.5 0.0 collective-permute-done.9.refs_5_
  154.5 4.6 %collective-permute-done.8.refs_4_ = f32[2,3456]{1,0:T(2,128)S(1)} collective-permute-done((f32[2,3456]{1,0:T(2,128)S(1)}, f32[2,3456]{1,0:T(2,128)S(1)}, u32[]{:S(2)}, u32[]{:S(2)}) %collective-permute-start.8) | collective-permute-done | bytes 27680 | tf_op jit(solution)/shard_map/ppermute | solution.py:290
  159.2 4.2 %collective-permute-start.12 = (f32[2,3456]{1,0:T(2,128)S(1)}, f32[2,3456]{1,0:T(2,128)S(1)}, u32[]{:S(2)}, u32[]{:S(2)}) collective-permute-start(f32[2,3456]{1,0:T(2,128)S(1)} %group.1.mine_ref), channel_id=1, source_target_pairs={{0,64},{64,0},{1,65},{65,1},{2,66},{66,2},{3,67},{67,3},{4,68},{68... | collective-permute-start | bytes 82952 | tf_op jit(solution)/shard_map/ppermute | solution.py:279
  163.4 0.8 collective-permute-done.12.theirs_ref
  164.2 0.7 total.1
  164.9 0.0 all-to-all-done.2
  164.9 0.4 reshape.38
  165.3 0.7 slice_bitcast_fusion.3
  166.0 0.1 slice_bitcast_fusion.2
  166.1 1.0 maximum_bitcast_fusion
  (1 shorter events, 0.0 us)
Async XLA Ops:
  54.3 9.4 %collective-permute-start = (bf16[128,1536]{1,0:T(8,128)(2,1)S(1)}, bf16[128,1536]{1,0:T(8,128)(2,1)S(1)}, u32[]{:S(2)}, u32[]{:S(2)}) collective-permute-start(bf16[128,1536]{1,0:T(8,128)(2,1)S(1)} %get-tuple-element.11.share_ref), channel_id=1, source_target_pairs={{0,64},{64,0},{1,65},{65,1},{2,66},{66,2},{3,67},{67,3},{4,68},{68... | collective-permute-start | bytes 1179656 | tf_op jit(solution)/shard_map/ppermute | solution.py:279
  65.1 44.6 %all-to-all-start.1 = ((bf16[32,2,6912]{2,1,0:T(2,128)(2,1)}), bf16[32,2,6912]{2,1,0:T(2,128)(2,1)S(1)}, u32[]{:S(2)}, u32[]{:S(2)}) async-start(bf16[32,2,6912]{2,1,0:T(2,128)(2,1)} %weight_grad.1), calls=%async_computation.1 | async-start | bytes 1769472 | tf_op jit(solution)/shard_map/all_to_all | solution.py:275
  71.5 12.9 %collective-permute-start.3 = (bf16[128,896]{1,0:T(8,128)(2,1)S(1)}, bf16[128,896]{1,0:T(8,128)(2,1)S(1)}, u32[]{:S(2)}, u32[]{:S(2)}) collective-permute-start(bf16[128,896]{1,0:T(8,128)(2,1)S(1)} %reshape.37), channel_id=1, source_target_pairs={{0,24},{8,0},{16,8},{24,16},{1,25},{9,1},{17,9},{25,17},{2,26},{10... | collective-permute-start | bytes 688136 | tf_op jit(solution)/shard_map/ppermute | solution.py:283
  75.9 15.3 %collective-permute-start.2 = (bf16[128,896]{1,0:T(8,128)(2,1)S(1)}, bf16[128,896]{1,0:T(8,128)(2,1)S(1)}, u32[]{:S(2)}, u32[]{:S(2)}) collective-permute-start(bf16[128,896]{1,0:T(8,128)(2,1)S(1)} %reshape.37), channel_id=1, source_target_pairs={{0,16},{8,24},{16,0},{24,8},{1,17},{9,25},{17,1},{25,9},{2,18},{10... | collective-permute-start | bytes 688136 | tf_op jit(solution)/shard_map/ppermute | solution.py:283
  78.3 20.2 %collective-permute-start.1 = (bf16[128,896]{1,0:T(8,128)(2,1)S(1)}, bf16[128,896]{1,0:T(8,128)(2,1)S(1)}, u32[]{:S(2)}, u32[]{:S(2)}) collective-permute-start(bf16[128,896]{1,0:T(8,128)(2,1)S(1)} %reshape.37), channel_id=1, source_target_pairs={{0,8},{8,16},{16,24},{24,0},{1,9},{9,17},{17,25},{25,1},{2,10},{10... | collective-permute-start | bytes 688136 | tf_op jit(solution)/shard_map/ppermute | solution.py:283
  98.6 4.6 %collective-permute-start.4 = (bf16[4,128,896]{2,1,0:T(8,128)(2,1)S(1)}, bf16[4,128,896]{2,1,0:T(8,128)(2,1)}, u32[]{:S(2)}, u32[]{:S(2)}) collective-permute-start(bf16[4,128,896]{2,1,0:T(8,128)(2,1)S(1)} %pad_maximum_fusion.mine_ref), channel_id=1, source_target_pairs={{0,64},{64,0},{1,65},{65,1},{2,66},{66,2},{3,67},{67,3},{4,68},{68... | collective-permute-start | bytes 2752520 | tf_op jit(solution)/shard_map/ppermute | solution.py:279
  109.7 55.1 %all-to-all-start.2 = ((bf16[64,2,4224]{2,1,0:T(2,128)(2,1)}), bf16[64,2,4224]{2,1,0:T(2,128)(2,1)S(1)}, u32[]{:S(2)}, u32[]{:S(2)}) async-start(bf16[64,2,4224]{2,1,0:T(2,128)(2,1)} %backward.1), calls=%async_computation.2 | async-start | bytes 2162688 | tf_op jit(solution)/shard_map/all_to_all | solution.py:275
  118.8 27.1 %collective-permute-start.7 = (f32[2,3456]{1,0:T(2,128)S(1)}, f32[2,3456]{1,0:T(2,128)S(1)}, u32[]{:S(2)}, u32[]{:S(2)}) collective-permute-start(f32[2,3456]{1,0:T(2,128)S(1)} %get-tuple-element.17.refs_0_), channel_id=1, source_target_pairs={{0,384},{128,0},{256,128},{384,256},{1,385},{129,1},{257,129},{385... | collective-permute-start | bytes 82952 | tf_op jit(solution)/shard_map/ppermute | solution.py:283
  121.9 28.8 %collective-permute-start.6 = (f32[2,3456]{1,0:T(2,128)S(1)}, f32[2,3456]{1,0:T(2,128)S(1)}, u32[]{:S(2)}, u32[]{:S(2)}) collective-permute-start(f32[2,3456]{1,0:T(2,128)S(1)} %get-tuple-element.17.refs_0_), channel_id=1, source_target_pairs={{0,256},{128,384},{256,0},{384,128},{1,257},{129,385},{257,1},{385... | collective-permute-start | bytes 82952 | tf_op jit(solution)/shard_map/ppermute | solution.py:283
  125.4 29.1 %collective-permute-start.5 = (f32[2,3456]{1,0:T(2,128)S(1)}, f32[2,3456]{1,0:T(2,128)S(1)}, u32[]{:S(2)}, u32[]{:S(2)}) collective-permute-start(f32[2,3456]{1,0:T(2,128)S(1)} %get-tuple-element.17.refs_0_), channel_id=1, source_target_pairs={{0,128},{128,256},{256,384},{384,0},{1,129},{129,257},{257,385},{3... | collective-permute-start | bytes 82952 | tf_op jit(solution)/shard_map/ppermute | solution.py:283
  127.3 27.2 %collective-permute-start.11 = (f32[2,3456]{1,0:T(2,128)S(1)}, f32[2,3456]{1,0:T(2,128)S(1)}, u32[]{:S(2)}, u32[]{:S(2)}) collective-permute-start(f32[2,3456]{1,0:T(2,128)S(1)} %get-tuple-element.18), channel_id=1, source_target_pairs={{0,416},{32,384},{128,32},{160,0},{256,160},{288,128},{384,288},{4... | collective-permute-start | bytes 82952 | tf_op jit(solution)/shard_map/ppermute | solution.py:290
  134.5 20.0 %collective-permute-start.10 = (f32[2,3456]{1,0:T(2,128)S(1)}, f32[2,3456]{1,0:T(2,128)S(1)}, u32[]{:S(2)}, u32[]{:S(2)}) collective-permute-start(f32[2,3456]{1,0:T(2,128)S(1)} %get-tuple-element.18), channel_id=1, source_target_pairs={{0,288},{32,256},{128,416},{160,384},{256,32},{288,0},{384,160},{4... | collective-permute-start | bytes 82952 | tf_op jit(solution)/shard_map/ppermute | solution.py:290
  145.9 8.7 %collective-permute-start.9 = (f32[2,3456]{1,0:T(2,128)S(1)}, f32[2,3456]{1,0:T(2,128)S(1)}, u32[]{:S(2)}, u32[]{:S(2)}) collective-permute-start(f32[2,3456]{1,0:T(2,128)S(1)} %get-tuple-element.18), channel_id=1, source_target_pairs={{0,160},{32,128},{128,288},{160,256},{256,416},{288,384},{384,32},... | collective-permute-start | bytes 82952 | tf_op jit(solution)/shard_map/ppermute | solution.py:290
  150.6 8.5 %collective-permute-start.8 = (f32[2,3456]{1,0:T(2,128)S(1)}, f32[2,3456]{1,0:T(2,128)S(1)}, u32[]{:S(2)}, u32[]{:S(2)}) collective-permute-start(f32[2,3456]{1,0:T(2,128)S(1)} %get-tuple-element.18), channel_id=1, source_target_pairs={{0,32},{32,0},{128,160},{160,128},{256,288},{288,256},{384,416},{4... | collective-permute-start | bytes 82952 | tf_op jit(solution)/shard_map/ppermute | solution.py:290
  159.2 5.0 %collective-permute-start.12 = (f32[2,3456]{1,0:T(2,128)S(1)}, f32[2,3456]{1,0:T(2,128)S(1)}, u32[]{:S(2)}, u32[]{:S(2)}) collective-permute-start(f32[2,3456]{1,0:T(2,128)S(1)} %group.1.mine_ref), channel_id=1, source_target_pairs={{0,64},{64,0},{1,65},{65,1},{2,66},{66,2},{3,67},{67,3},{4,68},{68... | collective-permute-start | bytes 82952 | tf_op jit(solution)/shard_map/ppermute | solution.py:279

commit v7 on v5

--- a/solution.py
+++ b/solution.py
@@ -155,23 +155,18 @@
     share_ref[:, WIDTH:] = channels_ref[:, pl.ds(other, HALF)]
 
 
-def weight_grad_kernel(x_ref, share_ref, received_ref, columns_ref, *refs):
-    *out_refs, partial_ref = refs
+def weight_grad_kernel(share_ref, received_ref, columns_ref, out_ref):
     columns = jnp.concatenate([columns_ref[...], received_ref[:, WIDTH:]], axis=0)
     features = jnp.concatenate([share_ref[:, :WIDTH], received_ref[:, :WIDTH]], axis=0)
-    partial_ref[...] = dot(columns, features, 0, 0).astype(BF16)
-    for step, out_ref in enumerate(out_refs):
-        target = ((x_ref[0] + step) & 3) * 16
-        for high in range(2):
-            for pair in range(3):
-                start = pl.multiple_of(pair * ROWS + high * 64 + target, 16)
-                out_ref[high * 16 : high * 16 + 16, pair * WIDTH : (pair + 1) * WIDTH] = (
-                    partial_ref[pl.ds(start, 16), :]
-                )
+    partial = dot(columns, features, 0, 0).astype(BF16)
+    for pair in range(3):
+        out_ref[:, :, pair * WIDTH : (pair + 1) * WIDTH] = partial[
+            pair * ROWS : (pair + 1) * ROWS
+        ].reshape(64, 2, WIDTH)
 
 
 def backward_kernel(
-    core_ref, sent_ref, mine_ref, theirs_ref,
+    sent_ref, pieces_ref,
     out_ref, rows_ref, weights_ref, channels_ref, attended_ref, matrix_ref, upstream_ref,
     grad_scores_ref,
 ):
@@ -182,12 +177,11 @@
         attended_ref[:, lanes(tile)] = value
 
     attend(rows_ref, weights_ref, put_attended)
-    own = pl.multiple_of(core_ref[0] * HALF, HALF)
-    other = pl.multiple_of((1 - core_ref[0]) * HALF, HALF)
-    for piece, place, pair, tile in half_tiles():
-        for start, half_ref in ((own, mine_ref), (other, theirs_ref)):
-            matrix_ref[pl.ds(start + pair * ROWS, ROWS), lanes(tile)] = half_ref[
-                piece, :, lanes(place)
+    for core in range(2):
+        for piece, place, pair, tile in half_tiles():
+            start = core * HALF + pair * ROWS
+            matrix_ref[start : start + ROWS, lanes(tile)] = pieces_ref[
+                4 * core + piece, :, lanes(place)
             ]
     upstream_ref[...] = dot(channels_ref[...], matrix_ref[...], 1, 0).astype(BF16)
     products = [
@@ -216,18 +210,10 @@
         )
 
 
-def merge_kernel(*refs):
-    *terms, out_ref = refs
-    total = terms[0][...].astype(F32)
-    for term in terms[1:]:
-        total += term[...].astype(F32)
-    out_ref[...] = total.astype(BF16).reshape(16, 2, HALF_WIDTH)
-
-
 def owned_kernel(terms_ref, out_ref):
-    rows = terms_ref[...].reshape(32, HALF_WIDTH)
-    target = lax.broadcasted_iota(jnp.int32, (8, 32), 0)
-    source = lax.broadcasted_iota(jnp.int32, (8, 32), 1)
+    rows = terms_ref[...].reshape(ROWS, HALF_WIDTH)
+    target = lax.broadcasted_iota(jnp.int32, (8, ROWS), 0)
+    source = lax.broadcasted_iota(jnp.int32, (8, ROWS), 1)
     chosen = jnp.where(target == (source & 1), 1.0, 0.0).astype(BF16)
     out_ref[...] = dot(chosen, rows, 1, 0)[:2]
 
@@ -283,7 +269,6 @@
 
 def on_device(query_key_value, out_weight, cotangent):
     core = lax.axis_index("c").astype(jnp.int32).reshape(1)
-    x_place = lax.axis_index("x").astype(jnp.int32).reshape(1)
     (packed,) = call(
         pack_kernel,
         "pack",
@@ -299,6 +284,7 @@
         grant=56,
     )
     sent = exchange(packed, SEQ)
+    pieces = lax.all_gather(sent[:, :, BASE:].reshape(ROWS, PIECE), ("c", "x"))
     share, columns = call(
         forward_kernel,
         "forward",
@@ -312,26 +298,19 @@
         ],
         micros=3,
     )
-    piece, _ = lax.optimization_barrier((sent[:, :, BASE:], share))
-    mine = exchange(jnp.broadcast_to(piece.reshape(1, ROWS, PIECE), (4, ROWS, PIECE)), "x")
-    partial = call(
+    (partial,) = call(
         weight_grad_kernel,
         "weight_grad",
-        (x_place, share, swap(share), columns),
-        [IN_SMEM] + [IN_VMEM] * 3,
-        [((32, HALF_WIDTH), BF16)] * 4,
-        [pltpu.VMEM((HALF, WIDTH), BF16)],
-    )
-    terms = [partial[0]] + [turn(partial[step], "x", step) for step in range(1, 4)]
-    (summed,) = call(
-        merge_kernel, "merge", terms, [IN_VMEM] * 4, [((16, 2, HALF_WIDTH), BF16)]
-    )
-    mine, summed = lax.optimization_barrier((mine, summed))
+        (share, swap(share), columns),
+        [IN_VMEM] * 3,
+        [((64, 2, HALF_WIDTH), BF16)],
+    )
+    collected = exchange(partial, SEQ)
     (results,) = call(
         backward_kernel,
         "backward",
-        (core, sent, mine, swap(mine)),
-        [IN_SMEM] + [IN_VMEM] * 3,
+        (sent, pieces),
+        [IN_VMEM] * 2,
         [((64, 2, BASE), BF16)],
         [
             pltpu.VMEM((ROWS, COLS), BF16),
@@ -344,11 +323,10 @@
         ],
         micros=4,
     )
-    collected = exchange(summed, ("yh", "z"))
     results, collected = lax.optimization_barrier((results, collected))
+    back = exchange(results, SEQ)
     (owned,) = call(owned_kernel, "owned", (collected,), [IN_VMEM], [((2, HALF_WIDTH), F32)])
     turned = [turn(owned, "yl", step) for step in range(1, 4)]
-    back = exchange(results, SEQ)
     (group,) = call(
         group_kernel, "group", (owned, *turned), [IN_VMEM] * 4, [((2, HALF_WIDTH), F32)]
     )

time: 160 us -> 163 us (1.019)
  starting transfers between devices: 38 us -> 23.7 us
  between operations: 0.8 us -> 14.1 us
  waiting for transfers between devices: 46.9 us -> 49.4 us
    ppermute x6 -> x3, waiting for transfers between devices: 27.8 us -> 16.3 us  [turn(): lax.ppermute(value, axis, [(place, (place + step) % 4) for place in range...]
    all_gather x0 -> x1, waiting for transfers between devices: none -> 11.5 us  [on_device(): pieces = lax.all_gather(sent[:, :, BASE:].reshape(ROWS, PIECE), ('c', 'x'))]
    ppermute x6 -> x3, starting transfers between devices: 17.3 us -> 9.4 us  [turn(): lax.ppermute(value, axis, [(place, (place + step) % 4) for place in range...]
    all_to_all x3 -> x2, starting transfers between devices: 15 us -> 10.5 us  [exchange(): return lax.all_to_all(value, axes, 0, 0, tiled=True)]
    ppermute x3 -> x2, starting transfers between devices: 5.76 us -> 3.84 us  [swap(): return lax.ppermute(value, 'c', [(0, 1), (1, 0)])]
    ppermute x3 -> x2, waiting for transfers between devices: 1.17 us -> 2.85 us  [swap(): return lax.ppermute(value, 'c', [(0, 1), (1, 0)])]
    all_to_all x3 -> x2, waiting for transfers between devices: 17.9 us -> 18.8 us  [exchange(): return lax.all_to_all(value, axes, 0, 0, tiled=True)]
    pallas_call x8 -> x7, Pallas kernels: 11.3 us -> 11.3 us  [call(): pl.pallas_call(kernel, out_shape=[jax.ShapeDtypeStruct(shape, dtype) for...]
  transfers between devices with their start and end apart: 12 -> 8, of which waited for: 7 -> 8; matrix products, arithmetic and copies ran while one was open for 1% -> 0% of each run, Pallas kernels for 5% -> 5%
where the time goes in v7:
time: 163 us; the launch traced here: 162 us
  blocking collectives  59 us (36%)
  waiting for transfers between devices  49.4 us (30%)
  starting transfers between devices  23.7 us (15%)
  between operations  14.1 us (9%)
  Pallas kernels  11.3 us (7%)
  local copies, waits for them, and re-layouts  3.66 us (2%)
    all_to_all x1, blocking collectives, exchange(): return lax.all_to_all(value, axes, 0, 0, tiled=True)  59 us
    all_to_all x2, waiting for transfers between devices, exchange(): return lax.all_to_all(value, axes, 0, 0, tiled=True)  18.8 us
    ppermute x3, waiting for transfers between devices, turn(): lax.ppermute(value, axis, [(place, (place + step) % 4) for place in range...  16.3 us
    all_gather x1, waiting for transfers between devices, on_device(): pieces = lax.all_gather(sent[:, :, BASE:].reshape(ROWS, PIECE), ('c', 'x'))  11.5 us
    pallas_call x7, Pallas kernels, call(): pl.pallas_call(kernel, out_shape=[jax.ShapeDtypeStruct(shape, dtype) for...  11.3 us
    all_to_all x2, starting transfers between devices, exchange(): return lax.all_to_all(value, axes, 0, 0, tiled=True)  10.5 us
    ppermute x3, starting transfers between devices, turn(): lax.ppermute(value, axis, [(place, (place + step) % 4) for place in range...  9.4 us
    ppermute x2, starting transfers between devices, swap(): return lax.ppermute(value, 'c', [(0, 1), (1, 0)])  3.84 us
  transfers between devices with their start and end apart: 8, of which 8 were waited for; matrix products, arithmetic and copies ran while one was open for 0% of the time, Pallas kernels for 5%

profile of v7, /device:TPU:14, one launch (start us, length us, event | category | flops | bytes accessed | tf_op | source)
XLA Modules:
  0.0 162.3 jit_solution(2067656129465996558)
XLA Ops:
  7.2 0.0 all-gather.2.cloned.1.call-start
  7.2 2.8 %pack.1 = bf16[64,2,5120]{2,1,0:T(2,128)(2,1)} custom-call(s32[1]{0:T(128)} %bitcast.core_ref, bf16[3,128,1152]{2,1,0:T(8,128)(2,1)} %bitcast.13, bf16[128,768]{1,0:T(8,128)(2,1)} %bitcast.14, bf16[12,1152]{1,0:T(8,128)(2,1)} %weight_hbm.1), custom_call_target="tpu_custom_call" | custom-call | flops 1000000000 | bytes 3000000 | tf_op jit(solution)/shard_map/pack/pallas_call | solution.py:243
  10.1 59.0 %all_to_all.15.sent_ref = bf16[64,2,5120]{2,1,0:T(2,128)(2,1)S(1)} all-to-all(bf16[64,2,5120]{2,1,0:T(2,128)(2,1)} %pack.1), channel_id=1, replica_groups=mesh['yl'=4,'c'=2,'yh'=2,'x'=4,'z'=8] {'yh','x','z'}, dimensions={0} | all-to-all | bytes 2621440 | tf_op jit(solution)/shard_map/all_to_all | solution.py:259
  69.1 0.2 slice.20
  69.3 0.8 all_gather_reshape.3
  70.1 0.0 all-gather.2.cloned.1.call-update
  70.1 1.3 forward.1
  71.4 1.9 %collective-permute-start = (bf16[128,1536]{1,0:T(8,128)(2,1)S(1)}, bf16[128,1536]{1,0:T(8,128)(2,1)S(1)}, u32[]{:S(2)}, u32[]{:S(2)}) collective-permute-start(bf16[128,1536]{1,0:T(8,128)(2,1)S(1)} %get-tuple-element.7.share_ref), channel_id=1, source_target_pairs={{0,64},{64,0},{1,65},{65,1},{2,66},{66,2},{3,67},{67,3},{4,68},{68... | collective-permute-start | bytes 1179656 | tf_op jit(solution)/shard_map/ppermute | solution.py:263
  73.3 1.7 %collective-permute-done.received_ref = bf16[128,1536]{1,0:T(8,128)(2,1)S(1)} collective-permute-done((bf16[128,1536]{1,0:T(8,128)(2,1)S(1)}, bf16[128,1536]{1,0:T(8,128)(2,1)S(1)}, u32[]{:S(2)}, u32[]{:S(2)}) %collective-permute-start) | collective-permute-done | bytes 393248 | tf_op jit(solution)/shard_map/ppermute | solution.py:263
  75.0 1.5 weight_grad.1
  76.4 5.3 %all-to-all-start.1 = ((bf16[64,2,3456]{2,1,0:T(2,128)(2,1)}), bf16[64,2,3456]{2,1,0:T(2,128)(2,1)S(1)}, u32[]{:S(2)}, u32[]{:S(2)}) async-start(bf16[64,2,3456]{2,1,0:T(2,128)(2,1)} %weight_grad.1), calls=%async_computation.1 | async-start | bytes 1769472 | tf_op jit(solution)/shard_map/all_to_all | solution.py:259
  81.8 11.5 %all-gather.2.cloned.1.call-done.pieces_ref = bf16[8,128,896]{2,1,0:T(8,128)(2,1)} async-done(((bf16[1,128,896]{2,1,0:T(8,128)(2,1)}), bf16[8,128,896]{2,1,0:T(8,128)(2,1)}) %all-gather.2.cloned.1.call-update) | async-done | bytes 1835024 | tf_op jit(solution)/shard_map/all_gather | solution.py:287
  93.2 0.0 copy-start
  93.3 1.5 copy-done
  94.7 4.8 %backward.1 = bf16[64,2,4224]{2,1,0:T(2,128)(2,1)} custom-call(bf16[64,2,5120]{2,1,0:T(2,128)(2,1)S(1)} %all_to_all.15.sent_ref, bf16[8,128,896]{2,1,0:T(8,128)(2,1)S(1)} %copy-done), custom_call_target="tpu_custom_call" | custom-call | flops 4000000000 | bytes 12000000 | tf_op jit(solution)/shard_map/backward/pallas_call | solution.py:243
  99.6 13.2 %all-to-all-done.1.terms_ref = bf16[64,2,3456]{2,1,0:T(2,128)(2,1)S(1)} async-done(((bf16[64,2,3456]{2,1,0:T(2,128)(2,1)}), bf16[64,2,3456]{2,1,0:T(2,128)(2,1)S(1)}, u32[]{:S(2)}, u32[]{:S(2)}) %all-to-all-start.1) | async-done | bytes 884768 | tf_op jit(solution)/shard_map/all_to_all | solution.py:259
  112.7 5.1 %all-to-all-start.2 = ((bf16[64,2,4224]{2,1,0:T(2,128)(2,1)}), bf16[64,2,4224]{2,1,0:T(2,128)(2,1)S(1)}, u32[]{:S(2)}, u32[]{:S(2)}) async-start(bf16[64,2,4224]{2,1,0:T(2,128)(2,1)} %backward.1), calls=%async_computation.2 | async-start | bytes 2162688 | tf_op jit(solution)/shard_map/all_to_all | solution.py:259
  117.9 0.2 owned.1.refs_0_
  118.1 2.6 %collective-permute-start.3 = (f32[2,3456]{1,0:T(2,128)S(1)}, f32[2,3456]{1,0:T(2,128)S(1)}, u32[]{:S(2)}, u32[]{:S(2)}) collective-permute-start(f32[2,3456]{1,0:T(2,128)S(1)} %owned.1.refs_0_), channel_id=1, source_target_pairs={{0,384},{128,0},{256,128},{384,256},{1,385},{129,1},{257,129},{385... | collective-permute-start | bytes 82952 | tf_op jit(solution)/shard_map/ppermute | solution.py:267
  120.7 2.5 %collective-permute-start.2 = (f32[2,3456]{1,0:T(2,128)S(1)}, f32[2,3456]{1,0:T(2,128)S(1)}, u32[]{:S(2)}, u32[]{:S(2)}) collective-permute-start(f32[2,3456]{1,0:T(2,128)S(1)} %owned.1.refs_0_), channel_id=1, source_target_pairs={{0,256},{128,384},{256,0},{384,128},{1,257},{129,385},{257,1},{385... | collective-permute-start | bytes 82952 | tf_op jit(solution)/shard_map/ppermute | solution.py:267
  123.2 4.3 %collective-permute-start.1 = (f32[2,3456]{1,0:T(2,128)S(1)}, f32[2,3456]{1,0:T(2,128)S(1)}, u32[]{:S(2)}, u32[]{:S(2)}) collective-permute-start(f32[2,3456]{1,0:T(2,128)S(1)} %owned.1.refs_0_), channel_id=1, source_target_pairs={{0,128},{128,256},{256,384},{384,0},{1,129},{129,257},{257,385},{3... | collective-permute-start | bytes 82952 | tf_op jit(solution)/shard_map/ppermute | solution.py:267
  127.5 14.6 %collective-permute-done.3.refs_3_ = f32[2,3456]{1,0:T(2,128)S(1)} collective-permute-done((f32[2,3456]{1,0:T(2,128)S(1)}, f32[2,3456]{1,0:T(2,128)S(1)}, u32[]{:S(2)}, u32[]{:S(2)}) %collective-permute-start.3) | collective-permute-done | bytes 27680 | tf_op jit(solution)/shard_map/ppermute | solution.py:267
  142.1 0.7 collective-permute-done.2.refs_2_
  142.8 1.0 collective-permute-done.1.refs_1_
  143.8 1.9 %collective-permute-start.4 = (f32[2,3456]{1,0:T(2,128)S(1)}, f32[2,3456]{1,0:T(2,128)S(1)}, u32[]{:S(2)}, u32[]{:S(2)}) collective-permute-start(f32[2,3456]{1,0:T(2,128)S(1)} %group.1.mine_ref), channel_id=1, source_target_pairs={{0,64},{64,0},{1,65},{65,1},{2,66},{66,2},{3,67},{67,3},{4,68},{68... | collective-permute-start | bytes 82952 | tf_op jit(solution)/shard_map/ppermute | solution.py:263
  145.7 1.2 collective-permute-done.4.theirs_ref
  146.9 0.7 total.1
  147.6 5.7 %all-to-all-done.2 = bf16[64,2,4224]{2,1,0:T(2,128)(2,1)S(1)} async-done(((bf16[64,2,4224]{2,1,0:T(2,128)(2,1)}), bf16[64,2,4224]{2,1,0:T(2,128)(2,1)S(1)}, u32[]{:S(2)}, u32[]{:S(2)}) %all-to-all-start.2) | async-done | bytes 1081376 | tf_op jit(solution)/shard_map/all_to_all | solution.py:259
  153.2 0.4 reshape.27
  153.7 0.7 slice_bitcast_fusion.3
  154.4 0.1 slice_bitcast_fusion.2
  154.4 1.0 maximum_bitcast_fusion
  (1 shorter events, 0.0 us)
Async XLA Ops:
  7.2 86.1 %all-gather.2.cloned.1.call-start = ((), (), s32[]{:S(2)}) async-start(), calls=%async_computation.3 | async-start | bytes 2064384 | tf_op jit(solution)/shard_map/all_gather | solution.py:287
  71.4 3.6 %collective-permute-start = (bf16[128,1536]{1,0:T(8,128)(2,1)S(1)}, bf16[128,1536]{1,0:T(8,128)(2,1)S(1)}, u32[]{:S(2)}, u32[]{:S(2)}) collective-permute-start(bf16[128,1536]{1,0:T(8,128)(2,1)S(1)} %get-tuple-element.7.share_ref), channel_id=1, source_target_pairs={{0,64},{64,0},{1,65},{65,1},{2,66},{66,2},{3,67},{67,3},{4,68},{68... | collective-permute-start | bytes 1179656 | tf_op jit(solution)/shard_map/ppermute | solution.py:263
  76.4 36.3 %all-to-all-start.1 = ((bf16[64,2,3456]{2,1,0:T(2,128)(2,1)}), bf16[64,2,3456]{2,1,0:T(2,128)(2,1)S(1)}, u32[]{:S(2)}, u32[]{:S(2)}) async-start(bf16[64,2,3456]{2,1,0:T(2,128)(2,1)} %weight_grad.1), calls=%async_computation.1 | async-start | bytes 1769472 | tf_op jit(solution)/shard_map/all_to_all | solution.py:259
  93.2 1.5 copy-start
  112.7 40.5 %all-to-all-start.2 = ((bf16[64,2,4224]{2,1,0:T(2,128)(2,1)}), bf16[64,2,4224]{2,1,0:T(2,128)(2,1)S(1)}, u32[]{:S(2)}, u32[]{:S(2)}) async-start(bf16[64,2,4224]{2,1,0:T(2,128)(2,1)} %backward.1), calls=%async_computation.2 | async-start | bytes 2162688 | tf_op jit(solution)/shard_map/all_to_all | solution.py:259
  118.1 24.0 %collective-permute-start.3 = (f32[2,3456]{1,0:T(2,128)S(1)}, f32[2,3456]{1,0:T(2,128)S(1)}, u32[]{:S(2)}, u32[]{:S(2)}) collective-permute-start(f32[2,3456]{1,0:T(2,128)S(1)} %owned.1.refs_0_), channel_id=1, source_target_pairs={{0,384},{128,0},{256,128},{384,256},{1,385},{129,1},{257,129},{385... | collective-permute-start | bytes 82952 | tf_op jit(solution)/shard_map/ppermute | solution.py:267
  120.7 22.1 %collective-permute-start.2 = (f32[2,3456]{1,0:T(2,128)S(1)}, f32[2,3456]{1,0:T(2,128)S(1)}, u32[]{:S(2)}, u32[]{:S(2)}) collective-permute-start(f32[2,3456]{1,0:T(2,128)S(1)} %owned.1.refs_0_), channel_id=1, source_target_pairs={{0,256},{128,384},{256,0},{384,128},{1,257},{129,385},{257,1},{385... | collective-permute-start | bytes 82952 | tf_op jit(solution)/shard_map/ppermute | solution.py:267
  123.2 20.6 %collective-permute-start.1 = (f32[2,3456]{1,0:T(2,128)S(1)}, f32[2,3456]{1,0:T(2,128)S(1)}, u32[]{:S(2)}, u32[]{:S(2)}) collective-permute-start(f32[2,3456]{1,0:T(2,128)S(1)} %owned.1.refs_0_), channel_id=1, source_target_pairs={{0,128},{128,256},{256,384},{384,0},{1,129},{129,257},{257,385},{3... | collective-permute-start | bytes 82952 | tf_op jit(solution)/shard_map/ppermute | solution.py:267
  143.8 3.1 %collective-permute-start.4 = (f32[2,3456]{1,0:T(2,128)S(1)}, f32[2,3456]{1,0:T(2,128)S(1)}, u32[]{:S(2)}, u32[]{:S(2)}) collective-permute-start(f32[2,3456]{1,0:T(2,128)S(1)} %group.1.mine_ref), channel_id=1, source_target_pairs={{0,64},{64,0},{1,65},{65,1},{2,66},{66,2},{3,67},{67,3},{4,68},{68... | collective-permute-start | bytes 82952 | tf_op jit(solution)/shard_map/ppermute | solution.py:263
Sparse Core Ops, SparseCore 0:
  70.2 22.9 all-gather.1

commit v8 on v7

--- a/solution.py
+++ b/solution.py
@@ -159,14 +159,17 @@
     columns = jnp.concatenate([columns_ref[...], received_ref[:, WIDTH:]], axis=0)
     features = jnp.concatenate([share_ref[:, :WIDTH], received_ref[:, :WIDTH]], axis=0)
     partial = dot(columns, features, 0, 0).astype(BF16)
-    for pair in range(3):
-        out_ref[:, :, pair * WIDTH : (pair + 1) * WIDTH] = partial[
-            pair * ROWS : (pair + 1) * ROWS
-        ].reshape(64, 2, WIDTH)
+    for target in range(4):
+        for high in range(2):
+            for pair in range(3):
+                start = pair * ROWS + high * 64 + target * 16
+                out_ref[
+                    target, high * 16 : high * 16 + 16, pair * WIDTH : (pair + 1) * WIDTH
+                ] = partial[start : start + 16]
 
 
 def backward_kernel(
-    sent_ref, pieces_ref,
+    core_ref, x_ref, sent_ref, mine_ref, theirs_ref,
     out_ref, rows_ref, weights_ref, channels_ref, attended_ref, matrix_ref, upstream_ref,
     grad_scores_ref,
 ):
@@ -177,12 +180,18 @@
         attended_ref[:, lanes(tile)] = value
 
     attend(rows_ref, weights_ref, put_attended)
-    for core in range(2):
-        for piece, place, pair, tile in half_tiles():
-            start = core * HALF + pair * ROWS
-            matrix_ref[start : start + ROWS, lanes(tile)] = pieces_ref[
-                4 * core + piece, :, lanes(place)
-            ]
+    own = pl.multiple_of(core_ref[0] * HALF, HALF)
+    other = pl.multiple_of((1 - core_ref[0]) * HALF, HALF)
+    for here in range(4):
+
+        @pl.when(x_ref[0] == here)
+        def _():
+            for piece, place, pair, tile in half_tiles():
+                for start, half_ref in ((own, mine_ref), (other, theirs_ref)):
+                    matrix_ref[pl.ds(start + pair * ROWS, ROWS), lanes(tile)] = half_ref[
+                        (here - piece) & 3, :, lanes(place)
+                    ]
+
     upstream_ref[...] = dot(channels_ref[...], matrix_ref[...], 1, 0).astype(BF16)
     products = [
         head_products(upstream_ref, 0, rows_ref, 2 * WIDTH, index) for index in range(HEADS)
@@ -210,10 +219,17 @@
         )
 
 
+def merge_kernel(terms_ref, out_ref):
+    total = terms_ref[0].astype(F32)
+    for place in range(1, 4):
+        total += terms_ref[place].astype(F32)
+    out_ref[...] = total.astype(BF16).reshape(16, 2, HALF_WIDTH)
+
+
 def owned_kernel(terms_ref, out_ref):
-    rows = terms_ref[...].reshape(ROWS, HALF_WIDTH)
-    target = lax.broadcasted_iota(jnp.int32, (8, ROWS), 0)
-    source = lax.broadcasted_iota(jnp.int32, (8, ROWS), 1)
+    rows = terms_ref[...].reshape(32, HALF_WIDTH)
+    target = lax.broadcasted_iota(jnp.int32, (8, 32), 0)
+    source = lax.broadcasted_iota(jnp.int32, (8, 32), 1)
     chosen = jnp.where(target == (source & 1), 1.0, 0.0).astype(BF16)
     out_ref[...] = dot(chosen, rows, 1, 0)[:2]
 
@@ -269,6 +285,7 @@
 
 def on_device(query_key_value, out_weight, cotangent):
     core = lax.axis_index("c").astype(jnp.int32).reshape(1)
+    x_place = lax.axis_index("x").astype(jnp.int32).reshape(1)
     (packed,) = call(
         pack_kernel,
         "pack",
@@ -284,7 +301,6 @@
         grant=56,
     )
     sent = exchange(packed, SEQ)
-    pieces = lax.all_gather(sent[:, :, BASE:].reshape(ROWS, PIECE), ("c", "x"))
     share, columns = call(
         forward_kernel,
         "forward",
@@ -303,14 +319,22 @@
         "weight_grad",
         (share, swap(share), columns),
         [IN_VMEM] * 3,
-        [((64, 2, HALF_WIDTH), BF16)],
-    )
-    collected = exchange(partial, SEQ)
+        [((4, 32, HALF_WIDTH), BF16)],
+    )
+    piece, partial = lax.optimization_barrier((sent[:, :, BASE:].reshape(ROWS, PIECE), partial))
+    terms = exchange(partial, "x")
+    turned = [turn(piece, "x", step) for step in range(1, 4)]
+    (summed,) = call(
+        merge_kernel, "merge", (terms,), [IN_VMEM], [((16, 2, HALF_WIDTH), BF16)]
+    )
+    collected = exchange(summed, ("yh", "z"))
+    piece, *turned = lax.optimization_barrier((piece, *turned, summed))[:4]
+    mine = jnp.stack([piece, *turned])
     (results,) = call(
         backward_kernel,
         "backward",
-        (sent, pieces),
-        [IN_VMEM] * 2,
+        (core, x_place, sent, mine, swap(mine)),
+        [IN_SMEM] * 2 + [IN_VMEM] * 3,
         [((64, 2, BASE), BF16)],
         [
             pltpu.VMEM((ROWS, COLS), BF16),
@@ -324,9 +348,9 @@
         micros=4,
     )
     results, collected = lax.optimization_barrier((results, collected))
-    back = exchange(results, SEQ)
     (owned,) = call(owned_kernel, "owned", (collected,), [IN_VMEM], [((2, HALF_WIDTH), F32)])
     turned = [turn(owned, "yl", step) for step in range(1, 4)]
+    back = exchange(results, SEQ)
     (group,) = call(
         group_kernel, "group", (owned, *turned), [IN_VMEM] * 4, [((2, HALF_WIDTH), F32)]
     )

time: 163 us -> 161 us (0.988)
  starting transfers between devices: 23.7 us -> 39.1 us
  between operations: 14.1 us -> 0.8 us
  waiting for transfers between devices: 49.4 us -> 46.3 us
  local copies, waits for them, and re-layouts: 3.66 us -> 1.44 us
    all_gather x1 -> x0, waiting for transfers between devices: 11.5 us -> none  [on_device(): pieces = lax.all_gather(sent[:, :, BASE:].reshape(ROWS, PIECE), ('c', 'x'))]
    ppermute x3 -> x6, starting transfers between devices: 9.4 us -> 18.4 us  [turn(): lax.ppermute(value, axis, [(place, (place + step) % 4) for place in range...]
    ppermute x3 -> x6, waiting for transfers between devices: 16.3 us -> 23.2 us  [turn(): lax.ppermute(value, axis, [(place, (place + step) % 4) for place in range...]
    all_to_all x2 -> x3, starting transfers between devices: 10.5 us -> 14.9 us  [exchange(): return lax.all_to_all(value, axes, 0, 0, tiled=True)]
    ppermute x2 -> x3, starting transfers between devices: 3.84 us -> 5.77 us  [swap(): return lax.ppermute(value, 'c', [(0, 1), (1, 0)])]
    all_to_all x2 -> x3, waiting for transfers between devices: 18.8 us -> 20.5 us  [exchange(): return lax.all_to_all(value, axes, 0, 0, tiled=True)]
    pallas_call x7 -> x8, Pallas kernels: 11.3 us -> 12.4 us  [call(): pl.pallas_call(kernel, out_shape=[jax.ShapeDtypeStruct(shape, dtype) for...]
  transfers between devices with their start and end apart: 8 -> 12, of which waited for: 8 -> 8; matrix products, arithmetic and copies ran while one was open for 0% -> 0% of each run, Pallas kernels for 5% -> 4%
where the time goes in v8:
time: 161 us; the launch traced here: 160 us
  blocking collectives  59 us (37%)
  waiting for transfers between devices  46.3 us (29%)
  starting transfers between devices  39.1 us (24%)
  Pallas kernels  12.4 us (8%)
    all_to_all x1, blocking collectives, exchange(): return lax.all_to_all(value, axes, 0, 0, tiled=True)  59 us
    ppermute x6, waiting for transfers between devices, turn(): lax.ppermute(value, axis, [(place, (place + step) % 4) for place in range...  23.2 us
    all_to_all x3, waiting for transfers between devices, exchange(): return lax.all_to_all(value, axes, 0, 0, tiled=True)  20.5 us
    ppermute x6, starting transfers between devices, turn(): lax.ppermute(value, axis, [(place, (place + step) % 4) for place in range...  18.4 us
    all_to_all x3, starting transfers between devices, exchange(): return lax.all_to_all(value, axes, 0, 0, tiled=True)  14.9 us
    pallas_call x8, Pallas kernels, call(): pl.pallas_call(kernel, out_shape=[jax.ShapeDtypeStruct(shape, dtype) for...  12.4 us
    ppermute x3, starting transfers between devices, swap(): return lax.ppermute(value, 'c', [(0, 1), (1, 0)])  5.77 us
  transfers between devices with their start and end apart: 12, of which 8 were waited for; matrix products, arithmetic and copies ran while one was open for 0% of the time, Pallas kernels for 4%

profile of v8, /device:TPU:14, one launch (start us, length us, event | category | flops | bytes accessed | tf_op | source)
XLA Modules:
  0.0 160.2 jit_solution(17691654140442171123)
XLA Ops:
  0.6 2.8 %pack.1 = bf16[64,2,5120]{2,1,0:T(2,128)(2,1)} custom-call(s32[1]{0:T(128)} %bitcast.core_ref, bf16[3,128,1152]{2,1,0:T(8,128)(2,1)} %bitcast.22, bf16[128,768]{1,0:T(8,128)(2,1)} %bitcast.23, bf16[12,1152]{1,0:T(8,128)(2,1)} %weight_hbm.1), custom_call_target="tpu_custom_call" | custom-call | flops 1000000000 | bytes 3000000 | tf_op jit(solution)/shard_map/pack/pallas_call | solution.py:259
  3.5 59.0 %all_to_all.20.sent_ref = bf16[64,2,5120]{2,1,0:T(2,128)(2,1)S(1)} all-to-all(bf16[64,2,5120]{2,1,0:T(2,128)(2,1)} %pack.1), channel_id=1, replica_groups=mesh['yl'=4,'c'=2,'yh'=2,'x'=4,'z'=8] {'yh','x','z'}, dimensions={0} | all-to-all | bytes 2621440 | tf_op jit(solution)/shard_map/all_to_all | solution.py:275
  62.5 1.3 forward.1
  63.8 1.9 %collective-permute-start = (bf16[128,1536]{1,0:T(8,128)(2,1)S(1)}, bf16[128,1536]{1,0:T(8,128)(2,1)S(1)}, u32[]{:S(2)}, u32[]{:S(2)}) collective-permute-start(bf16[128,1536]{1,0:T(8,128)(2,1)S(1)} %get-tuple-element.13.share_ref), channel_id=1, source_target_pairs={{0,64},{64,0},{1,65},{65,1},{2,66},{66,2},{3,67},{67,3},{4,68},{68... | collective-permute-start | bytes 1179656 | tf_op jit(solution)/shard_map/ppermute | solution.py:279
  65.7 0.2 slice.20
  65.9 0.1 reshape.34
  66.0 1.4 collective-permute-done.received_ref
  67.4 1.4 weight_grad.1
  68.8 4.5 %all-to-all-start.1 = ((bf16[4,32,3456]{2,1,0:T(8,128)(2,1)}), bf16[4,32,3456]{2,1,0:T(8,128)(2,1)S(1)}, u32[]{:S(2)}, u32[]{:S(2)}) async-start(bf16[4,32,3456]{2,1,0:T(8,128)(2,1)} %weight_grad.1), calls=%async_computation.1 | async-start | bytes 1769472 | tf_op jit(solution)/shard_map/all_to_all | solution.py:275
  73.3 2.8 %collective-permute-start.3 = (bf16[128,896]{1,0:T(8,128)(2,1)S(1)}, bf16[128,896]{1,0:T(8,128)(2,1)S(1)}, u32[]{:S(2)}, u32[]{:S(2)}) collective-permute-start(bf16[128,896]{1,0:T(8,128)(2,1)S(1)} %reshape.34), channel_id=1, source_target_pairs={{0,24},{8,0},{16,8},{24,16},{1,25},{9,1},{17,9},{25,17},{2,26},{10... | collective-permute-start | bytes 688136 | tf_op jit(solution)/shard_map/ppermute | solution.py:283
  76.1 2.5 %collective-permute-start.2 = (bf16[128,896]{1,0:T(8,128)(2,1)S(1)}, bf16[128,896]{1,0:T(8,128)(2,1)S(1)}, u32[]{:S(2)}, u32[]{:S(2)}) collective-permute-start(bf16[128,896]{1,0:T(8,128)(2,1)S(1)} %reshape.34), channel_id=1, source_target_pairs={{0,16},{8,24},{16,0},{24,8},{1,17},{9,25},{17,1},{25,9},{2,18},{10... | collective-permute-start | bytes 688136 | tf_op jit(solution)/shard_map/ppermute | solution.py:283
  78.6 4.5 %collective-permute-start.1 = (bf16[128,896]{1,0:T(8,128)(2,1)S(1)}, bf16[128,896]{1,0:T(8,128)(2,1)S(1)}, u32[]{:S(2)}, u32[]{:S(2)}) collective-permute-start(bf16[128,896]{1,0:T(8,128)(2,1)S(1)} %reshape.34), channel_id=1, source_target_pairs={{0,8},{8,16},{16,24},{24,0},{1,9},{9,17},{17,25},{25,1},{2,10},{10... | collective-permute-start | bytes 688136 | tf_op jit(solution)/shard_map/ppermute | solution.py:283
  83.1 2.9 %all-to-all-done.1.terms_ref = bf16[4,32,3456]{2,1,0:T(8,128)(2,1)S(1)} async-done(((bf16[4,32,3456]{2,1,0:T(8,128)(2,1)}), bf16[4,32,3456]{2,1,0:T(8,128)(2,1)S(1)}, u32[]{:S(2)}, u32[]{:S(2)}) %all-to-all-start.1) | async-done | bytes 884768 | tf_op jit(solution)/shard_map/all_to_all | solution.py:275
  86.0 0.8 merge.1
  86.9 2.2 %collective-permute-done.3 = bf16[128,896]{1,0:T(8,128)(2,1)S(1)} collective-permute-done((bf16[128,896]{1,0:T(8,128)(2,1)S(1)}, bf16[128,896]{1,0:T(8,128)(2,1)S(1)}, u32[]{:S(2)}, u32[]{:S(2)}) %collective-permute-start.3) | collective-permute-done | bytes 229408 | tf_op jit(solution)/shard_map/ppermute | solution.py:283
  89.0 5.7 %collective-permute-done.2 = bf16[128,896]{1,0:T(8,128)(2,1)S(1)} collective-permute-done((bf16[128,896]{1,0:T(8,128)(2,1)S(1)}, bf16[128,896]{1,0:T(8,128)(2,1)S(1)}, u32[]{:S(2)}, u32[]{:S(2)}) %collective-permute-start.2) | collective-permute-done | bytes 229408 | tf_op jit(solution)/shard_map/ppermute | solution.py:283
  94.7 0.0 collective-permute-done.1
  94.8 0.1 pad_maximum_fusion.mine_ref
  94.9 1.9 %collective-permute-start.4 = (bf16[4,128,896]{2,1,0:T(8,128)(2,1)S(1)}, bf16[4,128,896]{2,1,0:T(8,128)(2,1)S(1)}, u32[]{:S(2)}, u32[]{:S(2)}) collective-permute-start(bf16[4,128,896]{2,1,0:T(8,128)(2,1)S(1)} %pad_maximum_fusion.mine_ref), channel_id=1, source_target_pairs={{0,64},{64,0},{1,65},{65,1},{2,66},{66,2},{3,67},{67,3},{4,68},{68... | collective-permute-start | bytes 2752520 | tf_op jit(solution)/shard_map/ppermute | solution.py:279
  96.8 3.6 %all-to-all-start.2 = ((bf16[16,2,3456]{2,1,0:T(2,128)(2,1)}), bf16[16,2,3456]{2,1,0:T(2,128)(2,1)S(1)}, u32[]{:S(2)}, u32[]{:S(2)}) async-start(bf16[16,2,3456]{2,1,0:T(2,128)(2,1)} %merge.1), calls=%async_computation.2 | async-start | bytes 442368 | tf_op jit(solution)/shard_map/all_to_all | solution.py:275
  100.4 0.0 collective-permute-done.4.theirs_ref
  100.4 5.3 %backward.1 = bf16[64,2,4224]{2,1,0:T(2,128)(2,1)} custom-call(s32[1]{0:T(128)} %bitcast.core_ref, s32[1]{0:T(128)} %bitcast.1.x_ref, bf16[64,2,5120]{2,1,0:T(2,128)(2,1)S(1)} %all_to_all.20.sent_ref, bf16[4,128,896]{2,1,0:T(8,128)(2,1)S(1)} %pad_maximum_fusion.mine_ref, bf16[4,128,896]{2,1,0:T(8,128)(2,1)S(1)} %collective-permute-done.4.theirs_ref), custom_call_target="tpu_custom_call" | custom-call | flops 4000000000 | bytes 12000000 | tf_op jit(solution)/shard_map/backward/pallas_call | solution.py:259
  105.7 10.1 %all-to-all-done.2.terms_ref = bf16[16,2,3456]{2,1,0:T(2,128)(2,1)S(1)} async-done(((bf16[16,2,3456]{2,1,0:T(2,128)(2,1)}), bf16[16,2,3456]{2,1,0:T(2,128)(2,1)S(1)}, u32[]{:S(2)}, u32[]{:S(2)}) %all-to-all-start.2) | async-done | bytes 221216 | tf_op jit(solution)/shard_map/all_to_all | solution.py:275
  115.8 6.8 %all-to-all-start.3 = ((bf16[64,2,4224]{2,1,0:T(2,128)(2,1)}), bf16[64,2,4224]{2,1,0:T(2,128)(2,1)S(1)}, u32[]{:S(2)}, u32[]{:S(2)}) async-start(bf16[64,2,4224]{2,1,0:T(2,128)(2,1)} %backward.1), calls=%async_computation.3 | async-start | bytes 2162688 | tf_op jit(solution)/shard_map/all_to_all | solution.py:275
  122.6 0.2 owned.1.refs_0_
  122.8 1.9 %collective-permute-start.7 = (f32[2,3456]{1,0:T(2,128)S(1)}, f32[2,3456]{1,0:T(2,128)S(1)}, u32[]{:S(2)}, u32[]{:S(2)}) collective-permute-start(f32[2,3456]{1,0:T(2,128)S(1)} %owned.1.refs_0_), channel_id=1, source_target_pairs={{0,384},{128,0},{256,128},{384,256},{1,385},{129,1},{257,129},{385... | collective-permute-start | bytes 82952 | tf_op jit(solution)/shard_map/ppermute | solution.py:283
  124.7 3.3 %collective-permute-start.6 = (f32[2,3456]{1,0:T(2,128)S(1)}, f32[2,3456]{1,0:T(2,128)S(1)}, u32[]{:S(2)}, u32[]{:S(2)}) collective-permute-start(f32[2,3456]{1,0:T(2,128)S(1)} %owned.1.refs_0_), channel_id=1, source_target_pairs={{0,256},{128,384},{256,0},{384,128},{1,257},{129,385},{257,1},{385... | collective-permute-start | bytes 82952 | tf_op jit(solution)/shard_map/ppermute | solution.py:283
  128.1 3.4 %collective-permute-start.5 = (f32[2,3456]{1,0:T(2,128)S(1)}, f32[2,3456]{1,0:T(2,128)S(1)}, u32[]{:S(2)}, u32[]{:S(2)}) collective-permute-start(f32[2,3456]{1,0:T(2,128)S(1)} %owned.1.refs_0_), channel_id=1, source_target_pairs={{0,128},{128,256},{256,384},{384,0},{1,129},{129,257},{257,385},{3... | collective-permute-start | bytes 82952 | tf_op jit(solution)/shard_map/ppermute | solution.py:283
  131.4 15.3 %collective-permute-done.7.refs_3_ = f32[2,3456]{1,0:T(2,128)S(1)} collective-permute-done((f32[2,3456]{1,0:T(2,128)S(1)}, f32[2,3456]{1,0:T(2,128)S(1)}, u32[]{:S(2)}, u32[]{:S(2)}) %collective-permute-start.7) | collective-permute-done | bytes 27680 | tf_op jit(solution)/shard_map/ppermute | solution.py:283
  146.7 0.0 collective-permute-done.6.refs_2_
  146.7 0.0 collective-permute-done.5.refs_1_
  146.7 1.9 %collective-permute-start.8 = (f32[2,3456]{1,0:T(2,128)S(1)}, f32[2,3456]{1,0:T(2,128)S(1)}, u32[]{:S(2)}, u32[]{:S(2)}) collective-permute-start(f32[2,3456]{1,0:T(2,128)S(1)} %group.1.mine_ref), channel_id=1, source_target_pairs={{0,64},{64,0},{1,65},{65,1},{2,66},{66,2},{3,67},{67,3},{4,68},{68... | collective-permute-start | bytes 82952 | tf_op jit(solution)/shard_map/ppermute | solution.py:279
  148.7 1.2 collective-permute-done.8.theirs_ref
  149.8 0.7 total.1
  150.5 7.5 %all-to-all-done.3 = bf16[64,2,4224]{2,1,0:T(2,128)(2,1)S(1)} async-done(((bf16[64,2,4224]{2,1,0:T(2,128)(2,1)}), bf16[64,2,4224]{2,1,0:T(2,128)(2,1)S(1)}, u32[]{:S(2)}, u32[]{:S(2)}) %all-to-all-start.3) | async-done | bytes 1081376 | tf_op jit(solution)/shard_map/all_to_all | solution.py:275
  158.0 0.4 reshape.35
  158.4 0.7 slice_bitcast_fusion.3
  159.1 0.1 slice_bitcast_fusion.2
  159.2 1.0 maximum_bitcast_fusion
  (1 shorter events, 0.0 us)
Async XLA Ops:
  63.8 3.6 %collective-permute-start = (bf16[128,1536]{1,0:T(8,128)(2,1)S(1)}, bf16[128,1536]{1,0:T(8,128)(2,1)S(1)}, u32[]{:S(2)}, u32[]{:S(2)}) collective-permute-start(bf16[128,1536]{1,0:T(8,128)(2,1)S(1)} %get-tuple-element.13.share_ref), channel_id=1, source_target_pairs={{0,64},{64,0},{1,65},{65,1},{2,66},{66,2},{3,67},{67,3},{4,68},{68... | collective-permute-start | bytes 1179656 | tf_op jit(solution)/shard_map/ppermute | solution.py:279
  68.8 17.2 %all-to-all-start.1 = ((bf16[4,32,3456]{2,1,0:T(8,128)(2,1)}), bf16[4,32,3456]{2,1,0:T(8,128)(2,1)S(1)}, u32[]{:S(2)}, u32[]{:S(2)}) async-start(bf16[4,32,3456]{2,1,0:T(8,128)(2,1)} %weight_grad.1), calls=%async_computation.1 | async-start | bytes 1769472 | tf_op jit(solution)/shard_map/all_to_all | solution.py:275
  73.3 15.7 %collective-permute-start.3 = (bf16[128,896]{1,0:T(8,128)(2,1)S(1)}, bf16[128,896]{1,0:T(8,128)(2,1)S(1)}, u32[]{:S(2)}, u32[]{:S(2)}) collective-permute-start(bf16[128,896]{1,0:T(8,128)(2,1)S(1)} %reshape.34), channel_id=1, source_target_pairs={{0,24},{8,0},{16,8},{24,16},{1,25},{9,1},{17,9},{25,17},{2,26},{10... | collective-permute-start | bytes 688136 | tf_op jit(solution)/shard_map/ppermute | solution.py:283
  76.1 18.7 %collective-permute-start.2 = (bf16[128,896]{1,0:T(8,128)(2,1)S(1)}, bf16[128,896]{1,0:T(8,128)(2,1)S(1)}, u32[]{:S(2)}, u32[]{:S(2)}) collective-permute-start(bf16[128,896]{1,0:T(8,128)(2,1)S(1)} %reshape.34), channel_id=1, source_target_pairs={{0,16},{8,24},{16,0},{24,8},{1,17},{9,25},{17,1},{25,9},{2,18},{10... | collective-permute-start | bytes 688136 | tf_op jit(solution)/shard_map/ppermute | solution.py:283
  78.6 16.2 %collective-permute-start.1 = (bf16[128,896]{1,0:T(8,128)(2,1)S(1)}, bf16[128,896]{1,0:T(8,128)(2,1)S(1)}, u32[]{:S(2)}, u32[]{:S(2)}) collective-permute-start(bf16[128,896]{1,0:T(8,128)(2,1)S(1)} %reshape.34), channel_id=1, source_target_pairs={{0,8},{8,16},{16,24},{24,0},{1,9},{9,17},{17,25},{25,1},{2,10},{10... | collective-permute-start | bytes 688136 | tf_op jit(solution)/shard_map/ppermute | solution.py:283
  94.9 5.5 %collective-permute-start.4 = (bf16[4,128,896]{2,1,0:T(8,128)(2,1)S(1)}, bf16[4,128,896]{2,1,0:T(8,128)(2,1)S(1)}, u32[]{:S(2)}, u32[]{:S(2)}) collective-permute-start(bf16[4,128,896]{2,1,0:T(8,128)(2,1)S(1)} %pad_maximum_fusion.mine_ref), channel_id=1, source_target_pairs={{0,64},{64,0},{1,65},{65,1},{2,66},{66,2},{3,67},{67,3},{4,68},{68... | collective-permute-start | bytes 2752520 | tf_op jit(solution)/shard_map/ppermute | solution.py:279
  96.8 19.0 %all-to-all-start.2 = ((bf16[16,2,3456]{2,1,0:T(2,128)(2,1)}), bf16[16,2,3456]{2,1,0:T(2,128)(2,1)S(1)}, u32[]{:S(2)}, u32[]{:S(2)}) async-start(bf16[16,2,3456]{2,1,0:T(2,128)(2,1)} %merge.1), calls=%async_computation.2 | async-start | bytes 442368 | tf_op jit(solution)/shard_map/all_to_all | solution.py:275
  115.8 42.2 %all-to-all-start.3 = ((bf16[64,2,4224]{2,1,0:T(2,128)(2,1)}), bf16[64,2,4224]{2,1,0:T(2,128)(2,1)S(1)}, u32[]{:S(2)}, u32[]{:S(2)}) async-start(bf16[64,2,4224]{2,1,0:T(2,128)(2,1)} %backward.1), calls=%async_computation.3 | async-start | bytes 2162688 | tf_op jit(solution)/shard_map/all_to_all | solution.py:275
  122.8 23.9 %collective-permute-start.7 = (f32[2,3456]{1,0:T(2,128)S(1)}, f32[2,3456]{1,0:T(2,128)S(1)}, u32[]{:S(2)}, u32[]{:S(2)}) collective-permute-start(f32[2,3456]{1,0:T(2,128)S(1)} %owned.1.refs_0_), channel_id=1, source_target_pairs={{0,384},{128,0},{256,128},{384,256},{1,385},{129,1},{257,129},{385... | collective-permute-start | bytes 82952 | tf_op jit(solution)/shard_map/ppermute | solution.py:283
  124.7 22.0 %collective-permute-start.6 = (f32[2,3456]{1,0:T(2,128)S(1)}, f32[2,3456]{1,0:T(2,128)S(1)}, u32[]{:S(2)}, u32[]{:S(2)}) collective-permute-start(f32[2,3456]{1,0:T(2,128)S(1)} %owned.1.refs_0_), channel_id=1, source_target_pairs={{0,256},{128,384},{256,0},{384,128},{1,257},{129,385},{257,1},{385... | collective-permute-start | bytes 82952 | tf_op jit(solution)/shard_map/ppermute | solution.py:283
  128.1 18.7 %collective-permute-start.5 = (f32[2,3456]{1,0:T(2,128)S(1)}, f32[2,3456]{1,0:T(2,128)S(1)}, u32[]{:S(2)}, u32[]{:S(2)}) collective-permute-start(f32[2,3456]{1,0:T(2,128)S(1)} %owned.1.refs_0_), channel_id=1, source_target_pairs={{0,128},{128,256},{256,384},{384,0},{1,129},{129,257},{257,385},{3... | collective-permute-start | bytes 82952 | tf_op jit(solution)/shard_map/ppermute | solution.py:283
  146.7 3.1 %collective-permute-start.8 = (f32[2,3456]{1,0:T(2,128)S(1)}, f32[2,3456]{1,0:T(2,128)S(1)}, u32[]{:S(2)}, u32[]{:S(2)}) collective-permute-start(f32[2,3456]{1,0:T(2,128)S(1)} %group.1.mine_ref), channel_id=1, source_target_pairs={{0,64},{64,0},{1,65},{65,1},{2,66},{66,2},{3,67},{67,3},{4,68},{68... | collective-permute-start | bytes 82952 | tf_op jit(solution)/shard_map/ppermute | solution.py:279

commit v9 on v8

--- a/solution.py
+++ b/solution.py
@@ -169,7 +169,7 @@
 
 
 def backward_kernel(
-    core_ref, x_ref, sent_ref, mine_ref, theirs_ref,
+    core_ref, sent_ref, mine_ref, theirs_ref,
     out_ref, rows_ref, weights_ref, channels_ref, attended_ref, matrix_ref, upstream_ref,
     grad_scores_ref,
 ):
@@ -182,16 +182,11 @@
     attend(rows_ref, weights_ref, put_attended)
     own = pl.multiple_of(core_ref[0] * HALF, HALF)
     other = pl.multiple_of((1 - core_ref[0]) * HALF, HALF)
-    for here in range(4):
-
-        @pl.when(x_ref[0] == here)
-        def _():
-            for piece, place, pair, tile in half_tiles():
-                for start, half_ref in ((own, mine_ref), (other, theirs_ref)):
-                    matrix_ref[pl.ds(start + pair * ROWS, ROWS), lanes(tile)] = half_ref[
-                        (here - piece) & 3, :, lanes(place)
-                    ]
-
+    for piece, place, pair, tile in half_tiles():
+        for start, half_ref in ((own, mine_ref), (other, theirs_ref)):
+            matrix_ref[pl.ds(start + pair * ROWS, ROWS), lanes(tile)] = half_ref[
+                piece, :, lanes(place)
+            ]
     upstream_ref[...] = dot(channels_ref[...], matrix_ref[...], 1, 0).astype(BF16)
     products = [
         head_products(upstream_ref, 0, rows_ref, 2 * WIDTH, index) for index in range(HEADS)
@@ -234,6 +229,21 @@
     out_ref[...] = dot(chosen, rows, 1, 0)[:2]
 
 
+def unpack_kernel(back_ref, projected_hbm, grads_hbm, rows_ref, sems):
+    rows_ref[...] = back_ref[...].reshape(ROWS, BASE)
+    parts = [(rows_ref.at[:, 3 * WIDTH :], projected_hbm)]
+    for part in range(3):
+        parts.append((rows_ref.at[:, part * WIDTH : (part + 1) * WIDTH], grads_hbm.at[part]))
+    copies = [
+        pltpu.make_async_copy(source, target, sems.at[place])
+        for place, (source, target) in enumerate(parts)
+    ]
+    for copy in copies:
+        copy.start()
+    for copy in copies:
+        copy.wait()
+
+
 def group_kernel(*refs):
     *terms, out_ref = refs
     total = terms[0][...]
@@ -255,14 +265,13 @@
 IN_HBM = pl.BlockSpec(memory_space=pltpu.HBM)
 
 
-def call(kernel, name, operands, specs, outs, scratch=(), aliases=None, grant=12, micros=1):
+def call(kernel, name, operands, specs, outs, scratch=(), grant=12, micros=1, out_spec=IN_VMEM):
     return pl.pallas_call(
         kernel,
         out_shape=[jax.ShapeDtypeStruct(shape, dtype) for shape, dtype in outs],
         in_specs=specs,
-        out_specs=[IN_VMEM] * len(outs),
+        out_specs=[out_spec] * len(outs),
         scratch_shapes=list(scratch),
-        input_output_aliases=aliases or {},
         compiler_params=pltpu.CompilerParams(vmem_limit_bytes=grant << 20),
         cost_estimate=pl.CostEstimate(
             flops=micros * 10**9, bytes_accessed=micros * 3 * 10**6, transcendentals=0
@@ -285,7 +294,6 @@
 
 def on_device(query_key_value, out_weight, cotangent):
     core = lax.axis_index("c").astype(jnp.int32).reshape(1)
-    x_place = lax.axis_index("x").astype(jnp.int32).reshape(1)
     (packed,) = call(
         pack_kernel,
         "pack",
@@ -301,6 +309,8 @@
         grant=56,
     )
     sent = exchange(packed, SEQ)
+    piece = sent[:, :, BASE:].reshape(1, ROWS, PIECE)
+    mine = exchange(jnp.broadcast_to(piece, (4, ROWS, PIECE)), "x")
     share, columns = call(
         forward_kernel,
         "forward",
@@ -321,20 +331,13 @@
         [IN_VMEM] * 3,
         [((4, 32, HALF_WIDTH), BF16)],
     )
-    piece, partial = lax.optimization_barrier((sent[:, :, BASE:].reshape(ROWS, PIECE), partial))
+    mine, partial = lax.optimization_barrier((mine, partial))
     terms = exchange(partial, "x")
-    turned = [turn(piece, "x", step) for step in range(1, 4)]
-    (summed,) = call(
-        merge_kernel, "merge", (terms,), [IN_VMEM], [((16, 2, HALF_WIDTH), BF16)]
-    )
-    collected = exchange(summed, ("yh", "z"))
-    piece, *turned = lax.optimization_barrier((piece, *turned, summed))[:4]
-    mine = jnp.stack([piece, *turned])
     (results,) = call(
         backward_kernel,
         "backward",
-        (core, x_place, sent, mine, swap(mine)),
-        [IN_SMEM] * 2 + [IN_VMEM] * 3,
+        (core, sent, mine, swap(mine)),
+        [IN_SMEM] + [IN_VMEM] * 3,
         [((64, 2, BASE), BF16)],
         [
             pltpu.VMEM((ROWS, COLS), BF16),
@@ -347,6 +350,11 @@
         ],
         micros=4,
     )
+    results, terms = lax.optimization_barrier((results, terms))
+    (summed,) = call(
+        merge_kernel, "merge", (terms,), [IN_VMEM], [((16, 2, HALF_WIDTH), BF16)]
+    )
+    collected = exchange(summed, ("yh", "z"))
     results, collected = lax.optimization_barrier((results, collected))
     (owned,) = call(owned_kernel, "owned", (collected,), [IN_VMEM], [((2, HALF_WIDTH), F32)])
     turned = [turn(owned, "yl", step) for step in range(1, 4)]
@@ -361,10 +369,17 @@
         [IN_SMEM] + [IN_VMEM] * 2,
         [((12, WIDTH), F32)],
     )
-    frames = back.reshape(ROWS, BASE)
-    grads = jnp.stack([frames[:, part * WIDTH : (part + 1) * WIDTH] for part in range(3)])
+    projected, grads = call(
+        unpack_kernel,
+        "unpack",
+        (back,),
+        [IN_VMEM],
+        [((ROWS, OUT), BF16), ((3, ROWS, WIDTH), BF16)],
+        [pltpu.VMEM((ROWS, BASE), BF16), pltpu.SemaphoreType.DMA((4,))],
+        out_spec=IN_HBM,
+    )
     return (
-        frames[:, 3 * WIDTH :].reshape(1, 1, ROWS, OUT),
+        projected.reshape(1, 1, ROWS, OUT),
         grads.reshape(3, 1, 1, ROWS, WIDTH),
         total,
     )

time: 161 us -> 160 us (level)
  blocking collectives: 59 us -> 76 us
  waiting for transfers between devices: 46.3 us -> 36.3 us
  starting transfers between devices: 39.1 us -> 31.2 us
    all_to_all x1 -> x2, blocking collectives: 59 us -> 76 us  [exchange(): return lax.all_to_all(value, axes, 0, 0, tiled=True)]
    ppermute x6 -> x3, starting transfers between devices: 18.4 us -> 7.86 us  [turn(): lax.ppermute(value, axis, [(place, (place + step) % 4) for place in range...]
    ppermute x6 -> x3, waiting for transfers between devices: 23.2 us -> 15.2 us  [turn(): lax.ppermute(value, axis, [(place, (place + step) % 4) for place in range...]
    all_to_all x3, starting transfers between devices: 14.9 us -> 17.6 us  [exchange(): return lax.all_to_all(value, axes, 0, 0, tiled=True)]
    all_to_all x3, waiting for transfers between devices: 20.5 us -> 18.2 us  [exchange(): return lax.all_to_all(value, axes, 0, 0, tiled=True)]
    pallas_call x8 -> x9, Pallas kernels: 12.4 us -> 13.8 us  [call(): pl.pallas_call(kernel, out_shape=[jax.ShapeDtypeStruct(shape, dtype) for...]
  transfers between devices with their start and end apart: 12 -> 9, of which waited for: 8 -> 6; matrix products, arithmetic and copies ran while one was open for 0% -> 0% of each run, Pallas kernels for 4% -> 6%
where the time goes in v9:
time: 160 us; the launch traced here: 159 us
  blocking collectives  76 us (48%)
  waiting for transfers between devices  36.3 us (23%)
  starting transfers between devices  31.2 us (20%)
  Pallas kernels  13.8 us (9%)
    all_to_all x2, blocking collectives, exchange(): return lax.all_to_all(value, axes, 0, 0, tiled=True)  76 us
    all_to_all x3, waiting for transfers between devices, exchange(): return lax.all_to_all(value, axes, 0, 0, tiled=True)  18.2 us
    all_to_all x3, starting transfers between devices, exchange(): return lax.all_to_all(value, axes, 0, 0, tiled=True)  17.6 us
    ppermute x3, waiting for transfers between devices, turn(): lax.ppermute(value, axis, [(place, (place + step) % 4) for place in range...  15.2 us
    pallas_call x9, Pallas kernels, call(): pl.pallas_call(kernel, out_shape=[jax.ShapeDtypeStruct(shape, dtype) for...  13.8 us
    ppermute x3, starting transfers between devices, turn(): lax.ppermute(value, axis, [(place, (place + step) % 4) for place in range...  7.86 us
    ppermute x3, starting transfers between devices, swap(): return lax.ppermute(value, 'c', [(0, 1), (1, 0)])  5.76 us
  transfers between devices with their start and end apart: 9, of which 6 were waited for; matrix products, arithmetic and copies ran while one was open for 0% of the time, Pallas kernels for 6%

profile of v9, /device:TPU:14, one launch (start us, length us, event | category | flops | bytes accessed | tf_op | source)
XLA Modules:
  0.0 159.3 jit_solution(15395402232097613776)
XLA Ops:
  0.6 2.9 %pack.1 = bf16[64,2,5120]{2,1,0:T(2,128)(2,1)} custom-call(s32[1]{0:T(128)} %bitcast.core_ref, bf16[3,128,1152]{2,1,0:T(8,128)(2,1)} %bitcast.7, bf16[128,768]{1,0:T(8,128)(2,1)} %bitcast.8, bf16[12,1152]{1,0:T(8,128)(2,1)} %weight_hbm.1), custom_call_target="tpu_custom_call" | custom-call | flops 1000000000 | bytes 3000000 | tf_op jit(solution)/shard_map/pack/pallas_call | solution.py:269
  3.5 59.0 %all_to_all.25.sent_ref = bf16[64,2,5120]{2,1,0:T(2,128)(2,1)S(1)} all-to-all(bf16[64,2,5120]{2,1,0:T(2,128)(2,1)} %pack.1), channel_id=1, replica_groups=mesh['yl'=4,'c'=2,'yh'=2,'x'=4,'z'=8] {'yh','x','z'}, dimensions={0} | all-to-all | bytes 2621440 | tf_op jit(solution)/shard_map/all_to_all | solution.py:284
  62.5 0.2 slice.4
  62.7 0.1 broadcast_in_dim.7
  62.8 1.0 broadcast_in_dim.8
  63.8 4.5 %all-to-all-start.1 = ((bf16[4,128,896]{2,1,0:T(8,128)(2,1)}), bf16[4,128,896]{2,1,0:T(8,128)(2,1)S(1)}, u32[]{:S(2)}, u32[]{:S(2)}) async-start(bf16[4,128,896]{2,1,0:T(8,128)(2,1)} %broadcast_in_dim.8), calls=%async_computation.1 | async-start | bytes 1835008 | tf_op jit(solution)/shard_map/all_to_all | solution.py:284
  68.3 1.3 forward.1
  69.6 1.9 %collective-permute-start = (bf16[128,1536]{1,0:T(8,128)(2,1)S(1)}, bf16[128,1536]{1,0:T(8,128)(2,1)S(1)}, u32[]{:S(2)}, u32[]{:S(2)}) collective-permute-start(bf16[128,1536]{1,0:T(8,128)(2,1)S(1)} %get-tuple-element.13.share_ref), channel_id=1, source_target_pairs={{0,64},{64,0},{1,65},{65,1},{2,66},{66,2},{3,67},{67,3},{4,68},{68... | collective-permute-start | bytes 1179656 | tf_op jit(solution)/shard_map/ppermute | solution.py:288
  71.5 1.7 %collective-permute-done.received_ref = bf16[128,1536]{1,0:T(8,128)(2,1)S(1)} collective-permute-done((bf16[128,1536]{1,0:T(8,128)(2,1)S(1)}, bf16[128,1536]{1,0:T(8,128)(2,1)S(1)}, u32[]{:S(2)}, u32[]{:S(2)}) %collective-permute-start) | collective-permute-done | bytes 393248 | tf_op jit(solution)/shard_map/ppermute | solution.py:288
  73.2 1.4 weight_grad.1
  74.6 4.7 %all-to-all-done.1.mine_ref = bf16[4,128,896]{2,1,0:T(8,128)(2,1)S(1)} async-done(((bf16[4,128,896]{2,1,0:T(8,128)(2,1)}), bf16[4,128,896]{2,1,0:T(8,128)(2,1)S(1)}, u32[]{:S(2)}, u32[]{:S(2)}) %all-to-all-start.1) | async-done | bytes 917536 | tf_op jit(solution)/shard_map/all_to_all | solution.py:284
  79.3 1.9 %collective-permute-start.1 = (bf16[4,128,896]{2,1,0:T(8,128)(2,1)S(1)}, bf16[4,128,896]{2,1,0:T(8,128)(2,1)}, u32[]{:S(2)}, u32[]{:S(2)}) collective-permute-start(bf16[4,128,896]{2,1,0:T(8,128)(2,1)S(1)} %all-to-all-done.1.mine_ref), channel_id=1, source_target_pairs={{0,64},{64,0},{1,65},{65,1},{2,66},{66,2},{3,67},{67,3},{4,68},{68... | collective-permute-start | bytes 2752520 | tf_op jit(solution)/shard_map/ppermute | solution.py:288
  81.2 5.6 %all-to-all-start.2 = ((bf16[4,32,3456]{2,1,0:T(8,128)(2,1)}), bf16[4,32,3456]{2,1,0:T(8,128)(2,1)S(1)}, u32[]{:S(2)}, u32[]{:S(2)}) async-start(bf16[4,32,3456]{2,1,0:T(8,128)(2,1)} %weight_grad.1), calls=%async_computation.2 | async-start | bytes 1769472 | tf_op jit(solution)/shard_map/all_to_all | solution.py:284
  86.7 0.0 collective-permute-done.1.theirs_ref
  86.7 6.2 %backward.1 = bf16[64,2,4224]{2,1,0:T(2,128)(2,1)} custom-call(s32[1]{0:T(128)} %bitcast.core_ref, bf16[64,2,5120]{2,1,0:T(2,128)(2,1)S(1)} %all_to_all.25.sent_ref, bf16[4,128,896]{2,1,0:T(8,128)(2,1)S(1)} %all-to-all-done.1.mine_ref, bf16[4,128,896]{2,1,0:T(8,128)(2,1)} %collective-permute-done.1.theirs_ref), custom_call_target="tpu_custom_call" | custom-call | flops 4000000000 | bytes 12000000 | tf_op jit(solution)/shard_map/backward/pallas_call | solution.py:269
  93.0 6.0 %all-to-all-done.2.terms_ref = bf16[4,32,3456]{2,1,0:T(8,128)(2,1)S(1)} async-done(((bf16[4,32,3456]{2,1,0:T(8,128)(2,1)}), bf16[4,32,3456]{2,1,0:T(8,128)(2,1)S(1)}, u32[]{:S(2)}, u32[]{:S(2)}) %all-to-all-start.2) | async-done | bytes 884768 | tf_op jit(solution)/shard_map/all_to_all | solution.py:284
  99.0 0.1 merge.1
  99.1 16.9 %all_to_all.26.terms_ref = bf16[16,2,3456]{2,1,0:T(2,128)(2,1)S(1)} all-to-all(bf16[16,2,3456]{2,1,0:T(2,128)(2,1)S(1)} %merge.1), channel_id=1, replica_groups=mesh['yl'=4,'c'=2,'yh'=2,'x'=4,'z'=8] {'yh','z'}, dimensions={0} | all-to-all | bytes 442368 | tf_op jit(solution)/shard_map/all_to_all | solution.py:284
  116.0 7.6 %all-to-all-start.4 = ((bf16[64,2,4224]{2,1,0:T(2,128)(2,1)}), bf16[64,2,4224]{2,1,0:T(2,128)(2,1)S(1)}, u32[]{:S(2)}, u32[]{:S(2)}) async-start(bf16[64,2,4224]{2,1,0:T(2,128)(2,1)} %backward.1), calls=%async_computation.4 | async-start | bytes 2162688 | tf_op jit(solution)/shard_map/all_to_all | solution.py:284
  123.6 0.2 owned.1.refs_0_
  123.8 1.9 %collective-permute-start.4 = (f32[2,3456]{1,0:T(2,128)S(1)}, f32[2,3456]{1,0:T(2,128)S(1)}, u32[]{:S(2)}, u32[]{:S(2)}) collective-permute-start(f32[2,3456]{1,0:T(2,128)S(1)} %owned.1.refs_0_), channel_id=1, source_target_pairs={{0,384},{128,0},{256,128},{384,256},{1,385},{129,1},{257,129},{385... | collective-permute-start | bytes 82952 | tf_op jit(solution)/shard_map/ppermute | solution.py:292
  125.7 2.9 %collective-permute-start.3 = (f32[2,3456]{1,0:T(2,128)S(1)}, f32[2,3456]{1,0:T(2,128)S(1)}, u32[]{:S(2)}, u32[]{:S(2)}) collective-permute-start(f32[2,3456]{1,0:T(2,128)S(1)} %owned.1.refs_0_), channel_id=1, source_target_pairs={{0,256},{128,384},{256,0},{384,128},{1,257},{129,385},{257,1},{385... | collective-permute-start | bytes 82952 | tf_op jit(solution)/shard_map/ppermute | solution.py:292
  128.6 3.0 %collective-permute-start.2 = (f32[2,3456]{1,0:T(2,128)S(1)}, f32[2,3456]{1,0:T(2,128)S(1)}, u32[]{:S(2)}, u32[]{:S(2)}) collective-permute-start(f32[2,3456]{1,0:T(2,128)S(1)} %owned.1.refs_0_), channel_id=1, source_target_pairs={{0,128},{128,256},{256,384},{384,0},{1,129},{129,257},{257,385},{3... | collective-permute-start | bytes 82952 | tf_op jit(solution)/shard_map/ppermute | solution.py:292
  131.6 15.2 %collective-permute-done.4.refs_3_ = f32[2,3456]{1,0:T(2,128)S(1)} collective-permute-done((f32[2,3456]{1,0:T(2,128)S(1)}, f32[2,3456]{1,0:T(2,128)S(1)}, u32[]{:S(2)}, u32[]{:S(2)}) %collective-permute-start.4) | collective-permute-done | bytes 27680 | tf_op jit(solution)/shard_map/ppermute | solution.py:292
  146.9 0.0 collective-permute-done.3.refs_2_
  146.9 0.0 collective-permute-done.2.refs_1_
  146.9 1.9 %collective-permute-start.5 = (f32[2,3456]{1,0:T(2,128)S(1)}, f32[2,3456]{1,0:T(2,128)S(1)}, u32[]{:S(2)}, u32[]{:S(2)}) collective-permute-start(f32[2,3456]{1,0:T(2,128)S(1)} %group.1.mine_ref), channel_id=1, source_target_pairs={{0,64},{64,0},{1,65},{65,1},{2,66},{66,2},{3,67},{67,3},{4,68},{68... | collective-permute-start | bytes 82952 | tf_op jit(solution)/shard_map/ppermute | solution.py:288
  148.8 1.2 collective-permute-done.5.theirs_ref
  150.0 0.7 total.1
  150.6 7.6 %all-to-all-done.4.back_ref = bf16[64,2,4224]{2,1,0:T(2,128)(2,1)S(1)} async-done(((bf16[64,2,4224]{2,1,0:T(2,128)(2,1)}), bf16[64,2,4224]{2,1,0:T(2,128)(2,1)S(1)}, u32[]{:S(2)}, u32[]{:S(2)}) %all-to-all-start.4) | async-done | bytes 1081376 | tf_op jit(solution)/shard_map/all_to_all | solution.py:284
  158.2 1.1 unpack.1
  (1 shorter events, 0.0 us)
Async XLA Ops:
  63.8 15.5 %all-to-all-start.1 = ((bf16[4,128,896]{2,1,0:T(8,128)(2,1)}), bf16[4,128,896]{2,1,0:T(8,128)(2,1)S(1)}, u32[]{:S(2)}, u32[]{:S(2)}) async-start(bf16[4,128,896]{2,1,0:T(8,128)(2,1)} %broadcast_in_dim.8), calls=%async_computation.1 | async-start | bytes 1835008 | tf_op jit(solution)/shard_map/all_to_all | solution.py:284
  69.6 3.6 %collective-permute-start = (bf16[128,1536]{1,0:T(8,128)(2,1)S(1)}, bf16[128,1536]{1,0:T(8,128)(2,1)S(1)}, u32[]{:S(2)}, u32[]{:S(2)}) collective-permute-start(bf16[128,1536]{1,0:T(8,128)(2,1)S(1)} %get-tuple-element.13.share_ref), channel_id=1, source_target_pairs={{0,64},{64,0},{1,65},{65,1},{2,66},{66,2},{3,67},{67,3},{4,68},{68... | collective-permute-start | bytes 1179656 | tf_op jit(solution)/shard_map/ppermute | solution.py:288
  79.3 7.5 %collective-permute-start.1 = (bf16[4,128,896]{2,1,0:T(8,128)(2,1)S(1)}, bf16[4,128,896]{2,1,0:T(8,128)(2,1)}, u32[]{:S(2)}, u32[]{:S(2)}) collective-permute-start(bf16[4,128,896]{2,1,0:T(8,128)(2,1)S(1)} %all-to-all-done.1.mine_ref), channel_id=1, source_target_pairs={{0,64},{64,0},{1,65},{65,1},{2,66},{66,2},{3,67},{67,3},{4,68},{68... | collective-permute-start | bytes 2752520 | tf_op jit(solution)/shard_map/ppermute | solution.py:288
  81.2 17.8 %all-to-all-start.2 = ((bf16[4,32,3456]{2,1,0:T(8,128)(2,1)}), bf16[4,32,3456]{2,1,0:T(8,128)(2,1)S(1)}, u32[]{:S(2)}, u32[]{:S(2)}) async-start(bf16[4,32,3456]{2,1,0:T(8,128)(2,1)} %weight_grad.1), calls=%async_computation.2 | async-start | bytes 1769472 | tf_op jit(solution)/shard_map/all_to_all | solution.py:284
  116.0 42.2 %all-to-all-start.4 = ((bf16[64,2,4224]{2,1,0:T(2,128)(2,1)}), bf16[64,2,4224]{2,1,0:T(2,128)(2,1)S(1)}, u32[]{:S(2)}, u32[]{:S(2)}) async-start(bf16[64,2,4224]{2,1,0:T(2,128)(2,1)} %backward.1), calls=%async_computation.4 | async-start | bytes 2162688 | tf_op jit(solution)/shard_map/all_to_all | solution.py:284
  123.8 23.1 %collective-permute-start.4 = (f32[2,3456]{1,0:T(2,128)S(1)}, f32[2,3456]{1,0:T(2,128)S(1)}, u32[]{:S(2)}, u32[]{:S(2)}) collective-permute-start(f32[2,3456]{1,0:T(2,128)S(1)} %owned.1.refs_0_), channel_id=1, source_target_pairs={{0,384},{128,0},{256,128},{384,256},{1,385},{129,1},{257,129},{385... | collective-permute-start | bytes 82952 | tf_op jit(solution)/shard_map/ppermute | solution.py:292
  125.7 21.2 %collective-permute-start.3 = (f32[2,3456]{1,0:T(2,128)S(1)}, f32[2,3456]{1,0:T(2,128)S(1)}, u32[]{:S(2)}, u32[]{:S(2)}) collective-permute-start(f32[2,3456]{1,0:T(2,128)S(1)} %owned.1.refs_0_), channel_id=1, source_target_pairs={{0,256},{128,384},{256,0},{384,128},{1,257},{129,385},{257,1},{385... | collective-permute-start | bytes 82952 | tf_op jit(solution)/shard_map/ppermute | solution.py:292
  128.6 18.2 %collective-permute-start.2 = (f32[2,3456]{1,0:T(2,128)S(1)}, f32[2,3456]{1,0:T(2,128)S(1)}, u32[]{:S(2)}, u32[]{:S(2)}) collective-permute-start(f32[2,3456]{1,0:T(2,128)S(1)} %owned.1.refs_0_), channel_id=1, source_target_pairs={{0,128},{128,256},{256,384},{384,0},{1,129},{129,257},{257,385},{3... | collective-permute-start | bytes 82952 | tf_op jit(solution)/shard_map/ppermute | solution.py:292
  146.9 3.1 %collective-permute-start.5 = (f32[2,3456]{1,0:T(2,128)S(1)}, f32[2,3456]{1,0:T(2,128)S(1)}, u32[]{:S(2)}, u32[]{:S(2)}) collective-permute-start(f32[2,3456]{1,0:T(2,128)S(1)} %group.1.mine_ref), channel_id=1, source_target_pairs={{0,64},{64,0},{1,65},{65,1},{2,66},{66,2},{3,67},{67,3},{4,68},{68... | collective-permute-start | bytes 82952 | tf_op jit(solution)/shard_map/ppermute | solution.py:288

commit v10 on v7

--- a/solution.py
+++ b/solution.py
@@ -21,6 +21,7 @@
 PIECE_TILES = PIECE // LANES
 COLS = BASE + PIECE
 HALF_WIDTH = 3 * WIDTH
+SHARE = WIDTH + HALF + PIECE
 INV_ROOT = 1.0 / math.sqrt(HEAD_DIM)
 GRAD_SCALE = 1.0 / math.sqrt(512 * ROWS)
 BF16 = jnp.bfloat16
@@ -152,11 +153,16 @@
     own = pl.multiple_of(core_ref[0] * HALF, HALF)
     other = pl.multiple_of((1 - core_ref[0]) * HALF, HALF)
     columns_ref[...] = channels_ref[:, pl.ds(own, HALF)]
-    share_ref[:, WIDTH:] = channels_ref[:, pl.ds(other, HALF)]
-
-
-def weight_grad_kernel(share_ref, received_ref, columns_ref, out_ref):
-    columns = jnp.concatenate([columns_ref[...], received_ref[:, WIDTH:]], axis=0)
+    share_ref[:, WIDTH : WIDTH + HALF] = channels_ref[:, pl.ds(other, HALF)]
+    share_ref[:, WIDTH + HALF :] = rows_ref[:, BASE:]
+
+
+def weight_grad_kernel(core_ref, share_ref, received_ref, columns_ref, out_ref, pieces_ref):
+    own = pl.multiple_of(core_ref[0] * PIECE, PIECE)
+    other = pl.multiple_of((1 - core_ref[0]) * PIECE, PIECE)
+    pieces_ref[:, pl.ds(own, PIECE)] = share_ref[:, WIDTH + HALF :]
+    pieces_ref[:, pl.ds(other, PIECE)] = received_ref[:, WIDTH + HALF :]
+    columns = jnp.concatenate([columns_ref[...], received_ref[:, WIDTH : WIDTH + HALF]], axis=0)
     features = jnp.concatenate([share_ref[:, :WIDTH], received_ref[:, :WIDTH]], axis=0)
     partial = dot(columns, features, 0, 0).astype(BF16)
     for pair in range(3):
@@ -165,11 +171,12 @@
         ].reshape(64, 2, WIDTH)
 
 
-def backward_kernel(
-    sent_ref, pieces_ref,
-    out_ref, rows_ref, weights_ref, channels_ref, attended_ref, matrix_ref, upstream_ref,
-    grad_scores_ref,
-):
+def backward_kernel(x_ref, sent_ref, *refs):
+    pieces_refs, refs = refs[:4], refs[4:]
+    (
+        out_ref, rows_ref, weights_ref, channels_ref, attended_ref, matrix_ref, upstream_ref,
+        grad_scores_ref,
+    ) = refs
     rows_ref[...] = sent_ref[...].reshape(ROWS, COLS)
     channels_ref[...] = ordered_channels(rows_ref)
 
@@ -177,12 +184,17 @@
         attended_ref[:, lanes(tile)] = value
 
     attend(rows_ref, weights_ref, put_attended)
-    for core in range(2):
-        for piece, place, pair, tile in half_tiles():
-            start = core * HALF + pair * ROWS
-            matrix_ref[start : start + ROWS, lanes(tile)] = pieces_ref[
-                4 * core + piece, :, lanes(place)
-            ]
+    for here in range(4):
+
+        @pl.when(x_ref[0] == here)
+        def _():
+            for core in range(2):
+                for piece, place, pair, tile in half_tiles():
+                    start = core * HALF + pair * ROWS
+                    matrix_ref[start : start + ROWS, lanes(tile)] = pieces_refs[
+                        (here - piece) & 3
+                    ][:, lanes(place, core * PIECE)]
+
     upstream_ref[...] = dot(channels_ref[...], matrix_ref[...], 1, 0).astype(BF16)
     products = [
         head_products(upstream_ref, 0, rows_ref, 2 * WIDTH, index) for index in range(HEADS)
@@ -218,6 +230,21 @@
     out_ref[...] = dot(chosen, rows, 1, 0)[:2]
 
 
+def unpack_kernel(back_ref, projected_hbm, grads_hbm, rows_ref, sems):
+    rows_ref[...] = back_ref[...].reshape(ROWS, BASE)
+    parts = [(rows_ref.at[:, 3 * WIDTH :], projected_hbm)]
+    for part in range(3):
+        parts.append((rows_ref.at[:, part * WIDTH : (part + 1) * WIDTH], grads_hbm.at[part]))
+    copies = [
+        pltpu.make_async_copy(source, target, sems.at[place])
+        for place, (source, target) in enumerate(parts)
+    ]
+    for copy in copies:
+        copy.start()
+    for copy in copies:
+        copy.wait()
+
+
 def group_kernel(*refs):
     *terms, out_ref = refs
     total = terms[0][...]
@@ -239,14 +266,13 @@
 IN_HBM = pl.BlockSpec(memory_space=pltpu.HBM)
 
 
-def call(kernel, name, operands, specs, outs, scratch=(), aliases=None, grant=12, micros=1):
+def call(kernel, name, operands, specs, outs, scratch=(), grant=12, micros=1, out_spec=IN_VMEM):
     return pl.pallas_call(
         kernel,
         out_shape=[jax.ShapeDtypeStruct(shape, dtype) for shape, dtype in outs],
         in_specs=specs,
-        out_specs=[IN_VMEM] * len(outs),
+        out_specs=[out_spec] * len(outs),
         scratch_shapes=list(scratch),
-        input_output_aliases=aliases or {},
         compiler_params=pltpu.CompilerParams(vmem_limit_bytes=grant << 20),
         cost_estimate=pl.CostEstimate(
             flops=micros * 10**9, bytes_accessed=micros * 3 * 10**6, transcendentals=0
@@ -269,6 +295,7 @@
 
 def on_device(query_key_value, out_weight, cotangent):
     core = lax.axis_index("c").astype(jnp.int32).reshape(1)
+    x_place = lax.axis_index("x").astype(jnp.int32).reshape(1)
     (packed,) = call(
         pack_kernel,
         "pack",
@@ -284,13 +311,12 @@
         grant=56,
     )
     sent = exchange(packed, SEQ)
-    pieces = lax.all_gather(sent[:, :, BASE:].reshape(ROWS, PIECE), ("c", "x"))
     share, columns = call(
         forward_kernel,
         "forward",
         (core, sent),
         [IN_SMEM, IN_VMEM],
-        [((ROWS, WIDTH + HALF), BF16), ((ROWS, HALF), BF16)],
+        [((ROWS, SHARE), BF16), ((ROWS, HALF), BF16)],
         [
             pltpu.VMEM((ROWS, COLS), BF16),
             pltpu.VMEM((HEADS, ROWS, ROWS), F32),
@@ -298,19 +324,20 @@
         ],
         micros=3,
     )
-    (partial,) = call(
+    partial, pieces = call(
         weight_grad_kernel,
         "weight_grad",
-        (share, swap(share), columns),
-        [IN_VMEM] * 3,
-        [((64, 2, HALF_WIDTH), BF16)],
+        (core, share, swap(share), columns),
+        [IN_SMEM] + [IN_VMEM] * 3,
+        [((64, 2, HALF_WIDTH), BF16), ((ROWS, 2 * PIECE), BF16)],
     )
     collected = exchange(partial, SEQ)
+    turned = [turn(pieces, "x", step) for step in range(1, 4)]
     (results,) = call(
         backward_kernel,
         "backward",
-        (sent, pieces),
-        [IN_VMEM] * 2,
+        (x_place, sent, pieces, *turned),
+        [IN_SMEM] + [IN_VMEM] * 5,
         [((64, 2, BASE), BF16)],
         [
             pltpu.VMEM((ROWS, COLS), BF16),
@@ -337,10 +364,17 @@
         [IN_SMEM] + [IN_VMEM] * 2,
         [((12, WIDTH), F32)],
     )
-    frames = back.reshape(ROWS, BASE)
-    grads = jnp.stack([frames[:, part * WIDTH : (part + 1) * WIDTH] for part in range(3)])
+    projected, grads = call(
+        unpack_kernel,
+        "unpack",
+        (back,),
+        [IN_VMEM],
+        [((ROWS, OUT), BF16), ((3, ROWS, WIDTH), BF16)],
+        [pltpu.VMEM((ROWS, BASE), BF16), pltpu.SemaphoreType.DMA((4,))],
+        out_spec=IN_HBM,
+    )
     return (
-        frames[:, 3 * WIDTH :].reshape(1, 1, ROWS, OUT),
+        projected.reshape(1, 1, ROWS, OUT),
         grads.reshape(3, 1, 1, ROWS, WIDTH),
         total,
     )

time: 163 us -> 168 us (1.031)
  starting transfers between devices: 23.7 us -> 42.3 us
  between operations: 14.1 us -> 0.75 us
  local copies, waits for them, and re-layouts: 3.66 us -> 0 us
  Pallas kernels: 11.3 us -> 13.9 us
    ppermute x3 -> x6, waiting for transfers between devices: 16.3 us -> 40.2 us  [turn(): lax.ppermute(value, axis, [(place, (place + step) % 4) for place in range...]
    all_gather x1 -> x0, waiting for transfers between devices: 11.5 us -> none  [on_device(): pieces = lax.all_gather(sent[:, :, BASE:].reshape(ROWS, PIECE), ('c', 'x'))]
    all_to_all x2, waiting for transfers between devices: 18.8 us -> 7.66 us  [exchange(): return lax.all_to_all(value, axes, 0, 0, tiled=True)]
    ppermute x3 -> x6, starting transfers between devices: 9.4 us -> 19 us  [turn(): lax.ppermute(value, axis, [(place, (place + step) % 4) for place in range...]
    all_to_all x2, starting transfers between devices: 10.5 us -> 19.4 us  [exchange(): return lax.all_to_all(value, axes, 0, 0, tiled=True)]
    pallas_call x7 -> x8, Pallas kernels: 11.3 us -> 13.9 us  [call(): pl.pallas_call(kernel, out_shape=[jax.ShapeDtypeStruct(shape, dtype) for...]
  transfers between devices with their start and end apart: 8 -> 10, of which waited for: 8 -> 7; matrix products, arithmetic and copies ran while one was open for 0% -> 0% of each run, Pallas kernels for 5% -> 4%
where the time goes in v10:
time: 168 us; the launch traced here: 167 us
  blocking collectives  59 us (35%)
  waiting for transfers between devices  51 us (30%)
  starting transfers between devices  42.3 us (25%)
  Pallas kernels  13.9 us (8%)
    all_to_all x1, blocking collectives, exchange(): return lax.all_to_all(value, axes, 0, 0, tiled=True)  59 us
    ppermute x6, waiting for transfers between devices, turn(): lax.ppermute(value, axis, [(place, (place + step) % 4) for place in range...  40.2 us
    all_to_all x2, starting transfers between devices, exchange(): return lax.all_to_all(value, axes, 0, 0, tiled=True)  19.4 us
    ppermute x6, starting transfers between devices, turn(): lax.ppermute(value, axis, [(place, (place + step) % 4) for place in range...  19 us
    pallas_call x8, Pallas kernels, call(): pl.pallas_call(kernel, out_shape=[jax.ShapeDtypeStruct(shape, dtype) for...  13.9 us
    all_to_all x2, waiting for transfers between devices, exchange(): return lax.all_to_all(value, axes, 0, 0, tiled=True)  7.66 us
    ppermute x2, starting transfers between devices, swap(): return lax.ppermute(value, 'c', [(0, 1), (1, 0)])  3.84 us
  transfers between devices with their start and end apart: 10, of which 7 were waited for; matrix products, arithmetic and copies ran while one was open for 0% of the time, Pallas kernels for 4%

profile of v10, /device:TPU:14, one launch (start us, length us, event | category | flops | bytes accessed | tf_op | source)
XLA Modules:
  0.0 167.0 jit_solution(8871061298649790255)
XLA Ops:
  0.6 2.8 %pack.1 = bf16[64,2,5120]{2,1,0:T(2,128)(2,1)} custom-call(s32[1]{0:T(128)} %bitcast.1.core_ref, bf16[3,128,1152]{2,1,0:T(8,128)(2,1)} %bitcast.8, bf16[128,768]{1,0:T(8,128)(2,1)} %bitcast.9, bf16[12,1152]{1,0:T(8,128)(2,1)} %weight_hbm.1), custom_call_target="tpu_custom_call" | custom-call | flops 1000000000 | bytes 3000000 | tf_op jit(solution)/shard_map/pack/pallas_call | solution.py:270
  3.5 59.0 %all_to_all.15.sent_ref = bf16[64,2,5120]{2,1,0:T(2,128)(2,1)S(1)} all-to-all(bf16[64,2,5120]{2,1,0:T(2,128)(2,1)} %pack.1), channel_id=1, replica_groups=mesh['yl'=4,'c'=2,'yh'=2,'x'=4,'z'=8] {'yh','x','z'}, dimensions={0} | all-to-all | bytes 2621440 | tf_op jit(solution)/shard_map/all_to_all | solution.py:285
  62.5 1.3 forward.1
  63.8 1.9 %collective-permute-start = (bf16[128,2432]{1,0:T(8,128)(2,1)S(1)}, bf16[128,2432]{1,0:T(8,128)(2,1)S(1)}, u32[]{:S(2)}, u32[]{:S(2)}) collective-permute-start(bf16[128,2432]{1,0:T(8,128)(2,1)S(1)} %get-tuple-element.11.share_ref), channel_id=1, source_target_pairs={{0,64},{64,0},{1,65},{65,1},{2,66},{66,2},{3,67},{67,3},{4,68},{68... | collective-permute-start | bytes 1867784 | tf_op jit(solution)/shard_map/ppermute | solution.py:289
  65.8 2.0 %collective-permute-done.received_ref = bf16[128,2432]{1,0:T(8,128)(2,1)S(1)} collective-permute-done((bf16[128,2432]{1,0:T(8,128)(2,1)S(1)}, bf16[128,2432]{1,0:T(8,128)(2,1)S(1)}, u32[]{:S(2)}, u32[]{:S(2)}) %collective-permute-start) | collective-permute-done | bytes 622624 | tf_op jit(solution)/shard_map/ppermute | solution.py:289
  67.8 1.4 weight_grad.1
  69.2 5.3 %all-to-all-start.1 = ((bf16[64,2,3456]{2,1,0:T(2,128)(2,1)}), bf16[64,2,3456]{2,1,0:T(2,128)(2,1)S(1)}, u32[]{:S(2)}, u32[]{:S(2)}) async-start(bf16[64,2,3456]{2,1,0:T(2,128)(2,1)} %get-tuple-element.14), calls=%async_computation.1 | async-start | bytes 1769472 | tf_op jit(solution)/shard_map/all_to_all | solution.py:285
  74.6 2.7 %collective-permute-start.3 = (bf16[128,1792]{1,0:T(8,128)(2,1)S(1)}, bf16[128,1792]{1,0:T(8,128)(2,1)S(1)}, u32[]{:S(2)}, u32[]{:S(2)}) collective-permute-start(bf16[128,1792]{1,0:T(8,128)(2,1)S(1)} %get-tuple-element.13.refs_0_), channel_id=1, source_target_pairs={{0,24},{8,0},{16,8},{24,16},{1,25},{9,1},{17,9},{25,17},{2,26},{10... | collective-permute-start | bytes 1376264 | tf_op jit(solution)/shard_map/ppermute | solution.py:293
  77.3 3.0 %collective-permute-start.2 = (bf16[128,1792]{1,0:T(8,128)(2,1)S(1)}, bf16[128,1792]{1,0:T(8,128)(2,1)}, u32[]{:S(2)}, u32[]{:S(2)}) collective-permute-start(bf16[128,1792]{1,0:T(8,128)(2,1)S(1)} %get-tuple-element.13.refs_0_), channel_id=1, source_target_pairs={{0,16},{8,24},{16,0},{24,8},{1,17},{9,25},{17,1},{25,9},{2,18},{10... | collective-permute-start | bytes 1376264 | tf_op jit(solution)/shard_map/ppermute | solution.py:293
  80.3 4.1 %collective-permute-start.1 = (bf16[128,1792]{1,0:T(8,128)(2,1)S(1)}, bf16[128,1792]{1,0:T(8,128)(2,1)}, u32[]{:S(2)}, u32[]{:S(2)}) collective-permute-start(bf16[128,1792]{1,0:T(8,128)(2,1)S(1)} %get-tuple-element.13.refs_0_), channel_id=1, source_target_pairs={{0,8},{8,16},{16,24},{24,0},{1,9},{9,17},{17,25},{25,1},{2,10},{10... | collective-permute-start | bytes 1376264 | tf_op jit(solution)/shard_map/ppermute | solution.py:293
  84.4 10.4 %collective-permute-done.3.refs_3_ = bf16[128,1792]{1,0:T(8,128)(2,1)S(1)} collective-permute-done((bf16[128,1792]{1,0:T(8,128)(2,1)S(1)}, bf16[128,1792]{1,0:T(8,128)(2,1)S(1)}, u32[]{:S(2)}, u32[]{:S(2)}) %collective-permute-start.3) | collective-permute-done | bytes 458784 | tf_op jit(solution)/shard_map/ppermute | solution.py:293
  94.8 14.0 %collective-permute-done.2.refs_2_ = bf16[128,1792]{1,0:T(8,128)(2,1)} collective-permute-done((bf16[128,1792]{1,0:T(8,128)(2,1)S(1)}, bf16[128,1792]{1,0:T(8,128)(2,1)}, u32[]{:S(2)}, u32[]{:S(2)}) %collective-permute-start.2) | collective-permute-done | bytes 458784 | tf_op jit(solution)/shard_map/ppermute | solution.py:293
  108.8 1.1 collective-permute-done.1.refs_1_
  109.9 6.2 %backward.1 = bf16[64,2,4224]{2,1,0:T(2,128)(2,1)} custom-call(s32[1]{0:T(128)} %bitcast.x_ref, bf16[64,2,5120]{2,1,0:T(2,128)(2,1)S(1)} %all_to_all.15.sent_ref, bf16[128,1792]{1,0:T(8,128)(2,1)S(1)} %get-tuple-element.13.refs_0_, bf16[128,1792]{1,0:T(8,128)(2,1)} %collective-permute-done.1.refs_1_, bf16[128,1792]{1,0:T(8,128)(2,1)} %collective-permute-done.2.refs_2_, ...), custom_call_target="tpu_custom_call" | custom-call | flops 4000000000 | bytes 12000000 | tf_op jit(solution)/shard_map/backward/pallas_call | solution.py:270
  116.2 0.0 all-to-all-done.1.terms_ref
  116.2 14.1 %all-to-all-start.2 = ((bf16[64,2,4224]{2,1,0:T(2,128)(2,1)}), bf16[64,2,4224]{2,1,0:T(2,128)(2,1)S(1)}, u32[]{:S(2)}, u32[]{:S(2)}) async-start(bf16[64,2,4224]{2,1,0:T(2,128)(2,1)} %backward.1), calls=%async_computation.2 | async-start | bytes 2162688 | tf_op jit(solution)/shard_map/all_to_all | solution.py:285
  130.3 0.2 owned.1.refs_0_
  130.6 2.1 %collective-permute-start.6 = (f32[2,3456]{1,0:T(2,128)S(1)}, f32[2,3456]{1,0:T(2,128)S(1)}, u32[]{:S(2)}, u32[]{:S(2)}) collective-permute-start(f32[2,3456]{1,0:T(2,128)S(1)} %owned.1.refs_0_), channel_id=1, source_target_pairs={{0,384},{128,0},{256,128},{384,256},{1,385},{129,1},{257,129},{385... | collective-permute-start | bytes 82952 | tf_op jit(solution)/shard_map/ppermute | solution.py:293
  132.7 2.9 %collective-permute-start.5 = (f32[2,3456]{1,0:T(2,128)S(1)}, f32[2,3456]{1,0:T(2,128)S(1)}, u32[]{:S(2)}, u32[]{:S(2)}) collective-permute-start(f32[2,3456]{1,0:T(2,128)S(1)} %owned.1.refs_0_), channel_id=1, source_target_pairs={{0,256},{128,384},{256,0},{384,128},{1,257},{129,385},{257,1},{385... | collective-permute-start | bytes 82952 | tf_op jit(solution)/shard_map/ppermute | solution.py:293
  135.6 4.3 %collective-permute-start.4 = (f32[2,3456]{1,0:T(2,128)S(1)}, f32[2,3456]{1,0:T(2,128)S(1)}, u32[]{:S(2)}, u32[]{:S(2)}) collective-permute-start(f32[2,3456]{1,0:T(2,128)S(1)} %owned.1.refs_0_), channel_id=1, source_target_pairs={{0,128},{128,256},{256,384},{384,0},{1,129},{129,257},{257,385},{3... | collective-permute-start | bytes 82952 | tf_op jit(solution)/shard_map/ppermute | solution.py:293
  139.9 14.6 %collective-permute-done.6.refs_3_ = f32[2,3456]{1,0:T(2,128)S(1)} collective-permute-done((f32[2,3456]{1,0:T(2,128)S(1)}, f32[2,3456]{1,0:T(2,128)S(1)}, u32[]{:S(2)}, u32[]{:S(2)}) %collective-permute-start.6) | collective-permute-done | bytes 27680 | tf_op jit(solution)/shard_map/ppermute | solution.py:293
  154.4 0.0 collective-permute-done.5.refs_2_
  154.4 0.0 collective-permute-done.4.refs_1_
  154.5 1.9 %collective-permute-start.7 = (f32[2,3456]{1,0:T(2,128)S(1)}, f32[2,3456]{1,0:T(2,128)S(1)}, u32[]{:S(2)}, u32[]{:S(2)}) collective-permute-start(f32[2,3456]{1,0:T(2,128)S(1)} %group.1.mine_ref), channel_id=1, source_target_pairs={{0,64},{64,0},{1,65},{65,1},{2,66},{66,2},{3,67},{67,3},{4,68},{68... | collective-permute-start | bytes 82952 | tf_op jit(solution)/shard_map/ppermute | solution.py:289
  156.4 1.2 collective-permute-done.7.theirs_ref
  157.5 0.7 total.1
  158.2 7.7 %all-to-all-done.2.back_ref = bf16[64,2,4224]{2,1,0:T(2,128)(2,1)S(1)} async-done(((bf16[64,2,4224]{2,1,0:T(2,128)(2,1)}), bf16[64,2,4224]{2,1,0:T(2,128)(2,1)S(1)}, u32[]{:S(2)}, u32[]{:S(2)}) %all-to-all-start.2) | async-done | bytes 1081376 | tf_op jit(solution)/shard_map/all_to_all | solution.py:285
  165.9 1.1 unpack.1
  (1 shorter events, 0.0 us)
Async XLA Ops:
  63.8 3.9 %collective-permute-start = (bf16[128,2432]{1,0:T(8,128)(2,1)S(1)}, bf16[128,2432]{1,0:T(8,128)(2,1)S(1)}, u32[]{:S(2)}, u32[]{:S(2)}) collective-permute-start(bf16[128,2432]{1,0:T(8,128)(2,1)S(1)} %get-tuple-element.11.share_ref), channel_id=1, source_target_pairs={{0,64},{64,0},{1,65},{65,1},{2,66},{66,2},{3,67},{67,3},{4,68},{68... | collective-permute-start | bytes 1867784 | tf_op jit(solution)/shard_map/ppermute | solution.py:289
  69.2 47.0 %all-to-all-start.1 = ((bf16[64,2,3456]{2,1,0:T(2,128)(2,1)}), bf16[64,2,3456]{2,1,0:T(2,128)(2,1)S(1)}, u32[]{:S(2)}, u32[]{:S(2)}) async-start(bf16[64,2,3456]{2,1,0:T(2,128)(2,1)} %get-tuple-element.14), calls=%async_computation.1 | async-start | bytes 1769472 | tf_op jit(solution)/shard_map/all_to_all | solution.py:285
  74.6 20.2 %collective-permute-start.3 = (bf16[128,1792]{1,0:T(8,128)(2,1)S(1)}, bf16[128,1792]{1,0:T(8,128)(2,1)S(1)}, u32[]{:S(2)}, u32[]{:S(2)}) collective-permute-start(bf16[128,1792]{1,0:T(8,128)(2,1)S(1)} %get-tuple-element.13.refs_0_), channel_id=1, source_target_pairs={{0,24},{8,0},{16,8},{24,16},{1,25},{9,1},{17,9},{25,17},{2,26},{10... | collective-permute-start | bytes 1376264 | tf_op jit(solution)/shard_map/ppermute | solution.py:293
  77.3 31.5 %collective-permute-start.2 = (bf16[128,1792]{1,0:T(8,128)(2,1)S(1)}, bf16[128,1792]{1,0:T(8,128)(2,1)}, u32[]{:S(2)}, u32[]{:S(2)}) collective-permute-start(bf16[128,1792]{1,0:T(8,128)(2,1)S(1)} %get-tuple-element.13.refs_0_), channel_id=1, source_target_pairs={{0,16},{8,24},{16,0},{24,8},{1,17},{9,25},{17,1},{25,9},{2,18},{10... | collective-permute-start | bytes 1376264 | tf_op jit(solution)/shard_map/ppermute | solution.py:293
  80.3 29.7 %collective-permute-start.1 = (bf16[128,1792]{1,0:T(8,128)(2,1)S(1)}, bf16[128,1792]{1,0:T(8,128)(2,1)}, u32[]{:S(2)}, u32[]{:S(2)}) collective-permute-start(bf16[128,1792]{1,0:T(8,128)(2,1)S(1)} %get-tuple-element.13.refs_0_), channel_id=1, source_target_pairs={{0,8},{8,16},{16,24},{24,0},{1,9},{9,17},{17,25},{25,1},{2,10},{10... | collective-permute-start | bytes 1376264 | tf_op jit(solution)/shard_map/ppermute | solution.py:293
  116.2 49.7 %all-to-all-start.2 = ((bf16[64,2,4224]{2,1,0:T(2,128)(2,1)}), bf16[64,2,4224]{2,1,0:T(2,128)(2,1)S(1)}, u32[]{:S(2)}, u32[]{:S(2)}) async-start(bf16[64,2,4224]{2,1,0:T(2,128)(2,1)} %backward.1), calls=%async_computation.2 | async-start | bytes 2162688 | tf_op jit(solution)/shard_map/all_to_all | solution.py:285
  130.6 23.9 %collective-permute-start.6 = (f32[2,3456]{1,0:T(2,128)S(1)}, f32[2,3456]{1,0:T(2,128)S(1)}, u32[]{:S(2)}, u32[]{:S(2)}) collective-permute-start(f32[2,3456]{1,0:T(2,128)S(1)} %owned.1.refs_0_), channel_id=1, source_target_pairs={{0,384},{128,0},{256,128},{384,256},{1,385},{129,1},{257,129},{385... | collective-permute-start | bytes 82952 | tf_op jit(solution)/shard_map/ppermute | solution.py:293
  132.7 21.7 %collective-permute-start.5 = (f32[2,3456]{1,0:T(2,128)S(1)}, f32[2,3456]{1,0:T(2,128)S(1)}, u32[]{:S(2)}, u32[]{:S(2)}) collective-permute-start(f32[2,3456]{1,0:T(2,128)S(1)} %owned.1.refs_0_), channel_id=1, source_target_pairs={{0,256},{128,384},{256,0},{384,128},{1,257},{129,385},{257,1},{385... | collective-permute-start | bytes 82952 | tf_op jit(solution)/shard_map/ppermute | solution.py:293
  135.6 18.8 %collective-permute-start.4 = (f32[2,3456]{1,0:T(2,128)S(1)}, f32[2,3456]{1,0:T(2,128)S(1)}, u32[]{:S(2)}, u32[]{:S(2)}) collective-permute-start(f32[2,3456]{1,0:T(2,128)S(1)} %owned.1.refs_0_), channel_id=1, source_target_pairs={{0,128},{128,256},{256,384},{384,0},{1,129},{129,257},{257,385},{3... | collective-permute-start | bytes 82952 | tf_op jit(solution)/shard_map/ppermute | solution.py:293
  154.5 3.1 %collective-permute-start.7 = (f32[2,3456]{1,0:T(2,128)S(1)}, f32[2,3456]{1,0:T(2,128)S(1)}, u32[]{:S(2)}, u32[]{:S(2)}) collective-permute-start(f32[2,3456]{1,0:T(2,128)S(1)} %group.1.mine_ref), channel_id=1, source_target_pairs={{0,64},{64,0},{1,65},{65,1},{2,66},{66,2},{3,67},{67,3},{4,68},{68... | collective-permute-start | bytes 82952 | tf_op jit(solution)/shard_map/ppermute | solution.py:289

commit v11 on v10

--- a/solution.py
+++ b/solution.py
@@ -21,7 +21,6 @@
 PIECE_TILES = PIECE // LANES
 COLS = BASE + PIECE
 HALF_WIDTH = 3 * WIDTH
-SHARE = WIDTH + HALF + PIECE
 INV_ROOT = 1.0 / math.sqrt(HEAD_DIM)
 GRAD_SCALE = 1.0 / math.sqrt(512 * ROWS)
 BF16 = jnp.bfloat16
@@ -153,16 +152,11 @@
     own = pl.multiple_of(core_ref[0] * HALF, HALF)
     other = pl.multiple_of((1 - core_ref[0]) * HALF, HALF)
     columns_ref[...] = channels_ref[:, pl.ds(own, HALF)]
-    share_ref[:, WIDTH : WIDTH + HALF] = channels_ref[:, pl.ds(other, HALF)]
-    share_ref[:, WIDTH + HALF :] = rows_ref[:, BASE:]
-
-
-def weight_grad_kernel(core_ref, share_ref, received_ref, columns_ref, out_ref, pieces_ref):
-    own = pl.multiple_of(core_ref[0] * PIECE, PIECE)
-    other = pl.multiple_of((1 - core_ref[0]) * PIECE, PIECE)
-    pieces_ref[:, pl.ds(own, PIECE)] = share_ref[:, WIDTH + HALF :]
-    pieces_ref[:, pl.ds(other, PIECE)] = received_ref[:, WIDTH + HALF :]
-    columns = jnp.concatenate([columns_ref[...], received_ref[:, WIDTH : WIDTH + HALF]], axis=0)
+    share_ref[:, WIDTH:] = channels_ref[:, pl.ds(other, HALF)]
+
+
+def weight_grad_kernel(share_ref, received_ref, columns_ref, out_ref):
+    columns = jnp.concatenate([columns_ref[...], received_ref[:, WIDTH:]], axis=0)
     features = jnp.concatenate([share_ref[:, :WIDTH], received_ref[:, :WIDTH]], axis=0)
     partial = dot(columns, features, 0, 0).astype(BF16)
     for pair in range(3):
@@ -171,12 +165,11 @@
         ].reshape(64, 2, WIDTH)
 
 
-def backward_kernel(x_ref, sent_ref, *refs):
-    pieces_refs, refs = refs[:4], refs[4:]
-    (
-        out_ref, rows_ref, weights_ref, channels_ref, attended_ref, matrix_ref, upstream_ref,
-        grad_scores_ref,
-    ) = refs
+def backward_kernel(
+    core_ref, x_ref, sent_ref, mine_ref, theirs_ref,
+    out_ref, rows_ref, weights_ref, channels_ref, attended_ref, matrix_ref, upstream_ref,
+    grad_scores_ref,
+):
     rows_ref[...] = sent_ref[...].reshape(ROWS, COLS)
     channels_ref[...] = ordered_channels(rows_ref)
 
@@ -184,16 +177,17 @@
         attended_ref[:, lanes(tile)] = value
 
     attend(rows_ref, weights_ref, put_attended)
+    own = pl.multiple_of(core_ref[0] * HALF, HALF)
+    other = pl.multiple_of((1 - core_ref[0]) * HALF, HALF)
     for here in range(4):
 
         @pl.when(x_ref[0] == here)
         def _():
-            for core in range(2):
-                for piece, place, pair, tile in half_tiles():
-                    start = core * HALF + pair * ROWS
-                    matrix_ref[start : start + ROWS, lanes(tile)] = pieces_refs[
-                        (here - piece) & 3
-                    ][:, lanes(place, core * PIECE)]
+            for piece, place, pair, tile in half_tiles():
+                for start, half_ref in ((own, mine_ref), (other, theirs_ref)):
+                    matrix_ref[pl.ds(start + pair * ROWS, ROWS), lanes(tile)] = half_ref[
+                        (here - piece) & 3, :, lanes(place)
+                    ]
 
     upstream_ref[...] = dot(channels_ref[...], matrix_ref[...], 1, 0).astype(BF16)
     products = [
@@ -316,7 +310,7 @@
         "forward",
         (core, sent),
         [IN_SMEM, IN_VMEM],
-        [((ROWS, SHARE), BF16), ((ROWS, HALF), BF16)],
+        [((ROWS, WIDTH + HALF), BF16), ((ROWS, HALF), BF16)],
         [
             pltpu.VMEM((ROWS, COLS), BF16),
             pltpu.VMEM((HEADS, ROWS, ROWS), F32),
@@ -324,20 +318,23 @@
         ],
         micros=3,
     )
-    partial, pieces = call(
+    piece = sent[:, :, BASE:].reshape(ROWS, PIECE)
+    turned = [turn(piece, "x", step) for step in range(1, 4)]
+    (partial,) = call(
         weight_grad_kernel,
         "weight_grad",
-        (core, share, swap(share), columns),
-        [IN_SMEM] + [IN_VMEM] * 3,
-        [((64, 2, HALF_WIDTH), BF16), ((ROWS, 2 * PIECE), BF16)],
+        (share, swap(share), columns),
+        [IN_VMEM] * 3,
+        [((64, 2, HALF_WIDTH), BF16)],
     )
     collected = exchange(partial, SEQ)
-    turned = [turn(pieces, "x", step) for step in range(1, 4)]
+    piece, *turned = lax.optimization_barrier((piece, *turned, partial))[:4]
+    mine = jnp.stack([piece, *turned])
     (results,) = call(
         backward_kernel,
         "backward",
-        (x_place, sent, pieces, *turned),
-        [IN_SMEM] + [IN_VMEM] * 5,
+        (core, x_place, sent, mine, swap(mine)),
+        [IN_SMEM] * 2 + [IN_VMEM] * 3,
         [((64, 2, BASE), BF16)],
         [
             pltpu.VMEM((ROWS, COLS), BF16),
@@ -348,12 +345,12 @@
             pltpu.VMEM((ROWS, WIDTH), BF16),
             pltpu.VMEM((HEADS, ROWS, ROWS), BF16),
         ],
-        micros=4,
+        micros=7,
     )
     results, collected = lax.optimization_barrier((results, collected))
-    back = exchange(results, SEQ)
     (owned,) = call(owned_kernel, "owned", (collected,), [IN_VMEM], [((2, HALF_WIDTH), F32)])
     turned = [turn(owned, "yl", step) for step in range(1, 4)]
+    back = exchange(results, SEQ)
     (group,) = call(
         group_kernel, "group", (owned, *turned), [IN_VMEM] * 4, [((2, HALF_WIDTH), F32)]
     )

time: 168 us -> 157 us (0.935)
  starting transfers between devices: 42.3 us -> 35.5 us
  waiting for transfers between devices: 51 us -> 45.1 us
    ppermute x6, waiting for transfers between devices: 40.2 us -> 16.4 us  [turn(): lax.ppermute(value, axis, [(place, (place + step) % 4) for place in range...]
    all_to_all x2, waiting for transfers between devices: 7.66 us -> 25 us  [exchange(): return lax.all_to_all(value, axes, 0, 0, tiled=True)]
    all_to_all x2, starting transfers between devices: 19.4 us -> 12.3 us  [exchange(): return lax.all_to_all(value, axes, 0, 0, tiled=True)]
    ppermute x2 -> x3, starting transfers between devices: 3.84 us -> 5.77 us  [swap(): return lax.ppermute(value, 'c', [(0, 1), (1, 0)])]
    ppermute x2 -> x3, waiting for transfers between devices: 3.18 us -> 3.73 us  [swap(): return lax.ppermute(value, 'c', [(0, 1), (1, 0)])]
  transfers between devices with their start and end apart: 10 -> 11, of which waited for: 7 -> 6; matrix products, arithmetic and copies ran while one was open for 0% -> 1% of each run, Pallas kernels for 4% -> 6%
where the time goes in v11:
time: 157 us; the launch traced here: 156 us
  blocking collectives  59 us (38%)
  waiting for transfers between devices  45.1 us (29%)
  starting transfers between devices  35.5 us (23%)
  Pallas kernels  14.1 us (9%)
    all_to_all x1, blocking collectives, exchange(): return lax.all_to_all(value, axes, 0, 0, tiled=True)  59 us
    all_to_all x2, waiting for transfers between devices, exchange(): return lax.all_to_all(value, axes, 0, 0, tiled=True)  25 us
    ppermute x6, starting transfers between devices, turn(): lax.ppermute(value, axis, [(place, (place + step) % 4) for place in range...  17.5 us
    ppermute x6, waiting for transfers between devices, turn(): lax.ppermute(value, axis, [(place, (place + step) % 4) for place in range...  16.4 us
    pallas_call x8, Pallas kernels, call(): pl.pallas_call(kernel, out_shape=[jax.ShapeDtypeStruct(shape, dtype) for...  14.1 us
    all_to_all x2, starting transfers between devices, exchange(): return lax.all_to_all(value, axes, 0, 0, tiled=True)  12.3 us
    ppermute x3, starting transfers between devices, swap(): return lax.ppermute(value, 'c', [(0, 1), (1, 0)])  5.77 us
    ppermute x3, waiting for transfers between devices, swap(): return lax.ppermute(value, 'c', [(0, 1), (1, 0)])  3.73 us
  transfers between devices with their start and end apart: 11, of which 6 were waited for; matrix products, arithmetic and copies ran while one was open for 1% of the time, Pallas kernels for 6%

profile of v11, /device:TPU:14, one launch (start us, length us, event | category | flops | bytes accessed | tf_op | source)
XLA Modules:
  0.0 156.0 jit_solution(4497492990939174049)
XLA Ops:
  0.6 2.8 %pack.1 = bf16[64,2,5120]{2,1,0:T(2,128)(2,1)} custom-call(s32[1]{0:T(128)} %bitcast.core_ref, bf16[3,128,1152]{2,1,0:T(8,128)(2,1)} %bitcast.14, bf16[128,768]{1,0:T(8,128)(2,1)} %bitcast.15, bf16[12,1152]{1,0:T(8,128)(2,1)} %weight_hbm.1), custom_call_target="tpu_custom_call" | custom-call | flops 1000000000 | bytes 3000000 | tf_op jit(solution)/shard_map/pack/pallas_call | solution.py:264
  3.5 59.0 %all_to_all.15.sent_ref = bf16[64,2,5120]{2,1,0:T(2,128)(2,1)S(1)} all-to-all(bf16[64,2,5120]{2,1,0:T(2,128)(2,1)} %pack.1), channel_id=1, replica_groups=mesh['yl'=4,'c'=2,'yh'=2,'x'=4,'z'=8] {'yh','x','z'}, dimensions={0} | all-to-all | bytes 2621440 | tf_op jit(solution)/shard_map/all_to_all | solution.py:279
  62.5 1.3 forward.1
  63.8 1.9 %collective-permute-start.3 = (bf16[128,1536]{1,0:T(8,128)(2,1)S(1)}, bf16[128,1536]{1,0:T(8,128)(2,1)S(1)}, u32[]{:S(2)}, u32[]{:S(2)}) collective-permute-start(bf16[128,1536]{1,0:T(8,128)(2,1)S(1)} %get-tuple-element.13.share_ref), channel_id=1, source_target_pairs={{0,64},{64,0},{1,65},{65,1},{2,66},{66,2},{3,67},{67,3},{4,68},{68... | collective-permute-start | bytes 1179656 | tf_op jit(solution)/shard_map/ppermute | solution.py:283
  65.7 0.2 slice.4
  65.9 0.1 reshape.31
  66.0 1.9 %collective-permute-start.2 = (bf16[128,896]{1,0:T(8,128)(2,1)S(1)}, bf16[128,896]{1,0:T(8,128)(2,1)S(1)}, u32[]{:S(2)}, u32[]{:S(2)}) collective-permute-start(bf16[128,896]{1,0:T(8,128)(2,1)S(1)} %reshape.31), channel_id=1, source_target_pairs={{0,24},{8,0},{16,8},{24,16},{1,25},{9,1},{17,9},{25,17},{2,26},{10... | collective-permute-start | bytes 688136 | tf_op jit(solution)/shard_map/ppermute | solution.py:287
  67.9 3.6 %collective-permute-start.1 = (bf16[128,896]{1,0:T(8,128)(2,1)S(1)}, bf16[128,896]{1,0:T(8,128)(2,1)}, u32[]{:S(2)}, u32[]{:S(2)}) collective-permute-start(bf16[128,896]{1,0:T(8,128)(2,1)S(1)} %reshape.31), channel_id=1, source_target_pairs={{0,16},{8,24},{16,0},{24,8},{1,17},{9,25},{17,1},{25,9},{2,18},{10... | collective-permute-start | bytes 688136 | tf_op jit(solution)/shard_map/ppermute | solution.py:287
  71.6 3.4 %collective-permute-start = (bf16[128,896]{1,0:T(8,128)(2,1)S(1)}, bf16[128,896]{1,0:T(8,128)(2,1)}, u32[]{:S(2)}, u32[]{:S(2)}) collective-permute-start(bf16[128,896]{1,0:T(8,128)(2,1)S(1)} %reshape.31), channel_id=1, source_target_pairs={{0,8},{8,16},{16,24},{24,0},{1,9},{9,17},{17,25},{25,1},{2,10},{10... | collective-permute-start | bytes 688136 | tf_op jit(solution)/shard_map/ppermute | solution.py:287
  75.0 0.0 collective-permute-done.3.received_ref
  75.0 1.5 weight_grad.1
  76.5 7.2 %all-to-all-start.1 = ((bf16[64,2,3456]{2,1,0:T(2,128)(2,1)}), bf16[64,2,3456]{2,1,0:T(2,128)(2,1)S(1)}, u32[]{:S(2)}, u32[]{:S(2)}) async-start(bf16[64,2,3456]{2,1,0:T(2,128)(2,1)} %weight_grad.1), calls=%async_computation.1 | async-start | bytes 1769472 | tf_op jit(solution)/shard_map/all_to_all | solution.py:279
  83.6 0.0 collective-permute-done.2
  83.7 0.0 copy-start
  83.7 0.0 collective-permute-done.1
  83.7 1.2 collective-permute-done
  84.9 0.0 copy-done
  84.9 1.3 pad_maximum_fusion.mine_ref
  86.2 1.9 %collective-permute-start.4 = (bf16[4,128,896]{2,1,0:T(8,128)(2,1)S(1)}, bf16[4,128,896]{2,1,0:T(8,128)(2,1)}, u32[]{:S(2)}, u32[]{:S(2)}) collective-permute-start(bf16[4,128,896]{2,1,0:T(8,128)(2,1)S(1)} %pad_maximum_fusion.mine_ref), channel_id=1, source_target_pairs={{0,64},{64,0},{1,65},{65,1},{2,66},{66,2},{3,67},{67,3},{4,68},{68... | collective-permute-start | bytes 2752520 | tf_op jit(solution)/shard_map/ppermute | solution.py:283
  88.1 2.6 %collective-permute-done.4.theirs_ref = bf16[4,128,896]{2,1,0:T(8,128)(2,1)} collective-permute-done((bf16[4,128,896]{2,1,0:T(8,128)(2,1)S(1)}, bf16[4,128,896]{2,1,0:T(8,128)(2,1)}, u32[]{:S(2)}, u32[]{:S(2)}) %collective-permute-start.4) | collective-permute-done | bytes 917536 | tf_op jit(solution)/shard_map/ppermute | solution.py:283
  90.7 6.4 %backward.1 = bf16[64,2,4224]{2,1,0:T(2,128)(2,1)} custom-call(s32[1]{0:T(128)} %bitcast.core_ref, s32[1]{0:T(128)} %bitcast.1.x_ref, bf16[64,2,5120]{2,1,0:T(2,128)(2,1)S(1)} %all_to_all.15.sent_ref, bf16[4,128,896]{2,1,0:T(8,128)(2,1)S(1)} %pad_maximum_fusion.mine_ref, bf16[4,128,896]{2,1,0:T(8,128)(2,1)} %collective-permute-done.4.theirs_ref), custom_call_target="tpu_custom_call" | custom-call | flops 7000000000 | bytes 21000000 | tf_op jit(solution)/shard_map/backward/pallas_call | solution.py:264
  97.1 17.4 %all-to-all-done.1.terms_ref = bf16[64,2,3456]{2,1,0:T(2,128)(2,1)S(1)} async-done(((bf16[64,2,3456]{2,1,0:T(2,128)(2,1)}), bf16[64,2,3456]{2,1,0:T(2,128)(2,1)S(1)}, u32[]{:S(2)}, u32[]{:S(2)}) %all-to-all-start.1) | async-done | bytes 884768 | tf_op jit(solution)/shard_map/all_to_all | solution.py:279
  114.6 5.1 %all-to-all-start.2 = ((bf16[64,2,4224]{2,1,0:T(2,128)(2,1)}), bf16[64,2,4224]{2,1,0:T(2,128)(2,1)S(1)}, u32[]{:S(2)}, u32[]{:S(2)}) async-start(bf16[64,2,4224]{2,1,0:T(2,128)(2,1)} %backward.1), calls=%async_computation.2 | async-start | bytes 2162688 | tf_op jit(solution)/shard_map/all_to_all | solution.py:279
  119.7 0.2 owned.1.refs_0_
  119.9 1.9 %collective-permute-start.7 = (f32[2,3456]{1,0:T(2,128)S(1)}, f32[2,3456]{1,0:T(2,128)S(1)}, u32[]{:S(2)}, u32[]{:S(2)}) collective-permute-start(f32[2,3456]{1,0:T(2,128)S(1)} %owned.1.refs_0_), channel_id=1, source_target_pairs={{0,384},{128,0},{256,128},{384,256},{1,385},{129,1},{257,129},{385... | collective-permute-start | bytes 82952 | tf_op jit(solution)/shard_map/ppermute | solution.py:287
  121.9 3.1 %collective-permute-start.6 = (f32[2,3456]{1,0:T(2,128)S(1)}, f32[2,3456]{1,0:T(2,128)S(1)}, u32[]{:S(2)}, u32[]{:S(2)}) collective-permute-start(f32[2,3456]{1,0:T(2,128)S(1)} %owned.1.refs_0_), channel_id=1, source_target_pairs={{0,256},{128,384},{256,0},{384,128},{1,257},{129,385},{257,1},{385... | collective-permute-start | bytes 82952 | tf_op jit(solution)/shard_map/ppermute | solution.py:287
  124.9 3.5 %collective-permute-start.5 = (f32[2,3456]{1,0:T(2,128)S(1)}, f32[2,3456]{1,0:T(2,128)S(1)}, u32[]{:S(2)}, u32[]{:S(2)}) collective-permute-start(f32[2,3456]{1,0:T(2,128)S(1)} %owned.1.refs_0_), channel_id=1, source_target_pairs={{0,128},{128,256},{256,384},{384,0},{1,129},{129,257},{257,385},{3... | collective-permute-start | bytes 82952 | tf_op jit(solution)/shard_map/ppermute | solution.py:287
  128.4 15.2 %collective-permute-done.7.refs_3_ = f32[2,3456]{1,0:T(2,128)S(1)} collective-permute-done((f32[2,3456]{1,0:T(2,128)S(1)}, f32[2,3456]{1,0:T(2,128)S(1)}, u32[]{:S(2)}, u32[]{:S(2)}) %collective-permute-start.7) | collective-permute-done | bytes 27680 | tf_op jit(solution)/shard_map/ppermute | solution.py:287
  143.6 0.0 collective-permute-done.6.refs_2_
  143.6 0.0 collective-permute-done.5.refs_1_
  143.6 1.9 %collective-permute-start.8 = (f32[2,3456]{1,0:T(2,128)S(1)}, f32[2,3456]{1,0:T(2,128)S(1)}, u32[]{:S(2)}, u32[]{:S(2)}) collective-permute-start(f32[2,3456]{1,0:T(2,128)S(1)} %group.1.mine_ref), channel_id=1, source_target_pairs={{0,64},{64,0},{1,65},{65,1},{2,66},{66,2},{3,67},{67,3},{4,68},{68... | collective-permute-start | bytes 82952 | tf_op jit(solution)/shard_map/ppermute | solution.py:283
  145.5 1.2 collective-permute-done.8.theirs_ref
  146.7 0.7 total.1
  147.4 7.5 %all-to-all-done.2.back_ref = bf16[64,2,4224]{2,1,0:T(2,128)(2,1)S(1)} async-done(((bf16[64,2,4224]{2,1,0:T(2,128)(2,1)}), bf16[64,2,4224]{2,1,0:T(2,128)(2,1)S(1)}, u32[]{:S(2)}, u32[]{:S(2)}) %all-to-all-start.2) | async-done | bytes 1081376 | tf_op jit(solution)/shard_map/all_to_all | solution.py:279
  154.9 1.1 unpack.1
  (1 shorter events, 0.0 us)
Async XLA Ops:
  63.8 11.2 %collective-permute-start.3 = (bf16[128,1536]{1,0:T(8,128)(2,1)S(1)}, bf16[128,1536]{1,0:T(8,128)(2,1)S(1)}, u32[]{:S(2)}, u32[]{:S(2)}) collective-permute-start(bf16[128,1536]{1,0:T(8,128)(2,1)S(1)} %get-tuple-element.13.share_ref), channel_id=1, source_target_pairs={{0,64},{64,0},{1,65},{65,1},{2,66},{66,2},{3,67},{67,3},{4,68},{68... | collective-permute-start | bytes 1179656 | tf_op jit(solution)/shard_map/ppermute | solution.py:283
  66.0 17.7 %collective-permute-start.2 = (bf16[128,896]{1,0:T(8,128)(2,1)S(1)}, bf16[128,896]{1,0:T(8,128)(2,1)S(1)}, u32[]{:S(2)}, u32[]{:S(2)}) collective-permute-start(bf16[128,896]{1,0:T(8,128)(2,1)S(1)} %reshape.31), channel_id=1, source_target_pairs={{0,24},{8,0},{16,8},{24,16},{1,25},{9,1},{17,9},{25,17},{2,26},{10... | collective-permute-start | bytes 688136 | tf_op jit(solution)/shard_map/ppermute | solution.py:287
  67.9 15.8 %collective-permute-start.1 = (bf16[128,896]{1,0:T(8,128)(2,1)S(1)}, bf16[128,896]{1,0:T(8,128)(2,1)}, u32[]{:S(2)}, u32[]{:S(2)}) collective-permute-start(bf16[128,896]{1,0:T(8,128)(2,1)S(1)} %reshape.31), channel_id=1, source_target_pairs={{0,16},{8,24},{16,0},{24,8},{1,17},{9,25},{17,1},{25,9},{2,18},{10... | collective-permute-start | bytes 688136 | tf_op jit(solution)/shard_map/ppermute | solution.py:287
  71.6 13.3 %collective-permute-start = (bf16[128,896]{1,0:T(8,128)(2,1)S(1)}, bf16[128,896]{1,0:T(8,128)(2,1)}, u32[]{:S(2)}, u32[]{:S(2)}) collective-permute-start(bf16[128,896]{1,0:T(8,128)(2,1)S(1)} %reshape.31), channel_id=1, source_target_pairs={{0,8},{8,16},{16,24},{24,0},{1,9},{9,17},{17,25},{25,1},{2,10},{10... | collective-permute-start | bytes 688136 | tf_op jit(solution)/shard_map/ppermute | solution.py:287
  76.5 38.1 %all-to-all-start.1 = ((bf16[64,2,3456]{2,1,0:T(2,128)(2,1)}), bf16[64,2,3456]{2,1,0:T(2,128)(2,1)S(1)}, u32[]{:S(2)}, u32[]{:S(2)}) async-start(bf16[64,2,3456]{2,1,0:T(2,128)(2,1)} %weight_grad.1), calls=%async_computation.1 | async-start | bytes 1769472 | tf_op jit(solution)/shard_map/all_to_all | solution.py:279
  83.7 1.2 copy-start
  86.2 4.5 %collective-permute-start.4 = (bf16[4,128,896]{2,1,0:T(8,128)(2,1)S(1)}, bf16[4,128,896]{2,1,0:T(8,128)(2,1)}, u32[]{:S(2)}, u32[]{:S(2)}) collective-permute-start(bf16[4,128,896]{2,1,0:T(8,128)(2,1)S(1)} %pad_maximum_fusion.mine_ref), channel_id=1, source_target_pairs={{0,64},{64,0},{1,65},{65,1},{2,66},{66,2},{3,67},{67,3},{4,68},{68... | collective-permute-start | bytes 2752520 | tf_op jit(solution)/shard_map/ppermute | solution.py:283
  114.6 40.3 %all-to-all-start.2 = ((bf16[64,2,4224]{2,1,0:T(2,128)(2,1)}), bf16[64,2,4224]{2,1,0:T(2,128)(2,1)S(1)}, u32[]{:S(2)}, u32[]{:S(2)}) async-start(bf16[64,2,4224]{2,1,0:T(2,128)(2,1)} %backward.1), calls=%async_computation.2 | async-start | bytes 2162688 | tf_op jit(solution)/shard_map/all_to_all | solution.py:279
  119.9 23.7 %collective-permute-start.7 = (f32[2,3456]{1,0:T(2,128)S(1)}, f32[2,3456]{1,0:T(2,128)S(1)}, u32[]{:S(2)}, u32[]{:S(2)}) collective-permute-start(f32[2,3456]{1,0:T(2,128)S(1)} %owned.1.refs_0_), channel_id=1, source_target_pairs={{0,384},{128,0},{256,128},{384,256},{1,385},{129,1},{257,129},{385... | collective-permute-start | bytes 82952 | tf_op jit(solution)/shard_map/ppermute | solution.py:287
  121.9 21.7 %collective-permute-start.6 = (f32[2,3456]{1,0:T(2,128)S(1)}, f32[2,3456]{1,0:T(2,128)S(1)}, u32[]{:S(2)}, u32[]{:S(2)}) collective-permute-start(f32[2,3456]{1,0:T(2,128)S(1)} %owned.1.refs_0_), channel_id=1, source_target_pairs={{0,256},{128,384},{256,0},{384,128},{1,257},{129,385},{257,1},{385... | collective-permute-start | bytes 82952 | tf_op jit(solution)/shard_map/ppermute | solution.py:287
  124.9 18.7 %collective-permute-start.5 = (f32[2,3456]{1,0:T(2,128)S(1)}, f32[2,3456]{1,0:T(2,128)S(1)}, u32[]{:S(2)}, u32[]{:S(2)}) collective-permute-start(f32[2,3456]{1,0:T(2,128)S(1)} %owned.1.refs_0_), channel_id=1, source_target_pairs={{0,128},{128,256},{256,384},{384,0},{1,129},{129,257},{257,385},{3... | collective-permute-start | bytes 82952 | tf_op jit(solution)/shard_map/ppermute | solution.py:287
  143.6 3.1 %collective-permute-start.8 = (f32[2,3456]{1,0:T(2,128)S(1)}, f32[2,3456]{1,0:T(2,128)S(1)}, u32[]{:S(2)}, u32[]{:S(2)}) collective-permute-start(f32[2,3456]{1,0:T(2,128)S(1)} %group.1.mine_ref), channel_id=1, source_target_pairs={{0,64},{64,0},{1,65},{65,1},{2,66},{66,2},{3,67},{67,3},{4,68},{68... | collective-permute-start | bytes 82952 | tf_op jit(solution)/shard_map/ppermute | solution.py:283

commit v12 on v11

--- a/solution.py
+++ b/solution.py
@@ -155,7 +155,11 @@
     share_ref[:, WIDTH:] = channels_ref[:, pl.ds(other, HALF)]
 
 
-def weight_grad_kernel(share_ref, received_ref, columns_ref, out_ref):
+def weight_grad_kernel(
+    share_ref, received_ref, columns_ref, piece_ref, near_ref, out_ref, pieces_ref
+):
+    pieces_ref[0] = piece_ref[...]
+    pieces_ref[1] = near_ref[...]
     columns = jnp.concatenate([columns_ref[...], received_ref[:, WIDTH:]], axis=0)
     features = jnp.concatenate([share_ref[:, :WIDTH], received_ref[:, :WIDTH]], axis=0)
     partial = dot(columns, features, 0, 0).astype(BF16)
@@ -166,7 +170,7 @@
 
 
 def backward_kernel(
-    core_ref, x_ref, sent_ref, mine_ref, theirs_ref,
+    core_ref, x_ref, sent_ref, near_ref, far_ref, their_near_ref, their_far_ref,
     out_ref, rows_ref, weights_ref, channels_ref, attended_ref, matrix_ref, upstream_ref,
     grad_scores_ref,
 ):
@@ -184,9 +188,12 @@
         @pl.when(x_ref[0] == here)
         def _():
             for piece, place, pair, tile in half_tiles():
-                for start, half_ref in ((own, mine_ref), (other, theirs_ref)):
+                slot = here ^ piece
+                mine = (near_ref, far_ref)[slot >> 1]
+                theirs = (their_near_ref, their_far_ref)[slot >> 1]
+                for start, half_ref in ((own, mine), (other, theirs)):
                     matrix_ref[pl.ds(start + pair * ROWS, ROWS), lanes(tile)] = half_ref[
-                        (here - piece) & 3, :, lanes(place)
+                        slot & 1, :, lanes(place)
                     ]
 
     upstream_ref[...] = dot(channels_ref[...], matrix_ref[...], 1, 0).astype(BF16)
@@ -285,6 +292,10 @@
 
 def turn(value, axis, step):
     return lax.ppermute(value, axis, [(place, (place + step) % 4) for place in range(4)])
+
+
+def across(value, bit):
+    return lax.ppermute(value, "x", [(place, place ^ bit) for place in range(4)])
 
 
 def on_device(query_key_value, out_weight, cotangent):
@@ -319,22 +330,20 @@
         micros=3,
     )
     piece = sent[:, :, BASE:].reshape(ROWS, PIECE)
-    turned = [turn(piece, "x", step) for step in range(1, 4)]
-    (partial,) = call(
+    partial, pieces = call(
         weight_grad_kernel,
         "weight_grad",
-        (share, swap(share), columns),
-        [IN_VMEM] * 3,
-        [((64, 2, HALF_WIDTH), BF16)],
-    )
+        (share, swap(share), columns, piece, across(piece, 1)),
+        [IN_VMEM] * 5,
+        [((64, 2, HALF_WIDTH), BF16), ((2, ROWS, PIECE), BF16)],
+    )
+    far_pieces = across(pieces, 2)
     collected = exchange(partial, SEQ)
-    piece, *turned = lax.optimization_barrier((piece, *turned, partial))[:4]
-    mine = jnp.stack([piece, *turned])
     (results,) = call(
         backward_kernel,
         "backward",
-        (core, x_place, sent, mine, swap(mine)),
-        [IN_SMEM] * 2 + [IN_VMEM] * 3,
+        (core, x_place, sent, pieces, far_pieces, swap(pieces), swap(far_pieces)),
+        [IN_SMEM] * 2 + [IN_VMEM] * 5,
         [((64, 2, BASE), BF16)],
         [
             pltpu.VMEM((ROWS, COLS), BF16),
@@ -345,7 +354,7 @@
             pltpu.VMEM((ROWS, WIDTH), BF16),
             pltpu.VMEM((HEADS, ROWS, ROWS), BF16),
         ],
-        micros=7,
+        micros=10,
     )
     results, collected = lax.optimization_barrier((results, collected))
     (owned,) = call(owned_kernel, "owned", (collected,), [IN_VMEM], [((2, HALF_WIDTH), F32)])

time: 157 us -> 160 us (1.019)
  waiting for transfers between devices: 45.1 us -> 52.3 us
  starting transfers between devices: 35.5 us -> 32.9 us
    ppermute x0 -> x2, waiting for transfers between devices: none -> 15.5 us  [across(): lax.ppermute(value, 'x', [(place, place ^ bit) for place in range(4)])]
    ppermute x6 -> x3, starting transfers between devices: 17.5 us -> 8.48 us  [turn(): lax.ppermute(value, axis, [(place, (place + step) % 4) for place in range...]
    all_to_all x2, waiting for transfers between devices: 25 us -> 18.6 us  [exchange(): return lax.all_to_all(value, axes, 0, 0, tiled=True)]
    ppermute x0 -> x2, starting transfers between devices: none -> 3.84 us  [across(): lax.ppermute(value, 'x', [(place, place ^ bit) for place in range(4)])]
    ppermute x3 -> x4, starting transfers between devices: 5.77 us -> 7.68 us  [swap(): return lax.ppermute(value, 'c', [(0, 1), (1, 0)])]
    ppermute x6 -> x3, waiting for transfers between devices: 16.4 us -> 15.2 us  [turn(): lax.ppermute(value, axis, [(place, (place + step) % 4) for place in range...]
    ppermute x3 -> x4, waiting for transfers between devices: 3.73 us -> 3.06 us  [swap(): return lax.ppermute(value, 'c', [(0, 1), (1, 0)])]
  transfers between devices with their start and end apart: 11 -> 11, of which waited for: 6 -> 7; matrix products, arithmetic and copies ran while one was open for 1% -> 0% of each run, Pallas kernels for 6% -> 5%
where the time goes in v12:
time: 160 us; the launch traced here: 159 us
  blocking collectives  59 us (37%)
  waiting for transfers between devices  52.3 us (33%)
  starting transfers between devices  32.9 us (21%)
  Pallas kernels  14 us (9%)
    all_to_all x1, blocking collectives, exchange(): return lax.all_to_all(value, axes, 0, 0, tiled=True)  59 us
    all_to_all x2, waiting for transfers between devices, exchange(): return lax.all_to_all(value, axes, 0, 0, tiled=True)  18.6 us
    ppermute x2, waiting for transfers between devices, across(): lax.ppermute(value, 'x', [(place, place ^ bit) for place in range(4)])  15.5 us
    ppermute x3, waiting for transfers between devices, turn(): lax.ppermute(value, axis, [(place, (place + step) % 4) for place in range...  15.2 us
    pallas_call x8, Pallas kernels, call(): pl.pallas_call(kernel, out_shape=[jax.ShapeDtypeStruct(shape, dtype) for...  14 us
    all_to_all x2, starting transfers between devices, exchange(): return lax.all_to_all(value, axes, 0, 0, tiled=True)  12.9 us
    ppermute x3, starting transfers between devices, turn(): lax.ppermute(value, axis, [(place, (place + step) % 4) for place in range...  8.48 us
    ppermute x4, starting transfers between devices, swap(): return lax.ppermute(value, 'c', [(0, 1), (1, 0)])  7.68 us
  transfers between devices with their start and end apart: 11, of which 7 were waited for; matrix products, arithmetic and copies ran while one was open for 0% of the time, Pallas kernels for 5%

profile of v12, /device:TPU:14, one launch (start us, length us, event | category | flops | bytes accessed | tf_op | source)
XLA Modules:
  0.0 159.2 jit_solution(8159245274736925681)
XLA Ops:
  0.6 2.8 %pack.1 = bf16[64,2,5120]{2,1,0:T(2,128)(2,1)} custom-call(s32[1]{0:T(128)} %bitcast.core_ref, bf16[3,128,1152]{2,1,0:T(8,128)(2,1)} %bitcast.8, bf16[128,768]{1,0:T(8,128)(2,1)} %bitcast.9, bf16[12,1152]{1,0:T(8,128)(2,1)} %weight_hbm.1), custom_call_target="tpu_custom_call" | custom-call | flops 1000000000 | bytes 3000000 | tf_op jit(solution)/shard_map/pack/pallas_call | solution.py:271
  3.5 59.0 %all_to_all.15.sent_ref = bf16[64,2,5120]{2,1,0:T(2,128)(2,1)S(1)} all-to-all(bf16[64,2,5120]{2,1,0:T(2,128)(2,1)} %pack.1), channel_id=1, replica_groups=mesh['yl'=4,'c'=2,'yh'=2,'x'=4,'z'=8] {'yh','x','z'}, dimensions={0} | all-to-all | bytes 2621440 | tf_op jit(solution)/shard_map/all_to_all | solution.py:286
  62.5 1.3 forward.1
  63.8 1.9 %collective-permute-start = (bf16[128,1536]{1,0:T(8,128)(2,1)S(1)}, bf16[128,1536]{1,0:T(8,128)(2,1)S(1)}, u32[]{:S(2)}, u32[]{:S(2)}) collective-permute-start(bf16[128,1536]{1,0:T(8,128)(2,1)S(1)} %get-tuple-element.11.share_ref), channel_id=1, source_target_pairs={{0,64},{64,0},{1,65},{65,1},{2,66},{66,2},{3,67},{67,3},{4,68},{68... | collective-permute-start | bytes 1179656 | tf_op jit(solution)/shard_map/ppermute | solution.py:290
  65.7 0.2 slice.4
  65.9 0.1 reshape.31.piece_ref
  66.0 1.9 %collective-permute-start.1 = (bf16[128,896]{1,0:T(8,128)(2,1)S(1)}, bf16[128,896]{1,0:T(8,128)(2,1)S(1)}, u32[]{:S(2)}, u32[]{:S(2)}) collective-permute-start(bf16[128,896]{1,0:T(8,128)(2,1)S(1)} %reshape.31.piece_ref), channel_id=1, source_target_pairs={{0,8},{8,0},{16,24},{24,16},{1,9},{9,1},{17,25},{25,17},{2,10},{10... | collective-permute-start | bytes 688136 | tf_op jit(solution)/shard_map/ppermute | solution.py:298
  67.9 8.0 %collective-permute-done.1.near_ref = bf16[128,896]{1,0:T(8,128)(2,1)S(1)} collective-permute-done((bf16[128,896]{1,0:T(8,128)(2,1)S(1)}, bf16[128,896]{1,0:T(8,128)(2,1)S(1)}, u32[]{:S(2)}, u32[]{:S(2)}) %collective-permute-start.1) | collective-permute-done | bytes 229408 | tf_op jit(solution)/shard_map/ppermute | solution.py:298
  75.9 0.0 collective-permute-done.received_ref
  75.9 1.4 weight_grad.1
  77.3 1.9 %collective-permute-start.2 = (bf16[2,128,896]{2,1,0:T(8,128)(2,1)S(1)}, bf16[2,128,896]{2,1,0:T(8,128)(2,1)S(1)}, u32[]{:S(2)}, u32[]{:S(2)}) collective-permute-start(bf16[2,128,896]{2,1,0:T(8,128)(2,1)S(1)} %get-tuple-element.13.near_ref), channel_id=1, source_target_pairs={{0,16},{8,24},{16,0},{24,8},{1,17},{9,25},{17,1},{25,9},{2,18},{10... | collective-permute-start | bytes 1376264 | tf_op jit(solution)/shard_map/ppermute | solution.py:298
  79.3 7.8 %all-to-all-start.1 = ((bf16[64,2,3456]{2,1,0:T(2,128)(2,1)}), bf16[64,2,3456]{2,1,0:T(2,128)(2,1)S(1)}, u32[]{:S(2)}, u32[]{:S(2)}) async-start(bf16[64,2,3456]{2,1,0:T(2,128)(2,1)} %get-tuple-element.14), calls=%async_computation.1 | async-start | bytes 1769472 | tf_op jit(solution)/shard_map/all_to_all | solution.py:286
  87.1 1.9 %collective-permute-start.3 = (bf16[2,128,896]{2,1,0:T(8,128)(2,1)S(1)}, bf16[2,128,896]{2,1,0:T(8,128)(2,1)}, u32[]{:S(2)}, u32[]{:S(2)}) collective-permute-start(bf16[2,128,896]{2,1,0:T(8,128)(2,1)S(1)} %get-tuple-element.13.near_ref), channel_id=1, source_target_pairs={{0,64},{64,0},{1,65},{65,1},{2,66},{66,2},{3,67},{67,3},{4,68},{68... | collective-permute-start | bytes 1376264 | tf_op jit(solution)/shard_map/ppermute | solution.py:290
  89.0 7.5 %collective-permute-done.2.far_ref = bf16[2,128,896]{2,1,0:T(8,128)(2,1)S(1)} collective-permute-done((bf16[2,128,896]{2,1,0:T(8,128)(2,1)S(1)}, bf16[2,128,896]{2,1,0:T(8,128)(2,1)S(1)}, u32[]{:S(2)}, u32[]{:S(2)}) %collective-permute-start.2) | collective-permute-done | bytes 458784 | tf_op jit(solution)/shard_map/ppermute | solution.py:298
  96.5 1.9 %collective-permute-start.4 = (bf16[2,128,896]{2,1,0:T(8,128)(2,1)S(1)}, bf16[2,128,896]{2,1,0:T(8,128)(2,1)}, u32[]{:S(2)}, u32[]{:S(2)}) collective-permute-start(bf16[2,128,896]{2,1,0:T(8,128)(2,1)S(1)} %collective-permute-done.2.far_ref), channel_id=1, source_target_pairs={{0,64},{64,0},{1,65},{65,1},{2,66},{66,2},{3,67},{67,3},{4,68},{68... | collective-permute-start | bytes 1376264 | tf_op jit(solution)/shard_map/ppermute | solution.py:290
  98.4 0.0 collective-permute-done.3.their_near_ref
  98.4 1.9 %collective-permute-done.4.their_far_ref = bf16[2,128,896]{2,1,0:T(8,128)(2,1)} collective-permute-done((bf16[2,128,896]{2,1,0:T(8,128)(2,1)S(1)}, bf16[2,128,896]{2,1,0:T(8,128)(2,1)}, u32[]{:S(2)}, u32[]{:S(2)}) %collective-permute-start.4) | collective-permute-done | bytes 458784 | tf_op jit(solution)/shard_map/ppermute | solution.py:290
  100.3 6.4 %backward.1 = bf16[64,2,4224]{2,1,0:T(2,128)(2,1)} custom-call(s32[1]{0:T(128)} %bitcast.core_ref, s32[1]{0:T(128)} %bitcast.1.x_ref, bf16[64,2,5120]{2,1,0:T(2,128)(2,1)S(1)} %all_to_all.15.sent_ref, bf16[2,128,896]{2,1,0:T(8,128)(2,1)S(1)} %get-tuple-element.13.near_ref, bf16[2,128,896]{2,1,0:T(8,128)(2,1)S(1)} %collective-permute-done.2.far_ref, ...), custom_call_target="tpu_custom_call" | custom-call | flops 10000000000 | bytes 30000000 | tf_op jit(solution)/shard_map/backward/pallas_call | solution.py:271
  106.7 11.0 %all-to-all-done.1.terms_ref = bf16[64,2,3456]{2,1,0:T(2,128)(2,1)S(1)} async-done(((bf16[64,2,3456]{2,1,0:T(2,128)(2,1)}), bf16[64,2,3456]{2,1,0:T(2,128)(2,1)S(1)}, u32[]{:S(2)}, u32[]{:S(2)}) %all-to-all-start.1) | async-done | bytes 884768 | tf_op jit(solution)/shard_map/all_to_all | solution.py:286
  117.8 5.1 %all-to-all-start.2 = ((bf16[64,2,4224]{2,1,0:T(2,128)(2,1)}), bf16[64,2,4224]{2,1,0:T(2,128)(2,1)S(1)}, u32[]{:S(2)}, u32[]{:S(2)}) async-start(bf16[64,2,4224]{2,1,0:T(2,128)(2,1)} %backward.1), calls=%async_computation.2 | async-start | bytes 2162688 | tf_op jit(solution)/shard_map/all_to_all | solution.py:286
  122.9 0.2 owned.1.refs_0_
  123.1 1.9 %collective-permute-start.7 = (f32[2,3456]{1,0:T(2,128)S(1)}, f32[2,3456]{1,0:T(2,128)S(1)}, u32[]{:S(2)}, u32[]{:S(2)}) collective-permute-start(f32[2,3456]{1,0:T(2,128)S(1)} %owned.1.refs_0_), channel_id=1, source_target_pairs={{0,384},{128,0},{256,128},{384,256},{1,385},{129,1},{257,129},{385... | collective-permute-start | bytes 82952 | tf_op jit(solution)/shard_map/ppermute | solution.py:294
  125.1 3.1 %collective-permute-start.6 = (f32[2,3456]{1,0:T(2,128)S(1)}, f32[2,3456]{1,0:T(2,128)S(1)}, u32[]{:S(2)}, u32[]{:S(2)}) collective-permute-start(f32[2,3456]{1,0:T(2,128)S(1)} %owned.1.refs_0_), channel_id=1, source_target_pairs={{0,256},{128,384},{256,0},{384,128},{1,257},{129,385},{257,1},{385... | collective-permute-start | bytes 82952 | tf_op jit(solution)/shard_map/ppermute | solution.py:294
  128.1 3.5 %collective-permute-start.5 = (f32[2,3456]{1,0:T(2,128)S(1)}, f32[2,3456]{1,0:T(2,128)S(1)}, u32[]{:S(2)}, u32[]{:S(2)}) collective-permute-start(f32[2,3456]{1,0:T(2,128)S(1)} %owned.1.refs_0_), channel_id=1, source_target_pairs={{0,128},{128,256},{256,384},{384,0},{1,129},{129,257},{257,385},{3... | collective-permute-start | bytes 82952 | tf_op jit(solution)/shard_map/ppermute | solution.py:294
  131.6 15.2 %collective-permute-done.7.refs_3_ = f32[2,3456]{1,0:T(2,128)S(1)} collective-permute-done((f32[2,3456]{1,0:T(2,128)S(1)}, f32[2,3456]{1,0:T(2,128)S(1)}, u32[]{:S(2)}, u32[]{:S(2)}) %collective-permute-start.7) | collective-permute-done | bytes 27680 | tf_op jit(solution)/shard_map/ppermute | solution.py:294
  146.8 0.0 collective-permute-done.6.refs_2_
  146.8 0.0 collective-permute-done.5.refs_1_
  146.8 1.9 %collective-permute-start.8 = (f32[2,3456]{1,0:T(2,128)S(1)}, f32[2,3456]{1,0:T(2,128)S(1)}, u32[]{:S(2)}, u32[]{:S(2)}) collective-permute-start(f32[2,3456]{1,0:T(2,128)S(1)} %group.1.mine_ref), channel_id=1, source_target_pairs={{0,64},{64,0},{1,65},{65,1},{2,66},{66,2},{3,67},{67,3},{4,68},{68... | collective-permute-start | bytes 82952 | tf_op jit(solution)/shard_map/ppermute | solution.py:290
  148.7 1.2 collective-permute-done.8.theirs_ref
  149.9 0.7 total.1
  150.6 7.5 %all-to-all-done.2.back_ref = bf16[64,2,4224]{2,1,0:T(2,128)(2,1)S(1)} async-done(((bf16[64,2,4224]{2,1,0:T(2,128)(2,1)}), bf16[64,2,4224]{2,1,0:T(2,128)(2,1)S(1)}, u32[]{:S(2)}, u32[]{:S(2)}) %all-to-all-start.2) | async-done | bytes 1081376 | tf_op jit(solution)/shard_map/all_to_all | solution.py:286
  158.1 1.1 unpack.1
  (1 shorter events, 0.0 us)
Async XLA Ops:
  63.8 12.1 %collective-permute-start = (bf16[128,1536]{1,0:T(8,128)(2,1)S(1)}, bf16[128,1536]{1,0:T(8,128)(2,1)S(1)}, u32[]{:S(2)}, u32[]{:S(2)}) collective-permute-start(bf16[128,1536]{1,0:T(8,128)(2,1)S(1)} %get-tuple-element.11.share_ref), channel_id=1, source_target_pairs={{0,64},{64,0},{1,65},{65,1},{2,66},{66,2},{3,67},{67,3},{4,68},{68... | collective-permute-start | bytes 1179656 | tf_op jit(solution)/shard_map/ppermute | solution.py:290
  66.0 9.9 %collective-permute-start.1 = (bf16[128,896]{1,0:T(8,128)(2,1)S(1)}, bf16[128,896]{1,0:T(8,128)(2,1)S(1)}, u32[]{:S(2)}, u32[]{:S(2)}) collective-permute-start(bf16[128,896]{1,0:T(8,128)(2,1)S(1)} %reshape.31.piece_ref), channel_id=1, source_target_pairs={{0,8},{8,0},{16,24},{24,16},{1,9},{9,1},{17,25},{25,17},{2,10},{10... | collective-permute-start | bytes 688136 | tf_op jit(solution)/shard_map/ppermute | solution.py:298
  77.3 19.2 %collective-permute-start.2 = (bf16[2,128,896]{2,1,0:T(8,128)(2,1)S(1)}, bf16[2,128,896]{2,1,0:T(8,128)(2,1)S(1)}, u32[]{:S(2)}, u32[]{:S(2)}) collective-permute-start(bf16[2,128,896]{2,1,0:T(8,128)(2,1)S(1)} %get-tuple-element.13.near_ref), channel_id=1, source_target_pairs={{0,16},{8,24},{16,0},{24,8},{1,17},{9,25},{17,1},{25,9},{2,18},{10... | collective-permute-start | bytes 1376264 | tf_op jit(solution)/shard_map/ppermute | solution.py:298
  79.3 38.5 %all-to-all-start.1 = ((bf16[64,2,3456]{2,1,0:T(2,128)(2,1)}), bf16[64,2,3456]{2,1,0:T(2,128)(2,1)S(1)}, u32[]{:S(2)}, u32[]{:S(2)}) async-start(bf16[64,2,3456]{2,1,0:T(2,128)(2,1)} %get-tuple-element.14), calls=%async_computation.1 | async-start | bytes 1769472 | tf_op jit(solution)/shard_map/all_to_all | solution.py:286
  87.1 11.4 %collective-permute-start.3 = (bf16[2,128,896]{2,1,0:T(8,128)(2,1)S(1)}, bf16[2,128,896]{2,1,0:T(8,128)(2,1)}, u32[]{:S(2)}, u32[]{:S(2)}) collective-permute-start(bf16[2,128,896]{2,1,0:T(8,128)(2,1)S(1)} %get-tuple-element.13.near_ref), channel_id=1, source_target_pairs={{0,64},{64,0},{1,65},{65,1},{2,66},{66,2},{3,67},{67,3},{4,68},{68... | collective-permute-start | bytes 1376264 | tf_op jit(solution)/shard_map/ppermute | solution.py:290
  96.5 3.8 %collective-permute-start.4 = (bf16[2,128,896]{2,1,0:T(8,128)(2,1)S(1)}, bf16[2,128,896]{2,1,0:T(8,128)(2,1)}, u32[]{:S(2)}, u32[]{:S(2)}) collective-permute-start(bf16[2,128,896]{2,1,0:T(8,128)(2,1)S(1)} %collective-permute-done.2.far_ref), channel_id=1, source_target_pairs={{0,64},{64,0},{1,65},{65,1},{2,66},{66,2},{3,67},{67,3},{4,68},{68... | collective-permute-start | bytes 1376264 | tf_op jit(solution)/shard_map/ppermute | solution.py:290
  117.8 40.3 %all-to-all-start.2 = ((bf16[64,2,4224]{2,1,0:T(2,128)(2,1)}), bf16[64,2,4224]{2,1,0:T(2,128)(2,1)S(1)}, u32[]{:S(2)}, u32[]{:S(2)}) async-start(bf16[64,2,4224]{2,1,0:T(2,128)(2,1)} %backward.1), calls=%async_computation.2 | async-start | bytes 2162688 | tf_op jit(solution)/shard_map/all_to_all | solution.py:286
  123.1 23.7 %collective-permute-start.7 = (f32[2,3456]{1,0:T(2,128)S(1)}, f32[2,3456]{1,0:T(2,128)S(1)}, u32[]{:S(2)}, u32[]{:S(2)}) collective-permute-start(f32[2,3456]{1,0:T(2,128)S(1)} %owned.1.refs_0_), channel_id=1, source_target_pairs={{0,384},{128,0},{256,128},{384,256},{1,385},{129,1},{257,129},{385... | collective-permute-start | bytes 82952 | tf_op jit(solution)/shard_map/ppermute | solution.py:294
  125.1 21.7 %collective-permute-start.6 = (f32[2,3456]{1,0:T(2,128)S(1)}, f32[2,3456]{1,0:T(2,128)S(1)}, u32[]{:S(2)}, u32[]{:S(2)}) collective-permute-start(f32[2,3456]{1,0:T(2,128)S(1)} %owned.1.refs_0_), channel_id=1, source_target_pairs={{0,256},{128,384},{256,0},{384,128},{1,257},{129,385},{257,1},{385... | collective-permute-start | bytes 82952 | tf_op jit(solution)/shard_map/ppermute | solution.py:294
  128.1 18.7 %collective-permute-start.5 = (f32[2,3456]{1,0:T(2,128)S(1)}, f32[2,3456]{1,0:T(2,128)S(1)}, u32[]{:S(2)}, u32[]{:S(2)}) collective-permute-start(f32[2,3456]{1,0:T(2,128)S(1)} %owned.1.refs_0_), channel_id=1, source_target_pairs={{0,128},{128,256},{256,384},{384,0},{1,129},{129,257},{257,385},{3... | collective-permute-start | bytes 82952 | tf_op jit(solution)/shard_map/ppermute | solution.py:294
  146.8 3.1 %collective-permute-start.8 = (f32[2,3456]{1,0:T(2,128)S(1)}, f32[2,3456]{1,0:T(2,128)S(1)}, u32[]{:S(2)}, u32[]{:S(2)}) collective-permute-start(f32[2,3456]{1,0:T(2,128)S(1)} %group.1.mine_ref), channel_id=1, source_target_pairs={{0,64},{64,0},{1,65},{65,1},{2,66},{66,2},{3,67},{67,3},{4,68},{68... | collective-permute-start | bytes 82952 | tf_op jit(solution)/shard_map/ppermute | solution.py:290

commit v13 on v9

--- a/solution.py
+++ b/solution.py
@@ -168,11 +168,12 @@
                 ] = partial[start : start + 16]
 
 
-def backward_kernel(
-    core_ref, sent_ref, mine_ref, theirs_ref,
-    out_ref, rows_ref, weights_ref, channels_ref, attended_ref, matrix_ref, upstream_ref,
-    grad_scores_ref,
-):
+def backward_kernel(core_ref, x_ref, sent_ref, *refs):
+    mine_refs, their_refs, refs = refs[:4], refs[4:8], refs[8:]
+    (
+        out_ref, rows_ref, weights_ref, channels_ref, attended_ref, matrix_ref, upstream_ref,
+        grad_scores_ref,
+    ) = refs
     rows_ref[...] = sent_ref[...].reshape(ROWS, COLS)
     channels_ref[...] = ordered_channels(rows_ref)
 
@@ -182,11 +183,16 @@
     attend(rows_ref, weights_ref, put_attended)
     own = pl.multiple_of(core_ref[0] * HALF, HALF)
     other = pl.multiple_of((1 - core_ref[0]) * HALF, HALF)
-    for piece, place, pair, tile in half_tiles():
-        for start, half_ref in ((own, mine_ref), (other, theirs_ref)):
-            matrix_ref[pl.ds(start + pair * ROWS, ROWS), lanes(tile)] = half_ref[
-                piece, :, lanes(place)
-            ]
+    for here in range(4):
+
+        @pl.when(x_ref[0] == here)
+        def _():
+            for piece, place, pair, tile in half_tiles():
+                for start, half_refs in ((own, mine_refs), (other, their_refs)):
+                    matrix_ref[pl.ds(start + pair * ROWS, ROWS), lanes(tile)] = half_refs[
+                        (here - piece) & 3
+                    ][:, lanes(place)]
+
     upstream_ref[...] = dot(channels_ref[...], matrix_ref[...], 1, 0).astype(BF16)
     products = [
         head_products(upstream_ref, 0, rows_ref, 2 * WIDTH, index) for index in range(HEADS)
@@ -294,6 +300,7 @@
 
 def on_device(query_key_value, out_weight, cotangent):
     core = lax.axis_index("c").astype(jnp.int32).reshape(1)
+    x_place = lax.axis_index("x").astype(jnp.int32).reshape(1)
     (packed,) = call(
         pack_kernel,
         "pack",
@@ -309,8 +316,6 @@
         grant=56,
     )
     sent = exchange(packed, SEQ)
-    piece = sent[:, :, BASE:].reshape(1, ROWS, PIECE)
-    mine = exchange(jnp.broadcast_to(piece, (4, ROWS, PIECE)), "x")
     share, columns = call(
         forward_kernel,
         "forward",
@@ -331,13 +336,19 @@
         [IN_VMEM] * 3,
         [((4, 32, HALF_WIDTH), BF16)],
     )
-    mine, partial = lax.optimization_barrier((mine, partial))
+    piece, partial = lax.optimization_barrier((sent[:, :, BASE:].reshape(ROWS, PIECE), partial))
     terms = exchange(partial, "x")
+    turned = [turn(piece, "x", step) for step in range(1, 4)]
+    (summed,) = call(
+        merge_kernel, "merge", (terms,), [IN_VMEM], [((16, 2, HALF_WIDTH), BF16)]
+    )
+    collected = exchange(summed, ("yh", "z"))
+    mine = [piece, *lax.optimization_barrier((*turned, summed))[:3]]
     (results,) = call(
         backward_kernel,
         "backward",
-        (core, sent, mine, swap(mine)),
-        [IN_SMEM] + [IN_VMEM] * 3,
+        (core, x_place, sent, *mine, *(swap(part) for part in mine)),
+        [IN_SMEM] * 2 + [IN_VMEM] * 9,
         [((64, 2, BASE), BF16)],
         [
             pltpu.VMEM((ROWS, COLS), BF16),
@@ -348,13 +359,8 @@
             pltpu.VMEM((ROWS, WIDTH), BF16),
             pltpu.VMEM((HEADS, ROWS, ROWS), BF16),
         ],
-        micros=4,
-    )
-    results, terms = lax.optimization_barrier((results, terms))
-    (summed,) = call(
-        merge_kernel, "merge", (terms,), [IN_VMEM], [((16, 2, HALF_WIDTH), BF16)]
-    )
-    collected = exchange(summed, ("yh", "z"))
+        micros=0,
+    )
     results, collected = lax.optimization_barrier((results, collected))
     (owned,) = call(owned_kernel, "owned", (collected,), [IN_VMEM], [((2, HALF_WIDTH), F32)])
     turned = [turn(owned, "yl", step) for step in range(1, 4)]

time: 160 us -> 162 us (1.012)
  starting transfers between devices: 31.2 us -> 55.9 us
  blocking collectives: 76 us -> 59 us
  waiting for transfers between devices: 36.3 us -> 30.9 us
    all_to_all x2 -> x1, blocking collectives: 76 us -> 59 us  [exchange(): return lax.all_to_all(value, axes, 0, 0, tiled=True)]
    ppermute x3 -> x6, starting transfers between devices: 7.86 us -> 18.9 us  [turn(): lax.ppermute(value, axis, [(place, (place + step) % 4) for place in range...]
    all_to_all x3, waiting for transfers between devices: 18.2 us -> 10.5 us  [exchange(): return lax.all_to_all(value, axes, 0, 0, tiled=True)]
    all_to_all x3, starting transfers between devices: 17.6 us -> 25 us  [exchange(): return lax.all_to_all(value, axes, 0, 0, tiled=True)]
    ppermute x3 -> x6, starting transfers between devices: 5.76 us -> 12 us  [swap(): return lax.ppermute(value, 'c', [(0, 1), (1, 0)])]
    ppermute x3 -> x6, waiting for transfers between devices: 15.2 us -> 16.4 us  [turn(): lax.ppermute(value, axis, [(place, (place + step) % 4) for place in range...]
    ppermute x3 -> x6, waiting for transfers between devices: 2.85 us -> 4 us  [swap(): return lax.ppermute(value, 'c', [(0, 1), (1, 0)])]
  transfers between devices with their start and end apart: 9 -> 15, of which waited for: 6 -> 7; matrix products, arithmetic and copies ran while one was open for 0% -> 0% of each run, Pallas kernels for 6% -> 5%
where the time goes in v13:
time: 162 us; the launch traced here: 161 us
  blocking collectives  59 us (36%)
  starting transfers between devices  55.9 us (35%)
  waiting for transfers between devices  30.9 us (19%)
  Pallas kernels  14.5 us (9%)
    all_to_all x1, blocking collectives, exchange(): return lax.all_to_all(value, axes, 0, 0, tiled=True)  59 us
    all_to_all x3, starting transfers between devices, exchange(): return lax.all_to_all(value, axes, 0, 0, tiled=True)  25 us
    ppermute x6, starting transfers between devices, turn(): lax.ppermute(value, axis, [(place, (place + step) % 4) for place in range...  18.9 us
    ppermute x6, waiting for transfers between devices, turn(): lax.ppermute(value, axis, [(place, (place + step) % 4) for place in range...  16.4 us
    pallas_call x9, Pallas kernels, call(): pl.pallas_call(kernel, out_shape=[jax.ShapeDtypeStruct(shape, dtype) for...  14.5 us
    ppermute x6, starting transfers between devices, swap(): return lax.ppermute(value, 'c', [(0, 1), (1, 0)])  12 us
    all_to_all x3, waiting for transfers between devices, exchange(): return lax.all_to_all(value, axes, 0, 0, tiled=True)  10.5 us
    ppermute x6, waiting for transfers between devices, swap(): return lax.ppermute(value, 'c', [(0, 1), (1, 0)])  4 us
  transfers between devices with their start and end apart: 15, of which 7 were waited for; matrix products, arithmetic and copies ran while one was open for 0% of the time, Pallas kernels for 5%

profile of v13, /device:TPU:14, one launch (start us, length us, event | category | flops | bytes accessed | tf_op | source)
XLA Modules:
  0.0 161.4 jit_solution(16723696992521742208)
XLA Ops:
  0.6 2.9 %pack.1 = bf16[64,2,5120]{2,1,0:T(2,128)(2,1)} custom-call(s32[1]{0:T(128)} %bitcast.core_ref, bf16[3,128,1152]{2,1,0:T(8,128)(2,1)} %bitcast.8, bf16[128,768]{1,0:T(8,128)(2,1)} %bitcast.9, bf16[12,1152]{1,0:T(8,128)(2,1)} %weight_hbm.1), custom_call_target="tpu_custom_call" | custom-call | flops 1000000000 | bytes 3000000 | tf_op jit(solution)/shard_map/pack/pallas_call | solution.py:275
  3.5 59.0 %all_to_all.20.sent_ref = bf16[64,2,5120]{2,1,0:T(2,128)(2,1)S(1)} all-to-all(bf16[64,2,5120]{2,1,0:T(2,128)(2,1)} %pack.1), channel_id=1, replica_groups=mesh['yl'=4,'c'=2,'yh'=2,'x'=4,'z'=8] {'yh','x','z'}, dimensions={0} | all-to-all | bytes 2621440 | tf_op jit(solution)/shard_map/all_to_all | solution.py:290
  62.5 1.3 forward.1
  63.8 1.9 %collective-permute-start = (bf16[128,1536]{1,0:T(8,128)(2,1)S(1)}, bf16[128,1536]{1,0:T(8,128)(2,1)S(1)}, u32[]{:S(2)}, u32[]{:S(2)}) collective-permute-start(bf16[128,1536]{1,0:T(8,128)(2,1)S(1)} %get-tuple-element.14.share_ref), channel_id=1, source_target_pairs={{0,64},{64,0},{1,65},{65,1},{2,66},{66,2},{3,67},{67,3},{4,68},{68... | collective-permute-start | bytes 1179656 | tf_op jit(solution)/shard_map/ppermute | solution.py:294
  65.7 0.2 slice.4
  65.9 0.1 reshape.31.refs_0_
  66.0 1.4 collective-permute-done.received_ref
  67.4 1.4 weight_grad.1
  68.8 4.5 %all-to-all-start.1 = ((bf16[4,32,3456]{2,1,0:T(8,128)(2,1)}), bf16[4,32,3456]{2,1,0:T(8,128)(2,1)S(1)}, u32[]{:S(2)}, u32[]{:S(2)}) async-start(bf16[4,32,3456]{2,1,0:T(8,128)(2,1)} %weight_grad.1), calls=%async_computation.1 | async-start | bytes 1769472 | tf_op jit(solution)/shard_map/all_to_all | solution.py:290
  73.3 2.8 %collective-permute-start.3 = (bf16[128,896]{1,0:T(8,128)(2,1)S(1)}, bf16[128,896]{1,0:T(8,128)(2,1)S(1)}, u32[]{:S(2)}, u32[]{:S(2)}) collective-permute-start(bf16[128,896]{1,0:T(8,128)(2,1)S(1)} %reshape.31.refs_0_), channel_id=1, source_target_pairs={{0,24},{8,0},{16,8},{24,16},{1,25},{9,1},{17,9},{25,17},{2,26},{10... | collective-permute-start | bytes 688136 | tf_op jit(solution)/shard_map/ppermute | solution.py:298
  76.1 2.5 %collective-permute-start.2 = (bf16[128,896]{1,0:T(8,128)(2,1)S(1)}, bf16[128,896]{1,0:T(8,128)(2,1)S(1)}, u32[]{:S(2)}, u32[]{:S(2)}) collective-permute-start(bf16[128,896]{1,0:T(8,128)(2,1)S(1)} %reshape.31.refs_0_), channel_id=1, source_target_pairs={{0,16},{8,24},{16,0},{24,8},{1,17},{9,25},{17,1},{25,9},{2,18},{10... | collective-permute-start | bytes 688136 | tf_op jit(solution)/shard_map/ppermute | solution.py:298
  78.6 4.5 %collective-permute-start.1 = (bf16[128,896]{1,0:T(8,128)(2,1)S(1)}, bf16[128,896]{1,0:T(8,128)(2,1)S(1)}, u32[]{:S(2)}, u32[]{:S(2)}) collective-permute-start(bf16[128,896]{1,0:T(8,128)(2,1)S(1)} %reshape.31.refs_0_), channel_id=1, source_target_pairs={{0,8},{8,16},{16,24},{24,0},{1,9},{9,17},{17,25},{25,1},{2,10},{10... | collective-permute-start | bytes 688136 | tf_op jit(solution)/shard_map/ppermute | solution.py:298
  83.1 2.9 %all-to-all-done.1.terms_ref = bf16[4,32,3456]{2,1,0:T(8,128)(2,1)S(1)} async-done(((bf16[4,32,3456]{2,1,0:T(8,128)(2,1)}), bf16[4,32,3456]{2,1,0:T(8,128)(2,1)S(1)}, u32[]{:S(2)}, u32[]{:S(2)}) %all-to-all-start.1) | async-done | bytes 884768 | tf_op jit(solution)/shard_map/all_to_all | solution.py:290
  86.1 0.8 merge.1
  86.9 4.2 %all-to-all-start.2 = ((bf16[16,2,3456]{2,1,0:T(2,128)(2,1)}), bf16[16,2,3456]{2,1,0:T(2,128)(2,1)}, u32[]{:S(2)}, u32[]{:S(2)}) async-start(bf16[16,2,3456]{2,1,0:T(2,128)(2,1)} %merge.1), calls=%async_computation.2 | async-start | bytes 442368 | tf_op jit(solution)/shard_map/all_to_all | solution.py:290
  91.1 1.9 %collective-permute-start.4 = (bf16[128,896]{1,0:T(8,128)(2,1)S(1)}, bf16[128,896]{1,0:T(8,128)(2,1)S(1)}, u32[]{:S(2)}, u32[]{:S(2)}) collective-permute-start(bf16[128,896]{1,0:T(8,128)(2,1)S(1)} %reshape.31.refs_0_), channel_id=1, source_target_pairs={{0,64},{64,0},{1,65},{65,1},{2,66},{66,2},{3,67},{67,3},{4,68},{68... | collective-permute-start | bytes 688136 | tf_op jit(solution)/shard_map/ppermute | solution.py:294
  93.0 0.0 collective-permute-done.3.refs_3_
  93.0 1.7 %collective-permute-done.2.refs_2_ = bf16[128,896]{1,0:T(8,128)(2,1)S(1)} collective-permute-done((bf16[128,896]{1,0:T(8,128)(2,1)S(1)}, bf16[128,896]{1,0:T(8,128)(2,1)S(1)}, u32[]{:S(2)}, u32[]{:S(2)}) %collective-permute-start.2) | collective-permute-done | bytes 229408 | tf_op jit(solution)/shard_map/ppermute | solution.py:298
  94.8 0.0 collective-permute-done.1.refs_1_
  94.8 1.9 %collective-permute-start.5 = (bf16[128,896]{1,0:T(8,128)(2,1)S(1)}, bf16[128,896]{1,0:T(8,128)(2,1)S(1)}, u32[]{:S(2)}, u32[]{:S(2)}) collective-permute-start(bf16[128,896]{1,0:T(8,128)(2,1)S(1)} %collective-permute-done.1.refs_1_), channel_id=1, source_target_pairs={{0,64},{64,0},{1,65},{65,1},{2,66},{66,2},{3,67},{67,3},{4,68},{68... | collective-permute-start | bytes 688136 | tf_op jit(solution)/shard_map/ppermute | solution.py:294
  96.7 2.4 %collective-permute-start.6 = (bf16[128,896]{1,0:T(8,128)(2,1)S(1)}, bf16[128,896]{1,0:T(8,128)(2,1)S(1)}, u32[]{:S(2)}, u32[]{:S(2)}) collective-permute-start(bf16[128,896]{1,0:T(8,128)(2,1)S(1)} %collective-permute-done.2.refs_2_), channel_id=1, source_target_pairs={{0,64},{64,0},{1,65},{65,1},{2,66},{66,2},{3,67},{67,3},{4,68},{68... | collective-permute-start | bytes 688136 | tf_op jit(solution)/shard_map/ppermute | solution.py:294
  99.1 1.9 %collective-permute-start.7 = (bf16[128,896]{1,0:T(8,128)(2,1)S(1)}, bf16[128,896]{1,0:T(8,128)(2,1)S(1)}, u32[]{:S(2)}, u32[]{:S(2)}) collective-permute-start(bf16[128,896]{1,0:T(8,128)(2,1)S(1)} %collective-permute-done.3.refs_3_), channel_id=1, source_target_pairs={{0,64},{64,0},{1,65},{65,1},{2,66},{66,2},{3,67},{67,3},{4,68},{68... | collective-permute-start | bytes 688136 | tf_op jit(solution)/shard_map/ppermute | solution.py:294
  101.0 0.0 collective-permute-done.4.refs_4_
  101.0 0.0 collective-permute-done.5.refs_5_
  101.0 0.0 collective-permute-done.6.refs_6_
  101.1 1.4 collective-permute-done.7.refs_7_
  102.5 5.3 %backward.1 = bf16[64,2,4224]{2,1,0:T(2,128)(2,1)} custom-call(s32[1]{0:T(128)} %bitcast.core_ref, s32[1]{0:T(128)} %bitcast.1.x_ref, bf16[64,2,5120]{2,1,0:T(2,128)(2,1)S(1)} %all_to_all.20.sent_ref, bf16[128,896]{1,0:T(8,128)(2,1)S(1)} %reshape.31.refs_0_, bf16[128,896]{1,0:T(8,128)(2,1)S(1)} %collective-permute-done.1.refs_1_, ...), custom_call_target="tpu_custom_call" | custom-call | tf_op jit(solution)/shard_map/backward/pallas_call | solution.py:275
  107.7 0.0 all-to-all-done.2.terms_ref
  107.7 16.3 %all-to-all-start.3 = ((bf16[64,2,4224]{2,1,0:T(2,128)(2,1)}), bf16[64,2,4224]{2,1,0:T(2,128)(2,1)S(1)}, u32[]{:S(2)}, u32[]{:S(2)}) async-start(bf16[64,2,4224]{2,1,0:T(2,128)(2,1)} %backward.1), calls=%async_computation.3 | async-start | bytes 2162688 | tf_op jit(solution)/shard_map/all_to_all | solution.py:290
  124.0 1.1 owned.1.refs_0_
  125.1 1.9 %collective-permute-start.10 = (f32[2,3456]{1,0:T(2,128)S(1)}, f32[2,3456]{1,0:T(2,128)S(1)}, u32[]{:S(2)}, u32[]{:S(2)}) collective-permute-start(f32[2,3456]{1,0:T(2,128)S(1)} %owned.1.refs_0_), channel_id=1, source_target_pairs={{0,384},{128,0},{256,128},{384,256},{1,385},{129,1},{257,129},{385... | collective-permute-start | bytes 82952 | tf_op jit(solution)/shard_map/ppermute | solution.py:298
  127.1 3.2 %collective-permute-start.9 = (f32[2,3456]{1,0:T(2,128)S(1)}, f32[2,3456]{1,0:T(2,128)S(1)}, u32[]{:S(2)}, u32[]{:S(2)}) collective-permute-start(f32[2,3456]{1,0:T(2,128)S(1)} %owned.1.refs_0_), channel_id=1, source_target_pairs={{0,256},{128,384},{256,0},{384,128},{1,257},{129,385},{257,1},{385... | collective-permute-start | bytes 82952 | tf_op jit(solution)/shard_map/ppermute | solution.py:298
  130.3 4.0 %collective-permute-start.8 = (f32[2,3456]{1,0:T(2,128)S(1)}, f32[2,3456]{1,0:T(2,128)S(1)}, u32[]{:S(2)}, u32[]{:S(2)}) collective-permute-start(f32[2,3456]{1,0:T(2,128)S(1)} %owned.1.refs_0_), channel_id=1, source_target_pairs={{0,128},{128,256},{256,384},{384,0},{1,129},{129,257},{257,385},{3... | collective-permute-start | bytes 82952 | tf_op jit(solution)/shard_map/ppermute | solution.py:298
  134.3 14.6 %collective-permute-done.10.refs_3_ = f32[2,3456]{1,0:T(2,128)S(1)} collective-permute-done((f32[2,3456]{1,0:T(2,128)S(1)}, f32[2,3456]{1,0:T(2,128)S(1)}, u32[]{:S(2)}, u32[]{:S(2)}) %collective-permute-start.10) | collective-permute-done | bytes 27680 | tf_op jit(solution)/shard_map/ppermute | solution.py:298
  148.9 0.0 collective-permute-done.9.refs_2_
  148.9 0.0 collective-permute-done.8.refs_1_
  149.0 1.9 %collective-permute-start.11 = (f32[2,3456]{1,0:T(2,128)S(1)}, f32[2,3456]{1,0:T(2,128)S(1)}, u32[]{:S(2)}, u32[]{:S(2)}) collective-permute-start(f32[2,3456]{1,0:T(2,128)S(1)} %group.1.mine_ref), channel_id=1, source_target_pairs={{0,64},{64,0},{1,65},{65,1},{2,66},{66,2},{3,67},{67,3},{4,68},{68... | collective-permute-start | bytes 82952 | tf_op jit(solution)/shard_map/ppermute | solution.py:294
  150.9 1.1 collective-permute-done.11.theirs_ref
  152.1 0.7 total.1
  152.7 7.5 %all-to-all-done.3.back_ref = bf16[64,2,4224]{2,1,0:T(2,128)(2,1)S(1)} async-done(((bf16[64,2,4224]{2,1,0:T(2,128)(2,1)}), bf16[64,2,4224]{2,1,0:T(2,128)(2,1)S(1)}, u32[]{:S(2)}, u32[]{:S(2)}) %all-to-all-start.3) | async-done | bytes 1081376 | tf_op jit(solution)/shard_map/all_to_all | solution.py:290
  160.3 1.1 unpack.1
  (1 shorter events, 0.0 us)
Async XLA Ops:
  63.8 3.6 %collective-permute-start = (bf16[128,1536]{1,0:T(8,128)(2,1)S(1)}, bf16[128,1536]{1,0:T(8,128)(2,1)S(1)}, u32[]{:S(2)}, u32[]{:S(2)}) collective-permute-start(bf16[128,1536]{1,0:T(8,128)(2,1)S(1)} %get-tuple-element.14.share_ref), channel_id=1, source_target_pairs={{0,64},{64,0},{1,65},{65,1},{2,66},{66,2},{3,67},{67,3},{4,68},{68... | collective-permute-start | bytes 1179656 | tf_op jit(solution)/shard_map/ppermute | solution.py:294
  68.8 17.3 %all-to-all-start.1 = ((bf16[4,32,3456]{2,1,0:T(8,128)(2,1)}), bf16[4,32,3456]{2,1,0:T(8,128)(2,1)S(1)}, u32[]{:S(2)}, u32[]{:S(2)}) async-start(bf16[4,32,3456]{2,1,0:T(8,128)(2,1)} %weight_grad.1), calls=%async_computation.1 | async-start | bytes 1769472 | tf_op jit(solution)/shard_map/all_to_all | solution.py:290
  73.3 19.7 %collective-permute-start.3 = (bf16[128,896]{1,0:T(8,128)(2,1)S(1)}, bf16[128,896]{1,0:T(8,128)(2,1)S(1)}, u32[]{:S(2)}, u32[]{:S(2)}) collective-permute-start(bf16[128,896]{1,0:T(8,128)(2,1)S(1)} %reshape.31.refs_0_), channel_id=1, source_target_pairs={{0,24},{8,0},{16,8},{24,16},{1,25},{9,1},{17,9},{25,17},{2,26},{10... | collective-permute-start | bytes 688136 | tf_op jit(solution)/shard_map/ppermute | solution.py:298
  76.1 18.7 %collective-permute-start.2 = (bf16[128,896]{1,0:T(8,128)(2,1)S(1)}, bf16[128,896]{1,0:T(8,128)(2,1)S(1)}, u32[]{:S(2)}, u32[]{:S(2)}) collective-permute-start(bf16[128,896]{1,0:T(8,128)(2,1)S(1)} %reshape.31.refs_0_), channel_id=1, source_target_pairs={{0,16},{8,24},{16,0},{24,8},{1,17},{9,25},{17,1},{25,9},{2,18},{10... | collective-permute-start | bytes 688136 | tf_op jit(solution)/shard_map/ppermute | solution.py:298
  78.6 16.2 %collective-permute-start.1 = (bf16[128,896]{1,0:T(8,128)(2,1)S(1)}, bf16[128,896]{1,0:T(8,128)(2,1)S(1)}, u32[]{:S(2)}, u32[]{:S(2)}) collective-permute-start(bf16[128,896]{1,0:T(8,128)(2,1)S(1)} %reshape.31.refs_0_), channel_id=1, source_target_pairs={{0,8},{8,16},{16,24},{24,0},{1,9},{9,17},{17,25},{25,1},{2,10},{10... | collective-permute-start | bytes 688136 | tf_op jit(solution)/shard_map/ppermute | solution.py:298
  86.9 20.8 %all-to-all-start.2 = ((bf16[16,2,3456]{2,1,0:T(2,128)(2,1)}), bf16[16,2,3456]{2,1,0:T(2,128)(2,1)}, u32[]{:S(2)}, u32[]{:S(2)}) async-start(bf16[16,2,3456]{2,1,0:T(2,128)(2,1)} %merge.1), calls=%async_computation.2 | async-start | bytes 442368 | tf_op jit(solution)/shard_map/all_to_all | solution.py:290
  91.1 10.0 %collective-permute-start.4 = (bf16[128,896]{1,0:T(8,128)(2,1)S(1)}, bf16[128,896]{1,0:T(8,128)(2,1)S(1)}, u32[]{:S(2)}, u32[]{:S(2)}) collective-permute-start(bf16[128,896]{1,0:T(8,128)(2,1)S(1)} %reshape.31.refs_0_), channel_id=1, source_target_pairs={{0,64},{64,0},{1,65},{65,1},{2,66},{66,2},{3,67},{67,3},{4,68},{68... | collective-permute-start | bytes 688136 | tf_op jit(solution)/shard_map/ppermute | solution.py:294
  94.8 6.3 %collective-permute-start.5 = (bf16[128,896]{1,0:T(8,128)(2,1)S(1)}, bf16[128,896]{1,0:T(8,128)(2,1)S(1)}, u32[]{:S(2)}, u32[]{:S(2)}) collective-permute-start(bf16[128,896]{1,0:T(8,128)(2,1)S(1)} %collective-permute-done.1.refs_1_), channel_id=1, source_target_pairs={{0,64},{64,0},{1,65},{65,1},{2,66},{66,2},{3,67},{67,3},{4,68},{68... | collective-permute-start | bytes 688136 | tf_op jit(solution)/shard_map/ppermute | solution.py:294
  96.7 4.4 %collective-permute-start.6 = (bf16[128,896]{1,0:T(8,128)(2,1)S(1)}, bf16[128,896]{1,0:T(8,128)(2,1)S(1)}, u32[]{:S(2)}, u32[]{:S(2)}) collective-permute-start(bf16[128,896]{1,0:T(8,128)(2,1)S(1)} %collective-permute-done.2.refs_2_), channel_id=1, source_target_pairs={{0,64},{64,0},{1,65},{65,1},{2,66},{66,2},{3,67},{67,3},{4,68},{68... | collective-permute-start | bytes 688136 | tf_op jit(solution)/shard_map/ppermute | solution.py:294
  99.1 3.4 %collective-permute-start.7 = (bf16[128,896]{1,0:T(8,128)(2,1)S(1)}, bf16[128,896]{1,0:T(8,128)(2,1)S(1)}, u32[]{:S(2)}, u32[]{:S(2)}) collective-permute-start(bf16[128,896]{1,0:T(8,128)(2,1)S(1)} %collective-permute-done.3.refs_3_), channel_id=1, source_target_pairs={{0,64},{64,0},{1,65},{65,1},{2,66},{66,2},{3,67},{67,3},{4,68},{68... | collective-permute-start | bytes 688136 | tf_op jit(solution)/shard_map/ppermute | solution.py:294
  107.7 52.5 %all-to-all-start.3 = ((bf16[64,2,4224]{2,1,0:T(2,128)(2,1)}), bf16[64,2,4224]{2,1,0:T(2,128)(2,1)S(1)}, u32[]{:S(2)}, u32[]{:S(2)}) async-start(bf16[64,2,4224]{2,1,0:T(2,128)(2,1)} %backward.1), calls=%async_computation.3 | async-start | bytes 2162688 | tf_op jit(solution)/shard_map/all_to_all | solution.py:290
  125.1 23.8 %collective-permute-start.10 = (f32[2,3456]{1,0:T(2,128)S(1)}, f32[2,3456]{1,0:T(2,128)S(1)}, u32[]{:S(2)}, u32[]{:S(2)}) collective-permute-start(f32[2,3456]{1,0:T(2,128)S(1)} %owned.1.refs_0_), channel_id=1, source_target_pairs={{0,384},{128,0},{256,128},{384,256},{1,385},{129,1},{257,129},{385... | collective-permute-start | bytes 82952 | tf_op jit(solution)/shard_map/ppermute | solution.py:298
  127.1 21.9 %collective-permute-start.9 = (f32[2,3456]{1,0:T(2,128)S(1)}, f32[2,3456]{1,0:T(2,128)S(1)}, u32[]{:S(2)}, u32[]{:S(2)}) collective-permute-start(f32[2,3456]{1,0:T(2,128)S(1)} %owned.1.refs_0_), channel_id=1, source_target_pairs={{0,256},{128,384},{256,0},{384,128},{1,257},{129,385},{257,1},{385... | collective-permute-start | bytes 82952 | tf_op jit(solution)/shard_map/ppermute | solution.py:298
  130.3 18.6 %collective-permute-start.8 = (f32[2,3456]{1,0:T(2,128)S(1)}, f32[2,3456]{1,0:T(2,128)S(1)}, u32[]{:S(2)}, u32[]{:S(2)}) collective-permute-start(f32[2,3456]{1,0:T(2,128)S(1)} %owned.1.refs_0_), channel_id=1, source_target_pairs={{0,128},{128,256},{256,384},{384,0},{1,129},{129,257},{257,385},{3... | collective-permute-start | bytes 82952 | tf_op jit(solution)/shard_map/ppermute | solution.py:298
  149.0 3.1 %collective-permute-start.11 = (f32[2,3456]{1,0:T(2,128)S(1)}, f32[2,3456]{1,0:T(2,128)S(1)}, u32[]{:S(2)}, u32[]{:S(2)}) collective-permute-start(f32[2,3456]{1,0:T(2,128)S(1)} %group.1.mine_ref), channel_id=1, source_target_pairs={{0,64},{64,0},{1,65},{65,1},{2,66},{66,2},{3,67},{67,3},{4,68},{68... | collective-permute-start | bytes 82952 | tf_op jit(solution)/shard_map/ppermute | solution.py:294

commit v14 on v11

--- a/solution.py
+++ b/solution.py
@@ -159,10 +159,12 @@
     columns = jnp.concatenate([columns_ref[...], received_ref[:, WIDTH:]], axis=0)
     features = jnp.concatenate([share_ref[:, :WIDTH], received_ref[:, :WIDTH]], axis=0)
     partial = dot(columns, features, 0, 0).astype(BF16)
-    for pair in range(3):
-        out_ref[:, :, pair * WIDTH : (pair + 1) * WIDTH] = partial[
-            pair * ROWS : (pair + 1) * ROWS
-        ].reshape(64, 2, WIDTH)
+    for high in range(2):
+        for pair in range(3):
+            start, column = pair * ROWS + high * 64, high * HALF_WIDTH + pair * WIDTH
+            out_ref[:, :, column : column + WIDTH] = partial[start : start + 64].reshape(
+                32, 2, WIDTH
+            )
 
 
 def backward_kernel(
@@ -217,9 +219,9 @@
 
 
 def owned_kernel(terms_ref, out_ref):
-    rows = terms_ref[...].reshape(ROWS, HALF_WIDTH)
-    target = lax.broadcasted_iota(jnp.int32, (8, ROWS), 0)
-    source = lax.broadcasted_iota(jnp.int32, (8, ROWS), 1)
+    rows = terms_ref[...].reshape(64, 2 * HALF_WIDTH)
+    target = lax.broadcasted_iota(jnp.int32, (8, 64), 0)
+    source = lax.broadcasted_iota(jnp.int32, (8, 64), 1)
     chosen = jnp.where(target == (source & 1), 1.0, 0.0).astype(BF16)
     out_ref[...] = dot(chosen, rows, 1, 0)[:2]
 
@@ -239,17 +241,22 @@
         copy.wait()
 
 
-def group_kernel(*refs):
-    *terms, out_ref = refs
-    total = terms[0][...]
-    for term in terms[1:]:
-        total += term[...]
-    out_ref[...] = total * GRAD_SCALE
-
-
-def total_kernel(core_ref, mine_ref, theirs_ref, out_ref):
+def group_kernel(high_ref, *refs):
+    *terms, keep_ref, send_ref = refs
+    own = pl.multiple_of(high_ref[0] * HALF_WIDTH, LANES)
+    other = pl.multiple_of((1 - high_ref[0]) * HALF_WIDTH, LANES)
+    for start, out_ref in ((own, keep_ref), (other, send_ref)):
+        total = terms[0][:, pl.ds(start, HALF_WIDTH)]
+        for term in terms[1:]:
+            total += term[:, pl.ds(start, HALF_WIDTH)]
+        out_ref[...] = total * GRAD_SCALE
+
+
+def total_kernel(core_ref, keep_ref, crossed_ref, their_keep_ref, their_crossed_ref, out_ref):
+    mine = keep_ref[...] + crossed_ref[...]
+    theirs = their_keep_ref[...] + their_crossed_ref[...]
     for core in range(2):
-        total = jnp.where(core_ref[0] == core, mine_ref[...], theirs_ref[...])
+        total = jnp.where(core_ref[0] == core, mine, theirs)
         for pair in range(3):
             start = 6 * core + 2 * pair
             out_ref[start : start + 2, :] = total[:, pair * WIDTH : (pair + 1) * WIDTH]
@@ -290,6 +297,7 @@
 def on_device(query_key_value, out_weight, cotangent):
     core = lax.axis_index("c").astype(jnp.int32).reshape(1)
     x_place = lax.axis_index("x").astype(jnp.int32).reshape(1)
+    y_high = lax.axis_index("yh").astype(jnp.int32).reshape(1)
     (packed,) = call(
         pack_kernel,
         "pack",
@@ -325,9 +333,9 @@
         "weight_grad",
         (share, swap(share), columns),
         [IN_VMEM] * 3,
-        [((64, 2, HALF_WIDTH), BF16)],
-    )
-    collected = exchange(partial, SEQ)
+        [((32, 2, 2 * HALF_WIDTH), BF16)],
+    )
+    collected = exchange(partial, ("x", "z"))
     piece, *turned = lax.optimization_barrier((piece, *turned, partial))[:4]
     mine = jnp.stack([piece, *turned])
     (results,) = call(
@@ -348,17 +356,25 @@
         micros=7,
     )
     results, collected = lax.optimization_barrier((results, collected))
-    (owned,) = call(owned_kernel, "owned", (collected,), [IN_VMEM], [((2, HALF_WIDTH), F32)])
+    back = exchange(results, SEQ)
+    (owned,) = call(
+        owned_kernel, "owned", (collected,), [IN_VMEM], [((2, 2 * HALF_WIDTH), F32)]
+    )
     turned = [turn(owned, "yl", step) for step in range(1, 4)]
-    back = exchange(results, SEQ)
-    (group,) = call(
-        group_kernel, "group", (owned, *turned), [IN_VMEM] * 4, [((2, HALF_WIDTH), F32)]
-    )
+    keep, send = call(
+        group_kernel,
+        "group",
+        (y_high, owned, *turned),
+        [IN_SMEM] + [IN_VMEM] * 4,
+        [((2, HALF_WIDTH), F32)] * 2,
+    )
+    crossed = lax.ppermute(send, "yh", [(0, 1), (1, 0)])
+    both = lax.ppermute(send, ("c", "yh"), [(place, 3 - place) for place in range(4)])
     (total,) = call(
         total_kernel,
         "total",
-        (core, group, swap(group)),
-        [IN_SMEM] + [IN_VMEM] * 2,
+        (core, keep, crossed, swap(keep), both),
+        [IN_SMEM] + [IN_VMEM] * 4,
         [((12, WIDTH), F32)],
     )
     projected, grads = call(

time: 157 us -> 164 us (1.045)
  the two profiles are of different devices: /device:TPU:14 before, /device:TPU:6 now
where the time goes in v14:
time: 164 us
  starting transfers between devices  55.6 us (34%)
  blocking collectives  51.9 us (32%)
  waiting for transfers between devices  38.8 us (24%)
  Pallas kernels  14.1 us (9%)
    all_to_all x1, blocking collectives, exchange(): return lax.all_to_all(value, axes, 0, 0, tiled=True)  51.9 us
    ppermute x6, starting transfers between devices, turn(): lax.ppermute(value, axis, [(place, (place + step) % 4) for place in range...  23.4 us
    ppermute x6, waiting for transfers between devices, turn(): lax.ppermute(value, axis, [(place, (place + step) % 4) for place in range...  18.6 us
    all_to_all x2, starting transfers between devices, exchange(): return lax.all_to_all(value, axes, 0, 0, tiled=True)  15.8 us
    pallas_call x8, Pallas kernels, call(): pl.pallas_call(kernel, out_shape=[jax.ShapeDtypeStruct(shape, dtype) for...  14.1 us
    all_to_all x2, waiting for transfers between devices, exchange(): return lax.all_to_all(value, axes, 0, 0, tiled=True)  9.9 us
    ppermute x1, starting transfers between devices, on_device(): lax.ppermute(send, ('c', 'yh'), [(place, 3 - place) for place in range(4)])  8.72 us
    ppermute x1, waiting for transfers between devices, on_device(): crossed = lax.ppermute(send, 'yh', [(0, 1), (1, 0)])  7.71 us
  transfers between devices with their start and end apart: 13, of which 4 were waited for; matrix products, arithmetic and copies ran while one was open for 1% of the time, Pallas kernels for 5%

profile of v14, /device:TPU:6, one launch (start us, length us, event | category | flops | bytes accessed | tf_op | source)
XLA Modules:
  0.0 163.6 jit_solution(1555900499288682621)
XLA Ops:
  0.6 2.8 %pack.1 = bf16[64,2,5120]{2,1,0:T(2,128)(2,1)} custom-call(s32[1]{0:T(128)} %bitcast.core_ref, bf16[3,128,1152]{2,1,0:T(8,128)(2,1)} %bitcast.17, bf16[128,768]{1,0:T(8,128)(2,1)} %bitcast.18, bf16[12,1152]{1,0:T(8,128)(2,1)} %weight_hbm.1), custom_call_target="tpu_custom_call" | custom-call | flops 1000000000 | bytes 3000000 | tf_op jit(solution)/shard_map/pack/pallas_call | solution.py:271
  3.5 51.9 %all_to_all.15.sent_ref = bf16[64,2,5120]{2,1,0:T(2,128)(2,1)S(1)} all-to-all(bf16[64,2,5120]{2,1,0:T(2,128)(2,1)} %pack.1), channel_id=1, replica_groups=mesh['yl'=4,'c'=2,'yh'=2,'x'=4,'z'=8] {'yh','x','z'}, dimensions={0} | all-to-all | bytes 2621440 | tf_op jit(solution)/shard_map/all_to_all | solution.py:286
  55.4 1.3 forward.1
  56.6 1.9 %collective-permute-start.3 = (bf16[128,1536]{1,0:T(8,128)(2,1)S(1)}, bf16[128,1536]{1,0:T(8,128)(2,1)S(1)}, u32[]{:S(2)}, u32[]{:S(2)}) collective-permute-start(bf16[128,1536]{1,0:T(8,128)(2,1)S(1)} %get-tuple-element.15.share_ref), channel_id=1, source_target_pairs={{0,64},{64,0},{1,65},{65,1},{2,66},{66,2},{3,67},{67,3},{4,68},{68... | collective-permute-start | bytes 1179656 | tf_op jit(solution)/shard_map/ppermute | solution.py:290
  58.5 0.2 slice.4
  58.7 0.1 reshape.34
  58.8 6.5 %collective-permute-start.2 = (bf16[128,896]{1,0:T(8,128)(2,1)S(1)}, bf16[128,896]{1,0:T(8,128)(2,1)S(1)}, u32[]{:S(2)}, u32[]{:S(2)}) collective-permute-start(bf16[128,896]{1,0:T(8,128)(2,1)S(1)} %reshape.34), channel_id=1, source_target_pairs={{0,24},{8,0},{16,8},{24,16},{1,25},{9,1},{17,9},{25,17},{2,26},{10... | collective-permute-start | bytes 688136 | tf_op jit(solution)/shard_map/ppermute | solution.py:294
  65.3 2.8 %collective-permute-start.1 = (bf16[128,896]{1,0:T(8,128)(2,1)S(1)}, bf16[128,896]{1,0:T(8,128)(2,1)S(1)}, u32[]{:S(2)}, u32[]{:S(2)}) collective-permute-start(bf16[128,896]{1,0:T(8,128)(2,1)S(1)} %reshape.34), channel_id=1, source_target_pairs={{0,16},{8,24},{16,0},{24,8},{1,17},{9,25},{17,1},{25,9},{2,18},{10... | collective-permute-start | bytes 688136 | tf_op jit(solution)/shard_map/ppermute | solution.py:294
  68.1 4.5 %collective-permute-start = (bf16[128,896]{1,0:T(8,128)(2,1)S(1)}, bf16[128,896]{1,0:T(8,128)(2,1)S(1)}, u32[]{:S(2)}, u32[]{:S(2)}) collective-permute-start(bf16[128,896]{1,0:T(8,128)(2,1)S(1)} %reshape.34), channel_id=1, source_target_pairs={{0,8},{8,16},{16,24},{24,0},{1,9},{9,17},{17,25},{25,1},{2,10},{10... | collective-permute-start | bytes 688136 | tf_op jit(solution)/shard_map/ppermute | solution.py:294
  72.6 0.0 collective-permute-done.3.received_ref
  72.6 1.5 weight_grad.1
  74.1 6.6 %all-to-all-start.1 = ((bf16[32,2,6912]{2,1,0:T(2,128)(2,1)}), bf16[32,2,6912]{2,1,0:T(2,128)(2,1)S(1)}, u32[]{:S(2)}, u32[]{:S(2)}) async-start(bf16[32,2,6912]{2,1,0:T(2,128)(2,1)} %weight_grad.1), calls=%async_computation.1 | async-start | bytes 1769472 | tf_op jit(solution)/shard_map/all_to_all | solution.py:286
  80.7 0.0 collective-permute-done.2
  80.7 0.0 copy-start
  80.7 0.0 collective-permute-done.1
  80.7 0.0 copy-start.1
  80.7 0.0 collective-permute-done
  80.7 0.0 copy-start.2
  80.7 0.6 copy-done
  81.4 0.1 copy-done.1
  81.5 0.1 copy-done.2
  81.6 1.3 pad_maximum_fusion.mine_ref
  82.9 1.9 %collective-permute-start.4 = (bf16[4,128,896]{2,1,0:T(8,128)(2,1)S(1)}, bf16[4,128,896]{2,1,0:T(8,128)(2,1)}, u32[]{:S(2)}, u32[]{:S(2)}) collective-permute-start(bf16[4,128,896]{2,1,0:T(8,128)(2,1)S(1)} %pad_maximum_fusion.mine_ref), channel_id=1, source_target_pairs={{0,64},{64,0},{1,65},{65,1},{2,66},{66,2},{3,67},{67,3},{4,68},{68... | collective-permute-start | bytes 2752520 | tf_op jit(solution)/shard_map/ppermute | solution.py:290
  84.8 2.6 %collective-permute-done.4.theirs_ref = bf16[4,128,896]{2,1,0:T(8,128)(2,1)} collective-permute-done((bf16[4,128,896]{2,1,0:T(8,128)(2,1)S(1)}, bf16[4,128,896]{2,1,0:T(8,128)(2,1)}, u32[]{:S(2)}, u32[]{:S(2)}) %collective-permute-start.4) | collective-permute-done | bytes 917536 | tf_op jit(solution)/shard_map/ppermute | solution.py:290
  87.4 6.5 %backward.1 = bf16[64,2,4224]{2,1,0:T(2,128)(2,1)} custom-call(s32[1]{0:T(128)} %bitcast.core_ref, s32[1]{0:T(128)} %bitcast.1.x_ref, bf16[64,2,5120]{2,1,0:T(2,128)(2,1)S(1)} %all_to_all.15.sent_ref, bf16[4,128,896]{2,1,0:T(8,128)(2,1)S(1)} %pad_maximum_fusion.mine_ref, bf16[4,128,896]{2,1,0:T(8,128)(2,1)} %collective-permute-done.4.theirs_ref), custom_call_target="tpu_custom_call" | custom-call | flops 7000000000 | bytes 21000000 | tf_op jit(solution)/shard_map/backward/pallas_call | solution.py:271
  93.8 9.9 %all-to-all-done.1.terms_ref = bf16[32,2,6912]{2,1,0:T(2,128)(2,1)S(1)} async-done(((bf16[32,2,6912]{2,1,0:T(2,128)(2,1)}), bf16[32,2,6912]{2,1,0:T(2,128)(2,1)S(1)}, u32[]{:S(2)}, u32[]{:S(2)}) %all-to-all-start.1) | async-done | bytes 884768 | tf_op jit(solution)/shard_map/all_to_all | solution.py:286
  103.7 9.2 %all-to-all-start.2 = ((bf16[64,2,4224]{2,1,0:T(2,128)(2,1)}), bf16[64,2,4224]{2,1,0:T(2,128)(2,1)S(1)}, u32[]{:S(2)}, u32[]{:S(2)}) async-start(bf16[64,2,4224]{2,1,0:T(2,128)(2,1)} %backward.1), calls=%async_computation.2 | async-start | bytes 2162688 | tf_op jit(solution)/shard_map/all_to_all | solution.py:286
  112.9 0.2 owned.1.refs_0_
  113.2 4.4 %collective-permute-start.7 = (f32[2,6912]{1,0:T(2,128)S(1)}, f32[2,6912]{1,0:T(2,128)S(1)}, u32[]{:S(2)}, u32[]{:S(2)}) collective-permute-start(f32[2,6912]{1,0:T(2,128)S(1)} %owned.1.refs_0_), channel_id=1, source_target_pairs={{0,384},{128,0},{256,128},{384,256},{1,385},{129,1},{257,129},{385... | collective-permute-start | bytes 165896 | tf_op jit(solution)/shard_map/ppermute | solution.py:294
  117.6 3.3 %collective-permute-start.6 = (f32[2,6912]{1,0:T(2,128)S(1)}, f32[2,6912]{1,0:T(2,128)S(1)}, u32[]{:S(2)}, u32[]{:S(2)}) collective-permute-start(f32[2,6912]{1,0:T(2,128)S(1)} %owned.1.refs_0_), channel_id=1, source_target_pairs={{0,256},{128,384},{256,0},{384,128},{1,257},{129,385},{257,1},{385... | collective-permute-start | bytes 165896 | tf_op jit(solution)/shard_map/ppermute | solution.py:294
  120.8 2.0 %collective-permute-start.5 = (f32[2,6912]{1,0:T(2,128)S(1)}, f32[2,6912]{1,0:T(2,128)S(1)}, u32[]{:S(2)}, u32[]{:S(2)}) collective-permute-start(f32[2,6912]{1,0:T(2,128)S(1)} %owned.1.refs_0_), channel_id=1, source_target_pairs={{0,128},{128,256},{256,384},{384,0},{1,129},{129,257},{257,385},{3... | collective-permute-start | bytes 165896 | tf_op jit(solution)/shard_map/ppermute | solution.py:294
  122.8 18.6 %collective-permute-done.7.refs_3_ = f32[2,6912]{1,0:T(2,128)S(1)} collective-permute-done((f32[2,6912]{1,0:T(2,128)S(1)}, f32[2,6912]{1,0:T(2,128)S(1)}, u32[]{:S(2)}, u32[]{:S(2)}) %collective-permute-start.7) | collective-permute-done | bytes 55328 | tf_op jit(solution)/shard_map/ppermute | solution.py:294
  141.5 0.0 collective-permute-done.6.refs_2_
  141.5 0.0 collective-permute-done.5.refs_1_
  141.5 1.9 %collective-permute-start.9 = (f32[2,3456]{1,0:T(2,128)S(1)}, f32[2,3456]{1,0:T(2,128)S(1)}, u32[]{:S(2)}, u32[]{:S(2)}) collective-permute-start(f32[2,3456]{1,0:T(2,128)S(1)} %get-tuple-element.25.keep_ref), channel_id=1, source_target_pairs={{0,64},{64,0},{1,65},{65,1},{2,66},{66,2},{3,67},{67,3},{4,68},{68... | collective-permute-start | bytes 82952 | tf_op jit(solution)/shard_map/ppermute | solution.py:290
  143.4 8.7 %collective-permute-start.10 = (f32[2,3456]{1,0:T(2,128)S(1)}, f32[2,3456]{1,0:T(2,128)S(1)}, u32[]{:S(2)}, u32[]{:S(2)}) collective-permute-start(f32[2,3456]{1,0:T(2,128)S(1)} %get-tuple-element.26), channel_id=1, source_target_pairs={{0,96},{32,64},{64,32},{96,0},{1,97},{33,65},{65,33},{97,1},{2,98}... | collective-permute-start | bytes 82952 | tf_op jit(solution)/shard_map/ppermute | solution.py:372
  152.1 1.9 %collective-permute-start.8 = (f32[2,3456]{1,0:T(2,128)S(1)}, f32[2,3456]{1,0:T(2,128)S(1)}, u32[]{:S(2)}, u32[]{:S(2)}) collective-permute-start(f32[2,3456]{1,0:T(2,128)S(1)} %get-tuple-element.26), channel_id=1, source_target_pairs={{0,32},{32,0},{1,33},{33,1},{2,34},{34,2},{3,35},{35,3},{4,36},{36... | collective-permute-start | bytes 82952 | tf_op jit(solution)/shard_map/ppermute | solution.py:371
  154.1 0.0 collective-permute-done.9.their_keep_ref
  154.1 0.0 collective-permute-done.10.their_crossed_ref
  154.1 7.7 %collective-permute-done.8.crossed_ref = f32[2,3456]{1,0:T(2,128)S(1)} collective-permute-done((f32[2,3456]{1,0:T(2,128)S(1)}, f32[2,3456]{1,0:T(2,128)S(1)}, u32[]{:S(2)}, u32[]{:S(2)}) %collective-permute-start.8) | collective-permute-done | bytes 27680 | tf_op jit(solution)/shard_map/ppermute | solution.py:371
  161.8 0.7 total.1
  162.5 0.0 all-to-all-done.2.back_ref
  162.5 1.1 unpack.1
  (1 shorter events, 0.0 us)
Async XLA Ops:
  56.6 16.0 %collective-permute-start.3 = (bf16[128,1536]{1,0:T(8,128)(2,1)S(1)}, bf16[128,1536]{1,0:T(8,128)(2,1)S(1)}, u32[]{:S(2)}, u32[]{:S(2)}) collective-permute-start(bf16[128,1536]{1,0:T(8,128)(2,1)S(1)} %get-tuple-element.15.share_ref), channel_id=1, source_target_pairs={{0,64},{64,0},{1,65},{65,1},{2,66},{66,2},{3,67},{67,3},{4,68},{68... | collective-permute-start | bytes 1179656 | tf_op jit(solution)/shard_map/ppermute | solution.py:290
  58.8 21.9 %collective-permute-start.2 = (bf16[128,896]{1,0:T(8,128)(2,1)S(1)}, bf16[128,896]{1,0:T(8,128)(2,1)S(1)}, u32[]{:S(2)}, u32[]{:S(2)}) collective-permute-start(bf16[128,896]{1,0:T(8,128)(2,1)S(1)} %reshape.34), channel_id=1, source_target_pairs={{0,24},{8,0},{16,8},{24,16},{1,25},{9,1},{17,9},{25,17},{2,26},{10... | collective-permute-start | bytes 688136 | tf_op jit(solution)/shard_map/ppermute | solution.py:294
  65.3 15.4 %collective-permute-start.1 = (bf16[128,896]{1,0:T(8,128)(2,1)S(1)}, bf16[128,896]{1,0:T(8,128)(2,1)S(1)}, u32[]{:S(2)}, u32[]{:S(2)}) collective-permute-start(bf16[128,896]{1,0:T(8,128)(2,1)S(1)} %reshape.34), channel_id=1, source_target_pairs={{0,16},{8,24},{16,0},{24,8},{1,17},{9,25},{17,1},{25,9},{2,18},{10... | collective-permute-start | bytes 688136 | tf_op jit(solution)/shard_map/ppermute | solution.py:294
  68.1 12.6 %collective-permute-start = (bf16[128,896]{1,0:T(8,128)(2,1)S(1)}, bf16[128,896]{1,0:T(8,128)(2,1)S(1)}, u32[]{:S(2)}, u32[]{:S(2)}) collective-permute-start(bf16[128,896]{1,0:T(8,128)(2,1)S(1)} %reshape.34), channel_id=1, source_target_pairs={{0,8},{8,16},{16,24},{24,0},{1,9},{9,17},{17,25},{25,1},{2,10},{10... | collective-permute-start | bytes 688136 | tf_op jit(solution)/shard_map/ppermute | solution.py:294
  74.1 29.6 %all-to-all-start.1 = ((bf16[32,2,6912]{2,1,0:T(2,128)(2,1)}), bf16[32,2,6912]{2,1,0:T(2,128)(2,1)S(1)}, u32[]{:S(2)}, u32[]{:S(2)}) async-start(bf16[32,2,6912]{2,1,0:T(2,128)(2,1)} %weight_grad.1), calls=%async_computation.1 | async-start | bytes 1769472 | tf_op jit(solution)/shard_map/all_to_all | solution.py:286
  80.7 0.7 copy-start
  80.7 0.8 copy-start.1
  80.7 0.8 copy-start.2
  82.9 4.5 %collective-permute-start.4 = (bf16[4,128,896]{2,1,0:T(8,128)(2,1)S(1)}, bf16[4,128,896]{2,1,0:T(8,128)(2,1)}, u32[]{:S(2)}, u32[]{:S(2)}) collective-permute-start(bf16[4,128,896]{2,1,0:T(8,128)(2,1)S(1)} %pad_maximum_fusion.mine_ref), channel_id=1, source_target_pairs={{0,64},{64,0},{1,65},{65,1},{2,66},{66,2},{3,67},{67,3},{4,68},{68... | collective-permute-start | bytes 2752520 | tf_op jit(solution)/shard_map/ppermute | solution.py:290
  103.7 58.7 %all-to-all-start.2 = ((bf16[64,2,4224]{2,1,0:T(2,128)(2,1)}), bf16[64,2,4224]{2,1,0:T(2,128)(2,1)S(1)}, u32[]{:S(2)}, u32[]{:S(2)}) async-start(bf16[64,2,4224]{2,1,0:T(2,128)(2,1)} %backward.1), calls=%async_computation.2 | async-start | bytes 2162688 | tf_op jit(solution)/shard_map/all_to_all | solution.py:286
  113.2 28.3 %collective-permute-start.7 = (f32[2,6912]{1,0:T(2,128)S(1)}, f32[2,6912]{1,0:T(2,128)S(1)}, u32[]{:S(2)}, u32[]{:S(2)}) collective-permute-start(f32[2,6912]{1,0:T(2,128)S(1)} %owned.1.refs_0_), channel_id=1, source_target_pairs={{0,384},{128,0},{256,128},{384,256},{1,385},{129,1},{257,129},{385... | collective-permute-start | bytes 165896 | tf_op jit(solution)/shard_map/ppermute | solution.py:294
  117.6 23.9 %collective-permute-start.6 = (f32[2,6912]{1,0:T(2,128)S(1)}, f32[2,6912]{1,0:T(2,128)S(1)}, u32[]{:S(2)}, u32[]{:S(2)}) collective-permute-start(f32[2,6912]{1,0:T(2,128)S(1)} %owned.1.refs_0_), channel_id=1, source_target_pairs={{0,256},{128,384},{256,0},{384,128},{1,257},{129,385},{257,1},{385... | collective-permute-start | bytes 165896 | tf_op jit(solution)/shard_map/ppermute | solution.py:294
  120.8 20.6 %collective-permute-start.5 = (f32[2,6912]{1,0:T(2,128)S(1)}, f32[2,6912]{1,0:T(2,128)S(1)}, u32[]{:S(2)}, u32[]{:S(2)}) collective-permute-start(f32[2,6912]{1,0:T(2,128)S(1)} %owned.1.refs_0_), channel_id=1, source_target_pairs={{0,128},{128,256},{256,384},{384,0},{1,129},{129,257},{257,385},{3... | collective-permute-start | bytes 165896 | tf_op jit(solution)/shard_map/ppermute | solution.py:294
  141.5 12.6 %collective-permute-start.9 = (f32[2,3456]{1,0:T(2,128)S(1)}, f32[2,3456]{1,0:T(2,128)S(1)}, u32[]{:S(2)}, u32[]{:S(2)}) collective-permute-start(f32[2,3456]{1,0:T(2,128)S(1)} %get-tuple-element.25.keep_ref), channel_id=1, source_target_pairs={{0,64},{64,0},{1,65},{65,1},{2,66},{66,2},{3,67},{67,3},{4,68},{68... | collective-permute-start | bytes 82952 | tf_op jit(solution)/shard_map/ppermute | solution.py:290
  143.4 10.7 %collective-permute-start.10 = (f32[2,3456]{1,0:T(2,128)S(1)}, f32[2,3456]{1,0:T(2,128)S(1)}, u32[]{:S(2)}, u32[]{:S(2)}) collective-permute-start(f32[2,3456]{1,0:T(2,128)S(1)} %get-tuple-element.26), channel_id=1, source_target_pairs={{0,96},{32,64},{64,32},{96,0},{1,97},{33,65},{65,33},{97,1},{2,98}... | collective-permute-start | bytes 82952 | tf_op jit(solution)/shard_map/ppermute | solution.py:372
  152.1 9.7 %collective-permute-start.8 = (f32[2,3456]{1,0:T(2,128)S(1)}, f32[2,3456]{1,0:T(2,128)S(1)}, u32[]{:S(2)}, u32[]{:S(2)}) collective-permute-start(f32[2,3456]{1,0:T(2,128)S(1)} %get-tuple-element.26), channel_id=1, source_target_pairs={{0,32},{32,0},{1,33},{33,1},{2,34},{34,2},{3,35},{35,3},{4,36},{36... | collective-permute-start | bytes 82952 | tf_op jit(solution)/shard_map/ppermute | solution.py:371

commit v15 on v11

--- a/solution.py
+++ b/solution.py
@@ -90,8 +90,9 @@
 def pack_kernel(
     core_ref, parts_hbm, cotangent_hbm, weight_hbm, out_ref, parts, cotangent, weight, sems
 ):
-    pairs = [(parts_hbm.at[part], parts.at[part]) for part in range(3)]
-    pairs += [(cotangent_hbm, cotangent), (weight_hbm, weight)]
+    pairs = [(weight_hbm, weight)]
+    pairs += [(parts_hbm.at[part], parts.at[part]) for part in range(3)]
+    pairs += [(cotangent_hbm, cotangent)]
     copies = [
         pltpu.make_async_copy(source, target, sems.at[place])
         for place, (source, target) in enumerate(pairs)
@@ -100,7 +101,7 @@
         copy.start()
     row = lax.broadcasted_iota(jnp.int32, (ROWS, 12), 0)
     col = lax.broadcasted_iota(jnp.int32, (ROWS, 12), 1)
-    copies[4].wait()
+    copies[0].wait()
     repeated = []
     for pair in range(3):
         chosen = col == 6 * core_ref[0] + 2 * pair + (row & 1)
@@ -115,9 +116,9 @@
                 value = jnp.where(column == piece, repeated[pair][:, lanes(tile)], value)
         out_ref[:, :, lanes(place, BASE)] = value.reshape(64, 2, LANES)
     for part in range(3):
-        copies[part].wait()
+        copies[1 + part].wait()
         out_ref[:, :, part * WIDTH : (part + 1) * WIDTH] = parts[part].reshape(64, 2, WIDTH)
-    copies[3].wait()
+    copies[4].wait()
     out_ref[:, :, 3 * WIDTH : BASE] = cotangent[...].reshape(64, 2, OUT)
 
 

time: 157 us -> 157 us (level)
  no operation moved by 1% of the time
where the time goes in v15:
time: 157 us; the launch traced here: 156 us
  blocking collectives  59 us (38%)
  waiting for transfers between devices  45 us (29%)
  starting transfers between devices  35.7 us (23%)
  Pallas kernels  13.7 us (9%)
    all_to_all x1, blocking collectives, exchange(): return lax.all_to_all(value, axes, 0, 0, tiled=True)  59 us
    all_to_all x2, waiting for transfers between devices, exchange(): return lax.all_to_all(value, axes, 0, 0, tiled=True)  25.3 us
    ppermute x6, starting transfers between devices, turn(): lax.ppermute(value, axis, [(place, (place + step) % 4) for place in range...  17.4 us
    ppermute x6, waiting for transfers between devices, turn(): lax.ppermute(value, axis, [(place, (place + step) % 4) for place in range...  16.1 us
    pallas_call x8, Pallas kernels, call(): pl.pallas_call(kernel, out_shape=[jax.ShapeDtypeStruct(shape, dtype) for...  13.7 us
    all_to_all x2, starting transfers between devices, exchange(): return lax.all_to_all(value, axes, 0, 0, tiled=True)  12.5 us
    ppermute x3, starting transfers between devices, swap(): return lax.ppermute(value, 'c', [(0, 1), (1, 0)])  5.77 us
    ppermute x3, waiting for transfers between devices, swap(): return lax.ppermute(value, 'c', [(0, 1), (1, 0)])  3.73 us
  transfers between devices with their start and end apart: 11, of which 6 were waited for; matrix products, arithmetic and copies ran while one was open for 1% of the time, Pallas kernels for 6%

profile of v15, /device:TPU:14, one launch (start us, length us, event | category | flops | bytes accessed | tf_op | source)
XLA Modules:
  0.0 155.8 jit_solution(2141554577273288336)
XLA Ops:
  0.6 2.5 %pack.1 = bf16[64,2,5120]{2,1,0:T(2,128)(2,1)} custom-call(s32[1]{0:T(128)} %bitcast.core_ref, bf16[3,128,1152]{2,1,0:T(8,128)(2,1)} %bitcast.14, bf16[128,768]{1,0:T(8,128)(2,1)} %bitcast.15, bf16[12,1152]{1,0:T(8,128)(2,1)} %weight_hbm.1), custom_call_target="tpu_custom_call" | custom-call | flops 1000000000 | bytes 3000000 | tf_op jit(solution)/shard_map/pack/pallas_call | solution.py:265
  3.2 59.0 %all_to_all.15.sent_ref = bf16[64,2,5120]{2,1,0:T(2,128)(2,1)S(1)} all-to-all(bf16[64,2,5120]{2,1,0:T(2,128)(2,1)} %pack.1), channel_id=1, replica_groups=mesh['yl'=4,'c'=2,'yh'=2,'x'=4,'z'=8] {'yh','x','z'}, dimensions={0} | all-to-all | bytes 2621440 | tf_op jit(solution)/shard_map/all_to_all | solution.py:280
  62.2 1.3 forward.1
  63.5 1.9 %collective-permute-start.3 = (bf16[128,1536]{1,0:T(8,128)(2,1)S(1)}, bf16[128,1536]{1,0:T(8,128)(2,1)S(1)}, u32[]{:S(2)}, u32[]{:S(2)}) collective-permute-start(bf16[128,1536]{1,0:T(8,128)(2,1)S(1)} %get-tuple-element.13.share_ref), channel_id=1, source_target_pairs={{0,64},{64,0},{1,65},{65,1},{2,66},{66,2},{3,67},{67,3},{4,68},{68... | collective-permute-start | bytes 1179656 | tf_op jit(solution)/shard_map/ppermute | solution.py:284
  65.4 0.2 slice.4
  65.5 0.1 reshape.31
  65.6 1.9 %collective-permute-start.2 = (bf16[128,896]{1,0:T(8,128)(2,1)S(1)}, bf16[128,896]{1,0:T(8,128)(2,1)S(1)}, u32[]{:S(2)}, u32[]{:S(2)}) collective-permute-start(bf16[128,896]{1,0:T(8,128)(2,1)S(1)} %reshape.31), channel_id=1, source_target_pairs={{0,24},{8,0},{16,8},{24,16},{1,25},{9,1},{17,9},{25,17},{2,26},{10... | collective-permute-start | bytes 688136 | tf_op jit(solution)/shard_map/ppermute | solution.py:288
  67.6 3.7 %collective-permute-start.1 = (bf16[128,896]{1,0:T(8,128)(2,1)S(1)}, bf16[128,896]{1,0:T(8,128)(2,1)}, u32[]{:S(2)}, u32[]{:S(2)}) collective-permute-start(bf16[128,896]{1,0:T(8,128)(2,1)S(1)} %reshape.31), channel_id=1, source_target_pairs={{0,16},{8,24},{16,0},{24,8},{1,17},{9,25},{17,1},{25,9},{2,18},{10... | collective-permute-start | bytes 688136 | tf_op jit(solution)/shard_map/ppermute | solution.py:288
  71.3 3.3 %collective-permute-start = (bf16[128,896]{1,0:T(8,128)(2,1)S(1)}, bf16[128,896]{1,0:T(8,128)(2,1)}, u32[]{:S(2)}, u32[]{:S(2)}) collective-permute-start(bf16[128,896]{1,0:T(8,128)(2,1)S(1)} %reshape.31), channel_id=1, source_target_pairs={{0,8},{8,16},{16,24},{24,0},{1,9},{9,17},{17,25},{25,1},{2,10},{10... | collective-permute-start | bytes 688136 | tf_op jit(solution)/shard_map/ppermute | solution.py:288
  74.6 0.0 collective-permute-done.3.received_ref
  74.7 1.5 weight_grad.1
  76.1 7.3 %all-to-all-start.1 = ((bf16[64,2,3456]{2,1,0:T(2,128)(2,1)}), bf16[64,2,3456]{2,1,0:T(2,128)(2,1)S(1)}, u32[]{:S(2)}, u32[]{:S(2)}) async-start(bf16[64,2,3456]{2,1,0:T(2,128)(2,1)} %weight_grad.1), calls=%async_computation.1 | async-start | bytes 1769472 | tf_op jit(solution)/shard_map/all_to_all | solution.py:280
  83.5 0.0 collective-permute-done.2
  83.5 0.0 copy-start
  83.5 0.0 collective-permute-done.1
  83.5 0.9 collective-permute-done
  84.4 0.0 copy-done
  84.4 1.3 pad_maximum_fusion.mine_ref
  85.7 1.9 %collective-permute-start.4 = (bf16[4,128,896]{2,1,0:T(8,128)(2,1)S(1)}, bf16[4,128,896]{2,1,0:T(8,128)(2,1)}, u32[]{:S(2)}, u32[]{:S(2)}) collective-permute-start(bf16[4,128,896]{2,1,0:T(8,128)(2,1)S(1)} %pad_maximum_fusion.mine_ref), channel_id=1, source_target_pairs={{0,64},{64,0},{1,65},{65,1},{2,66},{66,2},{3,67},{67,3},{4,68},{68... | collective-permute-start | bytes 2752520 | tf_op jit(solution)/shard_map/ppermute | solution.py:284
  87.6 2.6 %collective-permute-done.4.theirs_ref = bf16[4,128,896]{2,1,0:T(8,128)(2,1)} collective-permute-done((bf16[4,128,896]{2,1,0:T(8,128)(2,1)S(1)}, bf16[4,128,896]{2,1,0:T(8,128)(2,1)}, u32[]{:S(2)}, u32[]{:S(2)}) %collective-permute-start.4) | collective-permute-done | bytes 917536 | tf_op jit(solution)/shard_map/ppermute | solution.py:284
  90.2 6.4 %backward.1 = bf16[64,2,4224]{2,1,0:T(2,128)(2,1)} custom-call(s32[1]{0:T(128)} %bitcast.core_ref, s32[1]{0:T(128)} %bitcast.1.x_ref, bf16[64,2,5120]{2,1,0:T(2,128)(2,1)S(1)} %all_to_all.15.sent_ref, bf16[4,128,896]{2,1,0:T(8,128)(2,1)S(1)} %pad_maximum_fusion.mine_ref, bf16[4,128,896]{2,1,0:T(8,128)(2,1)} %collective-permute-done.4.theirs_ref), custom_call_target="tpu_custom_call" | custom-call | flops 7000000000 | bytes 21000000 | tf_op jit(solution)/shard_map/backward/pallas_call | solution.py:265
  96.6 17.7 %all-to-all-done.1.terms_ref = bf16[64,2,3456]{2,1,0:T(2,128)(2,1)S(1)} async-done(((bf16[64,2,3456]{2,1,0:T(2,128)(2,1)}), bf16[64,2,3456]{2,1,0:T(2,128)(2,1)S(1)}, u32[]{:S(2)}, u32[]{:S(2)}) %all-to-all-start.1) | async-done | bytes 884768 | tf_op jit(solution)/shard_map/all_to_all | solution.py:280
  114.4 5.1 %all-to-all-start.2 = ((bf16[64,2,4224]{2,1,0:T(2,128)(2,1)}), bf16[64,2,4224]{2,1,0:T(2,128)(2,1)S(1)}, u32[]{:S(2)}, u32[]{:S(2)}) async-start(bf16[64,2,4224]{2,1,0:T(2,128)(2,1)} %backward.1), calls=%async_computation.2 | async-start | bytes 2162688 | tf_op jit(solution)/shard_map/all_to_all | solution.py:280
  119.5 0.2 owned.1.refs_0_
  119.7 1.9 %collective-permute-start.7 = (f32[2,3456]{1,0:T(2,128)S(1)}, f32[2,3456]{1,0:T(2,128)S(1)}, u32[]{:S(2)}, u32[]{:S(2)}) collective-permute-start(f32[2,3456]{1,0:T(2,128)S(1)} %owned.1.refs_0_), channel_id=1, source_target_pairs={{0,384},{128,0},{256,128},{384,256},{1,385},{129,1},{257,129},{385... | collective-permute-start | bytes 82952 | tf_op jit(solution)/shard_map/ppermute | solution.py:288
  121.7 3.1 %collective-permute-start.6 = (f32[2,3456]{1,0:T(2,128)S(1)}, f32[2,3456]{1,0:T(2,128)S(1)}, u32[]{:S(2)}, u32[]{:S(2)}) collective-permute-start(f32[2,3456]{1,0:T(2,128)S(1)} %owned.1.refs_0_), channel_id=1, source_target_pairs={{0,256},{128,384},{256,0},{384,128},{1,257},{129,385},{257,1},{385... | collective-permute-start | bytes 82952 | tf_op jit(solution)/shard_map/ppermute | solution.py:288
  124.7 3.5 %collective-permute-start.5 = (f32[2,3456]{1,0:T(2,128)S(1)}, f32[2,3456]{1,0:T(2,128)S(1)}, u32[]{:S(2)}, u32[]{:S(2)}) collective-permute-start(f32[2,3456]{1,0:T(2,128)S(1)} %owned.1.refs_0_), channel_id=1, source_target_pairs={{0,128},{128,256},{256,384},{384,0},{1,129},{129,257},{257,385},{3... | collective-permute-start | bytes 82952 | tf_op jit(solution)/shard_map/ppermute | solution.py:288
  128.2 15.2 %collective-permute-done.7.refs_3_ = f32[2,3456]{1,0:T(2,128)S(1)} collective-permute-done((f32[2,3456]{1,0:T(2,128)S(1)}, f32[2,3456]{1,0:T(2,128)S(1)}, u32[]{:S(2)}, u32[]{:S(2)}) %collective-permute-start.7) | collective-permute-done | bytes 27680 | tf_op jit(solution)/shard_map/ppermute | solution.py:288
  143.4 0.0 collective-permute-done.6.refs_2_
  143.4 0.0 collective-permute-done.5.refs_1_
  143.4 1.9 %collective-permute-start.8 = (f32[2,3456]{1,0:T(2,128)S(1)}, f32[2,3456]{1,0:T(2,128)S(1)}, u32[]{:S(2)}, u32[]{:S(2)}) collective-permute-start(f32[2,3456]{1,0:T(2,128)S(1)} %group.1.mine_ref), channel_id=1, source_target_pairs={{0,64},{64,0},{1,65},{65,1},{2,66},{66,2},{3,67},{67,3},{4,68},{68... | collective-permute-start | bytes 82952 | tf_op jit(solution)/shard_map/ppermute | solution.py:284
  145.3 1.2 collective-permute-done.8.theirs_ref
  146.5 0.7 total.1
  147.1 7.5 %all-to-all-done.2.back_ref = bf16[64,2,4224]{2,1,0:T(2,128)(2,1)S(1)} async-done(((bf16[64,2,4224]{2,1,0:T(2,128)(2,1)}), bf16[64,2,4224]{2,1,0:T(2,128)(2,1)S(1)}, u32[]{:S(2)}, u32[]{:S(2)}) %all-to-all-start.2) | async-done | bytes 1081376 | tf_op jit(solution)/shard_map/all_to_all | solution.py:280
  154.7 1.1 unpack.1
  (1 shorter events, 0.0 us)
Async XLA Ops:
  63.5 11.2 %collective-permute-start.3 = (bf16[128,1536]{1,0:T(8,128)(2,1)S(1)}, bf16[128,1536]{1,0:T(8,128)(2,1)S(1)}, u32[]{:S(2)}, u32[]{:S(2)}) collective-permute-start(bf16[128,1536]{1,0:T(8,128)(2,1)S(1)} %get-tuple-element.13.share_ref), channel_id=1, source_target_pairs={{0,64},{64,0},{1,65},{65,1},{2,66},{66,2},{3,67},{67,3},{4,68},{68... | collective-permute-start | bytes 1179656 | tf_op jit(solution)/shard_map/ppermute | solution.py:284
  65.6 17.8 %collective-permute-start.2 = (bf16[128,896]{1,0:T(8,128)(2,1)S(1)}, bf16[128,896]{1,0:T(8,128)(2,1)S(1)}, u32[]{:S(2)}, u32[]{:S(2)}) collective-permute-start(bf16[128,896]{1,0:T(8,128)(2,1)S(1)} %reshape.31), channel_id=1, source_target_pairs={{0,24},{8,0},{16,8},{24,16},{1,25},{9,1},{17,9},{25,17},{2,26},{10... | collective-permute-start | bytes 688136 | tf_op jit(solution)/shard_map/ppermute | solution.py:288
  67.6 15.9 %collective-permute-start.1 = (bf16[128,896]{1,0:T(8,128)(2,1)S(1)}, bf16[128,896]{1,0:T(8,128)(2,1)}, u32[]{:S(2)}, u32[]{:S(2)}) collective-permute-start(bf16[128,896]{1,0:T(8,128)(2,1)S(1)} %reshape.31), channel_id=1, source_target_pairs={{0,16},{8,24},{16,0},{24,8},{1,17},{9,25},{17,1},{25,9},{2,18},{10... | collective-permute-start | bytes 688136 | tf_op jit(solution)/shard_map/ppermute | solution.py:288
  71.3 13.1 %collective-permute-start = (bf16[128,896]{1,0:T(8,128)(2,1)S(1)}, bf16[128,896]{1,0:T(8,128)(2,1)}, u32[]{:S(2)}, u32[]{:S(2)}) collective-permute-start(bf16[128,896]{1,0:T(8,128)(2,1)S(1)} %reshape.31), channel_id=1, source_target_pairs={{0,8},{8,16},{16,24},{24,0},{1,9},{9,17},{17,25},{25,1},{2,10},{10... | collective-permute-start | bytes 688136 | tf_op jit(solution)/shard_map/ppermute | solution.py:288
  76.1 38.2 %all-to-all-start.1 = ((bf16[64,2,3456]{2,1,0:T(2,128)(2,1)}), bf16[64,2,3456]{2,1,0:T(2,128)(2,1)S(1)}, u32[]{:S(2)}, u32[]{:S(2)}) async-start(bf16[64,2,3456]{2,1,0:T(2,128)(2,1)} %weight_grad.1), calls=%async_computation.1 | async-start | bytes 1769472 | tf_op jit(solution)/shard_map/all_to_all | solution.py:280
  83.5 0.9 copy-start
  85.7 4.5 %collective-permute-start.4 = (bf16[4,128,896]{2,1,0:T(8,128)(2,1)S(1)}, bf16[4,128,896]{2,1,0:T(8,128)(2,1)}, u32[]{:S(2)}, u32[]{:S(2)}) collective-permute-start(bf16[4,128,896]{2,1,0:T(8,128)(2,1)S(1)} %pad_maximum_fusion.mine_ref), channel_id=1, source_target_pairs={{0,64},{64,0},{1,65},{65,1},{2,66},{66,2},{3,67},{67,3},{4,68},{68... | collective-permute-start | bytes 2752520 | tf_op jit(solution)/shard_map/ppermute | solution.py:284
  114.4 40.3 %all-to-all-start.2 = ((bf16[64,2,4224]{2,1,0:T(2,128)(2,1)}), bf16[64,2,4224]{2,1,0:T(2,128)(2,1)S(1)}, u32[]{:S(2)}, u32[]{:S(2)}) async-start(bf16[64,2,4224]{2,1,0:T(2,128)(2,1)} %backward.1), calls=%async_computation.2 | async-start | bytes 2162688 | tf_op jit(solution)/shard_map/all_to_all | solution.py:280
  119.7 23.6 %collective-permute-start.7 = (f32[2,3456]{1,0:T(2,128)S(1)}, f32[2,3456]{1,0:T(2,128)S(1)}, u32[]{:S(2)}, u32[]{:S(2)}) collective-permute-start(f32[2,3456]{1,0:T(2,128)S(1)} %owned.1.refs_0_), channel_id=1, source_target_pairs={{0,384},{128,0},{256,128},{384,256},{1,385},{129,1},{257,129},{385... | collective-permute-start | bytes 82952 | tf_op jit(solution)/shard_map/ppermute | solution.py:288
  121.7 21.7 %collective-permute-start.6 = (f32[2,3456]{1,0:T(2,128)S(1)}, f32[2,3456]{1,0:T(2,128)S(1)}, u32[]{:S(2)}, u32[]{:S(2)}) collective-permute-start(f32[2,3456]{1,0:T(2,128)S(1)} %owned.1.refs_0_), channel_id=1, source_target_pairs={{0,256},{128,384},{256,0},{384,128},{1,257},{129,385},{257,1},{385... | collective-permute-start | bytes 82952 | tf_op jit(solution)/shard_map/ppermute | solution.py:288
  124.7 18.6 %collective-permute-start.5 = (f32[2,3456]{1,0:T(2,128)S(1)}, f32[2,3456]{1,0:T(2,128)S(1)}, u32[]{:S(2)}, u32[]{:S(2)}) collective-permute-start(f32[2,3456]{1,0:T(2,128)S(1)} %owned.1.refs_0_), channel_id=1, source_target_pairs={{0,128},{128,256},{256,384},{384,0},{1,129},{129,257},{257,385},{3... | collective-permute-start | bytes 82952 | tf_op jit(solution)/shard_map/ppermute | solution.py:288
  143.4 3.1 %collective-permute-start.8 = (f32[2,3456]{1,0:T(2,128)S(1)}, f32[2,3456]{1,0:T(2,128)S(1)}, u32[]{:S(2)}, u32[]{:S(2)}) collective-permute-start(f32[2,3456]{1,0:T(2,128)S(1)} %group.1.mine_ref), channel_id=1, source_target_pairs={{0,64},{64,0},{1,65},{65,1},{2,66},{66,2},{3,67},{67,3},{4,68},{68... | collective-permute-start | bytes 82952 | tf_op jit(solution)/shard_map/ppermute | solution.py:284

commit v16 on v11

--- a/solution.py
+++ b/solution.py
@@ -88,10 +88,10 @@
 
 
 def pack_kernel(
-    core_ref, parts_hbm, cotangent_hbm, weight_hbm, out_ref, parts, cotangent, weight, sems
+    core_ref, parts_hbm, cotangent_hbm, weight_ref, out_ref, parts, cotangent, sems
 ):
     pairs = [(parts_hbm.at[part], parts.at[part]) for part in range(3)]
-    pairs += [(cotangent_hbm, cotangent), (weight_hbm, weight)]
+    pairs += [(cotangent_hbm, cotangent)]
     copies = [
         pltpu.make_async_copy(source, target, sems.at[place])
         for place, (source, target) in enumerate(pairs)
@@ -100,12 +100,11 @@
         copy.start()
     row = lax.broadcasted_iota(jnp.int32, (ROWS, 12), 0)
     col = lax.broadcasted_iota(jnp.int32, (ROWS, 12), 1)
-    copies[4].wait()
     repeated = []
     for pair in range(3):
         chosen = col == 6 * core_ref[0] + 2 * pair + (row & 1)
         repeated.append(
-            dot(jnp.where(chosen, 1.0, 0.0).astype(BF16), weight[...], 1, 0).astype(BF16)
+            dot(jnp.where(chosen, 1.0, 0.0).astype(BF16), weight_ref[...], 1, 0).astype(BF16)
         )
     column = (lax.broadcasted_iota(jnp.int32, (ROWS, LANES), 0) >> 4) & 3
     for place in range(PIECE_TILES):
@@ -294,13 +293,12 @@
         pack_kernel,
         "pack",
         (core, query_key_value.reshape(3, ROWS, WIDTH), cotangent.reshape(ROWS, OUT), out_weight),
-        [IN_SMEM] + [IN_HBM] * 3,
+        [IN_SMEM] + [IN_HBM] * 2 + [IN_VMEM],
         [((64, 2, COLS), BF16)],
         [
             pltpu.VMEM((3, ROWS, WIDTH), BF16),
             pltpu.VMEM((ROWS, OUT), BF16),
-            pltpu.VMEM((12, WIDTH), BF16),
-            pltpu.SemaphoreType.DMA((5,)),
+            pltpu.SemaphoreType.DMA((4,)),
         ],
         grant=56,
     )

time: 157 us -> 157 us (level)
  no operation moved by 1% of the time
where the time goes in v16:
time: 157 us; the launch traced here: 156 us
  blocking collectives  59 us (38%)
  waiting for transfers between devices  45.1 us (29%)
  starting transfers between devices  35.6 us (23%)
  Pallas kernels  14.3 us (9%)
    all_to_all x1, blocking collectives, exchange(): return lax.all_to_all(value, axes, 0, 0, tiled=True)  59 us
    all_to_all x2, waiting for transfers between devices, exchange(): return lax.all_to_all(value, axes, 0, 0, tiled=True)  25.1 us
    ppermute x6, starting transfers between devices, turn(): lax.ppermute(value, axis, [(place, (place + step) % 4) for place in range...  17.4 us
    ppermute x6, waiting for transfers between devices, turn(): lax.ppermute(value, axis, [(place, (place + step) % 4) for place in range...  16.3 us
    pallas_call x8, Pallas kernels, call(): pl.pallas_call(kernel, out_shape=[jax.ShapeDtypeStruct(shape, dtype) for...  14.3 us
    all_to_all x2, starting transfers between devices, exchange(): return lax.all_to_all(value, axes, 0, 0, tiled=True)  12.4 us
    ppermute x3, starting transfers between devices, swap(): return lax.ppermute(value, 'c', [(0, 1), (1, 0)])  5.77 us
    ppermute x3, waiting for transfers between devices, swap(): return lax.ppermute(value, 'c', [(0, 1), (1, 0)])  3.73 us
  transfers between devices with their start and end apart: 11, of which 6 were waited for; matrix products, arithmetic and copies ran while one was open for 1% of the time, Pallas kernels for 6%

profile of v16, /device:TPU:14, one launch (start us, length us, event | category | flops | bytes accessed | tf_op | source)
XLA Modules:
  0.0 156.3 jit_solution(6734335208196507220)
XLA Ops:
  0.6 3.1 %pack.1 = bf16[64,2,5120]{2,1,0:T(2,128)(2,1)} custom-call(s32[1]{0:T(128)} %bitcast.core_ref, bf16[3,128,1152]{2,1,0:T(8,128)(2,1)} %bitcast.14, bf16[128,768]{1,0:T(8,128)(2,1)} %bitcast.15, bf16[12,1152]{1,0:T(8,128)(2,1)} %weight_ref.1), custom_call_target="tpu_custom_call" | custom-call | flops 1000000000 | bytes 3000000 | tf_op jit(solution)/shard_map/pack/pallas_call | solution.py:263
  3.7 59.0 %all_to_all.15.sent_ref = bf16[64,2,5120]{2,1,0:T(2,128)(2,1)S(1)} all-to-all(bf16[64,2,5120]{2,1,0:T(2,128)(2,1)} %pack.1), channel_id=1, replica_groups=mesh['yl'=4,'c'=2,'yh'=2,'x'=4,'z'=8] {'yh','x','z'}, dimensions={0} | all-to-all | bytes 2621440 | tf_op jit(solution)/shard_map/all_to_all | solution.py:278
  62.8 1.3 forward.1
  64.0 1.9 %collective-permute-start.3 = (bf16[128,1536]{1,0:T(8,128)(2,1)S(1)}, bf16[128,1536]{1,0:T(8,128)(2,1)S(1)}, u32[]{:S(2)}, u32[]{:S(2)}) collective-permute-start(bf16[128,1536]{1,0:T(8,128)(2,1)S(1)} %get-tuple-element.13.share_ref), channel_id=1, source_target_pairs={{0,64},{64,0},{1,65},{65,1},{2,66},{66,2},{3,67},{67,3},{4,68},{68... | collective-permute-start | bytes 1179656 | tf_op jit(solution)/shard_map/ppermute | solution.py:282
  66.0 0.2 slice.4
  66.1 0.1 reshape.31
  66.2 1.9 %collective-permute-start.2 = (bf16[128,896]{1,0:T(8,128)(2,1)S(1)}, bf16[128,896]{1,0:T(8,128)(2,1)S(1)}, u32[]{:S(2)}, u32[]{:S(2)}) collective-permute-start(bf16[128,896]{1,0:T(8,128)(2,1)S(1)} %reshape.31), channel_id=1, source_target_pairs={{0,24},{8,0},{16,8},{24,16},{1,25},{9,1},{17,9},{25,17},{2,26},{10... | collective-permute-start | bytes 688136 | tf_op jit(solution)/shard_map/ppermute | solution.py:286
  68.2 3.7 %collective-permute-start.1 = (bf16[128,896]{1,0:T(8,128)(2,1)S(1)}, bf16[128,896]{1,0:T(8,128)(2,1)}, u32[]{:S(2)}, u32[]{:S(2)}) collective-permute-start(bf16[128,896]{1,0:T(8,128)(2,1)S(1)} %reshape.31), channel_id=1, source_target_pairs={{0,16},{8,24},{16,0},{24,8},{1,17},{9,25},{17,1},{25,9},{2,18},{10... | collective-permute-start | bytes 688136 | tf_op jit(solution)/shard_map/ppermute | solution.py:286
  71.9 3.4 %collective-permute-start = (bf16[128,896]{1,0:T(8,128)(2,1)S(1)}, bf16[128,896]{1,0:T(8,128)(2,1)}, u32[]{:S(2)}, u32[]{:S(2)}) collective-permute-start(bf16[128,896]{1,0:T(8,128)(2,1)S(1)} %reshape.31), channel_id=1, source_target_pairs={{0,8},{8,16},{16,24},{24,0},{1,9},{9,17},{17,25},{25,1},{2,10},{10... | collective-permute-start | bytes 688136 | tf_op jit(solution)/shard_map/ppermute | solution.py:286
  75.2 0.0 collective-permute-done.3.received_ref
  75.2 1.5 weight_grad.1
  76.7 7.2 %all-to-all-start.1 = ((bf16[64,2,3456]{2,1,0:T(2,128)(2,1)}), bf16[64,2,3456]{2,1,0:T(2,128)(2,1)S(1)}, u32[]{:S(2)}, u32[]{:S(2)}) async-start(bf16[64,2,3456]{2,1,0:T(2,128)(2,1)} %weight_grad.1), calls=%async_computation.1 | async-start | bytes 1769472 | tf_op jit(solution)/shard_map/all_to_all | solution.py:278
  83.9 0.0 collective-permute-done.2
  84.0 0.0 copy-start
  84.0 0.0 collective-permute-done.1
  84.0 1.1 collective-permute-done
  85.1 0.0 copy-done
  85.1 1.3 pad_maximum_fusion.mine_ref
  86.4 1.9 %collective-permute-start.4 = (bf16[4,128,896]{2,1,0:T(8,128)(2,1)S(1)}, bf16[4,128,896]{2,1,0:T(8,128)(2,1)}, u32[]{:S(2)}, u32[]{:S(2)}) collective-permute-start(bf16[4,128,896]{2,1,0:T(8,128)(2,1)S(1)} %pad_maximum_fusion.mine_ref), channel_id=1, source_target_pairs={{0,64},{64,0},{1,65},{65,1},{2,66},{66,2},{3,67},{67,3},{4,68},{68... | collective-permute-start | bytes 2752520 | tf_op jit(solution)/shard_map/ppermute | solution.py:282
  88.3 2.6 %collective-permute-done.4.theirs_ref = bf16[4,128,896]{2,1,0:T(8,128)(2,1)} collective-permute-done((bf16[4,128,896]{2,1,0:T(8,128)(2,1)S(1)}, bf16[4,128,896]{2,1,0:T(8,128)(2,1)}, u32[]{:S(2)}, u32[]{:S(2)}) %collective-permute-start.4) | collective-permute-done | bytes 917536 | tf_op jit(solution)/shard_map/ppermute | solution.py:282
  90.9 6.4 %backward.1 = bf16[64,2,4224]{2,1,0:T(2,128)(2,1)} custom-call(s32[1]{0:T(128)} %bitcast.core_ref, s32[1]{0:T(128)} %bitcast.1.x_ref, bf16[64,2,5120]{2,1,0:T(2,128)(2,1)S(1)} %all_to_all.15.sent_ref, bf16[4,128,896]{2,1,0:T(8,128)(2,1)S(1)} %pad_maximum_fusion.mine_ref, bf16[4,128,896]{2,1,0:T(8,128)(2,1)} %collective-permute-done.4.theirs_ref), custom_call_target="tpu_custom_call" | custom-call | flops 7000000000 | bytes 21000000 | tf_op jit(solution)/shard_map/backward/pallas_call | solution.py:263
  97.3 17.5 %all-to-all-done.1.terms_ref = bf16[64,2,3456]{2,1,0:T(2,128)(2,1)S(1)} async-done(((bf16[64,2,3456]{2,1,0:T(2,128)(2,1)}), bf16[64,2,3456]{2,1,0:T(2,128)(2,1)S(1)}, u32[]{:S(2)}, u32[]{:S(2)}) %all-to-all-start.1) | async-done | bytes 884768 | tf_op jit(solution)/shard_map/all_to_all | solution.py:278
  114.8 5.1 %all-to-all-start.2 = ((bf16[64,2,4224]{2,1,0:T(2,128)(2,1)}), bf16[64,2,4224]{2,1,0:T(2,128)(2,1)S(1)}, u32[]{:S(2)}, u32[]{:S(2)}) async-start(bf16[64,2,4224]{2,1,0:T(2,128)(2,1)} %backward.1), calls=%async_computation.2 | async-start | bytes 2162688 | tf_op jit(solution)/shard_map/all_to_all | solution.py:278
  120.0 0.2 owned.1.refs_0_
  120.2 1.9 %collective-permute-start.7 = (f32[2,3456]{1,0:T(2,128)S(1)}, f32[2,3456]{1,0:T(2,128)S(1)}, u32[]{:S(2)}, u32[]{:S(2)}) collective-permute-start(f32[2,3456]{1,0:T(2,128)S(1)} %owned.1.refs_0_), channel_id=1, source_target_pairs={{0,384},{128,0},{256,128},{384,256},{1,385},{129,1},{257,129},{385... | collective-permute-start | bytes 82952 | tf_op jit(solution)/shard_map/ppermute | solution.py:286
  122.1 3.1 %collective-permute-start.6 = (f32[2,3456]{1,0:T(2,128)S(1)}, f32[2,3456]{1,0:T(2,128)S(1)}, u32[]{:S(2)}, u32[]{:S(2)}) collective-permute-start(f32[2,3456]{1,0:T(2,128)S(1)} %owned.1.refs_0_), channel_id=1, source_target_pairs={{0,256},{128,384},{256,0},{384,128},{1,257},{129,385},{257,1},{385... | collective-permute-start | bytes 82952 | tf_op jit(solution)/shard_map/ppermute | solution.py:286
  125.2 3.5 %collective-permute-start.5 = (f32[2,3456]{1,0:T(2,128)S(1)}, f32[2,3456]{1,0:T(2,128)S(1)}, u32[]{:S(2)}, u32[]{:S(2)}) collective-permute-start(f32[2,3456]{1,0:T(2,128)S(1)} %owned.1.refs_0_), channel_id=1, source_target_pairs={{0,128},{128,256},{256,384},{384,0},{1,129},{129,257},{257,385},{3... | collective-permute-start | bytes 82952 | tf_op jit(solution)/shard_map/ppermute | solution.py:286
  128.7 15.2 %collective-permute-done.7.refs_3_ = f32[2,3456]{1,0:T(2,128)S(1)} collective-permute-done((f32[2,3456]{1,0:T(2,128)S(1)}, f32[2,3456]{1,0:T(2,128)S(1)}, u32[]{:S(2)}, u32[]{:S(2)}) %collective-permute-start.7) | collective-permute-done | bytes 27680 | tf_op jit(solution)/shard_map/ppermute | solution.py:286
  143.9 0.0 collective-permute-done.6.refs_2_
  143.9 0.0 collective-permute-done.5.refs_1_
  143.9 1.9 %collective-permute-start.8 = (f32[2,3456]{1,0:T(2,128)S(1)}, f32[2,3456]{1,0:T(2,128)S(1)}, u32[]{:S(2)}, u32[]{:S(2)}) collective-permute-start(f32[2,3456]{1,0:T(2,128)S(1)} %group.1.mine_ref), channel_id=1, source_target_pairs={{0,64},{64,0},{1,65},{65,1},{2,66},{66,2},{3,67},{67,3},{4,68},{68... | collective-permute-start | bytes 82952 | tf_op jit(solution)/shard_map/ppermute | solution.py:282
  145.8 1.2 collective-permute-done.8.theirs_ref
  147.0 0.7 total.1
  147.6 7.5 %all-to-all-done.2.back_ref = bf16[64,2,4224]{2,1,0:T(2,128)(2,1)S(1)} async-done(((bf16[64,2,4224]{2,1,0:T(2,128)(2,1)}), bf16[64,2,4224]{2,1,0:T(2,128)(2,1)S(1)}, u32[]{:S(2)}, u32[]{:S(2)}) %all-to-all-start.2) | async-done | bytes 1081376 | tf_op jit(solution)/shard_map/all_to_all | solution.py:278
  155.2 1.1 unpack.1
  (1 shorter events, 0.0 us)
Async XLA Ops:
  64.0 11.2 %collective-permute-start.3 = (bf16[128,1536]{1,0:T(8,128)(2,1)S(1)}, bf16[128,1536]{1,0:T(8,128)(2,1)S(1)}, u32[]{:S(2)}, u32[]{:S(2)}) collective-permute-start(bf16[128,1536]{1,0:T(8,128)(2,1)S(1)} %get-tuple-element.13.share_ref), channel_id=1, source_target_pairs={{0,64},{64,0},{1,65},{65,1},{2,66},{66,2},{3,67},{67,3},{4,68},{68... | collective-permute-start | bytes 1179656 | tf_op jit(solution)/shard_map/ppermute | solution.py:282
  66.2 17.7 %collective-permute-start.2 = (bf16[128,896]{1,0:T(8,128)(2,1)S(1)}, bf16[128,896]{1,0:T(8,128)(2,1)S(1)}, u32[]{:S(2)}, u32[]{:S(2)}) collective-permute-start(bf16[128,896]{1,0:T(8,128)(2,1)S(1)} %reshape.31), channel_id=1, source_target_pairs={{0,24},{8,0},{16,8},{24,16},{1,25},{9,1},{17,9},{25,17},{2,26},{10... | collective-permute-start | bytes 688136 | tf_op jit(solution)/shard_map/ppermute | solution.py:286
  68.2 15.8 %collective-permute-start.1 = (bf16[128,896]{1,0:T(8,128)(2,1)S(1)}, bf16[128,896]{1,0:T(8,128)(2,1)}, u32[]{:S(2)}, u32[]{:S(2)}) collective-permute-start(bf16[128,896]{1,0:T(8,128)(2,1)S(1)} %reshape.31), channel_id=1, source_target_pairs={{0,16},{8,24},{16,0},{24,8},{1,17},{9,25},{17,1},{25,9},{2,18},{10... | collective-permute-start | bytes 688136 | tf_op jit(solution)/shard_map/ppermute | solution.py:286
  71.9 13.2 %collective-permute-start = (bf16[128,896]{1,0:T(8,128)(2,1)S(1)}, bf16[128,896]{1,0:T(8,128)(2,1)}, u32[]{:S(2)}, u32[]{:S(2)}) collective-permute-start(bf16[128,896]{1,0:T(8,128)(2,1)S(1)} %reshape.31), channel_id=1, source_target_pairs={{0,8},{8,16},{16,24},{24,0},{1,9},{9,17},{17,25},{25,1},{2,10},{10... | collective-permute-start | bytes 688136 | tf_op jit(solution)/shard_map/ppermute | solution.py:286
  76.7 38.1 %all-to-all-start.1 = ((bf16[64,2,3456]{2,1,0:T(2,128)(2,1)}), bf16[64,2,3456]{2,1,0:T(2,128)(2,1)S(1)}, u32[]{:S(2)}, u32[]{:S(2)}) async-start(bf16[64,2,3456]{2,1,0:T(2,128)(2,1)} %weight_grad.1), calls=%async_computation.1 | async-start | bytes 1769472 | tf_op jit(solution)/shard_map/all_to_all | solution.py:278
  84.0 1.1 copy-start
  86.4 4.5 %collective-permute-start.4 = (bf16[4,128,896]{2,1,0:T(8,128)(2,1)S(1)}, bf16[4,128,896]{2,1,0:T(8,128)(2,1)}, u32[]{:S(2)}, u32[]{:S(2)}) collective-permute-start(bf16[4,128,896]{2,1,0:T(8,128)(2,1)S(1)} %pad_maximum_fusion.mine_ref), channel_id=1, source_target_pairs={{0,64},{64,0},{1,65},{65,1},{2,66},{66,2},{3,67},{67,3},{4,68},{68... | collective-permute-start | bytes 2752520 | tf_op jit(solution)/shard_map/ppermute | solution.py:282
  114.8 40.3 %all-to-all-start.2 = ((bf16[64,2,4224]{2,1,0:T(2,128)(2,1)}), bf16[64,2,4224]{2,1,0:T(2,128)(2,1)S(1)}, u32[]{:S(2)}, u32[]{:S(2)}) async-start(bf16[64,2,4224]{2,1,0:T(2,128)(2,1)} %backward.1), calls=%async_computation.2 | async-start | bytes 2162688 | tf_op jit(solution)/shard_map/all_to_all | solution.py:278
  120.2 23.6 %collective-permute-start.7 = (f32[2,3456]{1,0:T(2,128)S(1)}, f32[2,3456]{1,0:T(2,128)S(1)}, u32[]{:S(2)}, u32[]{:S(2)}) collective-permute-start(f32[2,3456]{1,0:T(2,128)S(1)} %owned.1.refs_0_), channel_id=1, source_target_pairs={{0,384},{128,0},{256,128},{384,256},{1,385},{129,1},{257,129},{385... | collective-permute-start | bytes 82952 | tf_op jit(solution)/shard_map/ppermute | solution.py:286
  122.1 21.7 %collective-permute-start.6 = (f32[2,3456]{1,0:T(2,128)S(1)}, f32[2,3456]{1,0:T(2,128)S(1)}, u32[]{:S(2)}, u32[]{:S(2)}) collective-permute-start(f32[2,3456]{1,0:T(2,128)S(1)} %owned.1.refs_0_), channel_id=1, source_target_pairs={{0,256},{128,384},{256,0},{384,128},{1,257},{129,385},{257,1},{385... | collective-permute-start | bytes 82952 | tf_op jit(solution)/shard_map/ppermute | solution.py:286
  125.2 18.6 %collective-permute-start.5 = (f32[2,3456]{1,0:T(2,128)S(1)}, f32[2,3456]{1,0:T(2,128)S(1)}, u32[]{:S(2)}, u32[]{:S(2)}) collective-permute-start(f32[2,3456]{1,0:T(2,128)S(1)} %owned.1.refs_0_), channel_id=1, source_target_pairs={{0,128},{128,256},{256,384},{384,0},{1,129},{129,257},{257,385},{3... | collective-permute-start | bytes 82952 | tf_op jit(solution)/shard_map/ppermute | solution.py:286
  143.9 3.1 %collective-permute-start.8 = (f32[2,3456]{1,0:T(2,128)S(1)}, f32[2,3456]{1,0:T(2,128)S(1)}, u32[]{:S(2)}, u32[]{:S(2)}) collective-permute-start(f32[2,3456]{1,0:T(2,128)S(1)} %group.1.mine_ref), channel_id=1, source_target_pairs={{0,64},{64,0},{1,65},{65,1},{2,66},{66,2},{3,67},{67,3},{4,68},{68... | collective-permute-start | bytes 82952 | tf_op jit(solution)/shard_map/ppermute | solution.py:282
